TPU v7x, 32 devices: a whole 2x2x4 slice. The times are simulated.
32 devices in a mesh: row: 4 (over z), col: 8 (over y, x, core).
Axes of the slice: x: 2, y: 2, z: 4, core: 2. Of those that a mesh axis runs over, the one named last changes fastest.
Arguments:
- obj: float32 [2, 1024, 2048], P(None, 'row', 'col'), may hold values from -4.2 to 4.2
- probe: float32 [2, 256, 256], replicated, may hold values from -4.2 to 4.2
- amplitudes: bfloat16 [128, 256, 256], P(('row', 'col')), may hold values from 0.049804688 to 4
- positions: int32 [128, 2], replicated, may hold values from 0 to 1792, as said below
Outputs:
- new_object: float32 [2, 1024, 2048], P(None, 'row', 'col')
- new_probe: float32 [2, 256, 256], replicated
Inputs may be any that keep to these rules, and one draw needn't show every extreme that they name: `positions`: entry p is the top-left cell (row, column) of pattern p's window of 256 x 256 cells, which lies inside the object. Pattern p is held by device p // 4 in row-major order of (row, col), and its row offset lies in that device's band of 256 object rows. One device holds at most 2 patterns whose window starts in one tile, and exactly 2 for some tile in every draw; at most 8 windows start in one tile, and in every row of tiles exactly 8 start in one tile.
All inputs are finite; a program needn't handle non-finite values.
Results may differ from a plain program's by a relative error of at most 0.0018.
Values may be sent and summed in bfloat16 or wider, within the bound.
No kernel may reach another device: no remote copies, remote signals or barrier semaphores. Data moves between devices by JAX's collectives and lax.ppermute only.
A program may use at most 128 MiB of HBM per device.

v0:
```python
import jax
import jax.numpy as jnp
from jax import lax
from jax.sharding import PartitionSpec as P

ITERS = 2
SEND = 2


amplitude_floor = 0.1
object_regular = 0.5
probe_regular = 1.0
highest = lax.Precision.HIGHEST


def passed_along(value, axis, steps):
    count = lax.axis_size(axis)
    leading, last = (max(0, -steps), min(count, count - steps))
    return lax.ppermute(value, axis, [(source, source + steps) for source in range(leading, last)])


def dft_tables(order):
    counter = jnp.arange(order, dtype=jnp.int32)
    phases = counter[:, None] * counter[None, :] % order
    angles = phases.astype(jnp.float32) * (2.0 * jnp.pi / order)
    norming = 1.0 / jnp.sqrt(jnp.float32(order))
    return (jnp.cos(angles) * norming, -jnp.sin(angles) * norming)


def left_apply(tables, real_part, imag_part):
    first = jnp.einsum("ab,sbc->sac", tables[0], real_part, precision=highest)
    second = jnp.einsum("ab,sbc->sac", tables[1], imag_part, precision=highest)
    third = jnp.einsum("ab,sbc->sac", tables[2], real_part + imag_part, precision=highest)
    return (first - second, third - first - second)


def right_apply(tables, real_part, imag_part):
    first = jnp.einsum("sab,bc->sac", real_part, tables[0], precision=highest)
    second = jnp.einsum("sab,bc->sac", imag_part, tables[1], precision=highest)
    third = jnp.einsum("sab,bc->sac", real_part + imag_part, tables[2], precision=highest)
    return (first - second, third - first - second)


def transform(tables, real_part, imag_part):
    inner_re, inner_im = right_apply(tables, real_part, imag_part)
    return left_apply(tables, inner_re, inner_im)


def extend_tile(current):
    from_right = passed_along(current, "col", -1)
    widened = jnp.concatenate([current, from_right], axis=2)
    from_below = passed_along(widened, "row", -1)
    return jnp.concatenate([widened, from_below], axis=1)


def fold_tile(sums, tile_rows, tile_cols, order):
    from_above = passed_along(sums[:, tile_rows:, :], "row", 1)
    upper = sums[:, :tile_rows, :].at[:, :order, :].add(from_above)
    from_left = passed_along(upper[:, :, tile_cols:], "col", 1)
    return upper[:, :, :tile_cols].at[:, :, :order].add(from_left)


def local(obj, probe, amplitudes, positions):
    col_count = lax.axis_size("col")
    my_row = lax.axis_index("row")
    my_col = lax.axis_index("col")
    device_id = my_row * col_count + my_col
    tile_rows = obj.shape[1]
    tile_cols = obj.shape[2]
    order = probe.shape[1]
    pat_count = amplitudes.shape[0]
    capacity = 2 * pat_count
    slot_count = col_count * SEND
    band_count = col_count * pat_count
    local_index = jnp.arange(pat_count, dtype=jnp.int32)
    my_ids = device_id * pat_count + local_index
    owner_col = positions[my_ids, 1] // tile_cols
    earlier = local_index[None, :] < local_index[:, None]
    same_owner = owner_col[:, None] == owner_col[None, :]
    send_rank = jnp.sum(same_owner & earlier, axis=1)
    send_slot = owner_col * SEND + send_rank
    placing = (jnp.arange(slot_count, dtype=jnp.int32)[:, None] == send_slot[None, :]).astype(
        jnp.bfloat16
    )
    outgoing = jnp.dot(
        placing, amplitudes.reshape(pat_count, order * order), preferred_element_type=jnp.float32
    ).astype(jnp.bfloat16)
    incoming = lax.all_to_all(outgoing, "col", split_axis=0, concat_axis=0, tiled=True)
    band_first = my_row * band_count
    band_pos = lax.dynamic_slice_in_dim(positions, band_first, band_count, 0)
    band_ids = band_first + jnp.arange(band_count, dtype=jnp.int32)
    in_mine = band_pos[:, 1] // tile_cols == my_col
    mine_count = in_mine.astype(jnp.int32)
    band_rank = jnp.cumsum(mine_count) - mine_count
    selection = (band_rank[None, :] == jnp.arange(capacity, dtype=jnp.int32)[:, None]) & in_mine[
        None, :
    ]
    valid = jnp.any(selection, axis=1)
    listed = jnp.sum(jnp.where(selection, band_ids[None, :], 0), axis=1)
    source_dev = listed // pat_count
    source_col = source_dev % col_count
    before = (
        (source_dev[None, :] == source_dev[:, None])
        & (listed[None, :] < listed[:, None])
        & valid[None, :]
    )
    recv_rank = jnp.sum(before, axis=1)
    recv_slot = source_col * SEND + recv_rank
    picking = (
        (jnp.arange(slot_count, dtype=jnp.int32)[None, :] == recv_slot[:, None]) & valid[:, None]
    ).astype(jnp.bfloat16)
    measured = jnp.dot(picking, incoming, preferred_element_type=jnp.float32).reshape(
        capacity, order, order
    )
    spots = positions[listed]
    offset_y = jnp.where(valid, spots[:, 0] - my_row * tile_rows, 0)
    offset_x = jnp.where(valid, spots[:, 1] - my_col * tile_cols, 0)
    weight = valid.astype(jnp.float32)[:, None, None]
    cos_part, sin_part = dft_tables(order)
    forward = (cos_part, sin_part, cos_part + sin_part)
    inverse = (cos_part, -sin_part, cos_part - sin_part)
    current = obj
    probe_now = probe
    for sweep in range(ITERS):
        extended = extend_tile(current)

        def cut_window(top, left):
            return lax.dynamic_slice(extended, (0, top, left), (2, order, order))

        windows = jax.vmap(cut_window)(offset_y, offset_x)
        win_re = windows[:, 0]
        win_im = windows[:, 1]
        probe_re = probe_now[0]
        probe_im = probe_now[1]
        exit_re = probe_re * win_re - probe_im * win_im
        exit_im = probe_re * win_im + probe_im * win_re
        far_re, far_im = transform(forward, exit_re, exit_im)
        factor = measured / jnp.sqrt(far_re * far_re + far_im * far_im + amplitude_floor)
        back_re, back_im = transform(inverse, far_re * factor, far_im * factor)
        change_re = (back_re - exit_re) * weight
        change_im = (back_im - exit_im) * weight
        power = probe_re * probe_re + probe_im * probe_im
        deposits = jnp.stack(
            [
                probe_re * change_re + probe_im * change_im,
                probe_re * change_im - probe_im * change_re,
                power[None] * weight + 0.0 * change_re,
            ],
            axis=1,
        )

        def deposit(index, total):
            start = (0, offset_y[index], offset_x[index])
            block = lax.dynamic_slice(total, start, (3, order, order))
            return lax.dynamic_update_slice(total, block + deposits[index], start)

        sums = lax.fori_loop(
            0, capacity, deposit, jnp.zeros((3, tile_rows + order, tile_cols + order), jnp.float32)
        )
        partials = jnp.stack(
            [
                jnp.sum(win_re * change_re + win_im * change_im, axis=0),
                jnp.sum(win_re * change_im - win_im * change_re, axis=0),
                jnp.sum((win_re * win_re + win_im * win_im) * weight, axis=0),
            ]
        )
        tile_sums = fold_tile(sums, tile_rows, tile_cols, order)
        current = current + tile_sums[:2] / (tile_sums[2] + object_regular)[None]
        totals = lax.psum(partials, ("row", "col"))
        probe_now = probe_now + totals[:2] / (totals[2] + probe_regular)[None]
    return (current, probe_now)


def solution(mesh):
    placed = (P(None, "row", "col"), P(), P(("row", "col"), None, None), P())
    return jax.shard_map(
        local, mesh=mesh, in_specs=placed, out_specs=(P(None, "row", "col"), P()), check_vma=False
    )
```

profile of v0, /device:TPU:0, one launch (start us, length us, event | category | flops | bytes accessed | tf_op | source)
XLA Modules:
  0.0 869.3 jit_solution(4662414717978935194)
XLA Ops:
  14.6 6.1 all-to-all-start
  26.2 24.3 %collective-permute-done.1 = f32[2,256,512]{2,1,0:T(8,128)} collective-permute-done((f32[2,256,512]{2,1,0:T(8,128)S(1)}, f32[2,256,512]{2,1,0:T(8,128)}, u32[]{:S(2)}, u32[]{:S(2)}) %collective-permute-start.1) | collective-permute-done | bytes 1048608 | tf_op jit(solution)/shard_map/ppermute | solution.py:19
  54.4 24.5 %while.38 = (s32[]{:T(128)}, f32[2,512,512]{2,1,0:T(8,128)S(1)}, s32[8,3]{0,1:T(4,128)S(1)}, f32[8,2,256,256]{2,3,0,1:T(8,128)}, s32[]{:T(128)}) while((s32[]{:T(128)}, f32[2,512,512]{2,1,0:T(8,128)S(1)}, s32[8,3]{0,1:T(4,128)S(1)}, f32[8,2,256,256]{2,3,0,1:T(8,128)}, s32[]{:T(128)}) %tuple.156), condition=%wide.while_cond.4, body=%wide.while_body.4.sunk | while | flops 2 | bytes 3146353 | solution.py:128
  95.6 5.7 fusion.112
  101.3 5.6 fusion.79
  116.4 12.4 %fusion.48 = (f32[8,256,256]{1,2,0:T(8,128)S(1)}, f32[8,256,256]{1,2,0:T(8,128)S(1)}) fusion(f32[8,256,256]{1,2,0:T(8,128)} %copy.167, f32[8,256,256]{2,1,0:T(8,128)} %fusion.112, f32[8,256,256]{2,1,0:T(8,128)} %fusion.79, f32[8,256,256]{2,1,0:T(8,128)} %copy-done.9, f32[8,256,256]{2,1,0:T(8,128)} %copy-done.4, f32[8,256,256]{2,1,0:T(8,128)} %copy-done.3), kind=kOutput, calls=%fused_computation.104 | convolution fusion | flops 1618083840 | bytes 16777216 | tf_op jit(solution)/shard_map/ab,sbc->sac/dot_general | solution.py:33
  151.6 6.5 fusion.27
  164.3 133.8 %while.36 = (s32[]{:T(128)}, f32[3,512,512]{2,1,0:T(8,128)}, s32[8]{0:T(128)S(1)}, s32[8]{0:T(128)S(1)}, f32[8,3,256,256]{2,3,0,1:T(8,128)}, /*index=5*/s32[]{:T(128)}, s32[]{:T(128)}, s32[]{:T(128)}) while((s32[]{:T(128)}, f32[3,512,512]{2,1,0:T(8,128)}, s32[8]{0:T(128)S(1)}, s32[8]{0:T(128)S(1)}, f32[8,3,256,256]{2,3,0,1:T(8,128)}, ...), condition=%wide.region_6.7_spmd, body=%wide.region_5.6_spmd.sunk | while | flops 196616 | bytes 7078081 | solution.py:157
  172.4 8.7 dynamic_update_slice.16
  189.2 9.3 %dynamic_update_slice.16 = f32[3,512,512]{2,1,0:T(8,128)} dynamic-update-slice(f32[3,512,512]{2,1,0:T(8,128)} %get-tuple-element.589, f32[3,256,256]{2,1,0:T(8,128)S(1)} %bitcast_add_fusion.4, s32[]{:T(128)} %constant.268.clone.1..sunk, s32[]{:T(128)S(6)} %select_n.360, s32[]{:T(128)S(6)} %select_n.361) | dynamic-update-slice | bytes 1572868 | tf_op jit(solution)/shard_map/while/body/eval_jaxpr/dynamic_update_slice | solution.py:155
  206.6 9.2 %dynamic_update_slice.16 = f32[3,512,512]{2,1,0:T(8,128)} dynamic-update-slice(f32[3,512,512]{2,1,0:T(8,128)} %get-tuple-element.589, f32[3,256,256]{2,1,0:T(8,128)S(1)} %bitcast_add_fusion.4, s32[]{:T(128)} %constant.268.clone.1..sunk, s32[]{:T(128)S(6)} %select_n.360, s32[]{:T(128)S(6)} %select_n.361) | dynamic-update-slice | bytes 1572868 | tf_op jit(solution)/shard_map/while/body/eval_jaxpr/dynamic_update_slice | solution.py:155
  224.0 8.3 dynamic_update_slice.16
  240.4 8.3 dynamic_update_slice.16
  256.9 8.3 dynamic_update_slice.16
  273.3 8.3 dynamic_update_slice.16
  289.8 8.3 dynamic_update_slice.16
  303.4 33.1 %collective-permute-done.2 = f32[3,256,512]{2,1,0:T(8,128)S(1)} collective-permute-done((f32[3,256,512]{2,1,0:T(8,128)S(1)}, f32[3,256,512]{2,1,0:T(8,128)S(1)}, u32[]{:S(2)}, u32[]{:S(2)}) %collective-permute-start.2) | collective-permute-done | bytes 1572896 | tf_op jit(solution)/shard_map/ppermute | solution.py:19
  343.0 11.4 %collective-permute-done.4 = f32[2,256,256]{2,1,0:T(8,128)S(1)} collective-permute-done((f32[2,256,256]{2,1,0:T(8,128)S(1)}, f32[2,256,256]{2,1,0:T(8,128)S(1)}, u32[]{:S(2)}, u32[]{:S(2)}) %collective-permute-start.4) | collective-permute-done | bytes 524320 | tf_op jit(solution)/shard_map/ppermute | solution.py:19
  356.6 129.5 %all-reduce.4.cloned.1.call-done = f32[3,256,256]{1,2,0:T(8,128)} async-done(((f32[3,256,256]{1,2,0:T(8,128)}), f32[3,256,256]{1,2,0:T(8,128)}) %all-reduce.4.cloned.1.call-update) | async-done | bytes 786448 | tf_op jit(solution)/shard_map/psum | solution.py:169
  493.2 26.1 %while.39 = (s32[]{:T(128)}, f32[2,512,512]{2,1,0:T(8,128)S(1)}, s32[8,3]{0,1:T(4,128)S(1)}, f32[8,2,256,256]{2,3,0,1:T(8,128)}, s32[]{:T(128)}) while((s32[]{:T(128)}, f32[2,512,512]{2,1,0:T(8,128)S(1)}, s32[8,3]{0,1:T(4,128)S(1)}, f32[8,2,256,256]{2,3,0,1:T(8,128)}, s32[]{:T(128)}) %tuple.172), condition=%wide.while_cond.5, body=%wide.while_body.5.sunk | while | flops 2 | bytes 3146353 | solution.py:128
  573.4 6.9 fusion.12
  586.5 130.0 %while.37 = (s32[]{:T(128)}, f32[3,512,512]{2,1,0:T(8,128)}, s32[8]{0:T(128)S(1)}, s32[8]{0:T(128)S(1)}, f32[8,3,256,256]{2,3,0,1:T(8,128)}, /*index=5*/s32[]{:T(128)}, s32[]{:T(128)}, s32[]{:T(128)}) while((s32[]{:T(128)}, f32[3,512,512]{2,1,0:T(8,128)}, s32[8]{0:T(128)S(1)}, s32[8]{0:T(128)S(1)}, f32[8,3,256,256]{2,3,0,1:T(8,128)}, ...), condition=%wide.region_12.13_spmd, body=%wide.region_11.12_spmd.sunk | while | flops 196616 | bytes 7078081 | solution.py:157
  594.2 8.7 dynamic_update_slice.17
  610.5 9.3 %dynamic_update_slice.17 = f32[3,512,512]{2,1,0:T(8,128)} dynamic-update-slice(f32[3,512,512]{2,1,0:T(8,128)} %get-tuple-element.628, f32[3,256,256]{2,1,0:T(8,128)S(1)} %bitcast_add_fusion.5, s32[]{:T(128)} %constant.268.clone.1..sunk.1, s32[]{:T(128)S(6)} %select_n.362, s32[]{:T(128)S(6)} %select_n.363) | dynamic-update-slice | bytes 1572868 | tf_op jit(solution)/shard_map/while/body/eval_jaxpr/dynamic_update_slice | solution.py:155
  627.4 9.2 %dynamic_update_slice.17 = f32[3,512,512]{2,1,0:T(8,128)} dynamic-update-slice(f32[3,512,512]{2,1,0:T(8,128)} %get-tuple-element.628, f32[3,256,256]{2,1,0:T(8,128)S(1)} %bitcast_add_fusion.5, s32[]{:T(128)} %constant.268.clone.1..sunk.1, s32[]{:T(128)S(6)} %select_n.362, s32[]{:T(128)S(6)} %select_n.363) | dynamic-update-slice | bytes 1572868 | tf_op jit(solution)/shard_map/while/body/eval_jaxpr/dynamic_update_slice | solution.py:155
  644.3 8.3 dynamic_update_slice.17
  660.2 8.3 dynamic_update_slice.17
  676.2 8.3 dynamic_update_slice.17
  692.2 8.3 dynamic_update_slice.17
  708.2 8.3 dynamic_update_slice.17
  724.8 33.0 %collective-permute-done.6 = f32[3,256,512]{2,1,0:T(8,128)} collective-permute-done((f32[3,256,512]{2,1,0:T(8,128)}, f32[3,256,512]{2,1,0:T(8,128)}, u32[]{:S(2)}, u32[]{:S(2)}) %collective-permute-start.6) | collective-permute-done | bytes 1572896 | tf_op jit(solution)/shard_map/ppermute | solution.py:19
  763.1 93.9 %all-reduce.6.cloned.1.call-done = f32[3,256,256]{1,2,0:T(8,128)} async-done(((f32[3,256,256]{1,2,0:T(8,128)}), f32[3,256,256]{1,2,0:T(8,128)}) %all-reduce.6.cloned.1.call-update) | async-done | bytes 786448 | tf_op jit(solution)/shard_map/psum | solution.py:169
  (328 shorter events, 289.2 us)
Async XLA Ops:
  7.2 15.4 %collective-permute-start = (f32[2,256,256]{2,1,0:T(8,128)}, f32[2,256,256]{2,1,0:T(8,128)S(1)}, u32[]{:S(2)}, u32[]{:S(2)}) collective-permute-start(f32[2,256,256]{2,1,0:T(8,128)} %param.24), channel_id=1, source_target_pairs={{1,0},{2,1},{3,2},{4,3},{5,4},{6,5},{7,6},{9,8},{10,9},{11,10},{12... | collective-permute-start | bytes 1572872 | tf_op jit(solution)/shard_map/ppermute | solution.py:19
  14.6 6.1 copy-start
  14.6 7.7 copy-start.19
  14.6 92.4 %all-to-all-start = ((bf16[8,2,65536]{2,1,0:T(2,128)(2,1)}), bf16[8,2,65536]{2,1,0:T(2,128)(2,1)}, u32[]{:S(2)}, u32[]{:S(2)}) async-start(bf16[8,2,65536]{2,1,0:T(2,128)(2,1)} %all_to_all.8), calls=%async_computation | async-start | bytes 4194304 | tf_op jit(solution)/shard_map/all_to_all | solution.py:88
  20.6 465.4 %all-reduce.4.cloned.1.call-start = ((), (), s32[]{:S(2)}) async-start(), calls=%async_computation.1 | async-start | bytes 1572864 | tf_op jit(solution)/shard_map/psum | solution.py:169
  22.6 27.9 %collective-permute-start.1 = (f32[2,256,512]{2,1,0:T(8,128)S(1)}, f32[2,256,512]{2,1,0:T(8,128)}, u32[]{:S(2)}, u32[]{:S(2)}) collective-permute-start(f32[2,256,512]{2,1,0:T(8,128)S(1)} %constant_dynamic-update-slice_fusion.2), channel_id=1, source_target_pairs={{8,0},{16,8},{24,16},{9,1},{17,9},{25,17},{10,2},{18,10},{26,18},{... | collective-permute-start | bytes 3145736 | tf_op jit(solution)/shard_map/ppermute | solution.py:19
  81.7 8.9 %copy-start.1 = (f32[8,256,256]{1,2,0:T(8,128)}, f32[8,256,256]{1,2,0:T(8,128)S(1)}, u32[]{:S(2)}) copy-start(f32[8,256,256]{1,2,0:T(8,128)S(1)} %get-tuple-element.427) | copy-start | bytes 6291460
  86.2 15.1 %copy-start.3 = (f32[8,256,256]{2,1,0:T(8,128)}, f32[8,256,256]{2,1,0:T(8,128)S(1)}, u32[]{:S(2)}) copy-start(f32[8,256,256]{2,1,0:T(8,128)S(1)} %fusion.114) | copy-start | bytes 6291460
  90.6 10.7 %copy-start.4 = (f32[8,256,256]{2,1,0:T(8,128)}, f32[8,256,256]{2,1,0:T(8,128)S(1)}, u32[]{:S(2)}) copy-start(f32[8,256,256]{2,1,0:T(8,128)S(1)} %fusion.126) | copy-start | bytes 6291460
  95.6 5.7 copy-start.9
  142.4 9.1 %copy-start.7 = (f32[8,2,256,256]{2,3,0,1:T(8,128)S(1)}, f32[8,2,256,256]{2,3,0,1:T(8,128)}, u32[]{:S(2)}) copy-start(f32[8,2,256,256]{2,3,0,1:T(8,128)} %get-tuple-element.279) | copy-start | bytes 12582916
  151.6 6.5 copy-start.18
  151.6 6.5 copy-start.28
  298.1 38.4 %copy-start.6 = (f32[3,512,512]{2,1,0:T(8,128)S(1)}, f32[3,512,512]{2,1,0:T(8,128)}, u32[]{:S(2)}) copy-start(f32[3,512,512]{2,1,0:T(8,128)} %get-tuple-element.270) | copy-start | bytes 9437188
  299.8 36.8 %collective-permute-start.2 = (f32[3,256,512]{2,1,0:T(8,128)S(1)}, f32[3,256,512]{2,1,0:T(8,128)S(1)}, u32[]{:S(2)}, u32[]{:S(2)}) collective-permute-start(f32[3,256,512]{2,1,0:T(8,128)S(1)} %slice.165), channel_id=1, source_target_pairs={{0,8},{8,16},{16,24},{1,9},{9,17},{17,25},{2,10},{10,18},{18,26},{... | collective-permute-start | bytes 4718600 | tf_op jit(solution)/shard_map/ppermute | solution.py:19
  337.0 3.3 collective-permute-start.3
  340.6 148.6 %copy-start.11 = (f32[2,256,256]{2,1,0:T(8,128)}, f32[2,256,256]{2,1,0:T(8,128)S(1)}, u32[]{:S(2)}) copy-start(f32[2,256,256]{2,1,0:T(8,128)S(1)} %fusion.84) | copy-start | bytes 1572868
  340.6 13.7 %collective-permute-start.4 = (f32[2,256,256]{2,1,0:T(8,128)S(1)}, f32[2,256,256]{2,1,0:T(8,128)S(1)}, u32[]{:S(2)}, u32[]{:S(2)}) collective-permute-start(f32[2,256,256]{2,1,0:T(8,128)S(1)} %fusion.84), channel_id=1, source_target_pairs={{1,0},{2,1},{3,2},{4,3},{5,4},{6,5},{7,6},{9,8},{10,9},{11,10},{12... | collective-permute-start | bytes 1572872 | tf_op jit(solution)/shard_map/ppermute | solution.py:19
  341.9 14.5 %copy-start.22 = (f32[2,256,256]{2,1,0:T(8,128)S(1)}, f32[2,256,256]{2,1,0:T(8,128)}, u32[]{:S(2)}) copy-start(f32[2,256,256]{2,1,0:T(8,128)} %param.25) | copy-start | bytes 1572868
  342.9 514.0 %all-reduce.6.cloned.1.call-start = ((), (), s32[]{:S(2)}) async-start(), calls=%async_computation.2 | async-start | bytes 1572864 | tf_op jit(solution)/shard_map/psum | solution.py:169
  355.1 134.1 %collective-permute-start.5 = (f32[2,256,512]{2,1,0:T(8,128)S(1)}, f32[2,256,512]{2,1,0:T(8,128)}, u32[]{:S(2)}, u32[]{:S(2)}) collective-permute-start(f32[2,256,512]{2,1,0:T(8,128)S(1)} %pad_maximum_fusion.4), channel_id=1, source_target_pairs={{8,0},{16,8},{24,16},{9,1},{17,9},{25,17},{10,2},{18,10},{26,18},{... | collective-permute-start | bytes 3145736 | tf_op jit(solution)/shard_map/ppermute | solution.py:19
  568.7 4.7 copy-start.8
  573.4 6.9 copy-start.17
  573.4 6.9 copy-start.27
  716.5 7.3 copy-start.24
  716.5 7.3 copy-start.25
  716.5 7.3 copy-start.26
  716.5 41.2 %copy-start.5 = (f32[3,512,512]{2,1,0:T(8,128)S(1)}, f32[3,512,512]{2,1,0:T(8,128)}, u32[]{:S(2)}) copy-start(f32[3,512,512]{2,1,0:T(8,128)} %get-tuple-element.271) | copy-start | bytes 9437188
  719.5 38.3 %collective-permute-start.6 = (f32[3,256,512]{2,1,0:T(8,128)}, f32[3,256,512]{2,1,0:T(8,128)}, u32[]{:S(2)}, u32[]{:S(2)}) collective-permute-start(f32[3,256,512]{2,1,0:T(8,128)} %slice.177), channel_id=1, source_target_pairs={{0,8},{8,16},{16,24},{1,9},{9,17},{17,25},{2,10},{10,18},{18,26},{... | collective-permute-start | bytes 4718600 | tf_op jit(solution)/shard_map/ppermute | solution.py:19
  760.7 97.2 %copy-start.16 = (f32[2,256,256]{1,2,0:T(8,128)S(1)}, f32[2,256,256]{1,2,0:T(8,128)}, u32[]{:S(2)}) copy-start(f32[2,256,256]{1,2,0:T(8,128)} %copy-done.15) | copy-start | bytes 1572868
  760.8 99.3 %copy-start.14 = (f32[3,256,512]{2,1,0:T(8,128)S(1)}, f32[3,256,512]{2,1,0:T(8,128)}, u32[]{:S(2)}) copy-start(f32[3,256,512]{2,1,0:T(8,128)} %copy-done.13) | copy-start | bytes 4718596
  760.8 99.3 %collective-permute-start.7 = (f32[3,256,256]{2,1,0:T(8,128)S(1)}, f32[3,256,256]{2,1,0:T(8,128)}, u32[]{:S(2)}, u32[]{:S(2)}) collective-permute-start(f32[3,256,256]{2,1,0:T(8,128)S(1)} %slice.227), channel_id=1, source_target_pairs={{0,1},{1,2},{2,3},{3,4},{4,5},{5,6},{6,7},{8,9},{9,10},{10,11},{11... | collective-permute-start | bytes 2359304 | tf_op jit(solution)/shard_map/ppermute | solution.py:19
  (8 other events, 21.3 us)
Sparse Core Ops, SparseCore 0:
  343.0 143.0 all-reduce.3
  724.9 131.9 all-reduce.5
where the time goes:
time: 878 us; the launch traced here: 869 us
  waiting for transfers between devices  327 us (37%)
  local copies, waits for them, and re-layouts  261 us (30%)
  matrix products  129 us (15%)
  loops' own time  59.2 us (7%)
  other arithmetic  55.1 us (6%)
  starting transfers between devices  23.1 us (3%)
  between operations  15 us (2%)
    psum x2, waiting for transfers between devices, local(): totals = lax.psum(partials, ('row', 'col'))  223 us
    dynamic_update_slice x16, local copies, waits for them, and re-layouts, deposit(): return lax.dynamic_update_slice(total, block + deposits[index], start)  138 us
    ppermute x8, waiting for transfers between devices, passed_along(): lax.ppermute(value, axis, [(source, source + steps) for source in range(l...  104 us
    another operation x2, loops' own time, local(): lax.fori_loop(0, capacity, deposit, jnp.zeros((3, tile_rows + order, tile...  58.7 us
    gather x80, local copies, waits for them, and re-layouts  50.2 us
    dot_general x4, matrix products, left_apply(): jnp.einsum('ab,sbc->sac', tables[2], real_part + imag_part, precision=hig...  31.3 us
    add x16, other arithmetic, deposit(): return lax.dynamic_update_slice(total, block + deposits[index], start)  25.4 us
    dynamic_slice x32, local copies, waits for them, and re-layouts, deposit(): return lax.dynamic_update_slice(total, block + deposits[index], start)  23.3 us
  transfers between devices with their start and end apart: 11, of which 7 were waited for; matrix products, arithmetic and copies ran while one was open for 9% of the time, Pallas kernels for 0%

commit v1 on v0

v1 whole, which is shorter than its diff:
```python
import functools

import jax
import jax.numpy as jnp
import numpy as np
from jax import lax
from jax.experimental import pallas as pl
from jax.experimental.pallas import tpu as pltpu
from jax.sharding import PartitionSpec as P

ITERS = 2
SEND = 2

amplitude_floor = 0.1
object_regular = 0.5
probe_regular = 1.0

LANES = 128
SUBLANES = 8
CHUNK = 32
VMEM = pl.BlockSpec(memory_space=pltpu.VMEM)
SMEM = pl.BlockSpec(memory_space=pltpu.SMEM)
ANY = pl.BlockSpec(memory_space=pl.ANY)
f32 = jnp.float32
bf16 = jnp.bfloat16


def tables(order):
    half = order // 2
    counter = np.arange(half)
    angles = 2.0 * np.pi * ((counter[:, None] * counter[None, :]) % half) / half
    cos, sin = np.cos(angles), np.sin(angles)
    scale = 1.0 / np.sqrt(order)
    plus = np.block([[cos, sin], [-sin, cos]]) * scale
    minus = np.block([[cos, -sin], [sin, cos]]) * scale

    def halves(matrix):
        high = matrix.astype(jnp.bfloat16)
        low = (matrix - high.astype(np.float64)).astype(jnp.bfloat16)
        return high, low

    plus_high, plus_low = halves(plus)
    minus_high, minus_low = halves(minus)
    along_rows = np.stack(
        [
            np.concatenate([plus_high, plus_high, plus_low], axis=1),
            np.concatenate([minus_high, minus_high, minus_low], axis=1),
        ]
    )
    along_cols = np.stack(
        [
            np.concatenate([minus_high, minus_high, minus_low], axis=0),
            np.concatenate([plus_high, plus_high, plus_low], axis=0),
        ]
    )
    turn = 2.0 * np.pi * counter / order
    twiddle = np.stack([np.cos(turn), -np.sin(turn)]).astype(np.float32)
    twiddle_cols = np.broadcast_to(twiddle[:, None, :], (2, 8, half))
    twiddle_rows = np.broadcast_to(twiddle[:, :, None], (2, half, half))
    sorting = np.zeros((order, order), np.float32)
    sorting[np.arange(half), 2 * np.arange(half)] = 1.0
    sorting[half + np.arange(half), 2 * np.arange(half) + 1] = 1.0
    return (
        jnp.asarray(along_rows),
        jnp.asarray(along_cols),
        jnp.asarray(np.ascontiguousarray(twiddle_cols)),
        jnp.asarray(np.ascontiguousarray(twiddle_rows)),
        jnp.asarray(np.stack([sorting, sorting.T]).astype(jnp.bfloat16)),
    )


def list_patterns(dims, pos_ref, me_ref, ys_ref, xs_ref, slots_ref):
    tile_rows, tile_cols, pat_count, col_count, capacity = dims
    my_row, my_col = me_ref[0], me_ref[1]
    band_count = pat_count * col_count
    first = my_row * band_count

    def visit(index, carry):
        found, source, rank = carry
        y = pos_ref[2 * (first + index)]
        x = pos_ref[2 * (first + index) + 1]
        here = lax.div(x, tile_cols) == my_col
        holder = lax.div(index, pat_count)
        rank = jnp.where(holder == source, rank, 0)

        @pl.when(here & (found < capacity))
        def _():
            ys_ref[found] = y - my_row * tile_rows
            xs_ref[found] = x - my_col * tile_cols
            slots_ref[found] = holder * SEND + jnp.minimum(rank, SEND - 1)

        step = here.astype(jnp.int32)
        return found + step, holder, rank + step

    found, _, _ = lax.fori_loop(0, band_count, visit, (jnp.int32(0), jnp.int32(-1), jnp.int32(0)))
    return jnp.minimum(found, capacity)


def lane_index(rows):
    return lax.broadcasted_iota(jnp.int32, (rows, LANES), 1)


def shifted_left(tiles, shift):
    lane = lane_index(tiles[0].shape[0])
    turn = lax.rem(LANES - shift, LANES)
    rolled = [pltpu.roll(tile, turn, axis=1) for tile in tiles]
    inside = lane < LANES - shift
    return [jnp.where(inside, a, b) for a, b in zip(rolled[:-1], rolled[1:])]


def shifted_right(tiles, shift):
    lane = lane_index(tiles[0].shape[0])
    rolled = [pltpu.roll(tile, shift, axis=1) for tile in tiles]
    outside = lane < shift
    zero = jnp.zeros_like(rolled[0])
    firsts = [zero] + rolled
    seconds = rolled + [zero]
    return [jnp.where(outside, a, b) for a, b in zip(firsts, seconds)]


def row_groups(tile):
    return [tile[k : k + SUBLANES] for k in range(0, tile.shape[0], SUBLANES)]


def shifted_up(tile, shift):
    row = lax.broadcasted_iota(jnp.int32, (SUBLANES, LANES), 0)
    turn = lax.rem(SUBLANES - shift, SUBLANES)
    rolled = [pltpu.roll(group, turn, axis=0) for group in row_groups(tile)]
    inside = row < SUBLANES - shift
    return jnp.concatenate([jnp.where(inside, a, b) for a, b in zip(rolled[:-1], rolled[1:])], axis=0)


def shifted_down(before, tile, shift):
    row = lax.broadcasted_iota(jnp.int32, (SUBLANES, LANES), 0)
    rolled = [before] + [pltpu.roll(group, shift, axis=0) for group in row_groups(tile)]
    outside = row < shift
    return rolled[-1], jnp.concatenate([jnp.where(outside, a, b) for a, b in zip(rolled[:-1], rolled[1:])], axis=0)


class Deposit:
    def __init__(self, add, top, left):
        self.add = add
        self.row = pl.multiple_of(lax.div(top, SUBLANES) * SUBLANES, SUBLANES)
        self.col = pl.multiple_of(lax.div(left, LANES) * LANES, LANES)
        self.down = lax.rem(top, SUBLANES)
        self.right = lax.rem(left, LANES)
        self.carried = None

    def place(self, first, tiles):
        moved = jnp.concatenate(shifted_right(tiles, self.right), axis=1)
        self.add(pl.ds(self.row + first, tiles[0].shape[0]), pl.ds(self.col, moved.shape[1]), moved)

    def put(self, first, tiles):
        if self.carried is None:
            self.carried = [jnp.zeros((SUBLANES, LANES), f32) for _ in tiles]
        pairs = [shifted_down(before, tile, self.down) for before, tile in zip(self.carried, tiles)]
        self.carried = [carried for carried, _ in pairs]
        self.place(first, [tile for _, tile in pairs])

    def finish(self, first):
        row = lax.broadcasted_iota(jnp.int32, (SUBLANES, LANES), 0)
        self.place(first, [jnp.where(row < self.down, tile, 0.0) for tile in self.carried])


def lane_tiles(value):
    return [value[:, k : k + LANES] for k in range(0, value.shape[1], LANES)]


def store_split(ref, rows, cols, value):
    high = value.astype(bf16)
    ref[0, rows, cols] = high
    ref[1, rows, cols] = (value - high.astype(f32)).astype(bf16)


def right_dot(x_ref, table):
    left = jnp.concatenate([x_ref[0], x_ref[1], x_ref[0]], axis=1)
    return jnp.dot(left, table, preferred_element_type=f32)


def left_dot(table, x_ref):
    right = jnp.concatenate([x_ref[0], x_ref[1], x_ref[0]], axis=0)
    return jnp.dot(table, right, preferred_element_type=f32)


def cut_chunk(ext_ref, comp, first, top, left, rows):
    row = pl.multiple_of(lax.div(top, SUBLANES) * SUBLANES, SUBLANES)
    col = pl.multiple_of(lax.div(left, LANES) * LANES, LANES)
    block = ext_ref[comp, pl.ds(row + first, rows + SUBLANES), pl.ds(col, 3 * LANES)]
    tiles = shifted_left(lane_tiles(block), lax.rem(left, LANES))
    return [shifted_up(tile, lax.rem(top, SUBLANES)) for tile in tiles]


def forward(order, ext_ref, probe_ref, consts, y, x, win_ref, power_ref, weight, xa_ref, xb_ref, ya_ref, yb_ref, far_ref):
    rows_table, cols_table, tw_cols, tw_rows = consts
    half = order // 2
    tw_re = jnp.concatenate([tw_cols[0]] * (CHUNK // 8), axis=0)
    tw_im = jnp.concatenate([tw_cols[1]] * (CHUNK // 8), axis=0)
    for first in range(0, order, CHUNK):
        rows = pl.ds(first, CHUNK)
        win_re = cut_chunk(ext_ref, 0, first, y, x, CHUNK)
        win_im = cut_chunk(ext_ref, 1, first, y, x, CHUNK)
        exits = []
        for k in range(2):
            cols = pl.ds(k * half, half)
            win_ref[0, rows, cols] = win_re[k]
            win_ref[1, rows, cols] = win_im[k]
            power_ref[rows, cols] += weight * (win_re[k] * win_re[k] + win_im[k] * win_im[k])
            p_re, p_im = probe_ref[0, rows, cols], probe_ref[1, rows, cols]
            exits.append((p_re * win_re[k] - p_im * win_im[k], p_re * win_im[k] + p_im * win_re[k]))
        (lo_re, lo_im), (hi_re, hi_im) = exits
        store_split(xa_ref, rows, pl.ds(0, half), lo_re + hi_re)
        store_split(xa_ref, rows, pl.ds(half, half), lo_im + hi_im)
        d_re, d_im = lo_re - hi_re, lo_im - hi_im
        store_split(xb_ref, rows, pl.ds(0, half), d_re * tw_re - d_im * tw_im)
        store_split(xb_ref, rows, pl.ds(half, half), d_re * tw_im + d_im * tw_re)
    yield
    ya_ref[...] = right_dot(xa_ref, cols_table[0])
    yb_ref[...] = right_dot(xb_ref, cols_table[0])
    yield
    for first in range(0, half, CHUNK):
        rows = pl.ds(first, CHUNK)
        below = pl.ds(half + first, CHUNK)
        t_re, t_im = tw_rows[0, rows, :], tw_rows[1, rows, :]
        for k, y_ref in enumerate((ya_ref, yb_ref)):
            cols = pl.ds(k * half, half)
            up_re, up_im = y_ref[rows, 0:half], y_ref[rows, half:order]
            dn_re, dn_im = y_ref[below, 0:half], y_ref[below, half:order]
            store_split(xa_ref, rows, cols, up_re + dn_re)
            store_split(xa_ref, below, cols, up_im + dn_im)
            d_re, d_im = up_re - dn_re, up_im - dn_im
            store_split(xb_ref, rows, cols, d_re * t_re - d_im * t_im)
            store_split(xb_ref, below, cols, d_re * t_im + d_im * t_re)
    yield
    far_ref[0] = left_dot(rows_table[0], xa_ref)
    far_ref[1] = left_dot(rows_table[0], xb_ref)
    yield


def backward(order, far_ref, amp_ref, consts, y, x, weight, probe_ref, win_ref, xa_ref, xb_ref, ya_ref, yb_ref, grad_ref, numer_ref):
    rows_table, cols_table, tw_cols, tw_rows = consts
    half = order // 2
    tw_re = jnp.concatenate([tw_cols[0]] * (CHUNK // 8), axis=0)
    tw_im = jnp.concatenate([tw_cols[1]] * (CHUNK // 8), axis=0)
    for k, x_ref in enumerate((xa_ref, xb_ref)):
        for first in range(0, half, CHUNK):
            rows = pl.ds(first, CHUNK)
            below = pl.ds(half + first, CHUNK)
            far_re, far_im = far_ref[k, rows, :], far_ref[k, below, :]
            amp = amp_ref[pl.ds(k * half + first, CHUNK), :].astype(f32)
            factor = amp * lax.rsqrt(far_re * far_re + far_im * far_im + amplitude_floor)
            store_split(x_ref, rows, slice(None), far_re * factor)
            store_split(x_ref, below, slice(None), far_im * factor)
    yield
    ya_ref[...] = left_dot(rows_table[1], xa_ref)
    yb_ref[...] = left_dot(rows_table[1], xb_ref)
    yield
    for first in range(0, half, CHUNK):
        rows = pl.ds(first, CHUNK)
        below = pl.ds(half + first, CHUNK)
        t_re, t_im = tw_rows[0, rows, :], tw_rows[1, rows, :]
        for k, x_ref in enumerate((xa_ref, xb_ref)):
            cols = slice(k * half, (k + 1) * half)
            a_re, a_im = ya_ref[rows, cols], ya_ref[below, cols]
            b_re, b_im = yb_ref[rows, cols], yb_ref[below, cols]
            c_re, c_im = b_re * t_re + b_im * t_im, b_im * t_re - b_re * t_im
            store_split(x_ref, rows, pl.ds(0, half), a_re + c_re)
            store_split(x_ref, rows, pl.ds(half, half), a_im + c_im)
            store_split(x_ref, below, pl.ds(0, half), a_re - c_re)
            store_split(x_ref, below, pl.ds(half, half), a_im - c_im)
    yield
    ya_ref[...] = right_dot(xa_ref, cols_table[1])
    yb_ref[...] = right_dot(xb_ref, cols_table[1])
    yield

    def adder(comp):
        def add(rows, cols, moved):
            grad_ref[comp, rows, cols] += moved

        return add

    deposits = [Deposit(adder(comp), y, x) for comp in range(2)]
    for first in range(0, order, CHUNK):
        rows = pl.ds(first, CHUNK)
        a_re, a_im = ya_ref[rows, 0:half], ya_ref[rows, half:order]
        b_re, b_im = yb_ref[rows, 0:half], yb_ref[rows, half:order]
        c_re, c_im = b_re * tw_re + b_im * tw_im, b_im * tw_re - b_re * tw_im
        waves = [(a_re + c_re, a_im + c_im), (a_re - c_re, a_im - c_im)]
        terms = ([], [])
        for k, (wave_re, wave_im) in enumerate(waves):
            cols = pl.ds(k * half, half)
            wave_re, wave_im = weight * wave_re, weight * wave_im
            p_re, p_im = probe_ref[0, rows, cols], probe_ref[1, rows, cols]
            w_re, w_im = win_ref[0, rows, cols], win_ref[1, rows, cols]
            terms[0].append(p_re * wave_re + p_im * wave_im)
            terms[1].append(p_re * wave_im - p_im * wave_re)
            numer_ref[0, rows, cols] += w_re * wave_re + w_im * wave_im
            numer_ref[1, rows, cols] += w_re * wave_im - w_im * wave_re
        for comp in range(2):
            deposits[comp].put(first, terms[comp])
    for deposit in deposits:
        deposit.finish(order)
    yield


def interleaved(*stages):
    live = list(stages)
    while live:
        still = []
        for stage in live:
            try:
                next(stage)
                still.append(stage)
            except StopIteration:
                pass
        live = still


def outgoing_kernel(dims, pos_ref, me_ref, amp_ref, out_ref, sems):
    tile_rows, tile_cols, pat_count, col_count, capacity = dims
    first = (me_ref[0] * col_count + me_ref[1]) * pat_count
    owners = [lax.div(pos_ref[2 * (first + k) + 1], tile_cols) for k in range(pat_count)]
    copies = []
    for k in range(pat_count):
        rank = sum(((owners[e] == owners[k]).astype(jnp.int32) for e in range(k)), jnp.int32(0))
        slot = owners[k] * SEND + jnp.minimum(rank, SEND - 1)
        copies.append(pltpu.make_async_copy(amp_ref.at[k], out_ref.at[slot], sems.at[k]))
        copies[-1].start()
    for copy in copies:
        copy.wait()


def weights_kernel(dims, span, pos_ref, me_ref, probe_ref, out_ref, sums_ref, power_ref):
    tile_rows, tile_cols, pat_count, col_count, capacity = dims
    order = probe_ref.shape[1]
    top = (me_ref[0] - 1) * tile_rows
    left = (me_ref[1] - 1) * tile_cols
    for first in range(0, sums_ref.shape[0], order):
        sums_ref[pl.ds(first, order), :] = jnp.zeros((order, sums_ref.shape[1]), f32)
    power_ref[...] = probe_ref[0] * probe_ref[0] + probe_ref[1] * probe_ref[1]

    def visit(index, carry):
        y = pos_ref[2 * index] - top
        x = pos_ref[2 * index + 1] - left

        @pl.when((y > 0) & (y < (span + 1) * tile_rows) & (x > 0) & (x < (span + 1) * tile_cols))
        def _():
            def add(rows, cols, moved):
                sums_ref[rows, cols] += moved

            deposit = Deposit(add, y, x)
            for first in range(0, order, CHUNK):
                deposit.put(first, lane_tiles(power_ref[pl.ds(first, CHUNK), :]))
            deposit.finish(order)

        return carry

    lax.fori_loop(0, pos_ref.shape[0] // 2, visit, 0)
    out_ref[...] = sums_ref[tile_rows : (span + 1) * tile_rows, tile_cols : (span + 1) * tile_cols]


def first_half_kernel(dims, pos_ref, me_ref, own_ref, right_ref, below_ref, diag_ref, probe_ref, rows_table, cols_table, tw_cols, tw_rows,
                      far_out, power_out, ext_ref, win_ref, xa_ref, xb_ref, ya_ref, yb_ref, far_ref, ys_ref, xs_ref, slots_ref, sems):
    tile_rows, tile_cols, pat_count, col_count, capacity = dims
    order = probe_ref.shape[1]
    count = list_patterns(dims, pos_ref, me_ref, ys_ref, xs_ref, slots_ref)
    ext_ref[:, 0:tile_rows, 0:tile_cols] = own_ref[...]
    ext_ref[:, 0:tile_rows, tile_cols:] = right_ref[...]
    ext_ref[:, tile_rows:, 0:tile_cols] = below_ref[...]
    ext_ref[:, tile_rows:, tile_cols:] = diag_ref[...]
    power_out[...] = jnp.zeros_like(power_out)
    consts = (rows_table, cols_table, tw_cols, tw_rows)

    def pair(step, carry):
        stages = []
        for k in range(2):
            listed = 2 * step + k
            weight = (listed < count).astype(f32)
            index = jnp.minimum(listed, count - 1)
            stages.append(forward(order, ext_ref, probe_ref, consts, ys_ref[index], xs_ref[index], win_ref.at[k], power_out, weight,
                                  xa_ref.at[k], xb_ref.at[k], ya_ref.at[k], yb_ref.at[k], far_ref.at[listed]))
        interleaved(*stages)
        for k in range(2):
            listed = 2 * step + k
            pltpu.make_async_copy(far_ref.at[listed], far_out.at[listed], sems.at[listed]).start()
        return carry

    pairs = lax.div(count + 1, 2)
    lax.fori_loop(0, pairs, pair, 0)

    def settle(listed, carry):
        pltpu.make_async_copy(far_ref.at[listed], far_out.at[listed], sems.at[listed]).wait()
        return carry

    lax.fori_loop(0, 2 * pairs, settle, 0)


def second_half_kernel(dims, pos_ref, me_ref, own_ref, right_ref, below_ref, diag_ref, probe_ref, far_in, amp_in, rows_table, cols_table, tw_cols, tw_rows, sorting,
                       top_out, bottom_out, numer_out, amp_out,
                       ext_ref, grad_ref, win_ref, xa_ref, xb_ref, ya_ref, yb_ref, far_ref, amp_ref, sorted_ref, ys_ref, xs_ref, slots_ref, far_sems, amp_sems, out_sems):
    tile_rows, tile_cols, pat_count, col_count, capacity = dims
    order = probe_ref.shape[1]
    half = order // 2
    count = list_patterns(dims, pos_ref, me_ref, ys_ref, xs_ref, slots_ref)
    pairs = lax.div(count + 1, 2)

    def copies(listed):
        return (
            pltpu.make_async_copy(far_in.at[listed], far_ref.at[listed], far_sems.at[listed]),
            pltpu.make_async_copy(amp_in.at[slots_ref[jnp.minimum(listed, count - 1)]], amp_ref.at[listed], amp_sems.at[listed]),
        )

    def begin(listed, carry):
        for copy in copies(listed):
            copy.start()
        return carry

    lax.fori_loop(0, 2 * pairs, begin, 0)
    ext_ref[:, 0:tile_rows, 0:tile_cols] = own_ref[...]
    ext_ref[:, 0:tile_rows, tile_cols:] = right_ref[...]
    ext_ref[:, tile_rows:, 0:tile_cols] = below_ref[...]
    ext_ref[:, tile_rows:, tile_cols:] = diag_ref[...]
    grad_ref[...] = jnp.zeros_like(grad_ref)
    numer_out[...] = jnp.zeros_like(numer_out)
    consts = (rows_table, cols_table, tw_cols, tw_rows)

    def pair(step, carry):
        stages = []
        for k in range(2):
            listed = 2 * step + k
            for copy in copies(listed):
                copy.wait()
        for k in range(2):
            listed = 2 * step + k
            weight = (listed < count).astype(f32)
            index = jnp.minimum(listed, count - 1)
            y, x = ys_ref[index], xs_ref[index]
            rows_sorted = jnp.dot(sorting[0], amp_ref[listed], preferred_element_type=f32).astype(bf16)
            sorted_ref[listed] = jnp.dot(rows_sorted, sorting[1], preferred_element_type=f32).astype(bf16)
            for first in range(0, order, CHUNK):
                for comp in range(2):
                    for c, tile in enumerate(cut_chunk(ext_ref, comp, first, y, x, CHUNK)):
                        win_ref[k, comp, pl.ds(first, CHUNK), pl.ds(c * half, half)] = tile
            stages.append(backward(order, far_ref.at[listed], sorted_ref.at[listed], consts, y, x, weight, probe_ref, win_ref.at[k],
                                   xa_ref.at[k], xb_ref.at[k], ya_ref.at[k], yb_ref.at[k], grad_ref, numer_out))
        interleaved(*stages)
        for k in range(2):
            listed = 2 * step + k
            pltpu.make_async_copy(sorted_ref.at[listed], amp_out.at[listed], out_sems.at[listed]).start()
        return carry

    lax.fori_loop(0, pairs, pair, 0)
    top_out[...] = grad_ref[:, 0:tile_rows, :]
    bottom_out[...] = grad_ref[:, tile_rows:, :]

    def settle(listed, carry):
        pltpu.make_async_copy(sorted_ref.at[listed], amp_out.at[listed], out_sems.at[listed]).wait()
        return carry

    lax.fori_loop(0, 2 * pairs, settle, 0)


def whole_kernel(dims, pos_ref, me_ref, own_ref, right_ref, below_ref, diag_ref, sum_left_ref, sum_right_ref, from_left_ref, from_right_ref, weights_ref,
                 probe_ref, amp_in, rows_table, cols_table, tw_cols, tw_rows,
                 current_out, own_out, right_out, below_out, diag_out, numer_out,
                 ext_ref, grad_ref, win_ref, xa_ref, xb_ref, ya_ref, yb_ref, far_ref, amp_ref, ys_ref, xs_ref, slots_ref, amp_sems):
    tile_rows, tile_cols, pat_count, col_count, capacity = dims
    order = probe_ref.shape[1]
    count = list_patterns(dims, pos_ref, me_ref, ys_ref, xs_ref, slots_ref)
    pairs = lax.div(count + 1, 2)

    def fetch(listed):
        return pltpu.make_async_copy(amp_in.at[jnp.minimum(listed, count - 1)], amp_ref.at[listed], amp_sems.at[listed])

    def begin(listed, carry):
        fetch(listed).start()
        return carry

    lax.fori_loop(0, 2 * pairs, begin, 0)
    olds = ((own_ref, right_ref), (below_ref, diag_ref))
    sums = ((sum_left_ref, from_left_ref), (sum_right_ref, from_right_ref))
    for i in range(2):
        for j in range(2):
            for first in range(0, tile_rows, CHUNK):
                rows = pl.ds(first, CHUNK)
                ext_rows = pl.ds(i * tile_rows + first, CHUNK)
                ext_cols = pl.ds(j * tile_cols, tile_cols)
                scale = 1.0 / (weights_ref[ext_rows, ext_cols] + object_regular)
                for comp in range(2):
                    total = sums[j][0][comp, ext_rows, :] + sums[j][1][comp, ext_rows, :]
                    ext_ref[comp, ext_rows, ext_cols] = (object_regular * olds[i][j][comp, rows, :] + total) * scale
    current_out[...] = ext_ref[:, 0:tile_rows, 0:tile_cols]
    grad_ref[...] = jnp.zeros_like(grad_ref)
    numer_out[...] = jnp.zeros_like(numer_out)
    consts = (rows_table, cols_table, tw_cols, tw_rows)

    def pair(step, carry):
        stages = []
        for k in range(2):
            fetch(2 * step + k).wait()
        for k in range(2):
            listed = 2 * step + k
            weight = (listed < count).astype(f32)
            index = jnp.minimum(listed, count - 1)
            y, x = ys_ref[index], xs_ref[index]

            def both(k=k, listed=listed, weight=weight, y=y, x=x):
                yield from forward(order, ext_ref, probe_ref, consts, y, x, win_ref.at[k], numer_out.at[2], weight,
                                   xa_ref.at[k], xb_ref.at[k], ya_ref.at[k], yb_ref.at[k], far_ref.at[k])
                yield from backward(order, far_ref.at[k], amp_ref.at[listed], consts, y, x, weight, probe_ref, win_ref.at[k],
                                    xa_ref.at[k], xb_ref.at[k], ya_ref.at[k], yb_ref.at[k], grad_ref, numer_out)

            stages.append(both())
        interleaved(*stages)
        return carry

    lax.fori_loop(0, pairs, pair, 0)
    own_out[...] = grad_ref[:, 0:tile_rows, 0:tile_cols]
    right_out[...] = grad_ref[:, 0:tile_rows, tile_cols:]
    below_out[...] = grad_ref[:, tile_rows:, 0:tile_cols]
    diag_out[...] = grad_ref[:, tile_rows:, tile_cols:]


def shape(dims, dtype=f32):
    return jax.ShapeDtypeStruct(dims, dtype)


def work_scratch(order):
    return [
        pltpu.VMEM((2, 2, order, order), f32),
        pltpu.VMEM((2, 2, order, order), bf16),
        pltpu.VMEM((2, 2, order, order), bf16),
        pltpu.VMEM((2, order, order), f32),
        pltpu.VMEM((2, order, order), f32),
    ]


def list_scratch(capacity):
    return [pltpu.SMEM((capacity,), jnp.int32)] * 3


def call(kernel, outs, out_specs, in_specs, scratch, flops, limit=48 << 20):
    return pl.pallas_call(
        kernel,
        out_shape=outs,
        out_specs=out_specs,
        in_specs=in_specs,
        scratch_shapes=scratch,
        compiler_params=pltpu.CompilerParams(vmem_limit_bytes=limit),
        cost_estimate=pl.CostEstimate(flops=flops, bytes_accessed=8 << 20, transcendentals=0),
    )


def passed_along(value, axis, steps):
    count = lax.axis_size(axis)
    leading, last = (max(0, -steps), min(count, count - steps))
    return lax.ppermute(value, axis, [(source, source + steps) for source in range(leading, last)])


def passed_both(value, row_steps, col_steps):
    rows, cols = lax.axis_size("row"), lax.axis_size("col")
    pairs = []
    for r in range(rows):
        for c in range(cols):
            if 0 <= r + row_steps < rows and 0 <= c + col_steps < cols:
                pairs.append((r * cols + c, (r + row_steps) * cols + c + col_steps))
    return lax.ppermute(value, ("row", "col"), pairs)


def swapped(value, axis, mask):
    return lax.ppermute(value, axis, [(k, k ^ mask) for k in range(lax.axis_size(axis))])


def summed_over_rows(value):
    parts = [value] + [swapped(value, "row", mask) for mask in range(1, lax.axis_size("row"))]
    while len(parts) > 1:
        parts = [a + b for a, b in zip(parts[::2], parts[1::2])]
    return parts[0]


def probe_update(probe, numer):
    cols = lax.axis_size("col")
    my_col = lax.axis_index("col")
    masks = [1 << k for k in range(cols.bit_length() - 1)]
    share, old = numer, probe
    for mask in masks:
        upper = (my_col & mask) != 0
        half = share.shape[1] // 2
        first, last = share[:, :half], share[:, half:]
        given = jnp.where(upper, first, last)
        share = jnp.where(upper, last, first) + swapped(given, "col", mask)
        old = jnp.where(upper, old[:, half:], old[:, :half])
    share = summed_over_rows(share)
    fresh = (old + share[:2]) / (share[2] + probe_regular)[None]
    for mask in reversed(masks):
        upper = (my_col & mask) != 0
        other = swapped(fresh, "col", mask)
        fresh = jnp.where(upper, jnp.concatenate([other, fresh], axis=1), jnp.concatenate([fresh, other], axis=1))
    return fresh


def local(obj, probe, amplitudes, positions):
    col_count = lax.axis_size("col")
    tile_rows, tile_cols = obj.shape[1], obj.shape[2]
    order = probe.shape[1]
    pat_count = amplitudes.shape[0]
    capacity = 2 * pat_count
    dims = (tile_rows, tile_cols, pat_count, col_count, capacity)
    me = jnp.stack([lax.axis_index("row"), lax.axis_index("col")]).astype(jnp.int32)
    pos = positions.reshape(-1)
    rows_table, cols_table, tw_cols, tw_rows, sorting = tables(order)
    consts = (rows_table, cols_table, tw_cols, tw_rows)
    tile = (2, tile_rows, tile_cols)
    window = (2, order, order)
    wide = (2, 2 * tile_rows, 2 * tile_cols)
    one_pattern = 24 * 2 * order**3

    outgoing = call(
        functools.partial(outgoing_kernel, dims), shape((col_count * SEND, order, order), bf16), ANY, [SMEM, SMEM, ANY],
        [pltpu.SemaphoreType.DMA((pat_count,))], 1 << 20,
    )(pos, me, amplitudes)
    incoming = lax.all_to_all(outgoing, "col", split_axis=0, concat_axis=0, tiled=True)

    right = passed_along(obj, "col", -1)
    below = passed_along(obj, "row", -1)
    diag = passed_both(obj, -1, -1)
    pieces = (obj, right, below, diag)

    def weights(probe_now, span):
        return call(
            functools.partial(weights_kernel, dims, span), shape((span * tile_rows, span * tile_cols)), VMEM, [SMEM, SMEM, VMEM],
            [pltpu.VMEM(((span + 2) * tile_rows, (span + 2) * tile_cols), f32), pltpu.VMEM((order, order), f32)], 8 << 30,
        )(pos, me, probe_now)

    weights_now = weights(probe, 2)

    far, power = call(
        functools.partial(first_half_kernel, dims), (shape((capacity,) + window), shape((order, order))), (ANY, VMEM),
        [SMEM, SMEM] + [VMEM] * 9,
        [pltpu.VMEM(wide, f32)] + work_scratch(order) + [pltpu.VMEM((capacity,) + window, f32)] + list_scratch(capacity)
        + [pltpu.SemaphoreType.DMA((capacity,))],
        capacity * one_pattern // 2,
    )(pos, me, *pieces, probe, *consts)

    top, bottom, numer, sorted_amps = call(
        functools.partial(second_half_kernel, dims),
        (shape((2, tile_rows, 2 * tile_cols)), shape((2, tile_rows, 2 * tile_cols)), shape(window), shape((capacity, order, order), bf16)),
        (VMEM, VMEM, VMEM, ANY),
        [SMEM, SMEM] + [VMEM] * 5 + [ANY, ANY] + [VMEM] * 5,
        [pltpu.VMEM(wide, f32), pltpu.VMEM(wide, f32)] + work_scratch(order)
        + [pltpu.VMEM((capacity,) + window, f32), pltpu.VMEM((capacity, order, order), bf16), pltpu.VMEM((capacity, order, order), bf16)]
        + list_scratch(capacity) + [pltpu.SemaphoreType.DMA((capacity,))] * 3,
        capacity * one_pattern // 2,
    )(pos, me, *pieces, probe, far, incoming, *consts, sorting)

    probe_now = probe_update(probe, jnp.concatenate([numer, power[None]]))
    sums = jnp.concatenate([top + passed_along(bottom, "row", 1), bottom + passed_along(top, "row", -1)], axis=1)
    sum_left, sum_right = sums[:, :, :tile_cols], sums[:, :, tile_cols:]
    from_left = passed_along(sum_right, "col", 1)
    from_right = passed_along(sum_left, "col", -1)

    current, own, to_right, to_below, to_diag, numer = call(
        functools.partial(whole_kernel, dims), (shape(tile),) * 5 + (shape((3, order, order)),), (VMEM,) * 6,
        [SMEM, SMEM] + [VMEM] * 10 + [ANY] + [VMEM] * 4,
        [pltpu.VMEM(wide, f32), pltpu.VMEM(wide, f32)] + work_scratch(order)
        + [pltpu.VMEM((2,) + window, f32), pltpu.VMEM((capacity, order, order), bf16)] + list_scratch(capacity) + [pltpu.SemaphoreType.DMA((capacity,))],
        capacity * one_pattern,
    )(pos, me, *pieces, sum_left, sum_right, from_left, from_right, weights_now, probe_now, sorted_amps, *consts)

    weights_now = weights(probe_now, 1)
    new_probe = probe_update(probe_now, numer)
    total = own + passed_along(to_right, "col", 1) + passed_along(to_below, "row", 1) + passed_both(to_diag, 1, 1)
    new_object = (object_regular * current + total) / (weights_now + object_regular)[None]
    return new_object, new_probe


def solution(mesh):
    placed = (P(None, "row", "col"), P(), P(("row", "col"), None, None), P())
    return jax.shard_map(local, mesh=mesh, in_specs=placed, out_specs=(P(None, "row", "col"), P()), check_vma=False)
```

time: 878 us -> 223 us (0.25)
  local copies, waits for them, and re-layouts: 261 us -> 11.9 us
  waiting for transfers between devices: 327 us -> 83.3 us
  matrix products: 129 us -> 0 us
  starting transfers between devices: 23.1 us -> 84.1 us
  loops' own time: 59.2 us -> 0 us
  other arithmetic: 55.1 us -> 6.07 us
  Pallas kernels: 0 us -> 35.1 us
  between operations: 15 us -> 1.22 us
    psum x2 -> x0, waiting for transfers between devices: 223 us -> none  [local(): totals = lax.psum(partials, ('row', 'col'))]
    dynamic_update_slice x16 -> x0, local copies, waits for them, and re-layouts: 138 us -> none  [deposit(): return lax.dynamic_update_slice(total, block + deposits[index], start)]
    dot_general x26 -> x0, matrix products: 129 us -> none  [the longest x4 31.3 us: left_apply(): jnp.einsum('ab,sbc->sac', tables[2], real_part + imag_part, precision=hig...]
    ppermute x8, waiting for transfers between devices: 104 us -> 14 us  [passed_along(): lax.ppermute(value, axis, [(source, source + steps) for source in range(l...]
    ppermute x0 -> x20, waiting for transfers between devices: none -> 69 us  [the longest x18 55.1 us: swapped(): lax.ppermute(value, axis, [(k, k ^ mask) for k in range(lax.axis_size(axi...]
    ppermute x0 -> x20, starting transfers between devices: none -> 68.3 us  [the longest x18 62.8 us: swapped(): lax.ppermute(value, axis, [(k, k ^ mask) for k in range(lax.axis_size(axi...]
    another operation x4 -> x0, loops' own time: 59.2 us -> none  [the longest x2 58.7 us: local(): lax.fori_loop(0, capacity, deposit, jnp.zeros((3, tile_rows + order, tile...]
    gather x82 -> x0, local copies, waits for them, and re-layouts: 52 us -> none
  transfers between devices with their start and end apart: 11 -> 29, of which waited for: 7 -> 15; matrix products, arithmetic and copies ran while one was open for 9% -> 1% of each run, Pallas kernels for 0% -> 7%
where the time goes in v1:
time: 223 us; the launch traced here: 222 us
  starting transfers between devices  84.1 us (38%)
  waiting for transfers between devices  83.3 us (37%)
  Pallas kernels  35.1 us (16%)
  local copies, waits for them, and re-layouts  11.9 us (5%)
  other arithmetic  6.07 us (3%)
    ppermute x18, starting transfers between devices, swapped(): lax.ppermute(value, axis, [(k, k ^ mask) for k in range(lax.axis_size(axi...  62.8 us
    ppermute x18, waiting for transfers between devices, swapped(): lax.ppermute(value, axis, [(k, k ^ mask) for k in range(lax.axis_size(axi...  55.1 us
    ppermute x8, waiting for transfers between devices, passed_along(): lax.ppermute(value, axis, [(source, source + steps) for source in range(l...  14 us
    ppermute x2, waiting for transfers between devices, passed_both(): return lax.ppermute(value, ('row', 'col'), pairs)  13.8 us
    unnamed x47, local copies, waits for them, and re-layouts  11.8 us
    pallas_call x1, Pallas kernels, local(): call(functools.partial(whole_kernel, dims), (shape(tile),) * 5 + (shape((...  10.6 us
    ppermute x8, starting transfers between devices, passed_along(): lax.ppermute(value, axis, [(source, source + steps) for source in range(l...  10.5 us
    pallas_call x2, Pallas kernels, weights(): call(functools.partial(weights_kernel, dims, span), shape((span * tile_ro...  9.2 us
  transfers between devices with their start and end apart: 29, of which 15 were waited for; matrix products, arithmetic and copies ran while one was open for 1% of the time, Pallas kernels for 7%

profile of v1, /device:TPU:0, one launch (start us, length us, event | category | flops | bytes accessed | tf_op | source)
XLA Modules:
  0.0 221.7 jit_solution(14846795415084828279)
XLA Ops:
  2.7 1.5 shard_map.105
  4.2 5.3 %all-to-all-start = ((bf16[16,256,256]{2,1,0:T(8,128)(2,1)}), bf16[16,256,256]{2,1,0:T(8,128)(2,1)}, u32[]{:S(2)}, u32[]{:S(2)}) async-start(bf16[16,256,256]{2,1,0:T(8,128)(2,1)} %shard_map.105), calls=%async_computation | async-start | bytes 4194304 | tf_op jit(solution)/shard_map/all_to_all | solution.py:621
  13.4 14.0 %collective-permute-done.1.below_ref = f32[2,256,256]{2,1,0:T(8,128)S(1)} collective-permute-done((f32[2,256,256]{2,1,0:T(8,128)S(1)}, f32[2,256,256]{2,1,0:T(8,128)S(1)}, u32[]{:S(2)}, u32[]{:S(2)}) %collective-permute-start.1) | collective-permute-done | bytes 524320 | tf_op jit(solution)/shard_map/ppermute | solution.py:556
  27.3 6.0 %collective-permute-done.2.diag_ref = f32[2,256,256]{2,1,0:T(8,128)S(1)} collective-permute-done((f32[2,256,256]{2,1,0:T(8,128)S(1)}, f32[2,256,256]{2,1,0:T(8,128)S(1)}, u32[]{:S(2)}, u32[]{:S(2)}) %collective-permute-start.2) | collective-permute-done | bytes 524320 | tf_op jit(solution)/shard_map/ppermute | solution.py:566
  35.6 5.5 %shard_map.104 = (f32[8,2,256,256]{3,2,1,0:T(8,128)}, f32[256,256]{1,0:T(8,128)S(1)}) custom-call(s32[256]{0:T(256)S(1)} %reshape.8.pos_ref, s32[2]{0:T(128)S(1)} %pad_add_fusion.me_ref, f32[2,256,256]{2,1,0:T(8,128)S(1)} %copy-done.2, f32[2,256,256]{2,1,0:T(8,128)S(1)} %collective-permute-done.right_ref, ...), custom_call_target="tpu_custom_call" | custom-call | flops 3221225472 | bytes 8388608 | tf_op jit(solution)/shard_map/pallas_call | solution.py:636
  46.8 8.3 %shard_map.106 = (f32[2,256,512]{2,1,0:T(8,128)S(1)}, f32[2,256,512]{2,1,0:T(8,128)}, f32[2,256,256]{2,1,0:T(8,128)S(1)}, bf16[8,256,256]{2,1,0:T(8,128)(2,1)}) custom-call(s32[256]{0:T(256)S(1)} %reshape.8.pos_ref, s32[2]{0:T(128)S(1)} %pad_add_fusion.me_ref, f32[2,256,256]{2,1,0:T(8,128)S(1)} %copy-done.2, ...), custom_call_target="tpu_custom_call" | custom-call | flops 3221225472 | bytes 8388608 | tf_op jit(solution)/shard_map/pallas_call | solution.py:644
  55.9 12.8 %collective-permute-start.7 = (f32[3,128,256]{2,1,0:T(8,128)}, f32[3,128,256]{2,1,0:T(8,128)}, u32[]{:S(2)}, u32[]{:S(2)}) collective-permute-start(f32[3,128,256]{2,1,0:T(8,128)} %broadcast_select_fusion), channel_id=1, source_target_pairs={{0,1},{1,0},{2,3},{3,2},{4,5},{5,4},{6,7},{7,6},{8,9},{9,8},{10,11... | collective-permute-start | bytes 1179656 | tf_op jit(solution)/shard_map/ppermute | solution.py:570
  68.7 1.7 collective-permute-done.7
  72.3 1.6 collective-permute-start.8
  73.9 5.7 %collective-permute-done.8 = f32[3,64,256]{2,1,0:T(8,128)S(1)} collective-permute-done((f32[3,64,256]{2,1,0:T(8,128)S(1)}, f32[3,64,256]{2,1,0:T(8,128)S(1)}, u32[]{:S(2)}, u32[]{:S(2)}) %collective-permute-start.8) | collective-permute-done | bytes 196640 | tf_op jit(solution)/shard_map/ppermute | solution.py:570
  80.6 7.3 %collective-permute-start.9 = (f32[3,32,256]{2,1,0:T(8,128)S(1)}, f32[3,32,256]{2,1,0:T(8,128)S(1)}, u32[]{:S(2)}, u32[]{:S(2)}) collective-permute-start(f32[3,32,256]{2,1,0:T(8,128)S(1)} %slice_select_fusion.8), channel_id=1, source_target_pairs={{0,4},{1,5},{2,6},{3,7},{4,0},{5,1},{6,2},{7,3},{8,12},{9,13},{10,... | collective-permute-start | bytes 294920 | tf_op jit(solution)/shard_map/ppermute | solution.py:570
  90.7 3.2 %collective-permute-start.10 = (f32[3,32,256]{2,1,0:T(8,128)S(1)}, f32[3,32,256]{2,1,0:T(8,128)S(1)}, u32[]{:S(2)}, u32[]{:S(2)}) collective-permute-start(f32[3,32,256]{2,1,0:T(8,128)S(1)} %select_add_fusion.5), channel_id=1, source_target_pairs={{0,8},{8,0},{16,24},{24,16},{1,9},{9,1},{17,25},{25,17},{2,10},{10... | collective-permute-start | bytes 294920 | tf_op jit(solution)/shard_map/ppermute | solution.py:570
  93.9 1.5 collective-permute-start.11
  95.4 1.4 collective-permute-start.12
  96.8 22.8 %collective-permute-done.10 = f32[3,32,256]{2,1,0:T(8,128)S(1)} collective-permute-done((f32[3,32,256]{2,1,0:T(8,128)S(1)}, f32[3,32,256]{2,1,0:T(8,128)S(1)}, u32[]{:S(2)}, u32[]{:S(2)}) %collective-permute-start.10) | collective-permute-done | bytes 98336 | tf_op jit(solution)/shard_map/ppermute | solution.py:570
  119.6 5.4 %collective-permute-done.11 = f32[3,32,256]{2,1,0:T(8,128)S(1)} collective-permute-done((f32[3,32,256]{2,1,0:T(8,128)S(1)}, f32[3,32,256]{2,1,0:T(8,128)S(1)}, u32[]{:S(2)}, u32[]{:S(2)}) %collective-permute-start.11) | collective-permute-done | bytes 98336 | tf_op jit(solution)/shard_map/ppermute | solution.py:570
  125.0 1.8 collective-permute-start.13
  126.8 2.5 %collective-permute-done.13 = f32[2,32,256]{2,1,0:T(8,128)S(1)} collective-permute-done((f32[2,32,256]{2,1,0:T(8,128)S(1)}, f32[2,32,256]{2,1,0:T(8,128)S(1)}, u32[]{:S(2)}, u32[]{:S(2)}) %collective-permute-start.13) | collective-permute-done | bytes 65568 | tf_op jit(solution)/shard_map/ppermute | solution.py:570
  129.4 1.5 collective-permute-start.14
  134.4 1.8 collective-permute-start.15
  136.2 5.7 %shard_map.107.weights_ref = f32[512,512]{1,0:T(8,128)S(1)} custom-call(s32[256]{0:T(256)S(1)} %reshape.8.pos_ref, s32[2]{0:T(128)S(1)} %pad_add_fusion.me_ref, f32[2,256,256]{2,1,0:T(8,128)S(1)} %copy-done), custom_call_target="tpu_custom_call" | custom-call | flops 8589934592 | bytes 8388608 | tf_op jit(solution)/shard_map/pallas_call | solution.py:629
  143.6 10.6 %shard_map.108 = (f32[2,256,256]{2,1,0:T(8,128)S(1)}, f32[2,256,256]{2,1,0:T(8,128)S(1)}, f32[2,256,256]{2,1,0:T(8,128)S(1)}, f32[2,256,256]{2,1,0:T(8,128)S(1)}...) custom-call(s32[256]{0:T(256)S(1)} %reshape.8.pos_ref, s32[2]{0:T(128)S(1)} %pad_add_fusion.me_ref, ...), custom_call_target="tpu_custom_call" | custom-call | flops 6442450944 | bytes 8388608 | tf_op jit(solution)/shard_map/pallas_call | solution.py:661
  154.4 17.3 %collective-permute-start.19 = (f32[3,128,256]{2,1,0:T(8,128)S(1)}, f32[3,128,256]{2,1,0:T(8,128)S(1)}, u32[]{:S(2)}, u32[]{:S(2)}) collective-permute-start(f32[3,128,256]{2,1,0:T(8,128)S(1)} %slice_select_fusion), channel_id=1, source_target_pairs={{0,1},{1,0},{2,3},{3,2},{4,5},{5,4},{6,7},{7,6},{8,9},{9,8},{10,11... | collective-permute-start | bytes 1179656 | tf_op jit(solution)/shard_map/ppermute | solution.py:570
  173.8 6.6 %collective-permute-done.20 = f32[3,64,256]{2,1,0:T(8,128)S(1)} collective-permute-done((f32[3,64,256]{2,1,0:T(8,128)S(1)}, f32[3,64,256]{2,1,0:T(8,128)S(1)}, u32[]{:S(2)}, u32[]{:S(2)}) %collective-permute-start.20) | collective-permute-done | bytes 196640 | tf_op jit(solution)/shard_map/ppermute | solution.py:570
  180.4 6.6 %collective-permute-start.21 = (f32[3,32,256]{2,1,0:T(8,128)S(1)}, f32[3,32,256]{2,1,0:T(8,128)S(1)}, u32[]{:S(2)}, u32[]{:S(2)}) collective-permute-start(f32[3,32,256]{2,1,0:T(8,128)S(1)} %slice_select_fusion.7), channel_id=1, source_target_pairs={{0,4},{1,5},{2,6},{3,7},{4,0},{5,1},{6,2},{7,3},{8,12},{9,13},{10,... | collective-permute-start | bytes 294920 | tf_op jit(solution)/shard_map/ppermute | solution.py:570
  187.0 2.6 %collective-permute-done.21 = f32[3,32,256]{2,1,0:T(8,128)S(1)} collective-permute-done((f32[3,32,256]{2,1,0:T(8,128)S(1)}, f32[3,32,256]{2,1,0:T(8,128)S(1)}, u32[]{:S(2)}, u32[]{:S(2)}) %collective-permute-start.21) | collective-permute-done | bytes 98336 | tf_op jit(solution)/shard_map/ppermute | solution.py:570
  190.0 4.0 %collective-permute-start.24 = (f32[3,32,256]{2,1,0:T(8,128)S(1)}, f32[3,32,256]{2,1,0:T(8,128)S(1)}, u32[]{:S(2)}, u32[]{:S(2)}) collective-permute-start(f32[3,32,256]{2,1,0:T(8,128)S(1)} %select_add_fusion.4), channel_id=1, source_target_pairs={{0,24},{8,16},{16,8},{24,0},{1,25},{9,17},{17,9},{25,1},{2,26},{10... | collective-permute-start | bytes 294920 | tf_op jit(solution)/shard_map/ppermute | solution.py:570
  196.7 4.3 %collective-permute-start.18 = (f32[2,256,256]{2,1,0:T(8,128)S(1)}, f32[2,256,256]{2,1,0:T(8,128)S(1)}, u32[]{:S(2)}, u32[]{:S(2)}) collective-permute-start(f32[2,256,256]{2,1,0:T(8,128)S(1)} %get-tuple-element.24), channel_id=1, source_target_pairs={{0,9},{1,10},{2,11},{3,12},{4,13},{5,14},{6,15},{8,17},{9,18},{10,... | collective-permute-start | bytes 1572872 | tf_op jit(solution)/shard_map/ppermute | solution.py:566
  201.4 3.5 %shard_map.109 = f32[256,256]{1,0:T(8,128)S(1)} custom-call(s32[256]{0:T(256)S(1)} %reshape.8.pos_ref, s32[2]{0:T(128)S(1)} %pad_add_fusion.me_ref, f32[2,256,256]{2,1,0:T(8,128)S(1)} %maximum_select_fusion.probe_ref), custom_call_target="tpu_custom_call" | custom-call | flops 8589934592 | bytes 8388608 | tf_op jit(solution)/shard_map/pallas_call | solution.py:629
  204.9 1.5 collective-permute-done.25
  207.0 4.9 %collective-permute-done.26 = f32[2,64,256]{2,1,0:T(8,128)S(1)} collective-permute-done((f32[2,64,256]{2,1,0:T(8,128)S(1)}, f32[2,64,256]{2,1,0:T(8,128)S(1)}, u32[]{:S(2)}, u32[]{:S(2)}) %collective-permute-start.26) | collective-permute-done | bytes 131104 | tf_op jit(solution)/shard_map/ppermute | solution.py:570
  212.0 7.9 %collective-permute-done.18 = f32[2,256,256]{2,1,0:T(8,128)S(1)} collective-permute-done((f32[2,256,256]{2,1,0:T(8,128)S(1)}, f32[2,256,256]{2,1,0:T(8,128)S(1)}, u32[]{:S(2)}, u32[]{:S(2)}) %collective-permute-start.18) | collective-permute-done | bytes 524320 | tf_op jit(solution)/shard_map/ppermute | solution.py:566
  (114 shorter events, 33.8 us)
Async XLA Ops:
  4.2 29.1 %copy-start = (f32[2,256,256]{2,1,0:T(8,128)S(1)}, f32[2,256,256]{2,1,0:T(8,128)}, u32[]{:S(2)}) copy-start(f32[2,256,256]{2,1,0:T(8,128)} %probe_ref.5) | copy-start | bytes 1572868
  4.2 29.1 %copy-start.14 = (f32[2,128,128]{2,1,0:T(8,128)S(1)}, f32[2,128,128]{2,1,0:T(8,128)}, u32[]{:S(2)}) copy-start(f32[2,128,128]{2,1,0:T(8,128)} %constant.34.clone.tw_rows) | copy-start | bytes 393220
  4.2 37.3 %all-to-all-start = ((bf16[16,256,256]{2,1,0:T(8,128)(2,1)}), bf16[16,256,256]{2,1,0:T(8,128)(2,1)}, u32[]{:S(2)}, u32[]{:S(2)}) async-start(bf16[16,256,256]{2,1,0:T(8,128)(2,1)} %shard_map.105), calls=%async_computation | async-start | bytes 4194304 | tf_op jit(solution)/shard_map/all_to_all | solution.py:621
  9.5 3.9 %collective-permute-start = (f32[2,256,256]{2,1,0:T(8,128)S(1)}, f32[2,256,256]{2,1,0:T(8,128)S(1)}, u32[]{:S(2)}, u32[]{:S(2)}) collective-permute-start(f32[2,256,256]{2,1,0:T(8,128)S(1)} %copy-done.2), channel_id=1, source_target_pairs={{1,0},{2,1},{3,2},{4,3},{5,4},{6,5},{7,6},{9,8},{10,9},{11,10},{12... | collective-permute-start | bytes 1572872 | tf_op jit(solution)/shard_map/ppermute | solution.py:556
  10.8 16.6 %collective-permute-start.1 = (f32[2,256,256]{2,1,0:T(8,128)S(1)}, f32[2,256,256]{2,1,0:T(8,128)S(1)}, u32[]{:S(2)}, u32[]{:S(2)}) collective-permute-start(f32[2,256,256]{2,1,0:T(8,128)S(1)} %copy-done.2), channel_id=1, source_target_pairs={{8,0},{16,8},{24,16},{9,1},{17,9},{25,17},{10,2},{18,10},{26,18},{... | collective-permute-start | bytes 1572872 | tf_op jit(solution)/shard_map/ppermute | solution.py:556
  12.1 21.2 %collective-permute-start.2 = (f32[2,256,256]{2,1,0:T(8,128)S(1)}, f32[2,256,256]{2,1,0:T(8,128)S(1)}, u32[]{:S(2)}, u32[]{:S(2)}) collective-permute-start(f32[2,256,256]{2,1,0:T(8,128)S(1)} %copy-done.2), channel_id=1, source_target_pairs={{9,0},{10,1},{11,2},{12,3},{13,4},{14,5},{15,6},{17,8},{18,9},{19,... | collective-permute-start | bytes 1572872 | tf_op jit(solution)/shard_map/ppermute | solution.py:566
  55.9 14.5 %collective-permute-start.7 = (f32[3,128,256]{2,1,0:T(8,128)}, f32[3,128,256]{2,1,0:T(8,128)}, u32[]{:S(2)}, u32[]{:S(2)}) collective-permute-start(f32[3,128,256]{2,1,0:T(8,128)} %broadcast_select_fusion), channel_id=1, source_target_pairs={{0,1},{1,0},{2,3},{3,2},{4,5},{5,4},{6,7},{7,6},{8,9},{9,8},{10,11... | collective-permute-start | bytes 1179656 | tf_op jit(solution)/shard_map/ppermute | solution.py:570
  72.3 7.2 %collective-permute-start.8 = (f32[3,64,256]{2,1,0:T(8,128)S(1)}, f32[3,64,256]{2,1,0:T(8,128)S(1)}, u32[]{:S(2)}, u32[]{:S(2)}) collective-permute-start(f32[3,64,256]{2,1,0:T(8,128)S(1)} %slice_select_fusion.4), channel_id=1, source_target_pairs={{0,2},{1,3},{2,0},{3,1},{4,6},{5,7},{6,4},{7,5},{8,10},{9,11},{10,... | collective-permute-start | bytes 589832 | tf_op jit(solution)/shard_map/ppermute | solution.py:570
  80.6 10.0 %collective-permute-start.9 = (f32[3,32,256]{2,1,0:T(8,128)S(1)}, f32[3,32,256]{2,1,0:T(8,128)S(1)}, u32[]{:S(2)}, u32[]{:S(2)}) collective-permute-start(f32[3,32,256]{2,1,0:T(8,128)S(1)} %slice_select_fusion.8), channel_id=1, source_target_pairs={{0,4},{1,5},{2,6},{3,7},{4,0},{5,1},{6,2},{7,3},{8,12},{9,13},{10,... | collective-permute-start | bytes 294920 | tf_op jit(solution)/shard_map/ppermute | solution.py:570
  88.0 42.9 %collective-permute-start.3 = (f32[2,256,512]{2,1,0:T(8,128)}, f32[2,256,512]{2,1,0:T(8,128)S(1)}, u32[]{:S(2)}, u32[]{:S(2)}) collective-permute-start(f32[2,256,512]{2,1,0:T(8,128)} %get-tuple-element.16), channel_id=1, source_target_pairs={{0,8},{8,16},{16,24},{1,9},{9,17},{17,25},{2,10},{10,18},{18,26},{... | collective-permute-start | bytes 3145736 | tf_op jit(solution)/shard_map/ppermute | solution.py:556
  89.3 41.7 %collective-permute-start.4 = (f32[2,256,512]{2,1,0:T(8,128)S(1)}, f32[2,256,512]{2,1,0:T(8,128)S(1)}, u32[]{:S(2)}, u32[]{:S(2)}) collective-permute-start(f32[2,256,512]{2,1,0:T(8,128)S(1)} %get-tuple-element.15), channel_id=1, source_target_pairs={{8,0},{16,8},{24,16},{9,1},{17,9},{25,17},{10,2},{18,10},{26,18},{... | collective-permute-start | bytes 3145736 | tf_op jit(solution)/shard_map/ppermute | solution.py:556
  90.7 28.9 %collective-permute-start.10 = (f32[3,32,256]{2,1,0:T(8,128)S(1)}, f32[3,32,256]{2,1,0:T(8,128)S(1)}, u32[]{:S(2)}, u32[]{:S(2)}) collective-permute-start(f32[3,32,256]{2,1,0:T(8,128)S(1)} %select_add_fusion.5), channel_id=1, source_target_pairs={{0,8},{8,0},{16,24},{24,16},{1,9},{9,1},{17,25},{25,17},{2,10},{10... | collective-permute-start | bytes 294920 | tf_op jit(solution)/shard_map/ppermute | solution.py:570
  93.9 31.1 %collective-permute-start.11 = (f32[3,32,256]{2,1,0:T(8,128)S(1)}, f32[3,32,256]{2,1,0:T(8,128)S(1)}, u32[]{:S(2)}, u32[]{:S(2)}) collective-permute-start(f32[3,32,256]{2,1,0:T(8,128)S(1)} %select_add_fusion.5), channel_id=1, source_target_pairs={{0,16},{8,24},{16,0},{24,8},{1,17},{9,25},{17,1},{25,9},{2,18},{10... | collective-permute-start | bytes 294920 | tf_op jit(solution)/shard_map/ppermute | solution.py:570
  95.4 29.6 %collective-permute-start.12 = (f32[3,32,256]{2,1,0:T(8,128)S(1)}, f32[3,32,256]{2,1,0:T(8,128)S(1)}, u32[]{:S(2)}, u32[]{:S(2)}) collective-permute-start(f32[3,32,256]{2,1,0:T(8,128)S(1)} %select_add_fusion.5), channel_id=1, source_target_pairs={{0,24},{8,16},{16,8},{24,0},{1,25},{9,17},{17,9},{25,1},{2,26},{10... | collective-permute-start | bytes 294920 | tf_op jit(solution)/shard_map/ppermute | solution.py:570
  96.8 34.3 %copy-start.18 = (f32[2,256,512]{2,1,0:T(8,128)S(1)}, f32[2,256,512]{2,1,0:T(8,128)}, u32[]{:S(2)}) copy-start(f32[2,256,512]{2,1,0:T(8,128)} %get-tuple-element.16) | copy-start | bytes 3145732
  125.0 4.3 %collective-permute-start.13 = (f32[2,32,256]{2,1,0:T(8,128)S(1)}, f32[2,32,256]{2,1,0:T(8,128)S(1)}, u32[]{:S(2)}, u32[]{:S(2)}) collective-permute-start(f32[2,32,256]{2,1,0:T(8,128)S(1)} %fusion.3), channel_id=1, source_target_pairs={{0,4},{1,5},{2,6},{3,7},{4,0},{5,1},{6,2},{7,3},{8,12},{9,13},{10,... | collective-permute-start | bytes 196616 | tf_op jit(solution)/shard_map/ppermute | solution.py:570
  129.4 5.0 %collective-permute-start.14 = (f32[2,64,256]{2,1,0:T(8,128)S(1)}, f32[2,64,256]{2,1,0:T(8,128)S(1)}, u32[]{:S(2)}, u32[]{:S(2)}) collective-permute-start(f32[2,64,256]{2,1,0:T(8,128)S(1)} %maximum_select_fusion.4), channel_id=1, source_target_pairs={{0,2},{1,3},{2,0},{3,1},{4,6},{5,7},{6,4},{7,5},{8,10},{9,11},{10,... | collective-permute-start | bytes 393224 | tf_op jit(solution)/shard_map/ppermute | solution.py:570
  131.5 10.5 %collective-permute-start.5 = (f32[2,512,256]{2,1,0:T(8,128)S(1)}, f32[2,512,256]{2,1,0:T(8,128)S(1)}, u32[]{:S(2)}, u32[]{:S(2)}) collective-permute-start(f32[2,512,256]{2,1,0:T(8,128)S(1)} %get-tuple-element.26.sum_right_ref), channel_id=1, source_target_pairs={{0,1},{1,2},{2,3},{3,4},{4,5},{5,6},{6,7},{8,9},{9,10},{10,11},{11... | collective-permute-start | bytes 3145736 | tf_op jit(solution)/shard_map/ppermute | solution.py:556
  132.9 9.1 %collective-permute-start.6 = (f32[2,512,256]{2,1,0:T(8,128)S(1)}, f32[2,512,256]{2,1,0:T(8,128)S(1)}, u32[]{:S(2)}, u32[]{:S(2)}) collective-permute-start(f32[2,512,256]{2,1,0:T(8,128)S(1)} %get-tuple-element.27.sum_left_ref), channel_id=1, source_target_pairs={{1,0},{2,1},{3,2},{4,3},{5,4},{6,5},{7,6},{9,8},{10,9},{11,10},{12... | collective-permute-start | bytes 3145736 | tf_op jit(solution)/shard_map/ppermute | solution.py:556
  134.4 7.5 %collective-permute-start.15 = (f32[2,128,256]{2,1,0:T(8,128)S(1)}, f32[2,128,256]{2,1,0:T(8,128)S(1)}, u32[]{:S(2)}, u32[]{:S(2)}) collective-permute-start(f32[2,128,256]{2,1,0:T(8,128)S(1)} %maximum_select_fusion.2), channel_id=1, source_target_pairs={{0,1},{1,0},{2,3},{3,2},{4,5},{5,4},{6,7},{7,6},{8,9},{9,8},{10,11... | collective-permute-start | bytes 786440 | tf_op jit(solution)/shard_map/ppermute | solution.py:570
  154.4 18.6 %collective-permute-start.19 = (f32[3,128,256]{2,1,0:T(8,128)S(1)}, f32[3,128,256]{2,1,0:T(8,128)S(1)}, u32[]{:S(2)}, u32[]{:S(2)}) collective-permute-start(f32[3,128,256]{2,1,0:T(8,128)S(1)} %slice_select_fusion), channel_id=1, source_target_pairs={{0,1},{1,0},{2,3},{3,2},{4,5},{5,4},{6,7},{7,6},{8,9},{9,8},{10,11... | collective-permute-start | bytes 1179656 | tf_op jit(solution)/shard_map/ppermute | solution.py:570
  173.1 7.2 %collective-permute-start.20 = (f32[3,64,256]{2,1,0:T(8,128)S(1)}, f32[3,64,256]{2,1,0:T(8,128)S(1)}, u32[]{:S(2)}, u32[]{:S(2)}) collective-permute-start(f32[3,64,256]{2,1,0:T(8,128)S(1)} %slice_select_fusion.3), channel_id=1, source_target_pairs={{0,2},{1,3},{2,0},{3,1},{4,6},{5,7},{6,4},{7,5},{8,10},{9,11},{10,... | collective-permute-start | bytes 589832 | tf_op jit(solution)/shard_map/ppermute | solution.py:570
  180.4 9.2 %collective-permute-start.21 = (f32[3,32,256]{2,1,0:T(8,128)S(1)}, f32[3,32,256]{2,1,0:T(8,128)S(1)}, u32[]{:S(2)}, u32[]{:S(2)}) collective-permute-start(f32[3,32,256]{2,1,0:T(8,128)S(1)} %slice_select_fusion.7), channel_id=1, source_target_pairs={{0,4},{1,5},{2,6},{3,7},{4,0},{5,1},{6,2},{7,3},{8,12},{9,13},{10,... | collective-permute-start | bytes 294920 | tf_op jit(solution)/shard_map/ppermute | solution.py:570
  189.6 7.1 %collective-permute-start.22 = (f32[3,32,256]{2,1,0:T(8,128)S(1)}, f32[3,32,256]{2,1,0:T(8,128)S(1)}, u32[]{:S(2)}, u32[]{:S(2)}) collective-permute-start(f32[3,32,256]{2,1,0:T(8,128)S(1)} %select_add_fusion.4), channel_id=1, source_target_pairs={{0,8},{8,0},{16,24},{24,16},{1,9},{9,1},{17,25},{25,17},{2,10},{10... | collective-permute-start | bytes 294920 | tf_op jit(solution)/shard_map/ppermute | solution.py:570
  189.7 11.3 %collective-permute-start.23 = (f32[3,32,256]{2,1,0:T(8,128)S(1)}, f32[3,32,256]{2,1,0:T(8,128)S(1)}, u32[]{:S(2)}, u32[]{:S(2)}) collective-permute-start(f32[3,32,256]{2,1,0:T(8,128)S(1)} %select_add_fusion.4), channel_id=1, source_target_pairs={{0,16},{8,24},{16,0},{24,8},{1,17},{9,25},{17,1},{25,9},{2,18},{10... | collective-permute-start | bytes 294920 | tf_op jit(solution)/shard_map/ppermute | solution.py:570
  190.0 11.0 %collective-permute-start.24 = (f32[3,32,256]{2,1,0:T(8,128)S(1)}, f32[3,32,256]{2,1,0:T(8,128)S(1)}, u32[]{:S(2)}, u32[]{:S(2)}) collective-permute-start(f32[3,32,256]{2,1,0:T(8,128)S(1)} %select_add_fusion.4), channel_id=1, source_target_pairs={{0,24},{8,16},{16,8},{24,0},{1,25},{9,17},{17,9},{25,1},{2,26},{10... | collective-permute-start | bytes 294920 | tf_op jit(solution)/shard_map/ppermute | solution.py:570
  194.0 18.0 %collective-permute-start.16 = (f32[2,256,256]{2,1,0:T(8,128)S(1)}, f32[2,256,256]{2,1,0:T(8,128)S(1)}, u32[]{:S(2)}, u32[]{:S(2)}) collective-permute-start(f32[2,256,256]{2,1,0:T(8,128)S(1)} %get-tuple-element.22), channel_id=1, source_target_pairs={{0,1},{1,2},{2,3},{3,4},{4,5},{5,6},{6,7},{8,9},{9,10},{10,11},{11... | collective-permute-start | bytes 1572872 | tf_op jit(solution)/shard_map/ppermute | solution.py:556
  195.4 16.6 %collective-permute-start.17 = (f32[2,256,256]{2,1,0:T(8,128)S(1)}, f32[2,256,256]{2,1,0:T(8,128)S(1)}, u32[]{:S(2)}, u32[]{:S(2)}) collective-permute-start(f32[2,256,256]{2,1,0:T(8,128)S(1)} %get-tuple-element.23), channel_id=1, source_target_pairs={{0,8},{8,16},{16,24},{1,9},{9,17},{17,25},{2,10},{10,18},{18,26},{... | collective-permute-start | bytes 1572872 | tf_op jit(solution)/shard_map/ppermute | solution.py:556
  196.7 23.2 %collective-permute-start.18 = (f32[2,256,256]{2,1,0:T(8,128)S(1)}, f32[2,256,256]{2,1,0:T(8,128)S(1)}, u32[]{:S(2)}, u32[]{:S(2)}) collective-permute-start(f32[2,256,256]{2,1,0:T(8,128)S(1)} %get-tuple-element.24), channel_id=1, source_target_pairs={{0,9},{1,10},{2,11},{3,12},{4,13},{5,14},{6,15},{8,17},{9,18},{10,... | collective-permute-start | bytes 1572872 | tf_op jit(solution)/shard_map/ppermute | solution.py:566
  201.1 5.3 %collective-permute-start.25 = (f32[2,32,256]{2,1,0:T(8,128)S(1)}, f32[2,32,256]{2,1,0:T(8,128)S(1)}, u32[]{:S(2)}, u32[]{:S(2)}) collective-permute-start(f32[2,32,256]{2,1,0:T(8,128)S(1)} %fusion.2), channel_id=1, source_target_pairs={{0,4},{1,5},{2,6},{3,7},{4,0},{5,1},{6,2},{7,3},{8,12},{9,13},{10,... | collective-permute-start | bytes 196616 | tf_op jit(solution)/shard_map/ppermute | solution.py:570
  206.4 5.5 %collective-permute-start.26 = (f32[2,64,256]{2,1,0:T(8,128)S(1)}, f32[2,64,256]{2,1,0:T(8,128)S(1)}, u32[]{:S(2)}, u32[]{:S(2)}) collective-permute-start(f32[2,64,256]{2,1,0:T(8,128)S(1)} %maximum_select_fusion.5), channel_id=1, source_target_pairs={{0,2},{1,3},{2,0},{3,1},{4,6},{5,7},{6,4},{7,5},{8,10},{9,11},{10,... | collective-permute-start | bytes 393224 | tf_op jit(solution)/shard_map/ppermute | solution.py:570
  211.9 9.0 %collective-permute-start.27 = (f32[2,128,256]{2,1,0:T(8,128)S(1)}, f32[2,128,256]{2,1,0:T(8,128)S(1)}, u32[]{:S(2)}, u32[]{:S(2)}) collective-permute-start(f32[2,128,256]{2,1,0:T(8,128)S(1)} %maximum_select_fusion.3), channel_id=1, source_target_pairs={{0,1},{1,0},{2,3},{3,2},{4,5},{5,4},{6,7},{7,6},{8,9},{9,8},{10,11... | collective-permute-start | bytes 786440 | tf_op jit(solution)/shard_map/ppermute | solution.py:570
  (20 other events, 106.3 us)

commit v2 on v1

--- a/solution.py
+++ b/solution.py
@@ -17,6 +17,7 @@
 
 LANES = 128
 SUBLANES = 8
+LEVELS = 32767.0
 CHUNK = 32
 VMEM = pl.BlockSpec(memory_space=pltpu.VMEM)
 SMEM = pl.BlockSpec(memory_space=pltpu.SMEM)
@@ -31,40 +32,22 @@
     angles = 2.0 * np.pi * ((counter[:, None] * counter[None, :]) % half) / half
     cos, sin = np.cos(angles), np.sin(angles)
     scale = 1.0 / np.sqrt(order)
-    plus = np.block([[cos, sin], [-sin, cos]]) * scale
-    minus = np.block([[cos, -sin], [sin, cos]]) * scale
-
-    def halves(matrix):
+    turns = []
+    for block in ([[cos, -sin], [sin, cos]], [[cos, sin], [-sin, cos]]):
+        matrix = np.block(block) * scale
         high = matrix.astype(jnp.bfloat16)
-        low = (matrix - high.astype(np.float64)).astype(jnp.bfloat16)
-        return high, low
-
-    plus_high, plus_low = halves(plus)
-    minus_high, minus_low = halves(minus)
-    along_rows = np.stack(
-        [
-            np.concatenate([plus_high, plus_high, plus_low], axis=1),
-            np.concatenate([minus_high, minus_high, minus_low], axis=1),
-        ]
-    )
-    along_cols = np.stack(
-        [
-            np.concatenate([minus_high, minus_high, minus_low], axis=0),
-            np.concatenate([plus_high, plus_high, plus_low], axis=0),
-        ]
-    )
+        turns.append(np.stack([high, (matrix - high.astype(np.float64)).astype(jnp.bfloat16)]))
     turn = 2.0 * np.pi * counter / order
     twiddle = np.stack([np.cos(turn), -np.sin(turn)]).astype(np.float32)
-    twiddle_cols = np.broadcast_to(twiddle[:, None, :], (2, 8, half))
-    twiddle_rows = np.broadcast_to(twiddle[:, :, None], (2, half, half))
+    twiddles = np.concatenate(
+        [np.broadcast_to(twiddle[:, :, None], (2, half, half)), np.broadcast_to(twiddle[:, None, :], (2, SUBLANES, half))], axis=1
+    )
     sorting = np.zeros((order, order), np.float32)
     sorting[np.arange(half), 2 * np.arange(half)] = 1.0
     sorting[half + np.arange(half), 2 * np.arange(half) + 1] = 1.0
     return (
-        jnp.asarray(along_rows),
-        jnp.asarray(along_cols),
-        jnp.asarray(np.ascontiguousarray(twiddle_cols)),
-        jnp.asarray(np.ascontiguousarray(twiddle_rows)),
+        jnp.asarray(np.stack(turns)),
+        jnp.asarray(np.ascontiguousarray(twiddles)),
         jnp.asarray(np.stack([sorting, sorting.T]).astype(jnp.bfloat16)),
     )
 
@@ -172,14 +155,46 @@
     ref[1, rows, cols] = (value - high.astype(f32)).astype(bf16)
 
 
-def right_dot(x_ref, table):
+def right_dot(x_ref, table_ref):
     left = jnp.concatenate([x_ref[0], x_ref[1], x_ref[0]], axis=1)
-    return jnp.dot(left, table, preferred_element_type=f32)
-
-
-def left_dot(table, x_ref):
+    right = jnp.concatenate([table_ref[0], table_ref[0], table_ref[1]], axis=0)
+    return jnp.dot(left, right, preferred_element_type=f32)
+
+
+def left_dot(table_ref, x_ref):
+    left = jnp.concatenate([table_ref[0], table_ref[0], table_ref[1]], axis=1)
     right = jnp.concatenate([x_ref[0], x_ref[1], x_ref[0]], axis=0)
-    return jnp.dot(table, right, preferred_element_type=f32)
+    return jnp.dot(left, right, preferred_element_type=f32)
+
+
+def repeated(group, rows):
+    return jnp.concatenate([group] * (rows // SUBLANES), axis=0)
+
+
+def encode(read, out_ref, rows, first, last):
+    for col in range(0, out_ref.shape[1], LANES):
+        cols = pl.ds(col, LANES)
+        largest = jnp.full((SUBLANES, LANES), 1e-30, f32)
+        for start in range(0, rows, CHUNK):
+            for comp in range(2):
+                for group in row_groups(jnp.abs(read(comp, pl.ds(start, CHUNK), cols))):
+                    largest = jnp.maximum(largest, group)
+        exponent = jnp.ceil(jnp.log2(largest))
+        out_ref[last : last + SUBLANES, cols] = exponent.astype(jnp.int32)
+        scale = repeated(jnp.exp2(-exponent) * LEVELS, CHUNK)
+        for start in range(0, rows, CHUNK):
+            codes = []
+            for comp in range(2):
+                scaled = jnp.clip(read(comp, pl.ds(start, CHUNK), cols) * scale, -LEVELS, LEVELS)
+                codes.append(jnp.round(scaled).astype(jnp.int32))
+            out_ref[pl.ds(first + start, CHUNK), cols] = (codes[0] << 16) | (codes[1] & 0xFFFF)
+
+
+def decode(ref, start, last, col):
+    cols = pl.ds(col, LANES)
+    words = ref[pl.ds(start, CHUNK), cols]
+    scale = repeated(jnp.exp2(ref[last : last + SUBLANES, cols].astype(f32)) * (1.0 / LEVELS), CHUNK)
+    return (words >> 16).astype(f32) * scale, ((words << 16) >> 16).astype(f32) * scale
 
 
 def cut_chunk(ext_ref, comp, first, top, left, rows):
@@ -191,10 +206,10 @@
 
 
 def forward(order, ext_ref, probe_ref, consts, y, x, win_ref, power_ref, weight, xa_ref, xb_ref, ya_ref, yb_ref, far_ref):
-    rows_table, cols_table, tw_cols, tw_rows = consts
+    turns, twiddles = consts
     half = order // 2
-    tw_re = jnp.concatenate([tw_cols[0]] * (CHUNK // 8), axis=0)
-    tw_im = jnp.concatenate([tw_cols[1]] * (CHUNK // 8), axis=0)
+    tw_re = repeated(twiddles[0, half : half + SUBLANES, :], CHUNK)
+    tw_im = repeated(twiddles[1, half : half + SUBLANES, :], CHUNK)
     for first in range(0, order, CHUNK):
         rows = pl.ds(first, CHUNK)
         win_re = cut_chunk(ext_ref, 0, first, y, x, CHUNK)
@@ -214,13 +229,13 @@
         store_split(xb_ref, rows, pl.ds(0, half), d_re * tw_re - d_im * tw_im)
         store_split(xb_ref, rows, pl.ds(half, half), d_re * tw_im + d_im * tw_re)
     yield
-    ya_ref[...] = right_dot(xa_ref, cols_table[0])
-    yb_ref[...] = right_dot(xb_ref, cols_table[0])
+    ya_ref[...] = right_dot(xa_ref, turns.at[0])
+    yb_ref[...] = right_dot(xb_ref, turns.at[0])
     yield
     for first in range(0, half, CHUNK):
         rows = pl.ds(first, CHUNK)
         below = pl.ds(half + first, CHUNK)
-        t_re, t_im = tw_rows[0, rows, :], tw_rows[1, rows, :]
+        t_re, t_im = twiddles[0, rows, :], twiddles[1, rows, :]
         for k, y_ref in enumerate((ya_ref, yb_ref)):
             cols = pl.ds(k * half, half)
             up_re, up_im = y_ref[rows, 0:half], y_ref[rows, half:order]
@@ -231,16 +246,16 @@
             store_split(xb_ref, rows, cols, d_re * t_re - d_im * t_im)
             store_split(xb_ref, below, cols, d_re * t_im + d_im * t_re)
     yield
-    far_ref[0] = left_dot(rows_table[0], xa_ref)
-    far_ref[1] = left_dot(rows_table[0], xb_ref)
+    far_ref[0] = left_dot(turns.at[1], xa_ref)
+    far_ref[1] = left_dot(turns.at[1], xb_ref)
     yield
 
 
 def backward(order, far_ref, amp_ref, consts, y, x, weight, probe_ref, win_ref, xa_ref, xb_ref, ya_ref, yb_ref, grad_ref, numer_ref):
-    rows_table, cols_table, tw_cols, tw_rows = consts
+    turns, twiddles = consts
     half = order // 2
-    tw_re = jnp.concatenate([tw_cols[0]] * (CHUNK // 8), axis=0)
-    tw_im = jnp.concatenate([tw_cols[1]] * (CHUNK // 8), axis=0)
+    tw_re = repeated(twiddles[0, half : half + SUBLANES, :], CHUNK)
+    tw_im = repeated(twiddles[1, half : half + SUBLANES, :], CHUNK)
     for k, x_ref in enumerate((xa_ref, xb_ref)):
         for first in range(0, half, CHUNK):
             rows = pl.ds(first, CHUNK)
@@ -251,13 +266,13 @@
             store_split(x_ref, rows, slice(None), far_re * factor)
             store_split(x_ref, below, slice(None), far_im * factor)
     yield
-    ya_ref[...] = left_dot(rows_table[1], xa_ref)
-    yb_ref[...] = left_dot(rows_table[1], xb_ref)
+    ya_ref[...] = left_dot(turns.at[0], xa_ref)
+    yb_ref[...] = left_dot(turns.at[0], xb_ref)
     yield
     for first in range(0, half, CHUNK):
         rows = pl.ds(first, CHUNK)
         below = pl.ds(half + first, CHUNK)
-        t_re, t_im = tw_rows[0, rows, :], tw_rows[1, rows, :]
+        t_re, t_im = twiddles[0, rows, :], twiddles[1, rows, :]
         for k, x_ref in enumerate((xa_ref, xb_ref)):
             cols = slice(k * half, (k + 1) * half)
             a_re, a_im = ya_ref[rows, cols], ya_ref[below, cols]
@@ -268,8 +283,8 @@
             store_split(x_ref, below, pl.ds(0, half), a_re - c_re)
             store_split(x_ref, below, pl.ds(half, half), a_im - c_im)
     yield
-    ya_ref[...] = right_dot(xa_ref, cols_table[1])
-    yb_ref[...] = right_dot(xb_ref, cols_table[1])
+    ya_ref[...] = right_dot(xa_ref, turns.at[1])
+    yb_ref[...] = right_dot(xb_ref, turns.at[1])
     yield
 
     def adder(comp):
@@ -315,7 +330,7 @@
         live = still
 
 
-def outgoing_kernel(dims, pos_ref, me_ref, amp_ref, out_ref, sems):
+def outgoing_kernel(dims, pos_ref, me_ref, amp_ref, after_ref, out_ref, sems):
     tile_rows, tile_cols, pat_count, col_count, capacity = dims
     first = (me_ref[0] * col_count + me_ref[1]) * pat_count
     owners = [lax.div(pos_ref[2 * (first + k) + 1], tile_cols) for k in range(pat_count)]
@@ -358,17 +373,37 @@
     out_ref[...] = sums_ref[tile_rows : (span + 1) * tile_rows, tile_cols : (span + 1) * tile_cols]
 
 
-def first_half_kernel(dims, pos_ref, me_ref, own_ref, right_ref, below_ref, diag_ref, probe_ref, rows_table, cols_table, tw_cols, tw_rows,
-                      far_out, power_out, ext_ref, win_ref, xa_ref, xb_ref, ya_ref, yb_ref, far_ref, ys_ref, xs_ref, slots_ref, sems):
+def encode_kernel(obj_ref, out_ref):
+    rows = obj_ref.shape[1]
+    encode(lambda comp, at, cols: obj_ref[comp, at, cols], out_ref, rows, 0, rows)
+
+
+def unfold(dims, ext_ref, own_ref, coded_refs):
+    tile_rows, tile_cols = dims[:2]
+    ext_ref[:, 0:tile_rows, 0:tile_cols] = own_ref[...]
+    for (i, j), ref in zip(((0, 1), (1, 0), (1, 1)), coded_refs):
+        for col in range(0, tile_cols, LANES):
+            for start in range(0, tile_rows, CHUNK):
+                parts = decode(ref, start, tile_rows, col)
+                for comp in range(2):
+                    ext_ref[comp, pl.ds(i * tile_rows + start, CHUNK), pl.ds(j * tile_cols + col, LANES)] = parts[comp]
+
+
+def chunked(out_ref, plane, planes, value_ref):
+    chunks = out_ref.shape[0]
+    rows = value_ref.shape[0] // chunks
+    for chunk in range(chunks):
+        out_ref[chunk, plane * rows : (plane + 1) * rows, :] = value_ref[chunk * rows : (chunk + 1) * rows, :]
+
+
+def first_half_kernel(dims, pos_ref, me_ref, own_ref, right_ref, below_ref, diag_ref, probe_ref, turns, twiddles,
+                      far_out, power_out, ext_out, win_ref, xa_ref, xb_ref, ya_ref, yb_ref, far_ref, ys_ref, xs_ref, slots_ref, sems):
     tile_rows, tile_cols, pat_count, col_count, capacity = dims
     order = probe_ref.shape[1]
     count = list_patterns(dims, pos_ref, me_ref, ys_ref, xs_ref, slots_ref)
-    ext_ref[:, 0:tile_rows, 0:tile_cols] = own_ref[...]
-    ext_ref[:, 0:tile_rows, tile_cols:] = right_ref[...]
-    ext_ref[:, tile_rows:, 0:tile_cols] = below_ref[...]
-    ext_ref[:, tile_rows:, tile_cols:] = diag_ref[...]
+    unfold(dims, ext_out, own_ref, (right_ref, below_ref, diag_ref))
     power_out[...] = jnp.zeros_like(power_out)
-    consts = (rows_table, cols_table, tw_cols, tw_rows)
+    consts = (turns, twiddles)
 
     def pair(step, carry):
         stages = []
@@ -376,7 +411,7 @@
             listed = 2 * step + k
             weight = (listed < count).astype(f32)
             index = jnp.minimum(listed, count - 1)
-            stages.append(forward(order, ext_ref, probe_ref, consts, ys_ref[index], xs_ref[index], win_ref.at[k], power_out, weight,
+            stages.append(forward(order, ext_out, probe_ref, consts, ys_ref[index], xs_ref[index], win_ref.at[k], power_out, weight,
                                   xa_ref.at[k], xb_ref.at[k], ya_ref.at[k], yb_ref.at[k], far_ref.at[listed]))
         interleaved(*stages)
         for k in range(2):
@@ -394,9 +429,9 @@
     lax.fori_loop(0, 2 * pairs, settle, 0)
 
 
-def second_half_kernel(dims, pos_ref, me_ref, own_ref, right_ref, below_ref, diag_ref, probe_ref, far_in, amp_in, rows_table, cols_table, tw_cols, tw_rows, sorting,
-                       top_out, bottom_out, numer_out, amp_out,
-                       ext_ref, grad_ref, win_ref, xa_ref, xb_ref, ya_ref, yb_ref, far_ref, amp_ref, sorted_ref, ys_ref, xs_ref, slots_ref, far_sems, amp_sems, out_sems):
+def second_half_kernel(dims, pos_ref, me_ref, ext_ref, probe_ref, power_ref, weights_ref, far_in, amp_in, turns, twiddles, sorting,
+                       share_out, top_out, bottom_out, numer_out, amp_out,
+                       win_ref, xa_ref, xb_ref, ya_ref, yb_ref, numer_ref, far_ref, amp_ref, sorted_ref, ys_ref, xs_ref, slots_ref, far_sems, amp_sems, out_sems):
     tile_rows, tile_cols, pat_count, col_count, capacity = dims
     order = probe_ref.shape[1]
     half = order // 2
@@ -415,13 +450,9 @@
         return carry
 
     lax.fori_loop(0, 2 * pairs, begin, 0)
-    ext_ref[:, 0:tile_rows, 0:tile_cols] = own_ref[...]
-    ext_ref[:, 0:tile_rows, tile_cols:] = right_ref[...]
-    ext_ref[:, tile_rows:, 0:tile_cols] = below_ref[...]
-    ext_ref[:, tile_rows:, tile_cols:] = diag_ref[...]
-    grad_ref[...] = jnp.zeros_like(grad_ref)
-    numer_out[...] = jnp.zeros_like(numer_out)
-    consts = (rows_table, cols_table, tw_cols, tw_rows)
+    share_out[...] = jnp.zeros_like(share_out)
+    numer_ref[...] = jnp.zeros_like(numer_ref)
+    consts = (turns, twiddles)
 
     def pair(step, carry):
         stages = []
@@ -441,7 +472,7 @@
                     for c, tile in enumerate(cut_chunk(ext_ref, comp, first, y, x, CHUNK)):
                         win_ref[k, comp, pl.ds(first, CHUNK), pl.ds(c * half, half)] = tile
             stages.append(backward(order, far_ref.at[listed], sorted_ref.at[listed], consts, y, x, weight, probe_ref, win_ref.at[k],
-                                   xa_ref.at[k], xb_ref.at[k], ya_ref.at[k], yb_ref.at[k], grad_ref, numer_out))
+                                   xa_ref.at[k], xb_ref.at[k], ya_ref.at[k], yb_ref.at[k], share_out, numer_ref))
         interleaved(*stages)
         for k in range(2):
             listed = 2 * step + k
@@ -449,8 +480,15 @@
         return carry
 
     lax.fori_loop(0, pairs, pair, 0)
-    top_out[...] = grad_ref[:, 0:tile_rows, :]
-    bottom_out[...] = grad_ref[:, tile_rows:, :]
+    for first in range(0, 2 * tile_rows, CHUNK):
+        rows = pl.ds(first, CHUNK)
+        scale = 1.0 / (weights_ref[rows, :] + object_regular)
+        for comp in range(2):
+            share_out[comp, rows, :] = share_out[comp, rows, :] * scale
+    encode(lambda comp, at, cols: share_out[comp, at, cols], top_out, tile_rows, 0, tile_rows)
+    encode(lambda comp, at, cols: share_out[comp, pl.ds(tile_rows + at.start, at.size), cols], bottom_out, tile_rows, 0, tile_rows)
+    for plane, ref in enumerate((numer_ref.at[0], numer_ref.at[1], power_ref)):
+        chunked(numer_out, plane, 3, ref)
 
     def settle(listed, carry):
         pltpu.make_async_copy(sorted_ref.at[listed], amp_out.at[listed], out_sems.at[listed]).wait()
@@ -459,10 +497,28 @@
     lax.fori_loop(0, 2 * pairs, settle, 0)
 
 
-def whole_kernel(dims, pos_ref, me_ref, own_ref, right_ref, below_ref, diag_ref, sum_left_ref, sum_right_ref, from_left_ref, from_right_ref, weights_ref,
-                 probe_ref, amp_in, rows_table, cols_table, tw_cols, tw_rows,
+def rows_sum_kernel(dims, share_ref, above_ref, below_ref, sum_out, left_out, right_out):
+    tile_rows, tile_cols = dims[:2]
+    for i, ref in enumerate((above_ref, below_ref)):
+        for col in range(0, 2 * tile_cols, LANES):
+            for start in range(0, tile_rows, CHUNK):
+                rows, cols = pl.ds(i * tile_rows + start, CHUNK), pl.ds(col, LANES)
+                parts = decode(ref, start, tile_rows, col)
+                for comp in range(2):
+                    sum_out[comp, rows, cols] = share_ref[comp, rows, cols] + parts[comp]
+    for j, ref in enumerate((left_out, right_out)):
+        for i in range(2):
+
+            def read(comp, at, cols, i=i, j=j):
+                return sum_out[comp, pl.ds(i * tile_rows + at.start, at.size), pl.ds(j * tile_cols + cols.start, cols.size)]
+
+            encode(read, ref, tile_rows, i * tile_rows, 2 * tile_rows + i * SUBLANES)
+
+
+def whole_kernel(dims, pos_ref, me_ref, old_ref, sum_ref, from_left_ref, from_right_ref, weights_ref,
+                 probe_ref, amp_in, turns, twiddles,
                  current_out, own_out, right_out, below_out, diag_out, numer_out,
-                 ext_ref, grad_ref, win_ref, xa_ref, xb_ref, ya_ref, yb_ref, far_ref, amp_ref, ys_ref, xs_ref, slots_ref, amp_sems):
+                 ext_ref, grad_ref, win_ref, xa_ref, xb_ref, ya_ref, yb_ref, numer_ref, far_ref, amp_ref, ys_ref, xs_ref, slots_ref, amp_sems):
     tile_rows, tile_cols, pat_count, col_count, capacity = dims
     order = probe_ref.shape[1]
     count = list_patterns(dims, pos_ref, me_ref, ys_ref, xs_ref, slots_ref)
@@ -476,22 +532,19 @@
         return carry
 
     lax.fori_loop(0, 2 * pairs, begin, 0)
-    olds = ((own_ref, right_ref), (below_ref, diag_ref))
-    sums = ((sum_left_ref, from_left_ref), (sum_right_ref, from_right_ref))
-    for i in range(2):
-        for j in range(2):
-            for first in range(0, tile_rows, CHUNK):
-                rows = pl.ds(first, CHUNK)
-                ext_rows = pl.ds(i * tile_rows + first, CHUNK)
-                ext_cols = pl.ds(j * tile_cols, tile_cols)
-                scale = 1.0 / (weights_ref[ext_rows, ext_cols] + object_regular)
-                for comp in range(2):
-                    total = sums[j][0][comp, ext_rows, :] + sums[j][1][comp, ext_rows, :]
-                    ext_ref[comp, ext_rows, ext_cols] = (object_regular * olds[i][j][comp, rows, :] + total) * scale
+    for j, ref in enumerate((from_left_ref, from_right_ref)):
+        for i in range(2):
+            for col in range(0, tile_cols, LANES):
+                for start in range(0, tile_rows, CHUNK):
+                    rows, cols = pl.ds(i * tile_rows + start, CHUNK), pl.ds(j * tile_cols + col, LANES)
+                    parts = decode(ref, i * tile_rows + start, 2 * tile_rows + i * SUBLANES, col)
+                    scale = object_regular / (weights_ref[rows, cols] + object_regular)
+                    for comp in range(2):
+                        ext_ref[comp, rows, cols] = old_ref[comp, rows, cols] * scale + (sum_ref[comp, rows, cols] + parts[comp])
     current_out[...] = ext_ref[:, 0:tile_rows, 0:tile_cols]
     grad_ref[...] = jnp.zeros_like(grad_ref)
-    numer_out[...] = jnp.zeros_like(numer_out)
-    consts = (rows_table, cols_table, tw_cols, tw_rows)
+    numer_ref[...] = jnp.zeros_like(numer_ref)
+    consts = (turns, twiddles)
 
     def pair(step, carry):
         stages = []
@@ -504,10 +557,10 @@
             y, x = ys_ref[index], xs_ref[index]
 
             def both(k=k, listed=listed, weight=weight, y=y, x=x):
-                yield from forward(order, ext_ref, probe_ref, consts, y, x, win_ref.at[k], numer_out.at[2], weight,
+                yield from forward(order, ext_ref, probe_ref, consts, y, x, win_ref.at[k], numer_ref.at[2], weight,
                                    xa_ref.at[k], xb_ref.at[k], ya_ref.at[k], yb_ref.at[k], far_ref.at[k])
                 yield from backward(order, far_ref.at[k], amp_ref.at[listed], consts, y, x, weight, probe_ref, win_ref.at[k],
-                                    xa_ref.at[k], xb_ref.at[k], ya_ref.at[k], yb_ref.at[k], grad_ref, numer_out)
+                                    xa_ref.at[k], xb_ref.at[k], ya_ref.at[k], yb_ref.at[k], grad_ref, numer_ref)
 
             stages.append(both())
         interleaved(*stages)
@@ -515,9 +568,29 @@
 
     lax.fori_loop(0, pairs, pair, 0)
     own_out[...] = grad_ref[:, 0:tile_rows, 0:tile_cols]
-    right_out[...] = grad_ref[:, 0:tile_rows, tile_cols:]
-    below_out[...] = grad_ref[:, tile_rows:, 0:tile_cols]
-    diag_out[...] = grad_ref[:, tile_rows:, tile_cols:]
+    for (i, j), ref in zip(((0, 1), (1, 0), (1, 1)), (right_out, below_out, diag_out)):
+
+        def read(comp, at, cols, i=i, j=j):
+            rows, cols = pl.ds(i * tile_rows + at.start, at.size), pl.ds(j * tile_cols + cols.start, cols.size)
+            return grad_ref[comp, rows, cols] / (weights_ref[rows, cols] + object_regular)
+
+        encode(read, ref, tile_rows, 0, tile_rows)
+    for plane in range(3):
+        chunked(numer_out, plane, 3, numer_ref.at[plane])
+
+
+def object_kernel(dims, current_ref, own_ref, left_ref, above_ref, diag_ref, before_ref, weights_ref, out_ref):
+    tile_rows, tile_cols = dims[:2]
+    for col in range(0, tile_cols, LANES):
+        for start in range(0, tile_rows, CHUNK):
+            rows, cols = pl.ds(start, CHUNK), pl.ds(col, LANES)
+            scale = 1.0 / (weights_ref[rows, cols] + object_regular)
+            back = (before_ref[rows, cols] + object_regular) * scale
+            parts = [decode(ref, start, tile_rows, col) for ref in (left_ref, above_ref, diag_ref)]
+            for comp in range(2):
+                coded = parts[0][comp] + parts[1][comp] + parts[2][comp]
+                old = object_regular * current_ref[comp, rows, cols] + own_ref[comp, rows, cols]
+                out_ref[comp, rows, cols] = old * scale + coded * back
 
 
 def shape(dims, dtype=f32):
@@ -578,24 +651,15 @@
 
 
 def probe_update(probe, numer):
-    cols = lax.axis_size("col")
-    my_col = lax.axis_index("col")
-    masks = [1 << k for k in range(cols.bit_length() - 1)]
-    share, old = numer, probe
-    for mask in masks:
-        upper = (my_col & mask) != 0
-        half = share.shape[1] // 2
-        first, last = share[:, :half], share[:, half:]
-        given = jnp.where(upper, first, last)
-        share = jnp.where(upper, last, first) + swapped(given, "col", mask)
-        old = jnp.where(upper, old[:, half:], old[:, :half])
-    share = summed_over_rows(share)
-    fresh = (old + share[:2]) / (share[2] + probe_regular)[None]
-    for mask in reversed(masks):
-        upper = (my_col & mask) != 0
-        other = swapped(fresh, "col", mask)
-        fresh = jnp.where(upper, jnp.concatenate([other, fresh], axis=1), jnp.concatenate([fresh, other], axis=1))
-    return fresh
+    cols, order = lax.axis_size("col"), probe.shape[1]
+    rows = order // cols
+    parts = lax.all_to_all(numer, "col", split_axis=0, concat_axis=0, tiled=True)
+    total = summed_over_rows(jnp.sum(parts, axis=0)).reshape(3, rows, order)
+    old = lax.dynamic_slice_in_dim(probe, lax.axis_index("col") * rows, rows, 1)
+    fresh = (old + total[:2]) / (total[2] + probe_regular)[None]
+    spread = jnp.broadcast_to(fresh.reshape(1, 2 * rows, order), (cols, 2 * rows, order))
+    chunks = lax.all_to_all(spread, "col", split_axis=0, concat_axis=0, tiled=True)
+    return chunks.reshape(cols, 2, rows, order).transpose(1, 0, 2, 3).reshape(2, order, order)
 
 
 def local(obj, probe, amplitudes, positions):
@@ -607,23 +671,26 @@
     dims = (tile_rows, tile_cols, pat_count, col_count, capacity)
     me = jnp.stack([lax.axis_index("row"), lax.axis_index("col")]).astype(jnp.int32)
     pos = positions.reshape(-1)
-    rows_table, cols_table, tw_cols, tw_rows, sorting = tables(order)
-    consts = (rows_table, cols_table, tw_cols, tw_rows)
+    turns, twiddles, sorting = tables(order)
     tile = (2, tile_rows, tile_cols)
     window = (2, order, order)
     wide = (2, 2 * tile_rows, 2 * tile_cols)
+    shares = (col_count, 3 * order // col_count, order)
+    coded_tile = shape((tile_rows + SUBLANES, tile_cols), jnp.int32)
+    coded_row = shape((tile_rows + SUBLANES, 2 * tile_cols), jnp.int32)
+    coded_col = shape((2 * (tile_rows + SUBLANES), tile_cols), jnp.int32)
     one_pattern = 24 * 2 * order**3
 
+    coded = call(encode_kernel, coded_tile, VMEM, [VMEM], [], 1 << 26)(obj)
+    right = passed_along(coded, "col", -1)
+    below = passed_along(coded, "row", -1)
+    diag = passed_both(coded, -1, -1)
+
     outgoing = call(
-        functools.partial(outgoing_kernel, dims), shape((col_count * SEND, order, order), bf16), ANY, [SMEM, SMEM, ANY],
+        functools.partial(outgoing_kernel, dims), shape((col_count * SEND, order, order), bf16), ANY, [SMEM, SMEM, ANY, ANY],
         [pltpu.SemaphoreType.DMA((pat_count,))], 1 << 20,
-    )(pos, me, amplitudes)
+    )(pos, me, amplitudes, coded)
     incoming = lax.all_to_all(outgoing, "col", split_axis=0, concat_axis=0, tiled=True)
-
-    right = passed_along(obj, "col", -1)
-    below = passed_along(obj, "row", -1)
-    diag = passed_both(obj, -1, -1)
-    pieces = (obj, right, below, diag)
 
     def weights(probe_now, span):
         return call(
@@ -631,45 +698,52 @@
             [pltpu.VMEM(((span + 2) * tile_rows, (span + 2) * tile_cols), f32), pltpu.VMEM((order, order), f32)], 8 << 30,
         )(pos, me, probe_now)
 
-    weights_now = weights(probe, 2)
-
-    far, power = call(
-        functools.partial(first_half_kernel, dims), (shape((capacity,) + window), shape((order, order))), (ANY, VMEM),
-        [SMEM, SMEM] + [VMEM] * 9,
-        [pltpu.VMEM(wide, f32)] + work_scratch(order) + [pltpu.VMEM((capacity,) + window, f32)] + list_scratch(capacity)
-        + [pltpu.SemaphoreType.DMA((capacity,))],
+    weights_old = weights(probe, 2)
+
+    far, power, ext = call(
+        functools.partial(first_half_kernel, dims), (shape((capacity,) + window), shape((order, order)), shape(wide)), (ANY, VMEM, VMEM),
+        [SMEM, SMEM] + [VMEM] * 7,
+        work_scratch(order) + [pltpu.VMEM((capacity,) + window, f32)] + list_scratch(capacity) + [pltpu.SemaphoreType.DMA((capacity,))],
         capacity * one_pattern // 2,
-    )(pos, me, *pieces, probe, *consts)
-
-    top, bottom, numer, sorted_amps = call(
+    )(pos, me, obj, right, below, diag, probe, turns, twiddles)
+
+    share, top, bottom, numer, sorted_amps = call(
         functools.partial(second_half_kernel, dims),
-        (shape((2, tile_rows, 2 * tile_cols)), shape((2, tile_rows, 2 * tile_cols)), shape(window), shape((capacity, order, order), bf16)),
-        (VMEM, VMEM, VMEM, ANY),
-        [SMEM, SMEM] + [VMEM] * 5 + [ANY, ANY] + [VMEM] * 5,
-        [pltpu.VMEM(wide, f32), pltpu.VMEM(wide, f32)] + work_scratch(order)
-        + [pltpu.VMEM((capacity,) + window, f32), pltpu.VMEM((capacity, order, order), bf16), pltpu.VMEM((capacity, order, order), bf16)]
+        (shape(wide), coded_row, coded_row, shape(shares), shape((capacity, order, order), bf16)),
+        (VMEM, VMEM, VMEM, VMEM, ANY),
+        [SMEM, SMEM] + [VMEM] * 4 + [ANY, ANY] + [VMEM] * 3,
+        work_scratch(order)
+        + [pltpu.VMEM(window, f32), pltpu.VMEM((capacity,) + window, f32), pltpu.VMEM((capacity, order, order), bf16), pltpu.VMEM((capacity, order, order), bf16)]
         + list_scratch(capacity) + [pltpu.SemaphoreType.DMA((capacity,))] * 3,
         capacity * one_pattern // 2,
-    )(pos, me, *pieces, probe, far, incoming, *consts, sorting)
-
-    probe_now = probe_update(probe, jnp.concatenate([numer, power[None]]))
-    sums = jnp.concatenate([top + passed_along(bottom, "row", 1), bottom + passed_along(top, "row", -1)], axis=1)
-    sum_left, sum_right = sums[:, :, :tile_cols], sums[:, :, tile_cols:]
-    from_left = passed_along(sum_right, "col", 1)
-    from_right = passed_along(sum_left, "col", -1)
+    )(pos, me, ext, probe, power, weights_old, far, incoming, turns, twiddles, sorting)
+
+    from_above = passed_along(bottom, "row", 1)
+    from_below = passed_along(top, "row", -1)
+    probe_now = probe_update(probe, numer)
+    sums, to_left, to_right = call(
+        functools.partial(rows_sum_kernel, dims), (shape(wide), coded_col, coded_col), (VMEM,) * 3, [VMEM] * 3, [], 1 << 26,
+    )(share, from_above, from_below)
+    from_left = passed_along(to_right, "col", 1)
+    from_right = passed_along(to_left, "col", -1)
 
     current, own, to_right, to_below, to_diag, numer = call(
-        functools.partial(whole_kernel, dims), (shape(tile),) * 5 + (shape((3, order, order)),), (VMEM,) * 6,
-        [SMEM, SMEM] + [VMEM] * 10 + [ANY] + [VMEM] * 4,
+        functools.partial(whole_kernel, dims), (shape(tile), shape(tile), coded_tile, coded_tile, coded_tile, shape(shares)), (VMEM,) * 6,
+        [SMEM, SMEM] + [VMEM] * 6 + [ANY] + [VMEM] * 2,
         [pltpu.VMEM(wide, f32), pltpu.VMEM(wide, f32)] + work_scratch(order)
-        + [pltpu.VMEM((2,) + window, f32), pltpu.VMEM((capacity, order, order), bf16)] + list_scratch(capacity) + [pltpu.SemaphoreType.DMA((capacity,))],
+        + [pltpu.VMEM((3, order, order), f32), pltpu.VMEM((2,) + window, f32), pltpu.VMEM((capacity, order, order), bf16)]
+        + list_scratch(capacity) + [pltpu.SemaphoreType.DMA((capacity,))],
         capacity * one_pattern,
-    )(pos, me, *pieces, sum_left, sum_right, from_left, from_right, weights_now, probe_now, sorted_amps, *consts)
-
-    weights_now = weights(probe_now, 1)
+    )(pos, me, ext, sums, from_left, from_right, weights_old, probe_now, sorted_amps, turns, twiddles)
+
+    from_left = passed_along(to_right, "col", 1)
+    from_above = passed_along(to_below, "row", 1)
+    from_diag = passed_both(to_diag, 1, 1)
+    weights_new = weights(probe_now, 1)
     new_probe = probe_update(probe_now, numer)
-    total = own + passed_along(to_right, "col", 1) + passed_along(to_below, "row", 1) + passed_both(to_diag, 1, 1)
-    new_object = (object_regular * current + total) / (weights_now + object_regular)[None]
+    new_object = call(functools.partial(object_kernel, dims), shape(tile), VMEM, [VMEM] * 7, [], 1 << 26)(
+        current, own, from_left, from_above, from_diag, weights_old[:tile_rows, :tile_cols], weights_new
+    )
     return new_object, new_probe
 
 

time: 223 us -> 182 us (0.82)
  waiting for transfers between devices: 83.3 us -> 30.5 us
  blocking collectives: 0 us -> 38.6 us
  starting transfers between devices: 84.1 us -> 56.2 us
  Pallas kernels: 35.1 us -> 40.9 us
  local copies, waits for them, and re-layouts: 11.9 us -> 8.91 us
  other arithmetic: 6.07 us -> 3.5 us
    ppermute x18 -> x6, starting transfers between devices: 62.8 us -> 9.14 us  [swapped(): lax.ppermute(value, axis, [(k, k ^ mask) for k in range(lax.axis_size(axi...]
    ppermute x18 -> x6, waiting for transfers between devices: 55.1 us -> 1.56 us  [swapped(): lax.ppermute(value, axis, [(k, k ^ mask) for k in range(lax.axis_size(axi...]
    all_to_all x0 -> x2, blocking collectives: none -> 38.6 us  [the longest x1 21.1 us: probe_update(): lax.all_to_all(numer, 'col', split_axis=0, concat_axis=0, tiled=True)]
    all_to_all x0 -> x2, starting transfers between devices: none -> 23.6 us  [the longest x1 19.5 us: probe_update(): lax.all_to_all(numer, 'col', split_axis=0, concat_axis=0, tiled=True)]
    all_to_all x0 -> x2, waiting for transfers between devices: none -> 11.5 us  [the longest x1 7.29 us: probe_update(): lax.all_to_all(numer, 'col', split_axis=0, concat_axis=0, tiled=True)]
    ppermute x2, waiting for transfers between devices: 13.8 us -> 4.1 us  [passed_both(): return lax.ppermute(value, ('row', 'col'), pairs)]
    ppermute x8, waiting for transfers between devices: 14 us -> 6.64 us  [passed_along(): lax.ppermute(value, axis, [(source, source + steps) for source in range(l...]
    pallas_call x2 -> x5, Pallas kernels: 19 us -> 25.5 us  [the longest x1 11.1 us: local(): call(functools.partial(second_half_kernel, dims), (shape(wide), coded_row...]
  transfers between devices with their start and end apart: 29 -> 19, of which waited for: 15 -> 8; matrix products, arithmetic and copies ran while one was open for 1% -> 2% of each run, Pallas kernels for 7% -> 10%
where the time goes in v2:
time: 182 us; the launch traced here: 180 us
  starting transfers between devices  56.2 us (31%)
  Pallas kernels  40.9 us (22%)
  blocking collectives  38.6 us (21%)
  waiting for transfers between devices  30.5 us (17%)
  local copies, waits for them, and re-layouts  8.91 us (5%)
  other arithmetic  3.5 us (2%)
    all_to_all x1, blocking collectives, probe_update(): lax.all_to_all(numer, 'col', split_axis=0, concat_axis=0, tiled=True)  21.1 us
    all_to_all x1, starting transfers between devices, probe_update(): lax.all_to_all(numer, 'col', split_axis=0, concat_axis=0, tiled=True)  19.5 us
    all_to_all x1, blocking collectives, probe_update(): lax.all_to_all(spread, 'col', split_axis=0, concat_axis=0, tiled=True)  17.5 us
    ppermute x8, starting transfers between devices, passed_along(): lax.ppermute(value, axis, [(source, source + steps) for source in range(l...  14 us
    pallas_call x1, Pallas kernels, local(): call(functools.partial(second_half_kernel, dims), (shape(wide), coded_row...  11.1 us
    pallas_call x1, Pallas kernels, local(): call(functools.partial(whole_kernel, dims), (shape(tile), shape(tile), co...  10.5 us
    ppermute x6, starting transfers between devices, swapped(): lax.ppermute(value, axis, [(k, k ^ mask) for k in range(lax.axis_size(axi...  9.14 us
    pallas_call x2, Pallas kernels, weights(): call(functools.partial(weights_kernel, dims, span), shape((span * tile_ro...  8.39 us
  transfers between devices with their start and end apart: 19, of which 8 were waited for; matrix products, arithmetic and copies ran while one was open for 2% of the time, Pallas kernels for 10%

profile of v2, /device:TPU:0, one launch (start us, length us, event | category | flops | bytes accessed | tf_op | source)
XLA Modules:
  0.0 179.7 jit_solution(622784913149134455)
XLA Ops:
  3.9 1.4 shard_map.89
  5.3 5.3 %all-to-all-start = ((bf16[16,256,256]{2,1,0:T(8,128)(2,1)}), bf16[16,256,256]{2,1,0:T(8,128)(2,1)}, u32[]{:S(2)}, u32[]{:S(2)}) async-start(bf16[16,256,256]{2,1,0:T(8,128)(2,1)} %shard_map.89), calls=%async_computation | async-start | bytes 4194304 | tf_op jit(solution)/shard_map/all_to_all | solution.py:693
  10.7 1.4 collective-permute-start
  12.1 1.3 collective-permute-start.1
  13.4 1.3 collective-permute-start.2
  14.7 4.9 %shard_map.88.weights_ref = f32[512,512]{1,0:T(8,128)S(1)} custom-call(s32[256]{0:T(256)S(1)} %reshape.37.pos_ref, s32[2]{0:T(128)S(1)} %pad_add_fusion.me_ref, f32[2,256,256]{2,1,0:T(8,128)S(1)} %copy-done.3), custom_call_target="tpu_custom_call" | custom-call | flops 8589934592 | bytes 8388608 | tf_op jit(solution)/shard_map/pallas_call | solution.py:696
  19.6 3.6 %collective-permute-done.1.below_ref = s32[264,256]{1,0:T(8,128)S(1)} collective-permute-done((s32[264,256]{1,0:T(8,128)S(1)}, s32[264,256]{1,0:T(8,128)S(1)}, u32[]{:S(2)}, u32[]{:S(2)}) %collective-permute-start.1) | collective-permute-done | bytes 270368 | tf_op jit(solution)/shard_map/ppermute | solution.py:629
  23.3 3.3 %collective-permute-done.2.diag_ref = s32[264,256]{1,0:T(8,128)S(1)} collective-permute-done((s32[264,256]{1,0:T(8,128)S(1)}, s32[264,256]{1,0:T(8,128)S(1)}, u32[]{:S(2)}, u32[]{:S(2)}) %collective-permute-start.2) | collective-permute-done | bytes 270368 | tf_op jit(solution)/shard_map/ppermute | solution.py:639
  26.5 5.7 %shard_map.87 = (f32[8,2,256,256]{3,2,1,0:T(8,128)}, f32[256,256]{1,0:T(8,128)S(1)}, f32[2,512,512]{2,1,0:T(8,128)S(1)}) custom-call(s32[256]{0:T(256)S(1)} %reshape.37.pos_ref, s32[2]{0:T(128)S(1)} %pad_add_fusion.me_ref, f32[2,256,256]{2,1,0:T(8,128)S(1)} %copy-done.1, s32[264,256]{1,0:T(8,128)S(1)} %collective-permute-done.right_ref, ...), custom_call_target="tpu_custom_call" | custom-call | flops 3221225472 | bytes 8388608 | tf_op jit(solution)/shard_map/pallas_call | solution.py:703
  32.2 1.4 copy-done.10
  33.6 6.7 %all-to-all-done.amp_in = bf16[16,256,256]{2,1,0:T(8,128)(2,1)} async-done(((bf16[16,256,256]{2,1,0:T(8,128)(2,1)}), bf16[16,256,256]{2,1,0:T(8,128)(2,1)}, u32[]{:S(2)}, u32[]{:S(2)}) %all-to-all-start) | async-done | bytes 2097184 | tf_op jit(solution)/shard_map/all_to_all | solution.py:693
  40.3 11.1 %shard_map.90 = (f32[2,512,512]{2,1,0:T(8,128)}, s32[264,512]{1,0:T(8,128)S(1)}, s32[264,512]{1,0:T(8,128)}, f32[8,96,256]{2,1,0:T(8,128)}, bf16[8,256,256]{2,1,0:T(8,128)(2,1)S(1)}) custom-call(s32[256]{0:T(256)S(1)} %reshape.37.pos_ref, s32[2]{0:T(128)S(1)} %pad_add_fusion.me_ref, f32[2,512,512]{2,1,0:T(8,128)} %copy-done.10, ...), custom_call_target="tpu_custom_call" | custom-call | flops 3221225472 | bytes 8388608 | tf_op jit(solution)/shard_map/pallas_call | solution.py:710
  52.4 19.5 %all-to-all-start.1 = ((f32[8,96,256]{2,1,0:T(8,128)}), f32[8,96,256]{2,1,0:T(8,128)}, u32[]{:S(2)}, u32[]{:S(2)}) async-start(f32[8,96,256]{2,1,0:T(8,128)} %get-tuple-element.28), calls=%async_computation.1 | async-start | bytes 1572864 | tf_op jit(solution)/shard_map/all_to_all | solution.py:656
  71.9 4.1 %collective-permute-start.3 = (s32[264,512]{1,0:T(8,128)}, s32[264,512]{1,0:T(8,128)S(1)}, u32[]{:S(2)}, u32[]{:S(2)}) collective-permute-start(s32[264,512]{1,0:T(8,128)} %get-tuple-element.23), channel_id=1, source_target_pairs={{0,8},{8,16},{16,24},{1,9},{9,17},{17,25},{2,10},{10,18},{18,26},{... | collective-permute-start | bytes 1622024 | tf_op jit(solution)/shard_map/ppermute | solution.py:629
  77.3 7.3 %all-to-all-done.1 = f32[8,96,256]{2,1,0:T(8,128)} async-done(((f32[8,96,256]{2,1,0:T(8,128)}), f32[8,96,256]{2,1,0:T(8,128)}, u32[]{:S(2)}, u32[]{:S(2)}) %all-to-all-start.1) | async-done | bytes 786464 | tf_op jit(solution)/shard_map/all_to_all | solution.py:656
  85.8 2.2 %collective-permute-start.7 = (f32[96,256]{1,0:T(8,128)S(1)}, f32[96,256]{1,0:T(8,128)S(1)}, u32[]{:S(2)}, u32[]{:S(2)}) collective-permute-start(f32[96,256]{1,0:T(8,128)S(1)} %reduce_sum.18), channel_id=1, source_target_pairs={{0,8},{8,0},{16,24},{24,16},{1,9},{9,1},{17,25},{25,17},{2,10},{10... | collective-permute-start | bytes 294920 | tf_op jit(solution)/shard_map/ppermute | solution.py:643
  89.1 1.4 collective-permute-start.9
  90.5 3.0 %collective-permute-done.4.below_ref = s32[264,512]{1,0:T(8,128)S(1)} collective-permute-done((s32[264,512]{1,0:T(8,128)S(1)}, s32[264,512]{1,0:T(8,128)S(1)}, u32[]{:S(2)}, u32[]{:S(2)}) %collective-permute-start.4) | collective-permute-done | bytes 540704 | tf_op jit(solution)/shard_map/ppermute | solution.py:629
  93.5 2.6 %shard_map.91 = (f32[2,512,512]{2,1,0:T(8,128)S(1)}, s32[528,256]{1,0:T(8,128)S(1)}, s32[528,256]{1,0:T(8,128)S(1)}) custom-call(f32[2,512,512]{2,1,0:T(8,128)} %get-tuple-element.22.share_ref, s32[264,512]{1,0:T(8,128)S(1)} %collective-permute-done.3.above_ref, s32[264,512]{1,0:T(8,128)S(1)} %collective-permute-done.4.below_ref), custom_call_target="tpu_custom_call" | custom-call | flops 67108864 | bytes 8388608 | tf_op jit(solution)/shard_map/pallas_call | solution.py:724
  96.0 1.5 collective-permute-start.5
  98.8 1.5 collective-permute-done.8
  101.4 17.5 %all_to_all.25 = f32[8,64,256]{2,1,0:T(8,128)S(1)} all-to-all(f32[8,64,256]{2,1,0:T(8,128)S(1)} %broadcast_in_dim.17), channel_id=1, replica_groups=mesh['row'=4,'col'=8] {'col'}, dimensions={0} | all-to-all | bytes 1048576 | tf_op jit(solution)/shard_map/all_to_all | solution.py:661
  119.0 10.5 %shard_map.92 = (f32[2,256,256]{2,1,0:T(8,128)S(1)}, f32[2,256,256]{2,1,0:T(8,128)S(1)}, s32[264,256]{1,0:T(8,128)S(1)}, s32[264,256]{1,0:T(8,128)S(1)}, s32[264...) custom-call(s32[256]{0:T(256)S(1)} %reshape.37.pos_ref, s32[2]{0:T(128)S(1)} %pad_add_fusion.me_ref, ...), custom_call_target="tpu_custom_call" | custom-call | flops 6442450944 | bytes 8388608 | tf_op jit(solution)/shard_map/pallas_call | solution.py:730
  130.2 21.1 %all_to_all.26 = f32[8,96,256]{2,1,0:T(8,128)} all-to-all(f32[8,96,256]{2,1,0:T(8,128)S(1)} %get-tuple-element.35), channel_id=1, replica_groups=mesh['row'=4,'col'=8] {'col'}, dimensions={0} | all-to-all | bytes 1572864 | tf_op jit(solution)/shard_map/all_to_all | solution.py:656
  153.4 3.6 %collective-permute-start.15 = (f32[96,256]{1,0:T(8,128)S(1)}, f32[96,256]{1,0:T(8,128)S(1)}, u32[]{:S(2)}, u32[]{:S(2)}) collective-permute-start(f32[96,256]{1,0:T(8,128)S(1)} %reduce_sum.19), channel_id=1, source_target_pairs={{0,24},{8,16},{16,8},{24,0},{1,25},{9,17},{17,9},{25,1},{2,26},{10... | collective-permute-start | bytes 294920 | tf_op jit(solution)/shard_map/ppermute | solution.py:643
  157.0 1.3 collective-permute-start.10
  158.3 1.8 %collective-permute-start.11 = (s32[264,256]{1,0:T(8,128)S(1)}, s32[264,256]{1,0:T(8,128)S(1)}, u32[]{:S(2)}, u32[]{:S(2)}) collective-permute-start(s32[264,256]{1,0:T(8,128)S(1)} %get-tuple-element.33), channel_id=1, source_target_pairs={{0,8},{8,16},{16,24},{1,9},{9,17},{17,25},{2,10},{10,18},{18,26},{... | collective-permute-start | bytes 811016 | tf_op jit(solution)/shard_map/ppermute | solution.py:629
  160.2 2.8 %collective-permute-start.12 = (s32[264,256]{1,0:T(8,128)S(1)}, s32[264,256]{1,0:T(8,128)S(1)}, u32[]{:S(2)}, u32[]{:S(2)}) collective-permute-start(s32[264,256]{1,0:T(8,128)S(1)} %get-tuple-element.34), channel_id=1, source_target_pairs={{0,9},{1,10},{2,11},{3,12},{4,13},{5,14},{6,15},{8,17},{9,18},{10,... | collective-permute-start | bytes 811016 | tf_op jit(solution)/shard_map/ppermute | solution.py:639
  163.9 4.2 %all-to-all-start.4 = ((f32[8,64,256]{2,1,0:T(8,128)}), f32[8,64,256]{2,1,0:T(8,128)}, u32[]{:S(2)}, u32[]{:S(2)}) async-start(f32[8,64,256]{2,1,0:T(8,128)} %broadcast_in_dim.19), calls=%async_computation.4 | async-start | bytes 1048576 | tf_op jit(solution)/shard_map/all_to_all | solution.py:661
  168.1 3.5 %shard_map.93.weights_ref = f32[256,256]{1,0:T(8,128)S(1)} custom-call(s32[256]{0:T(256)S(1)} %reshape.37.pos_ref, s32[2]{0:T(128)S(1)} %pad_add_fusion.me_ref, f32[2,256,256]{2,1,0:T(8,128)S(1)} %bitcast.16), custom_call_target="tpu_custom_call" | custom-call | flops 8589934592 | bytes 8388608 | tf_op jit(solution)/shard_map/pallas_call | solution.py:696
  173.6 4.2 %all-to-all-done.4 = f32[8,64,256]{2,1,0:T(8,128)} async-done(((f32[8,64,256]{2,1,0:T(8,128)}), f32[8,64,256]{2,1,0:T(8,128)}, u32[]{:S(2)}, u32[]{:S(2)}) %all-to-all-start.4) | async-done | bytes 524320 | tf_op jit(solution)/shard_map/all_to_all | solution.py:661
  177.8 1.9 %copy.13 = f32[2,8,32,256]{3,2,1,0:T(8,128)} copy(f32[2,8,32,256]{3,2,0,1:T(8,128)} %bitcast.10) | data formatting | bytes 1048576 | tf_op jit(solution)/shard_map/transpose | solution.py:662
  (59 shorter events, 15.9 us)
Async XLA Ops:
  1.6 1.0 copy-start
  2.9 1.0 copy-start.2
  5.3 9.4 %copy-start.3 = (f32[2,256,256]{2,1,0:T(8,128)S(1)}, f32[2,256,256]{2,1,0:T(8,128)}, u32[]{:S(2)}) copy-start(f32[2,256,256]{2,1,0:T(8,128)} %probe_ref.5) | copy-start | bytes 1572868
  5.3 35.0 %all-to-all-start = ((bf16[16,256,256]{2,1,0:T(8,128)(2,1)}), bf16[16,256,256]{2,1,0:T(8,128)(2,1)}, u32[]{:S(2)}, u32[]{:S(2)}) async-start(bf16[16,256,256]{2,1,0:T(8,128)(2,1)} %shard_map.89), calls=%async_computation | async-start | bytes 4194304 | tf_op jit(solution)/shard_map/all_to_all | solution.py:693
  10.6 15.9 %copy-start.1 = (f32[2,256,256]{2,1,0:T(8,128)S(1)}, f32[2,256,256]{2,1,0:T(8,128)}, u32[]{:S(2)}) copy-start(f32[2,256,256]{2,1,0:T(8,128)} %own_ref.1) | copy-start | bytes 1572868
  10.6 15.9 %copy-start.6 = (bf16[2,2,256,256]{3,2,1,0:T(8,128)(2,1)S(1)}, bf16[2,2,256,256]{3,2,1,0:T(8,128)(2,1)}, u32[]{:S(2)}) copy-start(bf16[2,2,256,256]{3,2,1,0:T(8,128)(2,1)} %constant.24.clone.turns) | copy-start | bytes 1572868
  10.7 15.9 %copy-start.9 = (f32[2,136,128]{2,1,0:T(8,128)S(1)}, f32[2,136,128]{2,1,0:T(8,128)}, u32[]{:S(2)}) copy-start(f32[2,136,128]{2,1,0:T(8,128)} %constant.25.clone.twiddles) | copy-start | bytes 417796
  10.7 9.0 %collective-permute-start = (s32[264,256]{1,0:T(8,128)S(1)}, s32[264,256]{1,0:T(8,128)S(1)}, u32[]{:S(2)}, u32[]{:S(2)}) collective-permute-start(s32[264,256]{1,0:T(8,128)S(1)} %shard_map.86.after_ref), channel_id=1, source_target_pairs={{1,0},{2,1},{3,2},{4,3},{5,4},{6,5},{7,6},{9,8},{10,9},{11,10},{12... | collective-permute-start | bytes 811016 | tf_op jit(solution)/shard_map/ppermute | solution.py:629
  12.1 11.2 %collective-permute-start.1 = (s32[264,256]{1,0:T(8,128)S(1)}, s32[264,256]{1,0:T(8,128)S(1)}, u32[]{:S(2)}, u32[]{:S(2)}) collective-permute-start(s32[264,256]{1,0:T(8,128)S(1)} %shard_map.86.after_ref), channel_id=1, source_target_pairs={{8,0},{16,8},{24,16},{9,1},{17,9},{25,17},{10,2},{18,10},{26,18},{... | collective-permute-start | bytes 811016 | tf_op jit(solution)/shard_map/ppermute | solution.py:629
  13.4 13.1 %collective-permute-start.2 = (s32[264,256]{1,0:T(8,128)S(1)}, s32[264,256]{1,0:T(8,128)S(1)}, u32[]{:S(2)}, u32[]{:S(2)}) collective-permute-start(s32[264,256]{1,0:T(8,128)S(1)} %shard_map.86.after_ref), channel_id=1, source_target_pairs={{9,0},{10,1},{11,2},{12,3},{13,4},{14,5},{15,6},{17,8},{18,9},{19,... | collective-permute-start | bytes 811016 | tf_op jit(solution)/shard_map/ppermute | solution.py:639
  19.6 20.7 %copy-start.8 = (bf16[2,256,256]{2,1,0:T(8,128)(2,1)S(1)}, bf16[2,256,256]{2,1,0:T(8,128)(2,1)}, u32[]{:S(2)}) copy-start(bf16[2,256,256]{2,1,0:T(8,128)(2,1)} %constant.26.clone.sorting) | copy-start | bytes 786436
  32.2 1.4 copy-start.10
  51.4 1.0 copy-start.11
  52.4 32.2 %all-to-all-start.1 = ((f32[8,96,256]{2,1,0:T(8,128)}), f32[8,96,256]{2,1,0:T(8,128)}, u32[]{:S(2)}, u32[]{:S(2)}) async-start(f32[8,96,256]{2,1,0:T(8,128)} %get-tuple-element.28), calls=%async_computation.1 | async-start | bytes 1572864 | tf_op jit(solution)/shard_map/all_to_all | solution.py:656
  71.9 18.6 %collective-permute-start.3 = (s32[264,512]{1,0:T(8,128)}, s32[264,512]{1,0:T(8,128)S(1)}, u32[]{:S(2)}, u32[]{:S(2)}) collective-permute-start(s32[264,512]{1,0:T(8,128)} %get-tuple-element.23), channel_id=1, source_target_pairs={{0,8},{8,16},{16,24},{1,9},{9,17},{17,25},{2,10},{10,18},{18,26},{... | collective-permute-start | bytes 1622024 | tf_op jit(solution)/shard_map/ppermute | solution.py:629
  76.0 17.5 %collective-permute-start.4 = (s32[264,512]{1,0:T(8,128)S(1)}, s32[264,512]{1,0:T(8,128)S(1)}, u32[]{:S(2)}, u32[]{:S(2)}) collective-permute-start(s32[264,512]{1,0:T(8,128)S(1)} %get-tuple-element.24), channel_id=1, source_target_pairs={{8,0},{16,8},{24,16},{9,1},{17,9},{25,17},{10,2},{18,10},{26,18},{... | collective-permute-start | bytes 1622024 | tf_op jit(solution)/shard_map/ppermute | solution.py:629
  85.8 13.0 %collective-permute-start.7 = (f32[96,256]{1,0:T(8,128)S(1)}, f32[96,256]{1,0:T(8,128)S(1)}, u32[]{:S(2)}, u32[]{:S(2)}) collective-permute-start(f32[96,256]{1,0:T(8,128)S(1)} %reduce_sum.18), channel_id=1, source_target_pairs={{0,8},{8,0},{16,24},{24,16},{1,9},{9,1},{17,25},{25,17},{2,10},{10... | collective-permute-start | bytes 294920 | tf_op jit(solution)/shard_map/ppermute | solution.py:643
  88.0 12.3 %collective-permute-start.8 = (f32[96,256]{1,0:T(8,128)S(1)}, f32[96,256]{1,0:T(8,128)}, u32[]{:S(2)}, u32[]{:S(2)}) collective-permute-start(f32[96,256]{1,0:T(8,128)S(1)} %reduce_sum.18), channel_id=1, source_target_pairs={{0,16},{8,24},{16,0},{24,8},{1,17},{9,25},{17,1},{25,9},{2,18},{10... | collective-permute-start | bytes 294920 | tf_op jit(solution)/shard_map/ppermute | solution.py:643
  89.1 11.3 %collective-permute-start.9 = (f32[96,256]{1,0:T(8,128)S(1)}, f32[96,256]{1,0:T(8,128)}, u32[]{:S(2)}, u32[]{:S(2)}) collective-permute-start(f32[96,256]{1,0:T(8,128)S(1)} %reduce_sum.18), channel_id=1, source_target_pairs={{0,24},{8,16},{16,8},{24,0},{1,25},{9,17},{17,9},{25,1},{2,26},{10... | collective-permute-start | bytes 294920 | tf_op jit(solution)/shard_map/ppermute | solution.py:643
  96.0 23.0 %copy-start.4 = (f32[2,512,512]{2,1,0:T(8,128)}, f32[2,512,512]{2,1,0:T(8,128)S(1)}, u32[]{:S(2)}) copy-start(f32[2,512,512]{2,1,0:T(8,128)S(1)} %get-tuple-element.25.sum_ref) | copy-start | bytes 6291460
  96.0 23.0 %copy-start.7 = (bf16[2,2,256,256]{3,2,1,0:T(8,128)(2,1)S(1)}, bf16[2,2,256,256]{3,2,1,0:T(8,128)(2,1)}, u32[]{:S(2)}) copy-start(bf16[2,2,256,256]{3,2,1,0:T(8,128)(2,1)} %constant.24.clone.turns) | copy-start | bytes 1572868
  96.0 22.9 %collective-permute-start.5 = (s32[528,256]{1,0:T(8,128)S(1)}, s32[528,256]{1,0:T(8,128)S(1)}, u32[]{:S(2)}, u32[]{:S(2)}) collective-permute-start(s32[528,256]{1,0:T(8,128)S(1)} %get-tuple-element.26), channel_id=1, source_target_pairs={{0,1},{1,2},{2,3},{3,4},{4,5},{5,6},{6,7},{8,9},{9,10},{10,11},{11... | collective-permute-start | bytes 1622024 | tf_op jit(solution)/shard_map/ppermute | solution.py:629
  97.5 21.5 %collective-permute-start.6 = (s32[528,256]{1,0:T(8,128)S(1)}, s32[528,256]{1,0:T(8,128)S(1)}, u32[]{:S(2)}, u32[]{:S(2)}) collective-permute-start(s32[528,256]{1,0:T(8,128)S(1)} %get-tuple-element.27), channel_id=1, source_target_pairs={{1,0},{2,1},{3,2},{4,3},{5,4},{6,5},{7,6},{9,8},{10,9},{11,10},{12... | collective-permute-start | bytes 1622024 | tf_op jit(solution)/shard_map/ppermute | solution.py:629
  129.5 0.7 copy-start.5
  152.5 7.6 %collective-permute-start.13 = (f32[96,256]{1,0:T(8,128)S(1)}, f32[96,256]{1,0:T(8,128)S(1)}, u32[]{:S(2)}, u32[]{:S(2)}) collective-permute-start(f32[96,256]{1,0:T(8,128)S(1)} %reduce_sum.19), channel_id=1, source_target_pairs={{0,8},{8,0},{16,24},{24,16},{1,9},{9,1},{17,25},{25,17},{2,10},{10... | collective-permute-start | bytes 294920 | tf_op jit(solution)/shard_map/ppermute | solution.py:643
  153.4 9.6 %collective-permute-start.14 = (f32[96,256]{1,0:T(8,128)S(1)}, f32[96,256]{1,0:T(8,128)S(1)}, u32[]{:S(2)}, u32[]{:S(2)}) collective-permute-start(f32[96,256]{1,0:T(8,128)S(1)} %reduce_sum.19), channel_id=1, source_target_pairs={{0,16},{8,24},{16,0},{24,8},{1,17},{9,25},{17,1},{25,9},{2,18},{10... | collective-permute-start | bytes 294920 | tf_op jit(solution)/shard_map/ppermute | solution.py:643
  153.4 9.6 %collective-permute-start.15 = (f32[96,256]{1,0:T(8,128)S(1)}, f32[96,256]{1,0:T(8,128)S(1)}, u32[]{:S(2)}, u32[]{:S(2)}) collective-permute-start(f32[96,256]{1,0:T(8,128)S(1)} %reduce_sum.19), channel_id=1, source_target_pairs={{0,24},{8,16},{16,8},{24,0},{1,25},{9,17},{17,9},{25,1},{2,26},{10... | collective-permute-start | bytes 294920 | tf_op jit(solution)/shard_map/ppermute | solution.py:643
  157.0 14.6 %collective-permute-start.10 = (s32[264,256]{1,0:T(8,128)}, s32[264,256]{1,0:T(8,128)S(1)}, u32[]{:S(2)}, u32[]{:S(2)}) collective-permute-start(s32[264,256]{1,0:T(8,128)} %copy-done.5), channel_id=1, source_target_pairs={{0,1},{1,2},{2,3},{3,4},{4,5},{5,6},{6,7},{8,9},{9,10},{10,11},{11... | collective-permute-start | bytes 811016 | tf_op jit(solution)/shard_map/ppermute | solution.py:629
  158.3 13.3 %collective-permute-start.11 = (s32[264,256]{1,0:T(8,128)S(1)}, s32[264,256]{1,0:T(8,128)S(1)}, u32[]{:S(2)}, u32[]{:S(2)}) collective-permute-start(s32[264,256]{1,0:T(8,128)S(1)} %get-tuple-element.33), channel_id=1, source_target_pairs={{0,8},{8,16},{16,24},{1,9},{9,17},{17,25},{2,10},{10,18},{18,26},{... | collective-permute-start | bytes 811016 | tf_op jit(solution)/shard_map/ppermute | solution.py:629
  160.2 12.3 %collective-permute-start.12 = (s32[264,256]{1,0:T(8,128)S(1)}, s32[264,256]{1,0:T(8,128)S(1)}, u32[]{:S(2)}, u32[]{:S(2)}) collective-permute-start(s32[264,256]{1,0:T(8,128)S(1)} %get-tuple-element.34), channel_id=1, source_target_pairs={{0,9},{1,10},{2,11},{3,12},{4,13},{5,14},{6,15},{8,17},{9,18},{10,... | collective-permute-start | bytes 811016 | tf_op jit(solution)/shard_map/ppermute | solution.py:639
  163.9 13.9 %all-to-all-start.4 = ((f32[8,64,256]{2,1,0:T(8,128)}), f32[8,64,256]{2,1,0:T(8,128)}, u32[]{:S(2)}, u32[]{:S(2)}) async-start(f32[8,64,256]{2,1,0:T(8,128)} %broadcast_in_dim.19), calls=%async_computation.4 | async-start | bytes 1048576 | tf_op jit(solution)/shard_map/all_to_all | solution.py:661

commit v3 on v2

--- a/solution.py
+++ b/solution.py
@@ -21,7 +21,8 @@
 CHUNK = 32
 VMEM = pl.BlockSpec(memory_space=pltpu.VMEM)
 SMEM = pl.BlockSpec(memory_space=pltpu.SMEM)
-ANY = pl.BlockSpec(memory_space=pl.ANY)
+HBM = pl.BlockSpec(memory_space=pltpu.HBM)
+LOAD = object()
 f32 = jnp.float32
 bf16 = jnp.bfloat16
 
@@ -57,11 +58,12 @@
     my_row, my_col = me_ref[0], me_ref[1]
     band_count = pat_count * col_count
     first = my_row * band_count
+    total = pos_ref.shape[0] // 2
 
     def visit(index, carry):
         found, source, rank = carry
-        y = pos_ref[2 * (first + index)]
-        x = pos_ref[2 * (first + index) + 1]
+        y = pos_ref[first + index]
+        x = pos_ref[total + first + index]
         here = lax.div(x, tile_cols) == my_col
         holder = lax.div(index, pat_count)
         rank = jnp.where(holder == source, rank, 0)
@@ -195,6 +197,64 @@
     words = ref[pl.ds(start, CHUNK), cols]
     scale = repeated(jnp.exp2(ref[last : last + SUBLANES, cols].astype(f32)) * (1.0 / LEVELS), CHUNK)
     return (words >> 16).astype(f32) * scale, ((words << 16) >> 16).astype(f32) * scale
+
+
+def largest_exponent(values):
+    largest = jnp.full((SUBLANES, LANES), 1e-30, f32)
+    for value in values:
+        for group in row_groups(jnp.abs(value)):
+            largest = jnp.maximum(largest, group)
+    return jnp.ceil(jnp.log2(largest))
+
+
+def fixed(value, exponent):
+    scaled = value * repeated(jnp.exp2(-exponent) * LEVELS, value.shape[0])
+    return jnp.round(jnp.clip(scaled, -LEVELS, LEVELS)).astype(jnp.int32)
+
+
+def paired(first, second):
+    return (first << 16) | (second & 0xFFFF)
+
+
+def unpaired(words):
+    return words >> 16, (words << 16) >> 16
+
+
+def scaled_back(codes, exponent):
+    return codes.astype(f32) * repeated(jnp.exp2(exponent.astype(f32)) * (1.0 / LEVELS), codes.shape[0])
+
+
+def sums_rows(rows):
+    return rows + rows // 2 + SUBLANES
+
+
+def encode_sums(out_ref, cols, u_re, u_im, v):
+    rows = v.shape[0]
+    half = rows // 2
+    of_u, of_v = largest_exponent([u_re, u_im]), largest_exponent([v])
+    out_ref[0:rows, cols] = paired(fixed(u_re, of_u), fixed(u_im, of_u))
+    codes = fixed(v, of_v)
+    out_ref[rows : rows + half, cols] = paired(codes[:half], codes[half:])
+    out_ref[rows + half : rows + half + SUBLANES, cols] = paired(of_u.astype(jnp.int32), of_v.astype(jnp.int32))
+
+
+def decode_sums(ref, cols, rows):
+    half = rows // 2
+    of_u, of_v = unpaired(ref[rows + half : rows + half + SUBLANES, cols])
+    u_re, u_im = unpaired(ref[0:rows, cols])
+    v = jnp.concatenate(unpaired(ref[rows : rows + half, cols]), axis=0)
+    return scaled_back(u_re, of_u), scaled_back(u_im, of_u), scaled_back(v, of_v)
+
+
+def decode_probe(out_ref, chunks_ref):
+    chunks = chunks_ref.shape[0]
+    rows = out_ref.shape[1] // chunks
+    for chunk in range(chunks):
+        for col in range(0, out_ref.shape[2], LANES):
+            cols = pl.ds(col, LANES)
+            exponent = chunks_ref[chunk, rows : rows + SUBLANES, cols]
+            for comp, codes in enumerate(unpaired(chunks_ref[chunk, 0:rows, cols])):
+                out_ref[comp, chunk * rows : (chunk + 1) * rows, cols] = scaled_back(codes, exponent)
 
 
 def cut_chunk(ext_ref, comp, first, top, left, rows):
@@ -333,7 +393,8 @@
 def outgoing_kernel(dims, pos_ref, me_ref, amp_ref, after_ref, out_ref, sems):
     tile_rows, tile_cols, pat_count, col_count, capacity = dims
     first = (me_ref[0] * col_count + me_ref[1]) * pat_count
-    owners = [lax.div(pos_ref[2 * (first + k) + 1], tile_cols) for k in range(pat_count)]
+    total = pos_ref.shape[0] // 2
+    owners = [lax.div(pos_ref[total + first + k], tile_cols) for k in range(pat_count)]
     copies = []
     for k in range(pat_count):
         rank = sum(((owners[e] == owners[k]).astype(jnp.int32) for e in range(k)), jnp.int32(0))
@@ -349,13 +410,14 @@
     order = probe_ref.shape[1]
     top = (me_ref[0] - 1) * tile_rows
     left = (me_ref[1] - 1) * tile_cols
+    total = pos_ref.shape[0] // 2
     for first in range(0, sums_ref.shape[0], order):
         sums_ref[pl.ds(first, order), :] = jnp.zeros((order, sums_ref.shape[1]), f32)
     power_ref[...] = probe_ref[0] * probe_ref[0] + probe_ref[1] * probe_ref[1]
 
     def visit(index, carry):
-        y = pos_ref[2 * index] - top
-        x = pos_ref[2 * index + 1] - left
+        y = pos_ref[index] - top
+        x = pos_ref[total + index] - left
 
         @pl.when((y > 0) & (y < (span + 1) * tile_rows) & (x > 0) & (x < (span + 1) * tile_cols))
         def _():
@@ -369,7 +431,7 @@
 
         return carry
 
-    lax.fori_loop(0, pos_ref.shape[0] // 2, visit, 0)
+    lax.fori_loop(0, total, visit, 0)
     out_ref[...] = sums_ref[tile_rows : (span + 1) * tile_rows, tile_cols : (span + 1) * tile_cols]
 
 
@@ -389,19 +451,57 @@
                     ext_ref[comp, pl.ds(i * tile_rows + start, CHUNK), pl.ds(j * tile_cols + col, LANES)] = parts[comp]
 
 
-def chunked(out_ref, plane, planes, value_ref):
+def spread_sums(out_ref, u_ref, v_ref):
     chunks = out_ref.shape[0]
-    rows = value_ref.shape[0] // chunks
+    rows = v_ref.shape[0] // chunks
     for chunk in range(chunks):
-        out_ref[chunk, plane * rows : (plane + 1) * rows, :] = value_ref[chunk * rows : (chunk + 1) * rows, :]
+        at = pl.ds(chunk * rows, rows)
+        for col in range(0, v_ref.shape[1], LANES):
+            cols = pl.ds(col, LANES)
+            encode_sums(out_ref.at[chunk], cols, u_ref[0, at, cols], u_ref[1, at, cols], v_ref[at, cols])
+
+
+def added(parts):
+    while len(parts) > 1:
+        parts = [tuple(x + y for x, y in zip(a, b)) for a, b in zip(parts[::2], parts[1::2])]
+    return parts[0]
+
+
+def sums_kernel(rows, parts_ref, out_ref):
+    for col in range(0, out_ref.shape[1], LANES):
+        cols = pl.ds(col, LANES)
+        total = added([decode_sums(parts_ref.at[k], cols, rows) for k in range(parts_ref.shape[0])])
+        encode_sums(out_ref, cols, *total)
+
+
+def update_kernel(rows, me_ref, probe_ref, *refs):
+    *parts, out_ref = refs
+    first = pl.multiple_of(me_ref[1] * rows, SUBLANES)
+    for col in range(0, out_ref.shape[2], LANES):
+        cols = pl.ds(col, LANES)
+        u_re, u_im, v = added([decode_sums(ref, cols, rows) for ref in parts])
+        scale = 1.0 / (v + probe_regular)
+        re = (probe_ref[0, pl.ds(first, rows), cols] + u_re) * scale
+        im = (probe_ref[1, pl.ds(first, rows), cols] + u_im) * scale
+        exponent = largest_exponent([re, im])
+        words = paired(fixed(re, exponent), fixed(im, exponent))
+        for chunk in range(out_ref.shape[0]):
+            out_ref[chunk, 0:rows, cols] = words
+            out_ref[chunk, rows : rows + SUBLANES, cols] = exponent.astype(jnp.int32)
+
+
+def probe_kernel(chunks_ref, out_ref):
+    decode_probe(out_ref, chunks_ref)
 
 
 def first_half_kernel(dims, pos_ref, me_ref, own_ref, right_ref, below_ref, diag_ref, probe_ref, turns, twiddles,
-                      far_out, power_out, ext_out, win_ref, xa_ref, xb_ref, ya_ref, yb_ref, far_ref, ys_ref, xs_ref, slots_ref, sems):
+                      far_out, power_out, ext_out, ext_ref, win_ref, xa_ref, xb_ref, ya_ref, yb_ref, far_ref, ys_ref, xs_ref, slots_ref, sems, ext_sem):
     tile_rows, tile_cols, pat_count, col_count, capacity = dims
     order = probe_ref.shape[1]
     count = list_patterns(dims, pos_ref, me_ref, ys_ref, xs_ref, slots_ref)
-    unfold(dims, ext_out, own_ref, (right_ref, below_ref, diag_ref))
+    unfold(dims, ext_ref, own_ref, (right_ref, below_ref, diag_ref))
+    keep = pltpu.make_async_copy(ext_ref, ext_out, ext_sem)
+    keep.start()
     power_out[...] = jnp.zeros_like(power_out)
     consts = (turns, twiddles)
 
@@ -411,7 +511,7 @@
             listed = 2 * step + k
             weight = (listed < count).astype(f32)
             index = jnp.minimum(listed, count - 1)
-            stages.append(forward(order, ext_out, probe_ref, consts, ys_ref[index], xs_ref[index], win_ref.at[k], power_out, weight,
+            stages.append(forward(order, ext_ref, probe_ref, consts, ys_ref[index], xs_ref[index], win_ref.at[k], power_out, weight,
                                   xa_ref.at[k], xb_ref.at[k], ya_ref.at[k], yb_ref.at[k], far_ref.at[listed]))
         interleaved(*stages)
         for k in range(2):
@@ -427,11 +527,12 @@
         return carry
 
     lax.fori_loop(0, 2 * pairs, settle, 0)
+    keep.wait()
 
 
 def second_half_kernel(dims, pos_ref, me_ref, ext_ref, probe_ref, power_ref, weights_ref, far_in, amp_in, turns, twiddles, sorting,
                        share_out, top_out, bottom_out, numer_out, amp_out,
-                       win_ref, xa_ref, xb_ref, ya_ref, yb_ref, numer_ref, far_ref, amp_ref, sorted_ref, ys_ref, xs_ref, slots_ref, far_sems, amp_sems, out_sems):
+                       sum_ref, win_ref, xa_ref, xb_ref, ya_ref, yb_ref, numer_ref, far_ref, amp_ref, sorted_ref, ys_ref, xs_ref, slots_ref, far_sems, amp_sems, out_sems, sum_sem):
     tile_rows, tile_cols, pat_count, col_count, capacity = dims
     order = probe_ref.shape[1]
     half = order // 2
@@ -450,7 +551,7 @@
         return carry
 
     lax.fori_loop(0, 2 * pairs, begin, 0)
-    share_out[...] = jnp.zeros_like(share_out)
+    sum_ref[...] = jnp.zeros_like(sum_ref)
     numer_ref[...] = jnp.zeros_like(numer_ref)
     consts = (turns, twiddles)
 
@@ -472,7 +573,7 @@
                     for c, tile in enumerate(cut_chunk(ext_ref, comp, first, y, x, CHUNK)):
                         win_ref[k, comp, pl.ds(first, CHUNK), pl.ds(c * half, half)] = tile
             stages.append(backward(order, far_ref.at[listed], sorted_ref.at[listed], consts, y, x, weight, probe_ref, win_ref.at[k],
-                                   xa_ref.at[k], xb_ref.at[k], ya_ref.at[k], yb_ref.at[k], share_out, numer_ref))
+                                   xa_ref.at[k], xb_ref.at[k], ya_ref.at[k], yb_ref.at[k], sum_ref, numer_ref))
         interleaved(*stages)
         for k in range(2):
             listed = 2 * step + k
@@ -484,20 +585,22 @@
         rows = pl.ds(first, CHUNK)
         scale = 1.0 / (weights_ref[rows, :] + object_regular)
         for comp in range(2):
-            share_out[comp, rows, :] = share_out[comp, rows, :] * scale
-    encode(lambda comp, at, cols: share_out[comp, at, cols], top_out, tile_rows, 0, tile_rows)
-    encode(lambda comp, at, cols: share_out[comp, pl.ds(tile_rows + at.start, at.size), cols], bottom_out, tile_rows, 0, tile_rows)
-    for plane, ref in enumerate((numer_ref.at[0], numer_ref.at[1], power_ref)):
-        chunked(numer_out, plane, 3, ref)
+            sum_ref[comp, rows, :] = sum_ref[comp, rows, :] * scale
+    keep = pltpu.make_async_copy(sum_ref, share_out, sum_sem)
+    keep.start()
+    encode(lambda comp, at, cols: sum_ref[comp, at, cols], top_out, tile_rows, 0, tile_rows)
+    encode(lambda comp, at, cols: sum_ref[comp, pl.ds(tile_rows + at.start, at.size), cols], bottom_out, tile_rows, 0, tile_rows)
+    spread_sums(numer_out, numer_ref, power_ref)
 
     def settle(listed, carry):
         pltpu.make_async_copy(sorted_ref.at[listed], amp_out.at[listed], out_sems.at[listed]).wait()
         return carry
 
     lax.fori_loop(0, 2 * pairs, settle, 0)
-
-
-def rows_sum_kernel(dims, share_ref, above_ref, below_ref, sum_out, left_out, right_out):
+    keep.wait()
+
+
+def rows_sum_kernel(dims, share_ref, above_ref, below_ref, after_ref, sum_out, left_out, right_out):
     tile_rows, tile_cols = dims[:2]
     for i, ref in enumerate((above_ref, below_ref)):
         for col in range(0, 2 * tile_cols, LANES):
@@ -516,13 +619,14 @@
 
 
 def whole_kernel(dims, pos_ref, me_ref, old_ref, sum_ref, from_left_ref, from_right_ref, weights_ref,
-                 probe_ref, amp_in, turns, twiddles,
-                 current_out, own_out, right_out, below_out, diag_out, numer_out,
-                 ext_ref, grad_ref, win_ref, xa_ref, xb_ref, ya_ref, yb_ref, numer_ref, far_ref, amp_ref, ys_ref, xs_ref, slots_ref, amp_sems):
+                 chunks_ref, amp_in, turns, twiddles,
+                 current_out, own_out, right_out, below_out, diag_out, numer_out, probe_ref,
+                 ext_ref, grad_ref, win_ref, xa_ref, xb_ref, ya_ref, yb_ref, numer_ref, far_ref, amp_ref, ys_ref, xs_ref, slots_ref, amp_sems, own_sem):
     tile_rows, tile_cols, pat_count, col_count, capacity = dims
     order = probe_ref.shape[1]
     count = list_patterns(dims, pos_ref, me_ref, ys_ref, xs_ref, slots_ref)
     pairs = lax.div(count + 1, 2)
+    decode_probe(probe_ref, chunks_ref)
 
     def fetch(listed):
         return pltpu.make_async_copy(amp_in.at[jnp.minimum(listed, count - 1)], amp_ref.at[listed], amp_sems.at[listed])
@@ -541,7 +645,8 @@
                     scale = object_regular / (weights_ref[rows, cols] + object_regular)
                     for comp in range(2):
                         ext_ref[comp, rows, cols] = old_ref[comp, rows, cols] * scale + (sum_ref[comp, rows, cols] + parts[comp])
-    current_out[...] = ext_ref[:, 0:tile_rows, 0:tile_cols]
+    keep = pltpu.make_async_copy(ext_ref.at[:, pl.ds(0, tile_rows), pl.ds(0, tile_cols)], current_out, own_sem)
+    keep.start()
     grad_ref[...] = jnp.zeros_like(grad_ref)
     numer_ref[...] = jnp.zeros_like(numer_ref)
     consts = (turns, twiddles)
@@ -575,8 +680,8 @@
             return grad_ref[comp, rows, cols] / (weights_ref[rows, cols] + object_regular)
 
         encode(read, ref, tile_rows, 0, tile_rows)
-    for plane in range(3):
-        chunked(numer_out, plane, 3, numer_ref.at[plane])
+    spread_sums(numer_out, numer_ref, numer_ref.at[2])
+    keep.wait()
 
 
 def object_kernel(dims, current_ref, own_ref, left_ref, above_ref, diag_ref, before_ref, weights_ref, out_ref):
@@ -611,16 +716,38 @@
     return [pltpu.SMEM((capacity,), jnp.int32)] * 3
 
 
-def call(kernel, outs, out_specs, in_specs, scratch, flops, limit=48 << 20):
-    return pl.pallas_call(
-        kernel,
-        out_shape=outs,
-        out_specs=out_specs,
-        in_specs=in_specs,
-        scratch_shapes=scratch,
-        compiler_params=pltpu.CompilerParams(vmem_limit_bytes=limit),
-        cost_estimate=pl.CostEstimate(flops=flops, bytes_accessed=8 << 20, transcendentals=0),
-    )
+def call(kernel, outs, out_specs, in_specs, scratch, flops, limit=26 << 20):
+    several = isinstance(outs, tuple)
+    out_count = len(outs) if several else 1
+    in_count = len(in_specs)
+    loaded = [k for k, spec in enumerate(in_specs) if spec is LOAD]
+
+    def body(*refs):
+        ins, rest = list(refs[:in_count]), refs[in_count:]
+        given, kept = rest[: out_count + len(scratch)], rest[out_count + len(scratch) :]
+        copies = [pltpu.make_async_copy(ins[k], kept[n], kept[-1].at[n]) for n, k in enumerate(loaded)]
+        for copy in copies:
+            copy.start()
+        for n, k in enumerate(loaded):
+            copies[n].wait()
+            ins[k] = kept[n]
+        kernel(*ins, *given)
+
+    def called(*args):
+        own = [pltpu.VMEM(args[k].shape, args[k].dtype) for k in loaded]
+        if loaded:
+            own.append(pltpu.SemaphoreType.DMA((len(loaded),)))
+        return pl.pallas_call(
+            body,
+            out_shape=outs,
+            out_specs=out_specs,
+            in_specs=[HBM if spec is LOAD else spec for spec in in_specs],
+            scratch_shapes=list(scratch) + own,
+            compiler_params=pltpu.CompilerParams(vmem_limit_bytes=limit),
+            cost_estimate=pl.CostEstimate(flops=flops, bytes_accessed=8 << 20, transcendentals=0),
+        )(*args)
+
+    return called
 
 
 def passed_along(value, axis, steps):
@@ -643,23 +770,17 @@
     return lax.ppermute(value, axis, [(k, k ^ mask) for k in range(lax.axis_size(axis))])
 
 
-def summed_over_rows(value):
-    parts = [value] + [swapped(value, "row", mask) for mask in range(1, lax.axis_size("row"))]
-    while len(parts) > 1:
-        parts = [a + b for a, b in zip(parts[::2], parts[1::2])]
-    return parts[0]
-
-
-def probe_update(probe, numer):
+def probe_update(me, probe, numer, kind):
     cols, order = lax.axis_size("col"), probe.shape[1]
     rows = order // cols
     parts = lax.all_to_all(numer, "col", split_axis=0, concat_axis=0, tiled=True)
-    total = summed_over_rows(jnp.sum(parts, axis=0)).reshape(3, rows, order)
-    old = lax.dynamic_slice_in_dim(probe, lax.axis_index("col") * rows, rows, 1)
-    fresh = (old + total[:2]) / (total[2] + probe_regular)[None]
-    spread = jnp.broadcast_to(fresh.reshape(1, 2 * rows, order), (cols, 2 * rows, order))
-    chunks = lax.all_to_all(spread, "col", split_axis=0, concat_axis=0, tiled=True)
-    return chunks.reshape(cols, 2, rows, order).transpose(1, 0, 2, 3).reshape(2, order, order)
+    total = call(functools.partial(sums_kernel, rows), shape((sums_rows(rows), order), jnp.int32), VMEM, [VMEM], [], 1 << 26)(parts)
+    totals = [total] + [swapped(total, "row", mask) for mask in range(1, lax.axis_size("row"))]
+    fresh = call(
+        functools.partial(update_kernel, rows), shape((cols, rows + SUBLANES, order), jnp.int32), VMEM,
+        [SMEM, kind] + [VMEM] * len(totals), [], 1 << 26,
+    )(me, probe, *totals)
+    return fresh, lax.all_to_all(fresh, "col", split_axis=0, concat_axis=0, tiled=True)
 
 
 def local(obj, probe, amplitudes, positions):
@@ -670,80 +791,82 @@
     capacity = 2 * pat_count
     dims = (tile_rows, tile_cols, pat_count, col_count, capacity)
     me = jnp.stack([lax.axis_index("row"), lax.axis_index("col")]).astype(jnp.int32)
-    pos = positions.reshape(-1)
+    pos = positions.T.reshape(-1)
     turns, twiddles, sorting = tables(order)
     tile = (2, tile_rows, tile_cols)
     window = (2, order, order)
     wide = (2, 2 * tile_rows, 2 * tile_cols)
-    shares = (col_count, 3 * order // col_count, order)
+    shares = shape((col_count, sums_rows(order // col_count), order), jnp.int32)
     coded_tile = shape((tile_rows + SUBLANES, tile_cols), jnp.int32)
     coded_row = shape((tile_rows + SUBLANES, 2 * tile_cols), jnp.int32)
     coded_col = shape((2 * (tile_rows + SUBLANES), tile_cols), jnp.int32)
     one_pattern = 24 * 2 * order**3
 
-    coded = call(encode_kernel, coded_tile, VMEM, [VMEM], [], 1 << 26)(obj)
+    coded = call(encode_kernel, coded_tile, VMEM, [LOAD], [], 1 << 26)(obj)
     right = passed_along(coded, "col", -1)
     below = passed_along(coded, "row", -1)
-    diag = passed_both(coded, -1, -1)
+    diag = passed_along(right, "row", -1)
 
     outgoing = call(
-        functools.partial(outgoing_kernel, dims), shape((col_count * SEND, order, order), bf16), ANY, [SMEM, SMEM, ANY, ANY],
+        functools.partial(outgoing_kernel, dims), shape((col_count * SEND, order, order), bf16), HBM, [SMEM, SMEM, HBM, HBM],
         [pltpu.SemaphoreType.DMA((pat_count,))], 1 << 20,
-    )(pos, me, amplitudes, coded)
+    )(pos, me, amplitudes, right)
     incoming = lax.all_to_all(outgoing, "col", split_axis=0, concat_axis=0, tiled=True)
 
-    def weights(probe_now, span):
+    def weights(probe_now, span, kind):
         return call(
-            functools.partial(weights_kernel, dims, span), shape((span * tile_rows, span * tile_cols)), VMEM, [SMEM, SMEM, VMEM],
+            functools.partial(weights_kernel, dims, span), shape((span * tile_rows, span * tile_cols)), VMEM, [SMEM, SMEM, kind],
             [pltpu.VMEM(((span + 2) * tile_rows, (span + 2) * tile_cols), f32), pltpu.VMEM((order, order), f32)], 8 << 30,
         )(pos, me, probe_now)
 
-    weights_old = weights(probe, 2)
+    weights_old = weights(probe, 2, LOAD)
 
     far, power, ext = call(
-        functools.partial(first_half_kernel, dims), (shape((capacity,) + window), shape((order, order)), shape(wide)), (ANY, VMEM, VMEM),
-        [SMEM, SMEM] + [VMEM] * 7,
-        work_scratch(order) + [pltpu.VMEM((capacity,) + window, f32)] + list_scratch(capacity) + [pltpu.SemaphoreType.DMA((capacity,))],
+        functools.partial(first_half_kernel, dims), (shape((capacity,) + window), shape((order, order)), shape(wide)), (HBM, VMEM, HBM),
+        [SMEM, SMEM, LOAD] + [VMEM] * 3 + [LOAD] * 3,
+        [pltpu.VMEM(wide, f32)] + work_scratch(order) + [pltpu.VMEM((capacity,) + window, f32)] + list_scratch(capacity)
+        + [pltpu.SemaphoreType.DMA((capacity,)), pltpu.SemaphoreType.DMA],
         capacity * one_pattern // 2,
     )(pos, me, obj, right, below, diag, probe, turns, twiddles)
 
     share, top, bottom, numer, sorted_amps = call(
         functools.partial(second_half_kernel, dims),
-        (shape(wide), coded_row, coded_row, shape(shares), shape((capacity, order, order), bf16)),
-        (VMEM, VMEM, VMEM, VMEM, ANY),
-        [SMEM, SMEM] + [VMEM] * 4 + [ANY, ANY] + [VMEM] * 3,
-        work_scratch(order)
+        (shape(wide), coded_row, coded_row, shares, shape((capacity, order, order), bf16)),
+        (HBM, VMEM, VMEM, VMEM, HBM),
+        [SMEM, SMEM, LOAD, LOAD, VMEM, LOAD, HBM, HBM] + [LOAD] * 3,
+        [pltpu.VMEM(wide, f32)] + work_scratch(order)
         + [pltpu.VMEM(window, f32), pltpu.VMEM((capacity,) + window, f32), pltpu.VMEM((capacity, order, order), bf16), pltpu.VMEM((capacity, order, order), bf16)]
-        + list_scratch(capacity) + [pltpu.SemaphoreType.DMA((capacity,))] * 3,
+        + list_scratch(capacity) + [pltpu.SemaphoreType.DMA((capacity,))] * 3 + [pltpu.SemaphoreType.DMA],
         capacity * one_pattern // 2,
     )(pos, me, ext, probe, power, weights_old, far, incoming, turns, twiddles, sorting)
 
     from_above = passed_along(bottom, "row", 1)
     from_below = passed_along(top, "row", -1)
-    probe_now = probe_update(probe, numer)
+    fresh, chunks = probe_update(me, probe, numer, LOAD)
     sums, to_left, to_right = call(
-        functools.partial(rows_sum_kernel, dims), (shape(wide), coded_col, coded_col), (VMEM,) * 3, [VMEM] * 3, [], 1 << 26,
-    )(share, from_above, from_below)
+        functools.partial(rows_sum_kernel, dims), (shape(wide), coded_col, coded_col), (VMEM,) * 3, [LOAD, VMEM, VMEM, HBM], [], 1 << 26,
+    )(share, from_above, from_below, fresh)
     from_left = passed_along(to_right, "col", 1)
     from_right = passed_along(to_left, "col", -1)
 
-    current, own, to_right, to_below, to_diag, numer = call(
-        functools.partial(whole_kernel, dims), (shape(tile), shape(tile), coded_tile, coded_tile, coded_tile, shape(shares)), (VMEM,) * 6,
-        [SMEM, SMEM] + [VMEM] * 6 + [ANY] + [VMEM] * 2,
+    current, own, to_right, to_below, to_diag, numer, probe_now = call(
+        functools.partial(whole_kernel, dims), (shape(tile), shape(tile), coded_tile, coded_tile, coded_tile, shares, shape(window)), (HBM,) + (VMEM,) * 6,
+        [SMEM, SMEM, LOAD] + [VMEM] * 3 + [LOAD, VMEM, HBM, LOAD, LOAD],
         [pltpu.VMEM(wide, f32), pltpu.VMEM(wide, f32)] + work_scratch(order)
         + [pltpu.VMEM((3, order, order), f32), pltpu.VMEM((2,) + window, f32), pltpu.VMEM((capacity, order, order), bf16)]
-        + list_scratch(capacity) + [pltpu.SemaphoreType.DMA((capacity,))],
+        + list_scratch(capacity) + [pltpu.SemaphoreType.DMA((capacity,)), pltpu.SemaphoreType.DMA],
         capacity * one_pattern,
-    )(pos, me, ext, sums, from_left, from_right, weights_old, probe_now, sorted_amps, turns, twiddles)
+    )(pos, me, ext, sums, from_left, from_right, weights_old, chunks, sorted_amps, turns, twiddles)
 
     from_left = passed_along(to_right, "col", 1)
     from_above = passed_along(to_below, "row", 1)
     from_diag = passed_both(to_diag, 1, 1)
-    weights_new = weights(probe_now, 1)
-    new_probe = probe_update(probe_now, numer)
-    new_object = call(functools.partial(object_kernel, dims), shape(tile), VMEM, [VMEM] * 7, [], 1 << 26)(
-        current, own, from_left, from_above, from_diag, weights_old[:tile_rows, :tile_cols], weights_new
+    weights_new = weights(probe_now, 1, VMEM)
+    new_object = call(functools.partial(object_kernel, dims), shape(tile), VMEM, [LOAD] + [VMEM] * 4 + [LOAD, VMEM], [], 1 << 26)(
+        current, own, from_left, from_above, from_diag, weights_old, weights_new
     )
+    _, chunks = probe_update(me, probe_now, numer, VMEM)
+    new_probe = call(probe_kernel, shape(window), VMEM, [VMEM], [], 1 << 26)(chunks)
     return new_object, new_probe
 
 

time: 182 us -> 173 us (0.951)
  Pallas kernels: 40.9 us -> 59.8 us
  starting transfers between devices: 56.2 us -> 37.9 us
  waiting for transfers between devices: 30.5 us -> 14.9 us
  local copies, waits for them, and re-layouts: 8.91 us -> 16.5 us
  other arithmetic: 3.5 us -> 0.08 us
  blocking collectives: 38.6 us -> 40.5 us
    all_to_all x2 -> x1, starting transfers between devices: 23.6 us -> 3.43 us  [probe_update(): lax.all_to_all(fresh, 'col', split_axis=0, concat_axis=0, tiled=True)]
    pallas_call x9 -> x14, Pallas kernels: 40.9 us -> 59.8 us  [called(): pl.pallas_call(body, out_shape=outs, out_specs=out_specs, in_specs=[HBM i...]
    unnamed x25 -> x44, local copies, waits for them, and re-layouts: 5.95 us -> 16.5 us
    all_to_all x2 -> x1, waiting for transfers between devices: 11.5 us -> 1.09 us  [probe_update(): lax.all_to_all(fresh, 'col', split_axis=0, concat_axis=0, tiled=True)]
    all_to_all x1, waiting for transfers between devices: 6.73 us -> 0.01 us  [local(): lax.all_to_all(outgoing, 'col', split_axis=0, concat_axis=0, tiled=True)]
    ppermute x2 -> x1, waiting for transfers between devices: 4.1 us -> 0.01 us  [passed_both(): return lax.ppermute(value, ('row', 'col'), pairs)]
    all_to_all x1, starting transfers between devices: 5.32 us -> 8.91 us  [local(): lax.all_to_all(outgoing, 'col', split_axis=0, concat_axis=0, tiled=True)]
    ppermute x6, waiting for transfers between devices: 1.56 us -> 4.89 us  [swapped(): lax.ppermute(value, axis, [(k, k ^ mask) for k in range(lax.axis_size(axi...]
  transfers between devices with their start and end apart: 19 -> 18, of which waited for: 8 -> 6; matrix products, arithmetic and copies ran while one was open for 2% -> 0% of each run, Pallas kernels for 10% -> 14%
where the time goes in v3:
time: 173 us; the launch traced here: 171 us
  Pallas kernels  59.8 us (35%)
  blocking collectives  40.5 us (23%)
  starting transfers between devices  37.9 us (22%)
  local copies, waits for them, and re-layouts  16.5 us (10%)
  waiting for transfers between devices  14.9 us (9%)
    pallas_call x14, Pallas kernels, called(): pl.pallas_call(body, out_shape=outs, out_specs=out_specs, in_specs=[HBM i...  59.8 us
    all_to_all x2, blocking collectives, probe_update(): lax.all_to_all(numer, 'col', split_axis=0, concat_axis=0, tiled=True)  23.2 us
    all_to_all x1, blocking collectives, probe_update(): lax.all_to_all(fresh, 'col', split_axis=0, concat_axis=0, tiled=True)  17.3 us
    unnamed x44, local copies, waits for them, and re-layouts  16.5 us
    ppermute x9, starting transfers between devices, passed_along(): lax.ppermute(value, axis, [(source, source + steps) for source in range(l...  13.2 us
    ppermute x6, starting transfers between devices, swapped(): lax.ppermute(value, axis, [(k, k ^ mask) for k in range(lax.axis_size(axi...  9.27 us
    all_to_all x1, starting transfers between devices, local(): lax.all_to_all(outgoing, 'col', split_axis=0, concat_axis=0, tiled=True)  8.91 us
    ppermute x9, waiting for transfers between devices, passed_along(): lax.ppermute(value, axis, [(source, source + steps) for source in range(l...  8.91 us
  transfers between devices with their start and end apart: 18, of which 6 were waited for; matrix products, arithmetic and copies ran while one was open for 0% of the time, Pallas kernels for 14%

profile of v3, /device:TPU:0, one launch (start us, length us, event | category | flops | bytes accessed | tf_op | source)
XLA Modules:
  0.0 170.6 jit_solution(12849009682444166295)
XLA Ops:
  4.0 2.3 %collective-permute-done.refs_3_ = s32[264,256]{1,0:T(8,128)S(1)} collective-permute-done((s32[264,256]{1,0:T(8,128)}, s32[264,256]{1,0:T(8,128)S(1)}, u32[]{:S(2)}, u32[]{:S(2)}) %collective-permute-start) | collective-permute-done | bytes 270368 | tf_op jit(solution)/shard_map/ppermute | solution.py:756
  8.0 1.4 shard_map.89
  9.4 8.9 %all-to-all-start = ((bf16[16,256,256]{2,1,0:T(8,128)(2,1)}), bf16[16,256,256]{2,1,0:T(8,128)(2,1)S(1)}, u32[]{:S(2)}, u32[]{:S(2)}) async-start(bf16[16,256,256]{2,1,0:T(8,128)(2,1)} %shard_map.89), calls=%async_computation | async-start | bytes 4194304 | tf_op jit(solution)/shard_map/all_to_all | solution.py:814
  18.3 1.4 collective-permute-start.1
  19.7 1.3 collective-permute-start.2
  22.1 6.5 %shard_map.88.refs_5_.refs_6_ = f32[512,512]{1,0:T(8,128)S(1)} custom-call(s32[256]{0:T(256)S(1)} %bitcast.6, s32[2]{0:T(128)S(1)} %pad_add_fusion.refs_1_.refs_0_, f32[2,256,256]{2,1,0:T(8,128)S(1)} %copy-done.2), custom_call_target="tpu_custom_call" | custom-call | flops 8589934592 | bytes 8388608 | tf_op jit(solution)/shard_map/pallas_call | solution.py:740
  29.8 5.4 %collective-permute-done.2.refs_5_ = s32[264,256]{1,0:T(8,128)S(1)} collective-permute-done((s32[264,256]{1,0:T(8,128)S(1)}, s32[264,256]{1,0:T(8,128)S(1)}, u32[]{:S(2)}, u32[]{:S(2)}) %collective-permute-start.2) | collective-permute-done | bytes 270368 | tf_op jit(solution)/shard_map/ppermute | solution.py:756
  35.2 8.7 %shard_map.87 = (f32[8,2,256,256]{3,2,1,0:T(8,128)S(1)}, f32[256,256]{1,0:T(8,128)S(1)}, f32[2,512,512]{2,1,0:T(8,128)S(1)}) custom-call(s32[256]{0:T(256)S(1)} %bitcast.7, s32[2]{0:T(128)S(1)} %pad_add_fusion.refs_1_.refs_0_, f32[2,256,256]{2,1,0:T(8,128)S(1)} %copy-done.1, s32[264,256]{1,0:T(8,128)S(1)} %collective-permute-done.refs_3_, ...), custom_call_target="tpu_custom_call" | custom-call | flops 3221225472 | bytes 8388608 | tf_op jit(solution)/shard_map/pallas_call | solution.py:740
  43.9 2.0 %copy-done.16 = f32[8,2,256,256]{3,2,1,0:T(8,128)} copy-done((f32[8,2,256,256]{3,2,1,0:T(8,128)}, f32[8,2,256,256]{3,2,1,0:T(8,128)S(1)}, u32[]{:S(2)}) %copy-start.16) | copy-done | bytes 4194328
  45.9 1.4 copy-done.18
  51.9 2.2 %copy-done.17 = f32[8,2,256,256]{3,2,1,0:T(8,128)S(1)} copy-done((f32[8,2,256,256]{3,2,1,0:T(8,128)S(1)}, f32[8,2,256,256]{3,2,1,0:T(8,128)}, u32[]{:S(2)}) %copy-start.17) | copy-done | bytes 4194328
  54.1 1.6 copy-done.19
  56.6 14.0 %shard_map.90 = (f32[2,512,512]{2,1,0:T(8,128)S(1)}, s32[264,512]{1,0:T(8,128)S(1)}, s32[264,512]{1,0:T(8,128)S(1)}, s32[8,56,256]{2,1,0:T(8,128)S(1)}, bf16[8,256,256]{2,1,0:T(8,128)(2,1)S(1)}) custom-call(s32[256]{0:T(256)S(1)} %bitcast.8, s32[2]{0:T(128)S(1)} %pad_add_fusion.refs_1_.refs_0_, f32[2,512,512]{2,1,0:T(8,128)S(1)} %copy-done.19, ...), custom_call_target="tpu_custom_call" | custom-call | flops 3221225472 | bytes 8388608 | tf_op jit(solution)/shard_map/pallas_call | solution.py:740
  70.6 1.3 collective-permute-start.3
  71.9 1.3 collective-permute-start.4
  73.2 11.8 %all_to_all.25.refs_0_ = s32[8,56,256]{2,1,0:T(8,128)S(1)} all-to-all(s32[8,56,256]{2,1,0:T(8,128)S(1)} %get-tuple-element.26), channel_id=1, replica_groups=mesh['row'=4,'col'=8] {'col'}, dimensions={0} | all-to-all | bytes 917504 | tf_op jit(solution)/shard_map/all_to_all | solution.py:776
  85.2 4.0 %collective-permute-start.7 = (s32[56,256]{1,0:T(8,128)S(1)}, s32[56,256]{1,0:T(8,128)S(1)}, u32[]{:S(2)}, u32[]{:S(2)}) collective-permute-start(s32[56,256]{1,0:T(8,128)S(1)} %shard_map.91.refs_2_), channel_id=1, source_target_pairs={{0,24},{8,16},{16,8},{24,0},{1,25},{9,17},{17,9},{25,1},{2,26},{10... | collective-permute-start | bytes 172040 | tf_op jit(solution)/shard_map/ppermute | solution.py:770
  90.0 1.5 collective-permute-done.7.refs_5_
  91.5 3.3 %collective-permute-done.6.refs_4_ = s32[56,256]{1,0:T(8,128)S(1)} collective-permute-done((s32[56,256]{1,0:T(8,128)S(1)}, s32[56,256]{1,0:T(8,128)S(1)}, u32[]{:S(2)}, u32[]{:S(2)}) %collective-permute-start.6) | collective-permute-done | bytes 57376 | tf_op jit(solution)/shard_map/ppermute | solution.py:770
  96.7 1.3 collective-permute-start.8
  99.3 17.3 %all_to_all.26.refs_7_ = s32[8,40,256]{2,1,0:T(8,128)S(1)} all-to-all(s32[8,40,256]{2,1,0:T(8,128)S(1)} %shard_map.92.refs_3_), channel_id=1, replica_groups=mesh['row'=4,'col'=8] {'col'}, dimensions={0} | all-to-all | bytes 655360 | tf_op jit(solution)/shard_map/all_to_all | solution.py:783
  116.6 17.6 %shard_map.94 = (f32[2,256,256]{2,1,0:T(8,128)S(1)}, f32[2,256,256]{2,1,0:T(8,128)S(1)}, s32[264,256]{1,0:T(8,128)}, s32[264,256]{1,0:T(8,128)}, s32[264,256]{1,...) custom-call(s32[256]{0:T(256)S(1)} %bitcast.9, s32[2]{0:T(128)S(1)} %pad_add_fusion.refs_1_.refs_0_, ...), custom_call_target="tpu_custom_call" | custom-call | flops 6442450944 | bytes 8388608 | tf_op jit(solution)/shard_map/pallas_call | solution.py:740
  134.2 11.4 %all_to_all.27.refs_0_ = s32[8,56,256]{2,1,0:T(8,128)S(1)} all-to-all(s32[8,56,256]{2,1,0:T(8,128)S(1)} %get-tuple-element.37), channel_id=1, replica_groups=mesh['row'=4,'col'=8] {'col'}, dimensions={0} | all-to-all | bytes 917504 | tf_op jit(solution)/shard_map/all_to_all | solution.py:776
  145.8 1.4 collective-permute-start.15
  147.3 3.0 %collective-permute-start.13 = (s32[56,256]{1,0:T(8,128)S(1)}, s32[56,256]{1,0:T(8,128)S(1)}, u32[]{:S(2)}, u32[]{:S(2)}) collective-permute-start(s32[56,256]{1,0:T(8,128)S(1)} %shard_map.97.refs_2_), channel_id=1, source_target_pairs={{0,8},{8,0},{16,24},{24,16},{1,9},{9,1},{17,25},{25,17},{2,10},{10... | collective-permute-start | bytes 172040 | tf_op jit(solution)/shard_map/ppermute | solution.py:770
  150.3 1.3 collective-permute-start.10
  151.6 2.6 %collective-permute-start.11 = (s32[264,256]{1,0:T(8,128)}, s32[264,256]{1,0:T(8,128)}, u32[]{:S(2)}, u32[]{:S(2)}) collective-permute-start(s32[264,256]{1,0:T(8,128)} %get-tuple-element.34), channel_id=1, source_target_pairs={{0,8},{8,16},{16,24},{1,9},{9,17},{17,25},{2,10},{10,18},{18,26},{... | collective-permute-start | bytes 811016 | tf_op jit(solution)/shard_map/ppermute | solution.py:756
  154.2 3.2 %collective-permute-start.12 = (s32[264,256]{1,0:T(8,128)}, s32[264,256]{1,0:T(8,128)}, u32[]{:S(2)}, u32[]{:S(2)}) collective-permute-start(s32[264,256]{1,0:T(8,128)} %get-tuple-element.35), channel_id=1, source_target_pairs={{0,9},{1,10},{2,11},{3,12},{4,13},{5,14},{6,15},{8,17},{9,18},{10,... | collective-permute-start | bytes 811016 | tf_op jit(solution)/shard_map/ppermute | solution.py:766
  157.4 1.4 shard_map.98
  158.8 3.4 %all-to-all-start.4 = ((s32[8,40,256]{2,1,0:T(8,128)}), s32[8,40,256]{2,1,0:T(8,128)S(1)}, u32[]{:S(2)}, u32[]{:S(2)}) async-start(s32[8,40,256]{2,1,0:T(8,128)} %shard_map.98), calls=%async_computation.4 | async-start | bytes 655360 | tf_op jit(solution)/shard_map/all_to_all | solution.py:783
  162.2 4.1 %shard_map.95.refs_6_ = f32[256,256]{1,0:T(8,128)S(1)} custom-call(s32[256]{0:T(256)S(1)} %bitcast.10, s32[2]{0:T(128)S(1)} %pad_add_fusion.refs_1_.refs_0_, f32[2,256,256]{2,1,0:T(8,128)S(1)} %get-tuple-element.36.refs_2_.refs_1_), custom_call_target="tpu_custom_call" | custom-call | flops 8589934592 | bytes 8388608 | tf_op jit(solution)/shard_map/pallas_call | solution.py:740
  166.4 2.3 %shard_map.96 = f32[2,256,256]{2,1,0:T(8,128)} custom-call(f32[2,256,256]{2,1,0:T(8,128)S(1)} %get-tuple-element.31.refs_0_, f32[2,256,256]{2,1,0:T(8,128)S(1)} %get-tuple-element.32.refs_1_, s32[264,256]{1,0:T(8,128)S(1)} %collective-permute-done.10.refs_2_, s32[264,256]{1,0:T(8,128)} %collective-permute-done.11.refs_3_, ...), custom_call_target="tpu_custom_call" | custom-call | flops 67108864 | bytes 8388608 | tf_op jit(solution)/shard_map/pallas_call | solution.py:740
  (66 shorter events, 19.1 us)
Async XLA Ops:
  0.6 1.0 copy-start
  2.6 3.7 %collective-permute-start = (s32[264,256]{1,0:T(8,128)}, s32[264,256]{1,0:T(8,128)S(1)}, u32[]{:S(2)}, u32[]{:S(2)}) collective-permute-start(s32[264,256]{1,0:T(8,128)} %shard_map.86), channel_id=1, source_target_pairs={{1,0},{2,1},{3,2},{4,3},{5,4},{6,5},{7,6},{9,8},{10,9},{11,10},{12... | collective-permute-start | bytes 811016 | tf_op jit(solution)/shard_map/ppermute | solution.py:756
  9.4 11.7 %copy-start.8 = (s32[128,2]{0,1:T(2,128)S(1)}, s32[128,2]{0,1:T(2,128)}, u32[]{:S(2)}) copy-start(s32[128,2]{0,1:T(2,128)} %param.10) | copy-start | bytes 3076
  9.4 38.6 %all-to-all-start = ((bf16[16,256,256]{2,1,0:T(8,128)(2,1)}), bf16[16,256,256]{2,1,0:T(8,128)(2,1)S(1)}, u32[]{:S(2)}, u32[]{:S(2)}) async-start(bf16[16,256,256]{2,1,0:T(8,128)(2,1)} %shard_map.89), calls=%async_computation | async-start | bytes 4194304 | tf_op jit(solution)/shard_map/all_to_all | solution.py:814
  18.3 16.9 %copy-start.1 = (f32[2,256,256]{2,1,0:T(8,128)S(1)}, f32[2,256,256]{2,1,0:T(8,128)}, u32[]{:S(2)}) copy-start(f32[2,256,256]{2,1,0:T(8,128)} %refs_2_.3) | copy-start | bytes 1572868
  18.3 11.5 %collective-permute-start.1 = (s32[264,256]{1,0:T(8,128)}, s32[264,256]{1,0:T(8,128)S(1)}, u32[]{:S(2)}, u32[]{:S(2)}) collective-permute-start(s32[264,256]{1,0:T(8,128)} %shard_map.86), channel_id=1, source_target_pairs={{8,0},{16,8},{24,16},{9,1},{17,9},{25,17},{10,2},{18,10},{26,18},{... | collective-permute-start | bytes 811016 | tf_op jit(solution)/shard_map/ppermute | solution.py:756
  19.7 15.5 %collective-permute-start.2 = (s32[264,256]{1,0:T(8,128)S(1)}, s32[264,256]{1,0:T(8,128)S(1)}, u32[]{:S(2)}, u32[]{:S(2)}) collective-permute-start(s32[264,256]{1,0:T(8,128)S(1)} %collective-permute-done.refs_3_), channel_id=1, source_target_pairs={{8,0},{16,8},{24,16},{9,1},{17,9},{25,17},{10,2},{18,10},{26,18},{... | collective-permute-start | bytes 811016 | tf_op jit(solution)/shard_map/ppermute | solution.py:756
  21.1 1.0 copy-start.2
  22.1 13.1 %copy-start.3 = (f32[2,256,256]{2,1,0:T(8,128)S(1)}, f32[2,256,256]{2,1,0:T(8,128)}, u32[]{:S(2)}) copy-start(f32[2,256,256]{2,1,0:T(8,128)} %refs_1_.1) | copy-start | bytes 1572868
  22.1 13.1 %copy-start.9 = (bf16[2,2,256,256]{3,2,1,0:T(8,128)(2,1)S(1)}, bf16[2,2,256,256]{3,2,1,0:T(8,128)(2,1)}, u32[]{:S(2)}) copy-start(bf16[2,2,256,256]{3,2,1,0:T(8,128)(2,1)} %constant.14.clone.refs_7_.refs_8_.refs_9_) | copy-start | bytes 1572868
  22.1 13.1 %copy-start.13 = (f32[2,136,128]{2,1,0:T(8,128)S(1)}, f32[2,136,128]{2,1,0:T(8,128)}, u32[]{:S(2)}) copy-start(f32[2,136,128]{2,1,0:T(8,128)} %constant.15.clone.refs_8_.refs_9_.refs_10_) | copy-start | bytes 417796
  43.9 2.0 %copy-start.16 = (f32[8,2,256,256]{3,2,1,0:T(8,128)}, f32[8,2,256,256]{3,2,1,0:T(8,128)S(1)}, u32[]{:S(2)}) copy-start(f32[8,2,256,256]{3,2,1,0:T(8,128)S(1)} %get-tuple-element.22.refs_6_) | copy-start | bytes 12582916
  45.9 1.4 copy-start.18
  51.9 2.2 %copy-start.17 = (f32[8,2,256,256]{3,2,1,0:T(8,128)S(1)}, f32[8,2,256,256]{3,2,1,0:T(8,128)}, u32[]{:S(2)}) copy-start(f32[8,2,256,256]{3,2,1,0:T(8,128)} %copy-done.16) | copy-start | bytes 12582916
  54.1 1.6 copy-start.19
  56.6 38.2 %copy-start.5 = (f32[2,256,256]{2,1,0:T(8,128)S(1)}, f32[2,256,256]{2,1,0:T(8,128)}, u32[]{:S(2)}) copy-start(f32[2,256,256]{2,1,0:T(8,128)} %refs_1_.1) | copy-start | bytes 1572868
  70.6 25.0 %collective-permute-start.3 = (s32[264,512]{1,0:T(8,128)S(1)}, s32[264,512]{1,0:T(8,128)S(1)}, u32[]{:S(2)}, u32[]{:S(2)}) collective-permute-start(s32[264,512]{1,0:T(8,128)S(1)} %get-tuple-element.24), channel_id=1, source_target_pairs={{0,8},{8,16},{16,24},{1,9},{9,17},{17,25},{2,10},{10,18},{18,26},{... | collective-permute-start | bytes 1622024 | tf_op jit(solution)/shard_map/ppermute | solution.py:756
  71.9 23.7 %collective-permute-start.4 = (s32[264,512]{1,0:T(8,128)S(1)}, s32[264,512]{1,0:T(8,128)S(1)}, u32[]{:S(2)}, u32[]{:S(2)}) collective-permute-start(s32[264,512]{1,0:T(8,128)S(1)} %get-tuple-element.25), channel_id=1, source_target_pairs={{8,0},{16,8},{24,16},{9,1},{17,9},{25,17},{10,2},{18,10},{26,18},{... | collective-permute-start | bytes 1622024 | tf_op jit(solution)/shard_map/ppermute | solution.py:756
  85.2 6.4 %collective-permute-start.7 = (s32[56,256]{1,0:T(8,128)S(1)}, s32[56,256]{1,0:T(8,128)S(1)}, u32[]{:S(2)}, u32[]{:S(2)}) collective-permute-start(s32[56,256]{1,0:T(8,128)S(1)} %shard_map.91.refs_2_), channel_id=1, source_target_pairs={{0,24},{8,16},{16,8},{24,0},{1,25},{9,17},{17,9},{25,1},{2,26},{10... | collective-permute-start | bytes 172040 | tf_op jit(solution)/shard_map/ppermute | solution.py:770
  89.2 5.7 %collective-permute-start.6 = (s32[56,256]{1,0:T(8,128)S(1)}, s32[56,256]{1,0:T(8,128)S(1)}, u32[]{:S(2)}, u32[]{:S(2)}) collective-permute-start(s32[56,256]{1,0:T(8,128)S(1)} %shard_map.91.refs_2_), channel_id=1, source_target_pairs={{0,16},{8,24},{16,0},{24,8},{1,17},{9,25},{17,1},{25,9},{2,18},{10... | collective-permute-start | bytes 172040 | tf_op jit(solution)/shard_map/ppermute | solution.py:770
  89.7 5.2 %collective-permute-start.5 = (s32[56,256]{1,0:T(8,128)S(1)}, s32[56,256]{1,0:T(8,128)S(1)}, u32[]{:S(2)}, u32[]{:S(2)}) collective-permute-start(s32[56,256]{1,0:T(8,128)S(1)} %shard_map.91.refs_2_), channel_id=1, source_target_pairs={{0,8},{8,0},{16,24},{24,16},{1,9},{9,1},{17,25},{25,17},{2,10},{10... | collective-permute-start | bytes 172040 | tf_op jit(solution)/shard_map/ppermute | solution.py:770
  95.6 21.0 %copy-start.11 = (bf16[2,2,256,256]{3,2,1,0:T(8,128)(2,1)S(1)}, bf16[2,2,256,256]{3,2,1,0:T(8,128)(2,1)}, u32[]{:S(2)}) copy-start(bf16[2,2,256,256]{3,2,1,0:T(8,128)(2,1)} %constant.14.clone.refs_7_.refs_8_.refs_9_) | copy-start | bytes 1572868
  95.6 21.0 %copy-start.15 = (f32[2,136,128]{2,1,0:T(8,128)S(1)}, f32[2,136,128]{2,1,0:T(8,128)}, u32[]{:S(2)}) copy-start(f32[2,136,128]{2,1,0:T(8,128)} %constant.15.clone.refs_8_.refs_9_.refs_10_) | copy-start | bytes 417796
  96.7 19.9 %collective-permute-start.8 = (s32[528,256]{1,0:T(8,128)S(1)}, s32[528,256]{1,0:T(8,128)S(1)}, u32[]{:S(2)}, u32[]{:S(2)}) collective-permute-start(s32[528,256]{1,0:T(8,128)S(1)} %get-tuple-element.28), channel_id=1, source_target_pairs={{0,1},{1,2},{2,3},{3,4},{4,5},{5,6},{6,7},{8,9},{9,10},{10,11},{11... | collective-permute-start | bytes 1622024 | tf_op jit(solution)/shard_map/ppermute | solution.py:756
  98.0 18.6 %collective-permute-start.9 = (s32[528,256]{1,0:T(8,128)S(1)}, s32[528,256]{1,0:T(8,128)S(1)}, u32[]{:S(2)}, u32[]{:S(2)}) collective-permute-start(s32[528,256]{1,0:T(8,128)S(1)} %get-tuple-element.29), channel_id=1, source_target_pairs={{1,0},{2,1},{3,2},{4,3},{5,4},{6,5},{7,6},{9,8},{10,9},{11,10},{12... | collective-permute-start | bytes 1622024 | tf_op jit(solution)/shard_map/ppermute | solution.py:756
  145.8 8.4 %collective-permute-start.15 = (s32[56,256]{1,0:T(8,128)S(1)}, s32[56,256]{1,0:T(8,128)S(1)}, u32[]{:S(2)}, u32[]{:S(2)}) collective-permute-start(s32[56,256]{1,0:T(8,128)S(1)} %shard_map.97.refs_2_), channel_id=1, source_target_pairs={{0,24},{8,16},{16,8},{24,0},{1,25},{9,17},{17,9},{25,1},{2,26},{10... | collective-permute-start | bytes 172040 | tf_op jit(solution)/shard_map/ppermute | solution.py:770
  147.3 10.1 %collective-permute-start.14 = (s32[56,256]{1,0:T(8,128)S(1)}, s32[56,256]{1,0:T(8,128)S(1)}, u32[]{:S(2)}, u32[]{:S(2)}) collective-permute-start(s32[56,256]{1,0:T(8,128)S(1)} %shard_map.97.refs_2_), channel_id=1, source_target_pairs={{0,16},{8,24},{16,0},{24,8},{1,17},{9,25},{17,1},{25,9},{2,18},{10... | collective-permute-start | bytes 172040 | tf_op jit(solution)/shard_map/ppermute | solution.py:770
  147.3 10.1 %collective-permute-start.13 = (s32[56,256]{1,0:T(8,128)S(1)}, s32[56,256]{1,0:T(8,128)S(1)}, u32[]{:S(2)}, u32[]{:S(2)}) collective-permute-start(s32[56,256]{1,0:T(8,128)S(1)} %shard_map.97.refs_2_), channel_id=1, source_target_pairs={{0,8},{8,0},{16,24},{24,16},{1,9},{9,1},{17,25},{25,17},{2,10},{10... | collective-permute-start | bytes 172040 | tf_op jit(solution)/shard_map/ppermute | solution.py:770
  150.3 16.1 %collective-permute-start.10 = (s32[264,256]{1,0:T(8,128)}, s32[264,256]{1,0:T(8,128)S(1)}, u32[]{:S(2)}, u32[]{:S(2)}) collective-permute-start(s32[264,256]{1,0:T(8,128)} %get-tuple-element.33), channel_id=1, source_target_pairs={{0,1},{1,2},{2,3},{3,4},{4,5},{5,6},{6,7},{8,9},{9,10},{10,11},{11... | collective-permute-start | bytes 811016 | tf_op jit(solution)/shard_map/ppermute | solution.py:756
  151.6 14.8 %collective-permute-start.11 = (s32[264,256]{1,0:T(8,128)}, s32[264,256]{1,0:T(8,128)}, u32[]{:S(2)}, u32[]{:S(2)}) collective-permute-start(s32[264,256]{1,0:T(8,128)} %get-tuple-element.34), channel_id=1, source_target_pairs={{0,8},{8,16},{16,24},{1,9},{9,17},{17,25},{2,10},{10,18},{18,26},{... | collective-permute-start | bytes 811016 | tf_op jit(solution)/shard_map/ppermute | solution.py:756
  154.2 12.1 %collective-permute-start.12 = (s32[264,256]{1,0:T(8,128)}, s32[264,256]{1,0:T(8,128)}, u32[]{:S(2)}, u32[]{:S(2)}) collective-permute-start(s32[264,256]{1,0:T(8,128)} %get-tuple-element.35), channel_id=1, source_target_pairs={{0,9},{1,10},{2,11},{3,12},{4,13},{5,14},{6,15},{8,17},{9,18},{10,... | collective-permute-start | bytes 811016 | tf_op jit(solution)/shard_map/ppermute | solution.py:766
  158.8 11.0 %all-to-all-start.4 = ((s32[8,40,256]{2,1,0:T(8,128)}), s32[8,40,256]{2,1,0:T(8,128)S(1)}, u32[]{:S(2)}, u32[]{:S(2)}) async-start(s32[8,40,256]{2,1,0:T(8,128)} %shard_map.98), calls=%async_computation.4 | async-start | bytes 655360 | tf_op jit(solution)/shard_map/all_to_all | solution.py:783
  (8 other events, 7.3 us)

commit v4 on v3

--- a/solution.py
+++ b/solution.py
@@ -53,7 +53,7 @@
     )
 
 
-def list_patterns(dims, pos_ref, me_ref, ys_ref, xs_ref, slots_ref):
+def list_patterns(dims, pos_ref, me_ref, ys_ref, xs_ref, holders_ref, ranks_ref):
     tile_rows, tile_cols, pat_count, col_count, capacity = dims
     my_row, my_col = me_ref[0], me_ref[1]
     band_count = pat_count * col_count
@@ -72,7 +72,8 @@
         def _():
             ys_ref[found] = y - my_row * tile_rows
             xs_ref[found] = x - my_col * tile_cols
-            slots_ref[found] = holder * SEND + jnp.minimum(rank, SEND - 1)
+            holders_ref[found] = holder
+            ranks_ref[found] = rank
 
         step = here.astype(jnp.int32)
         return found + step, holder, rank + step
@@ -390,7 +391,7 @@
         live = still
 
 
-def outgoing_kernel(dims, pos_ref, me_ref, amp_ref, after_ref, out_ref, sems):
+def outgoing_kernel(dims, wanted, pos_ref, me_ref, amp_ref, after_ref, out_ref, sems):
     tile_rows, tile_cols, pat_count, col_count, capacity = dims
     first = (me_ref[0] * col_count + me_ref[1]) * pat_count
     total = pos_ref.shape[0] // 2
@@ -398,11 +399,11 @@
     copies = []
     for k in range(pat_count):
         rank = sum(((owners[e] == owners[k]).astype(jnp.int32) for e in range(k)), jnp.int32(0))
-        slot = owners[k] * SEND + jnp.minimum(rank, SEND - 1)
-        copies.append(pltpu.make_async_copy(amp_ref.at[k], out_ref.at[slot], sems.at[k]))
-        copies[-1].start()
-    for copy in copies:
-        copy.wait()
+        copies.append((rank == wanted, pltpu.make_async_copy(amp_ref.at[k], out_ref.at[owners[k]], sems.at[k])))
+    for chosen, copy in copies:
+        pl.when(chosen)(copy.start)
+    for chosen, copy in copies:
+        pl.when(chosen)(copy.wait)
 
 
 def weights_kernel(dims, span, pos_ref, me_ref, probe_ref, out_ref, sums_ref, power_ref):
@@ -495,10 +496,10 @@
 
 
 def first_half_kernel(dims, pos_ref, me_ref, own_ref, right_ref, below_ref, diag_ref, probe_ref, turns, twiddles,
-                      far_out, power_out, ext_out, ext_ref, win_ref, xa_ref, xb_ref, ya_ref, yb_ref, far_ref, ys_ref, xs_ref, slots_ref, sems, ext_sem):
+                      far_out, power_out, ext_out, ext_ref, win_ref, xa_ref, xb_ref, ya_ref, yb_ref, far_ref, ys_ref, xs_ref, holders_ref, ranks_ref, sems, ext_sem):
     tile_rows, tile_cols, pat_count, col_count, capacity = dims
     order = probe_ref.shape[1]
-    count = list_patterns(dims, pos_ref, me_ref, ys_ref, xs_ref, slots_ref)
+    count = list_patterns(dims, pos_ref, me_ref, ys_ref, xs_ref, holders_ref, ranks_ref)
     unfold(dims, ext_ref, own_ref, (right_ref, below_ref, diag_ref))
     keep = pltpu.make_async_copy(ext_ref, ext_out, ext_sem)
     keep.start()
@@ -530,24 +531,31 @@
     keep.wait()
 
 
-def second_half_kernel(dims, pos_ref, me_ref, ext_ref, probe_ref, power_ref, weights_ref, far_in, amp_in, turns, twiddles, sorting,
+def second_half_kernel(dims, pos_ref, me_ref, ext_ref, probe_ref, power_ref, weights_ref, far_in, amp_first, amp_second, turns, twiddles, sorting,
                        share_out, top_out, bottom_out, numer_out, amp_out,
-                       sum_ref, win_ref, xa_ref, xb_ref, ya_ref, yb_ref, numer_ref, far_ref, amp_ref, sorted_ref, ys_ref, xs_ref, slots_ref, far_sems, amp_sems, out_sems, sum_sem):
+                       sum_ref, win_ref, xa_ref, xb_ref, ya_ref, yb_ref, numer_ref, far_ref, amp_ref, sorted_ref, ys_ref, xs_ref, holders_ref, ranks_ref, far_sems, amp_sems, out_sems, sum_sem):
     tile_rows, tile_cols, pat_count, col_count, capacity = dims
     order = probe_ref.shape[1]
     half = order // 2
-    count = list_patterns(dims, pos_ref, me_ref, ys_ref, xs_ref, slots_ref)
+    amp_ins = (amp_first, amp_second)
+    count = list_patterns(dims, pos_ref, me_ref, ys_ref, xs_ref, holders_ref, ranks_ref)
     pairs = lax.div(count + 1, 2)
 
-    def copies(listed):
-        return (
-            pltpu.make_async_copy(far_in.at[listed], far_ref.at[listed], far_sems.at[listed]),
-            pltpu.make_async_copy(amp_in.at[slots_ref[jnp.minimum(listed, count - 1)]], amp_ref.at[listed], amp_sems.at[listed]),
-        )
+    def far_copy(listed):
+        return pltpu.make_async_copy(far_in.at[listed], far_ref.at[listed], far_sems.at[listed])
+
+    def amp_copy(listed, source):
+        return pltpu.make_async_copy(source.at[holders_ref[jnp.minimum(listed, count - 1)]], amp_ref.at[listed], amp_sems.at[listed])
 
     def begin(listed, carry):
-        for copy in copies(listed):
-            copy.start()
+        far_copy(listed).start()
+        rank = ranks_ref[jnp.minimum(listed, count - 1)]
+        for wanted, source in enumerate(amp_ins):
+
+            @pl.when(rank == wanted)
+            def _():
+                amp_copy(listed, source).start()
+
         return carry
 
     lax.fori_loop(0, 2 * pairs, begin, 0)
@@ -559,8 +567,8 @@
         stages = []
         for k in range(2):
             listed = 2 * step + k
-            for copy in copies(listed):
-                copy.wait()
+            far_copy(listed).wait()
+            amp_copy(listed, amp_ins[0]).wait()
         for k in range(2):
             listed = 2 * step + k
             weight = (listed < count).astype(f32)
@@ -620,11 +628,11 @@
 
 def whole_kernel(dims, pos_ref, me_ref, old_ref, sum_ref, from_left_ref, from_right_ref, weights_ref,
                  chunks_ref, amp_in, turns, twiddles,
-                 current_out, own_out, right_out, below_out, diag_out, numer_out, probe_ref,
-                 ext_ref, grad_ref, win_ref, xa_ref, xb_ref, ya_ref, yb_ref, numer_ref, far_ref, amp_ref, ys_ref, xs_ref, slots_ref, amp_sems, own_sem):
+                 current_out, top_out, bottom_out, numer_out, probe_ref,
+                 ext_ref, grad_ref, win_ref, xa_ref, xb_ref, ya_ref, yb_ref, numer_ref, far_ref, amp_ref, ys_ref, xs_ref, holders_ref, ranks_ref, amp_sems, own_sem):
     tile_rows, tile_cols, pat_count, col_count, capacity = dims
     order = probe_ref.shape[1]
-    count = list_patterns(dims, pos_ref, me_ref, ys_ref, xs_ref, slots_ref)
+    count = list_patterns(dims, pos_ref, me_ref, ys_ref, xs_ref, holders_ref, ranks_ref)
     pairs = lax.div(count + 1, 2)
     decode_probe(probe_ref, chunks_ref)
 
@@ -672,30 +680,46 @@
         return carry
 
     lax.fori_loop(0, pairs, pair, 0)
-    own_out[...] = grad_ref[:, 0:tile_rows, 0:tile_cols]
-    for (i, j), ref in zip(((0, 1), (1, 0), (1, 1)), (right_out, below_out, diag_out)):
-
-        def read(comp, at, cols, i=i, j=j):
-            rows, cols = pl.ds(i * tile_rows + at.start, at.size), pl.ds(j * tile_cols + cols.start, cols.size)
-            return grad_ref[comp, rows, cols] / (weights_ref[rows, cols] + object_regular)
-
-        encode(read, ref, tile_rows, 0, tile_rows)
+    for first in range(0, tile_rows, CHUNK):
+        rows = pl.ds(first, CHUNK)
+        scale = 1.0 / (weights_ref[rows, :] + object_regular)
+        for comp in range(2):
+            top_out[comp, rows, :] = grad_ref[comp, rows, :] * scale
+
+    def read(comp, at, cols):
+        rows = pl.ds(tile_rows + at.start, at.size)
+        return grad_ref[comp, rows, cols] / (weights_ref[rows, cols] + object_regular)
+
+    encode(read, bottom_out, tile_rows, 0, tile_rows)
     spread_sums(numer_out, numer_ref, numer_ref.at[2])
     keep.wait()
 
 
-def object_kernel(dims, current_ref, own_ref, left_ref, above_ref, diag_ref, before_ref, weights_ref, out_ref):
+def fold_kernel(dims, top_ref, above_ref, own_out, right_out):
+    tile_rows, tile_cols = dims[:2]
+    for col in range(0, 2 * tile_cols, LANES):
+        for start in range(0, tile_rows, CHUNK):
+            rows, cols = pl.ds(start, CHUNK), pl.ds(col, LANES)
+            parts = decode(above_ref, start, tile_rows, col)
+            for comp in range(2):
+                if col < tile_cols:
+                    own_out[comp, rows, cols] = top_ref[comp, rows, cols] + parts[comp]
+                else:
+                    top_ref[comp, rows, cols] += parts[comp]
+    encode(lambda comp, at, cols: top_ref[comp, at, pl.ds(tile_cols + cols.start, cols.size)], right_out, tile_rows, 0, tile_rows)
+
+
+def object_kernel(dims, current_ref, own_ref, left_ref, before_ref, weights_ref, out_ref):
     tile_rows, tile_cols = dims[:2]
     for col in range(0, tile_cols, LANES):
         for start in range(0, tile_rows, CHUNK):
             rows, cols = pl.ds(start, CHUNK), pl.ds(col, LANES)
             scale = 1.0 / (weights_ref[rows, cols] + object_regular)
             back = (before_ref[rows, cols] + object_regular) * scale
-            parts = [decode(ref, start, tile_rows, col) for ref in (left_ref, above_ref, diag_ref)]
+            parts = decode(left_ref, start, tile_rows, col)
             for comp in range(2):
-                coded = parts[0][comp] + parts[1][comp] + parts[2][comp]
-                old = object_regular * current_ref[comp, rows, cols] + own_ref[comp, rows, cols]
-                out_ref[comp, rows, cols] = old * scale + coded * back
+                old = object_regular * scale * current_ref[comp, rows, cols]
+                out_ref[comp, rows, cols] = old + (own_ref[comp, rows, cols] + parts[comp]) * back
 
 
 def shape(dims, dtype=f32):
@@ -713,10 +737,10 @@
 
 
 def list_scratch(capacity):
-    return [pltpu.SMEM((capacity,), jnp.int32)] * 3
-
-
-def call(kernel, outs, out_specs, in_specs, scratch, flops, limit=26 << 20):
+    return [pltpu.SMEM((capacity,), jnp.int32)] * 4
+
+
+def call(kernel, outs, out_specs, in_specs, scratch, flops, limit=48 << 20):
     several = isinstance(outs, tuple)
     out_count = len(outs) if several else 1
     in_count = len(in_specs)
@@ -756,16 +780,6 @@
     return lax.ppermute(value, axis, [(source, source + steps) for source in range(leading, last)])
 
 
-def passed_both(value, row_steps, col_steps):
-    rows, cols = lax.axis_size("row"), lax.axis_size("col")
-    pairs = []
-    for r in range(rows):
-        for c in range(cols):
-            if 0 <= r + row_steps < rows and 0 <= c + col_steps < cols:
-                pairs.append((r * cols + c, (r + row_steps) * cols + c + col_steps))
-    return lax.ppermute(value, ("row", "col"), pairs)
-
-
 def swapped(value, axis, mask):
     return lax.ppermute(value, axis, [(k, k ^ mask) for k in range(lax.axis_size(axis))])
 
@@ -780,7 +794,7 @@
         functools.partial(update_kernel, rows), shape((cols, rows + SUBLANES, order), jnp.int32), VMEM,
         [SMEM, kind] + [VMEM] * len(totals), [], 1 << 26,
     )(me, probe, *totals)
-    return fresh, lax.all_to_all(fresh, "col", split_axis=0, concat_axis=0, tiled=True)
+    return totals[1], lax.all_to_all(fresh, "col", split_axis=0, concat_axis=0, tiled=True)
 
 
 def local(obj, probe, amplitudes, positions):
@@ -807,11 +821,13 @@
     below = passed_along(coded, "row", -1)
     diag = passed_along(right, "row", -1)
 
-    outgoing = call(
-        functools.partial(outgoing_kernel, dims), shape((col_count * SEND, order, order), bf16), HBM, [SMEM, SMEM, HBM, HBM],
-        [pltpu.SemaphoreType.DMA((pat_count,))], 1 << 20,
-    )(pos, me, amplitudes, right)
-    incoming = lax.all_to_all(outgoing, "col", split_axis=0, concat_axis=0, tiled=True)
+    incoming = []
+    for wanted, after in enumerate((coded, right)):
+        outgoing = call(
+            functools.partial(outgoing_kernel, dims, wanted), shape((col_count, order, order), bf16), HBM, [SMEM, SMEM, HBM, HBM],
+            [pltpu.SemaphoreType.DMA((pat_count,))], 1 << 20,
+        )(pos, me, amplitudes, after)
+        incoming.append(lax.all_to_all(outgoing, "col", split_axis=0, concat_axis=0, tiled=True))
 
     def weights(probe_now, span, kind):
         return call(
@@ -833,24 +849,24 @@
         functools.partial(second_half_kernel, dims),
         (shape(wide), coded_row, coded_row, shares, shape((capacity, order, order), bf16)),
         (HBM, VMEM, VMEM, VMEM, HBM),
-        [SMEM, SMEM, LOAD, LOAD, VMEM, LOAD, HBM, HBM] + [LOAD] * 3,
+        [SMEM, SMEM, LOAD, LOAD, VMEM, LOAD, HBM, HBM, HBM] + [LOAD] * 3,
         [pltpu.VMEM(wide, f32)] + work_scratch(order)
         + [pltpu.VMEM(window, f32), pltpu.VMEM((capacity,) + window, f32), pltpu.VMEM((capacity, order, order), bf16), pltpu.VMEM((capacity, order, order), bf16)]
         + list_scratch(capacity) + [pltpu.SemaphoreType.DMA((capacity,))] * 3 + [pltpu.SemaphoreType.DMA],
         capacity * one_pattern // 2,
-    )(pos, me, ext, probe, power, weights_old, far, incoming, turns, twiddles, sorting)
+    )(pos, me, ext, probe, power, weights_old, far, *incoming, turns, twiddles, sorting)
 
     from_above = passed_along(bottom, "row", 1)
     from_below = passed_along(top, "row", -1)
-    fresh, chunks = probe_update(me, probe, numer, LOAD)
+    begun, chunks = probe_update(me, probe, numer, LOAD)
     sums, to_left, to_right = call(
         functools.partial(rows_sum_kernel, dims), (shape(wide), coded_col, coded_col), (VMEM,) * 3, [LOAD, VMEM, VMEM, HBM], [], 1 << 26,
-    )(share, from_above, from_below, fresh)
+    )(share, from_above, from_below, begun)
     from_left = passed_along(to_right, "col", 1)
     from_right = passed_along(to_left, "col", -1)
 
-    current, own, to_right, to_below, to_diag, numer, probe_now = call(
-        functools.partial(whole_kernel, dims), (shape(tile), shape(tile), coded_tile, coded_tile, coded_tile, shares, shape(window)), (HBM,) + (VMEM,) * 6,
+    current, top, bottom, numer, probe_now = call(
+        functools.partial(whole_kernel, dims), (shape(tile), shape((2, tile_rows, 2 * tile_cols)), coded_row, shares, shape(window)), (HBM,) + (VMEM,) * 4,
         [SMEM, SMEM, LOAD] + [VMEM] * 3 + [LOAD, VMEM, HBM, LOAD, LOAD],
         [pltpu.VMEM(wide, f32), pltpu.VMEM(wide, f32)] + work_scratch(order)
         + [pltpu.VMEM((3, order, order), f32), pltpu.VMEM((2,) + window, f32), pltpu.VMEM((capacity, order, order), bf16)]
@@ -858,14 +874,16 @@
         capacity * one_pattern,
     )(pos, me, ext, sums, from_left, from_right, weights_old, chunks, sorted_amps, turns, twiddles)
 
+    from_above = passed_along(bottom, "row", 1)
+    _, chunks = probe_update(me, probe_now, numer, VMEM)
+    own, to_right = call(
+        functools.partial(fold_kernel, dims), (shape(tile), coded_tile), (VMEM, VMEM), [LOAD, VMEM], [], 1 << 26,
+    )(top, from_above)
     from_left = passed_along(to_right, "col", 1)
-    from_above = passed_along(to_below, "row", 1)
-    from_diag = passed_both(to_diag, 1, 1)
     weights_new = weights(probe_now, 1, VMEM)
-    new_object = call(functools.partial(object_kernel, dims), shape(tile), VMEM, [LOAD] + [VMEM] * 4 + [LOAD, VMEM], [], 1 << 26)(
-        current, own, from_left, from_above, from_diag, weights_old, weights_new
+    new_object = call(functools.partial(object_kernel, dims), shape(tile), VMEM, [LOAD, VMEM, VMEM, LOAD, VMEM], [], 1 << 26)(
+        current, own, from_left, weights_old, weights_new
     )
-    _, chunks = probe_update(me, probe_now, numer, VMEM)
     new_probe = call(probe_kernel, shape(window), VMEM, [VMEM], [], 1 << 26)(chunks)
     return new_object, new_probe
 

time: 173 us -> 179 us (1.035)
  waiting for transfers between devices: 14.9 us -> 22.1 us
  local copies, waits for them, and re-layouts: 16.5 us -> 10.9 us
  Pallas kernels: 59.8 us -> 61.7 us
    all_to_all x1 -> x2, waiting for transfers between devices: 0.01 us -> 9.9 us  [local(): lax.all_to_all(outgoing, 'col', split_axis=0, concat_axis=0, tiled=True)]
    ppermute x9, waiting for transfers between devices: 8.91 us -> 0.86 us  [passed_along(): lax.ppermute(value, axis, [(source, source + steps) for source in range(l...]
    ppermute x6, waiting for transfers between devices: 4.89 us -> 11.4 us  [swapped(): lax.ppermute(value, axis, [(k, k ^ mask) for k in range(lax.axis_size(axi...]
    unnamed x44 -> x46, local copies, waits for them, and re-layouts: 16.5 us -> 10.9 us
    all_to_all x1, blocking collectives: 17.3 us -> 11.7 us  [probe_update(): lax.all_to_all(fresh, 'col', split_axis=0, concat_axis=0, tiled=True)]
    all_to_all x2, blocking collectives: 23.2 us -> 28.8 us  [probe_update(): lax.all_to_all(numer, 'col', split_axis=0, concat_axis=0, tiled=True)]
    ppermute x1 -> x0, starting transfers between devices: 3.16 us -> none  [passed_both(): return lax.ppermute(value, ('row', 'col'), pairs)]
    all_to_all x1 -> x2, starting transfers between devices: 8.91 us -> 11.9 us  [local(): lax.all_to_all(outgoing, 'col', split_axis=0, concat_axis=0, tiled=True)]
  transfers between devices with their start and end apart: 18 -> 18, of which waited for: 6 -> 7; matrix products, arithmetic and copies ran while one was open for 0% -> 0% of each run, Pallas kernels for 14% -> 14%
where the time goes in v4:
time: 179 us; the launch traced here: 175 us
  Pallas kernels  61.7 us (34%)
  blocking collectives  40.5 us (23%)
  starting transfers between devices  38.9 us (22%)
  waiting for transfers between devices  22.1 us (12%)
  local copies, waits for them, and re-layouts  10.9 us (6%)
    pallas_call x16, Pallas kernels, called(): pl.pallas_call(body, out_shape=outs, out_specs=out_specs, in_specs=[HBM i...  61.7 us
    all_to_all x2, blocking collectives, probe_update(): lax.all_to_all(numer, 'col', split_axis=0, concat_axis=0, tiled=True)  28.8 us
    ppermute x9, starting transfers between devices, passed_along(): lax.ppermute(value, axis, [(source, source + steps) for source in range(l...  12.8 us
    all_to_all x2, starting transfers between devices, local(): lax.all_to_all(outgoing, 'col', split_axis=0, concat_axis=0, tiled=True)  11.9 us
    all_to_all x1, blocking collectives, probe_update(): lax.all_to_all(fresh, 'col', split_axis=0, concat_axis=0, tiled=True)  11.7 us
    ppermute x6, waiting for transfers between devices, swapped(): lax.ppermute(value, axis, [(k, k ^ mask) for k in range(lax.axis_size(axi...  11.4 us
    unnamed x46, local copies, waits for them, and re-layouts  10.9 us
    ppermute x6, starting transfers between devices, swapped(): lax.ppermute(value, axis, [(k, k ^ mask) for k in range(lax.axis_size(axi...  10.7 us
  transfers between devices with their start and end apart: 18, of which 7 were waited for; matrix products, arithmetic and copies ran while one was open for 0% of the time, Pallas kernels for 14%

profile of v4, /device:TPU:0, one launch (start us, length us, event | category | flops | bytes accessed | tf_op | source)
XLA Modules:
  0.0 175.4 jit_solution(8188552076240944411)
XLA Ops:
  3.7 1.4 shard_map.89
  5.1 5.1 %all-to-all-start = ((bf16[8,256,256]{2,1,0:T(8,128)(2,1)}), bf16[8,256,256]{2,1,0:T(8,128)(2,1)S(1)}, u32[]{:S(2)}, u32[]{:S(2)}) async-start(bf16[8,256,256]{2,1,0:T(8,128)(2,1)} %shard_map.89), calls=%async_computation | async-start | bytes 2097152 | tf_op jit(solution)/shard_map/all_to_all | solution.py:830
  10.3 1.4 collective-permute-start
  11.7 1.3 collective-permute-start.1
  15.8 9.9 %all-to-all-done.refs_7_ = bf16[8,256,256]{2,1,0:T(8,128)(2,1)S(1)} async-done(((bf16[8,256,256]{2,1,0:T(8,128)(2,1)}), bf16[8,256,256]{2,1,0:T(8,128)(2,1)S(1)}, u32[]{:S(2)}, u32[]{:S(2)}) %all-to-all-start) | async-done | bytes 1048608 | tf_op jit(solution)/shard_map/all_to_all | solution.py:830
  26.6 6.8 %all-to-all-start.1 = ((bf16[8,256,256]{2,1,0:T(8,128)(2,1)}), bf16[8,256,256]{2,1,0:T(8,128)(2,1)}, u32[]{:S(2)}, u32[]{:S(2)}) async-start(bf16[8,256,256]{2,1,0:T(8,128)(2,1)} %shard_map.90), calls=%async_computation.1 | async-start | bytes 2097152 | tf_op jit(solution)/shard_map/all_to_all | solution.py:830
  33.5 5.7 %shard_map.88.refs_5_.refs_6_.refs_3_ = f32[512,512]{1,0:T(8,128)S(1)} custom-call(s32[256]{0:T(256)S(1)} %bitcast.7, s32[2]{0:T(128)S(1)} %pad_add_fusion.refs_1_.refs_0_, f32[2,256,256]{2,1,0:T(8,128)S(1)} %copy-done.4), custom_call_target="tpu_custom_call" | custom-call | flops 8589934592 | bytes 8388608 | tf_op jit(solution)/shard_map/pallas_call | solution.py:764
  39.2 9.2 %shard_map.87 = (f32[8,2,256,256]{3,2,1,0:T(8,128)}, f32[256,256]{1,0:T(8,128)S(1)}, f32[2,512,512]{2,1,0:T(8,128)S(1)}) custom-call(s32[256]{0:T(256)S(1)} %bitcast.8, s32[2]{0:T(128)S(1)} %pad_add_fusion.refs_1_.refs_0_, f32[2,256,256]{2,1,0:T(8,128)S(1)} %copy-done.3, s32[264,256]{1,0:T(8,128)S(1)} %collective-permute-done.refs_3_, ...), custom_call_target="tpu_custom_call" | custom-call | flops 3221225472 | bytes 8388608 | tf_op jit(solution)/shard_map/pallas_call | solution.py:764
  48.5 1.4 copy-done.18
  51.5 14.6 %shard_map.91 = (f32[2,512,512]{2,1,0:T(8,128)}, s32[264,512]{1,0:T(8,128)S(1)}, s32[264,512]{1,0:T(8,128)S(1)}, s32[8,56,256]{2,1,0:T(8,128)S(1)}, bf16[8,256,256]{2,1,0:T(8,128)(2,1)S(1)}) custom-call(s32[256]{0:T(256)S(1)} %bitcast.9, s32[2]{0:T(128)S(1)} %pad_add_fusion.refs_1_.refs_0_, f32[2,512,512]{2,1,0:T(8,128)} %copy-done.18, ...), custom_call_target="tpu_custom_call" | custom-call | flops 3221225472 | bytes 8388608 | tf_op jit(solution)/shard_map/pallas_call | solution.py:764
  67.0 1.3 collective-permute-start.3
  68.3 1.3 collective-permute-start.4
  69.6 17.3 %all_to_all.30.refs_0_ = s32[8,56,256]{2,1,0:T(8,128)S(1)} all-to-all(s32[8,56,256]{2,1,0:T(8,128)S(1)} %get-tuple-element.26), channel_id=1, replica_groups=mesh['row'=4,'col'=8] {'col'}, dimensions={0} | all-to-all | bytes 917504 | tf_op jit(solution)/shard_map/all_to_all | solution.py:790
  87.1 2.7 %collective-permute-start.5 = (s32[56,256]{1,0:T(8,128)S(1)}, s32[56,256]{1,0:T(8,128)S(1)}, u32[]{:S(2)}, u32[]{:S(2)}) collective-permute-start(s32[56,256]{1,0:T(8,128)S(1)} %shard_map.92.refs_2_), channel_id=1, source_target_pairs={{0,8},{8,0},{16,24},{24,16},{1,9},{9,1},{17,25},{25,17},{2,10},{10... | collective-permute-start | bytes 172040 | tf_op jit(solution)/shard_map/ppermute | solution.py:784
  89.9 2.2 %collective-permute-done.5.refs_3_ = s32[56,256]{1,0:T(8,128)S(1)} collective-permute-done((s32[56,256]{1,0:T(8,128)S(1)}, s32[56,256]{1,0:T(8,128)S(1)}, u32[]{:S(2)}, u32[]{:S(2)}) %collective-permute-start.5) | collective-permute-done | bytes 57376 | tf_op jit(solution)/shard_map/ppermute | solution.py:784
  92.0 2.5 %shard_map.93 = (f32[2,512,512]{2,1,0:T(8,128)S(1)}, s32[528,256]{1,0:T(8,128)S(1)}, s32[528,256]{1,0:T(8,128)S(1)}) custom-call(f32[2,512,512]{2,1,0:T(8,128)} %get-tuple-element.23.refs_0_, s32[264,512]{1,0:T(8,128)S(1)} %collective-permute-done.3.refs_1_, s32[264,512]{1,0:T(8,128)S(1)} %collective-permute-done.4.refs_2_, ...), custom_call_target="tpu_custom_call" | custom-call | flops 67108864 | bytes 8388608 | tf_op jit(solution)/shard_map/pallas_call | solution.py:764
  94.6 1.3 copy-done.13
  95.9 1.3 collective-permute-start.6
  97.2 1.3 collective-permute-start.7
  98.5 3.1 %collective-permute-start.9 = (s32[56,256]{1,0:T(8,128)S(1)}, s32[56,256]{1,0:T(8,128)S(1)}, u32[]{:S(2)}, u32[]{:S(2)}) collective-permute-start(s32[56,256]{1,0:T(8,128)S(1)} %shard_map.92.refs_2_), channel_id=1, source_target_pairs={{0,24},{8,16},{16,8},{24,0},{1,25},{9,17},{17,9},{25,1},{2,26},{10... | collective-permute-start | bytes 172040 | tf_op jit(solution)/shard_map/ppermute | solution.py:784
  102.1 2.6 %collective-permute-done.9.refs_5_ = s32[56,256]{1,0:T(8,128)S(1)} collective-permute-done((s32[56,256]{1,0:T(8,128)S(1)}, s32[56,256]{1,0:T(8,128)S(1)}, u32[]{:S(2)}, u32[]{:S(2)}) %collective-permute-start.9) | collective-permute-done | bytes 57376 | tf_op jit(solution)/shard_map/ppermute | solution.py:784
  104.7 3.4 %collective-permute-done.8.refs_4_ = s32[56,256]{1,0:T(8,128)S(1)} collective-permute-done((s32[56,256]{1,0:T(8,128)S(1)}, s32[56,256]{1,0:T(8,128)S(1)}, u32[]{:S(2)}, u32[]{:S(2)}) %collective-permute-start.8) | collective-permute-done | bytes 57376 | tf_op jit(solution)/shard_map/ppermute | solution.py:784
  108.8 11.7 %all_to_all.31.refs_7_ = s32[8,40,256]{2,1,0:T(8,128)S(1)} all-to-all(s32[8,40,256]{2,1,0:T(8,128)S(1)} %shard_map.94), channel_id=1, replica_groups=mesh['row'=4,'col'=8] {'col'}, dimensions={0} | all-to-all | bytes 655360 | tf_op jit(solution)/shard_map/all_to_all | solution.py:797
  120.5 17.8 %shard_map.95 = (f32[2,256,256]{2,1,0:T(8,128)S(1)}, f32[2,256,512]{2,1,0:T(8,128)S(1)}, s32[264,512]{1,0:T(8,128)}, s32[8,56,256]{2,1,0:T(8,128)S(1)}, f32[2,256,256]{2,1,0:T(8,128)S(1)}) custom-call(s32[256]{0:T(256)S(1)} %bitcast.10, s32[2]{0:T(128)S(1)} %pad_add_fusion.refs_1_.refs_0_, f32[2,512,512]{2,1,0:T(8,128)} %copy-done.18, ...), custom_call_target="tpu_custom_call" | custom-call | flops 6442450944 | bytes 8388608 | tf_op jit(solution)/shard_map/pallas_call | solution.py:764
  138.3 1.3 collective-permute-start.10
  139.7 11.4 %all_to_all.32.refs_0_ = s32[8,56,256]{2,1,0:T(8,128)S(1)} all-to-all(s32[8,56,256]{2,1,0:T(8,128)S(1)} %get-tuple-element.37), channel_id=1, replica_groups=mesh['row'=4,'col'=8] {'col'}, dimensions={0} | all-to-all | bytes 917504 | tf_op jit(solution)/shard_map/all_to_all | solution.py:790
  153.1 2.7 %collective-permute-start.12 = (s32[56,256]{1,0:T(8,128)S(1)}, s32[56,256]{1,0:T(8,128)S(1)}, u32[]{:S(2)}, u32[]{:S(2)}) collective-permute-start(s32[56,256]{1,0:T(8,128)S(1)} %shard_map.99.refs_2_), channel_id=1, source_target_pairs={{0,8},{8,0},{16,24},{24,16},{1,9},{9,1},{17,25},{25,17},{2,10},{10... | collective-permute-start | bytes 172040 | tf_op jit(solution)/shard_map/ppermute | solution.py:784
  155.7 2.1 %collective-permute-done.14.refs_5_ = s32[56,256]{1,0:T(8,128)S(1)} collective-permute-done((s32[56,256]{1,0:T(8,128)S(1)}, s32[56,256]{1,0:T(8,128)S(1)}, u32[]{:S(2)}, u32[]{:S(2)}) %collective-permute-start.14) | collective-permute-done | bytes 57376 | tf_op jit(solution)/shard_map/ppermute | solution.py:784
  158.9 1.4 shard_map.100
  160.3 3.4 %all-to-all-start.5 = ((s32[8,40,256]{2,1,0:T(8,128)}), s32[8,40,256]{2,1,0:T(8,128)S(1)}, u32[]{:S(2)}, u32[]{:S(2)}) async-start(s32[8,40,256]{2,1,0:T(8,128)} %shard_map.100), calls=%async_computation.5 | async-start | bytes 655360 | tf_op jit(solution)/shard_map/all_to_all | solution.py:797
  165.7 2.3 %collective-permute-start.11 = (s32[264,256]{1,0:T(8,128)}, s32[264,256]{1,0:T(8,128)S(1)}, u32[]{:S(2)}, u32[]{:S(2)}) collective-permute-start(s32[264,256]{1,0:T(8,128)} %get-tuple-element.35), channel_id=1, source_target_pairs={{0,1},{1,2},{2,3},{3,4},{4,5},{5,6},{6,7},{8,9},{9,10},{10,11},{11... | collective-permute-start | bytes 811016 | tf_op jit(solution)/shard_map/ppermute | solution.py:780
  169.1 4.1 %shard_map.97.refs_4_ = f32[256,256]{1,0:T(8,128)S(1)} custom-call(s32[256]{0:T(256)S(1)} %bitcast.11, s32[2]{0:T(128)S(1)} %pad_add_fusion.refs_1_.refs_0_, f32[2,256,256]{2,1,0:T(8,128)S(1)} %copy-done.6), custom_call_target="tpu_custom_call" | custom-call | flops 8589934592 | bytes 8388608 | tf_op jit(solution)/shard_map/pallas_call | solution.py:764
  (70 shorter events, 18.9 us)
Async XLA Ops:
  1.7 13.5 %copy-start.1 = (bf16[4,256,256]{2,1,0:T(8,128)(2,1)S(1)}, bf16[4,256,256]{2,1,0:T(8,128)(2,1)}, u32[]{:S(2)}) copy-start(bf16[4,256,256]{2,1,0:T(8,128)(2,1)} %refs_2_.7) | copy-start | bytes 1572868
  1.9 13.2 %copy-start.12 = (s32[128,2]{0,1:T(2,128)S(1)}, s32[128,2]{0,1:T(2,128)}, u32[]{:S(2)}) copy-start(s32[128,2]{0,1:T(2,128)} %param.10) | copy-start | bytes 3076
  5.1 20.6 %all-to-all-start = ((bf16[8,256,256]{2,1,0:T(8,128)(2,1)}), bf16[8,256,256]{2,1,0:T(8,128)(2,1)S(1)}, u32[]{:S(2)}, u32[]{:S(2)}) async-start(bf16[8,256,256]{2,1,0:T(8,128)(2,1)} %shard_map.89), calls=%async_computation | async-start | bytes 2097152 | tf_op jit(solution)/shard_map/all_to_all | solution.py:830
  10.3 23.2 %copy-start.4 = (f32[2,256,256]{2,1,0:T(8,128)S(1)}, f32[2,256,256]{2,1,0:T(8,128)}, u32[]{:S(2)}) copy-start(f32[2,256,256]{2,1,0:T(8,128)} %refs_1_.1) | copy-start | bytes 1572868
  10.3 3.6 %collective-permute-start = (s32[264,256]{1,0:T(8,128)S(1)}, s32[264,256]{1,0:T(8,128)S(1)}, u32[]{:S(2)}, u32[]{:S(2)}) collective-permute-start(s32[264,256]{1,0:T(8,128)S(1)} %shard_map.86.refs_3_), channel_id=1, source_target_pairs={{1,0},{2,1},{3,2},{4,3},{5,4},{6,5},{7,6},{9,8},{10,9},{11,10},{12... | collective-permute-start | bytes 811016 | tf_op jit(solution)/shard_map/ppermute | solution.py:780
  11.7 27.5 %collective-permute-start.1 = (s32[264,256]{1,0:T(8,128)S(1)}, s32[264,256]{1,0:T(8,128)S(1)}, u32[]{:S(2)}, u32[]{:S(2)}) collective-permute-start(s32[264,256]{1,0:T(8,128)S(1)} %shard_map.86.refs_3_), channel_id=1, source_target_pairs={{8,0},{16,8},{24,16},{9,1},{17,9},{25,17},{10,2},{18,10},{26,18},{... | collective-permute-start | bytes 811016 | tf_op jit(solution)/shard_map/ppermute | solution.py:780
  13.8 25.4 %collective-permute-start.2 = (s32[264,256]{1,0:T(8,128)S(1)}, s32[264,256]{1,0:T(8,128)S(1)}, u32[]{:S(2)}, u32[]{:S(2)}) collective-permute-start(s32[264,256]{1,0:T(8,128)S(1)} %collective-permute-done.refs_3_), channel_id=1, source_target_pairs={{8,0},{16,8},{24,16},{9,1},{17,9},{25,17},{10,2},{18,10},{26,18},{... | collective-permute-start | bytes 811016 | tf_op jit(solution)/shard_map/ppermute | solution.py:780
  26.6 23.9 %all-to-all-start.1 = ((bf16[8,256,256]{2,1,0:T(8,128)(2,1)}), bf16[8,256,256]{2,1,0:T(8,128)(2,1)}, u32[]{:S(2)}, u32[]{:S(2)}) async-start(bf16[8,256,256]{2,1,0:T(8,128)(2,1)} %shard_map.90), calls=%async_computation.1 | async-start | bytes 2097152 | tf_op jit(solution)/shard_map/all_to_all | solution.py:830
  33.5 5.8 %copy-start.3 = (f32[2,256,256]{2,1,0:T(8,128)S(1)}, f32[2,256,256]{2,1,0:T(8,128)}, u32[]{:S(2)}) copy-start(f32[2,256,256]{2,1,0:T(8,128)} %refs_2_.4) | copy-start | bytes 1572868
  33.5 5.8 %copy-start.14 = (bf16[2,2,256,256]{3,2,1,0:T(8,128)(2,1)S(1)}, bf16[2,2,256,256]{3,2,1,0:T(8,128)(2,1)}, u32[]{:S(2)}) copy-start(bf16[2,2,256,256]{3,2,1,0:T(8,128)(2,1)} %constant.14.clone.refs_7_.refs_9_) | copy-start | bytes 1572868
  33.5 5.8 %copy-start.16 = (f32[2,136,128]{2,1,0:T(8,128)S(1)}, f32[2,136,128]{2,1,0:T(8,128)}, u32[]{:S(2)}) copy-start(f32[2,136,128]{2,1,0:T(8,128)} %constant.15.clone.refs_8_.refs_10_) | copy-start | bytes 417796
  39.2 11.3 %copy-start.15 = (bf16[2,256,256]{2,1,0:T(8,128)(2,1)S(1)}, bf16[2,256,256]{2,1,0:T(8,128)(2,1)}, u32[]{:S(2)}) copy-start(bf16[2,256,256]{2,1,0:T(8,128)(2,1)} %constant.16.clone.refs_11_) | copy-start | bytes 786436
  48.5 1.4 copy-start.18
  67.0 25.0 %collective-permute-start.3 = (s32[264,512]{1,0:T(8,128)S(1)}, s32[264,512]{1,0:T(8,128)S(1)}, u32[]{:S(2)}, u32[]{:S(2)}) collective-permute-start(s32[264,512]{1,0:T(8,128)S(1)} %get-tuple-element.24), channel_id=1, source_target_pairs={{0,8},{8,16},{16,24},{1,9},{9,17},{17,25},{2,10},{10,18},{18,26},{... | collective-permute-start | bytes 1622024 | tf_op jit(solution)/shard_map/ppermute | solution.py:780
  68.3 23.7 %collective-permute-start.4 = (s32[264,512]{1,0:T(8,128)S(1)}, s32[264,512]{1,0:T(8,128)S(1)}, u32[]{:S(2)}, u32[]{:S(2)}) collective-permute-start(s32[264,512]{1,0:T(8,128)S(1)} %get-tuple-element.25), channel_id=1, source_target_pairs={{8,0},{16,8},{24,16},{9,1},{17,9},{25,17},{10,2},{18,10},{26,18},{... | collective-permute-start | bytes 1622024 | tf_op jit(solution)/shard_map/ppermute | solution.py:780
  87.1 4.9 %collective-permute-start.5 = (s32[56,256]{1,0:T(8,128)S(1)}, s32[56,256]{1,0:T(8,128)S(1)}, u32[]{:S(2)}, u32[]{:S(2)}) collective-permute-start(s32[56,256]{1,0:T(8,128)S(1)} %shard_map.92.refs_2_), channel_id=1, source_target_pairs={{0,8},{8,0},{16,24},{24,16},{1,9},{9,1},{17,25},{25,17},{2,10},{10... | collective-permute-start | bytes 172040 | tf_op jit(solution)/shard_map/ppermute | solution.py:784
  92.0 28.5 %copy-start.17 = (f32[2,136,128]{2,1,0:T(8,128)S(1)}, f32[2,136,128]{2,1,0:T(8,128)}, u32[]{:S(2)}) copy-start(f32[2,136,128]{2,1,0:T(8,128)} %constant.15.clone.refs_8_.refs_10_) | copy-start | bytes 417796
  94.6 1.3 copy-start.13
  95.9 24.6 %collective-permute-start.6 = (s32[528,256]{1,0:T(8,128)S(1)}, s32[528,256]{1,0:T(8,128)S(1)}, u32[]{:S(2)}, u32[]{:S(2)}) collective-permute-start(s32[528,256]{1,0:T(8,128)S(1)} %get-tuple-element.28), channel_id=1, source_target_pairs={{0,1},{1,2},{2,3},{3,4},{4,5},{5,6},{6,7},{8,9},{9,10},{10,11},{11... | collective-permute-start | bytes 1622024 | tf_op jit(solution)/shard_map/ppermute | solution.py:780
  97.2 23.3 %collective-permute-start.7 = (s32[528,256]{1,0:T(8,128)S(1)}, s32[528,256]{1,0:T(8,128)S(1)}, u32[]{:S(2)}, u32[]{:S(2)}) collective-permute-start(s32[528,256]{1,0:T(8,128)S(1)} %get-tuple-element.29), channel_id=1, source_target_pairs={{1,0},{2,1},{3,2},{4,3},{5,4},{6,5},{7,6},{9,8},{10,9},{11,10},{12... | collective-permute-start | bytes 1622024 | tf_op jit(solution)/shard_map/ppermute | solution.py:780
  98.5 6.1 %collective-permute-start.9 = (s32[56,256]{1,0:T(8,128)S(1)}, s32[56,256]{1,0:T(8,128)S(1)}, u32[]{:S(2)}, u32[]{:S(2)}) collective-permute-start(s32[56,256]{1,0:T(8,128)S(1)} %shard_map.92.refs_2_), channel_id=1, source_target_pairs={{0,24},{8,16},{16,8},{24,0},{1,25},{9,17},{17,9},{25,1},{2,26},{10... | collective-permute-start | bytes 172040 | tf_op jit(solution)/shard_map/ppermute | solution.py:784
  101.6 6.5 %collective-permute-start.8 = (s32[56,256]{1,0:T(8,128)S(1)}, s32[56,256]{1,0:T(8,128)S(1)}, u32[]{:S(2)}, u32[]{:S(2)}) collective-permute-start(s32[56,256]{1,0:T(8,128)S(1)} %shard_map.92.refs_2_), channel_id=1, source_target_pairs={{0,16},{8,24},{16,0},{24,8},{1,17},{9,25},{17,1},{25,9},{2,18},{10... | collective-permute-start | bytes 172040 | tf_op jit(solution)/shard_map/ppermute | solution.py:784
  138.3 13.0 %copy-start.7 = (f32[2,256,256]{2,1,0:T(8,128)}, f32[2,256,256]{2,1,0:T(8,128)S(1)}, u32[]{:S(2)}) copy-start(f32[2,256,256]{2,1,0:T(8,128)S(1)} %get-tuple-element.31.refs_0_) | copy-start | bytes 1572868
  138.3 20.6 %copy-start.5 = (f32[2,256,256]{2,1,0:T(8,128)}, f32[2,256,256]{2,1,0:T(8,128)S(1)}, u32[]{:S(2)}) copy-start(f32[2,256,256]{2,1,0:T(8,128)S(1)} %get-tuple-element.36.refs_2_.refs_1_) | copy-start | bytes 1572868
  138.3 25.4 %collective-permute-start.10 = (s32[264,512]{1,0:T(8,128)}, s32[264,512]{1,0:T(8,128)S(1)}, u32[]{:S(2)}, u32[]{:S(2)}) collective-permute-start(s32[264,512]{1,0:T(8,128)} %get-tuple-element.33), channel_id=1, source_target_pairs={{0,8},{8,16},{16,24},{1,9},{9,17},{17,25},{2,10},{10,18},{18,26},{... | collective-permute-start | bytes 1622024 | tf_op jit(solution)/shard_map/ppermute | solution.py:780
  151.3 6.5 %collective-permute-start.14 = (s32[56,256]{1,0:T(8,128)S(1)}, s32[56,256]{1,0:T(8,128)S(1)}, u32[]{:S(2)}, u32[]{:S(2)}) collective-permute-start(s32[56,256]{1,0:T(8,128)S(1)} %shard_map.99.refs_2_), channel_id=1, source_target_pairs={{0,24},{8,16},{16,8},{24,0},{1,25},{9,17},{17,9},{25,1},{2,26},{10... | collective-permute-start | bytes 172040 | tf_op jit(solution)/shard_map/ppermute | solution.py:784
  152.1 6.9 %collective-permute-start.13 = (s32[56,256]{1,0:T(8,128)S(1)}, s32[56,256]{1,0:T(8,128)S(1)}, u32[]{:S(2)}, u32[]{:S(2)}) collective-permute-start(s32[56,256]{1,0:T(8,128)S(1)} %shard_map.99.refs_2_), channel_id=1, source_target_pairs={{0,16},{8,24},{16,0},{24,8},{1,17},{9,25},{17,1},{25,9},{2,18},{10... | collective-permute-start | bytes 172040 | tf_op jit(solution)/shard_map/ppermute | solution.py:784
  153.1 5.8 %collective-permute-start.12 = (s32[56,256]{1,0:T(8,128)S(1)}, s32[56,256]{1,0:T(8,128)S(1)}, u32[]{:S(2)}, u32[]{:S(2)}) collective-permute-start(s32[56,256]{1,0:T(8,128)S(1)} %shard_map.99.refs_2_), channel_id=1, source_target_pairs={{0,8},{8,0},{16,24},{24,16},{1,9},{9,1},{17,25},{25,17},{2,10},{10... | collective-permute-start | bytes 172040 | tf_op jit(solution)/shard_map/ppermute | solution.py:784
  160.3 12.9 %all-to-all-start.5 = ((s32[8,40,256]{2,1,0:T(8,128)}), s32[8,40,256]{2,1,0:T(8,128)S(1)}, u32[]{:S(2)}, u32[]{:S(2)}) async-start(s32[8,40,256]{2,1,0:T(8,128)} %shard_map.100), calls=%async_computation.5 | async-start | bytes 655360 | tf_op jit(solution)/shard_map/all_to_all | solution.py:797
  165.7 8.4 %collective-permute-start.11 = (s32[264,256]{1,0:T(8,128)}, s32[264,256]{1,0:T(8,128)S(1)}, u32[]{:S(2)}, u32[]{:S(2)}) collective-permute-start(s32[264,256]{1,0:T(8,128)} %get-tuple-element.35), channel_id=1, source_target_pairs={{0,1},{1,2},{2,3},{3,4},{4,5},{5,6},{6,7},{8,9},{9,10},{10,11},{11... | collective-permute-start | bytes 811016 | tf_op jit(solution)/shard_map/ppermute | solution.py:780
  169.1 5.0 %copy-start.8 = (f32[2,256,256]{2,1,0:T(8,128)S(1)}, f32[2,256,256]{2,1,0:T(8,128)}, u32[]{:S(2)}) copy-start(f32[2,256,256]{2,1,0:T(8,128)} %copy-done.7) | copy-start | bytes 1572868
  169.1 5.0 %copy-start.10 = (f32[2,256,256]{2,1,0:T(8,128)S(1)}, f32[2,256,256]{2,1,0:T(8,128)}, u32[]{:S(2)}) copy-start(f32[2,256,256]{2,1,0:T(8,128)} %copy-done.9) | copy-start | bytes 1572868
  (9 other events, 8.2 us)

commit v5 on v3

--- a/solution.py
+++ b/solution.py
@@ -23,6 +23,7 @@
 SMEM = pl.BlockSpec(memory_space=pltpu.SMEM)
 HBM = pl.BlockSpec(memory_space=pltpu.HBM)
 LOAD = object()
+FREE = pl.BlockSpec(memory_space=pl.ANY)
 f32 = jnp.float32
 bf16 = jnp.bfloat16
 
@@ -390,7 +391,7 @@
         live = still
 
 
-def outgoing_kernel(dims, pos_ref, me_ref, amp_ref, after_ref, out_ref, sems):
+def outgoing_kernel(dims, pos_ref, me_ref, amp_ref, after_ref, also_ref, out_ref, sems):
     tile_rows, tile_cols, pat_count, col_count, capacity = dims
     first = (me_ref[0] * col_count + me_ref[1]) * pat_count
     total = pos_ref.shape[0] // 2
@@ -432,7 +433,7 @@
         return carry
 
     lax.fori_loop(0, total, visit, 0)
-    out_ref[...] = sums_ref[tile_rows : (span + 1) * tile_rows, tile_cols : (span + 1) * tile_cols]
+    pltpu.sync_copy(sums_ref.at[pl.ds(tile_rows, span * tile_rows), pl.ds(tile_cols, span * tile_cols)], out_ref)
 
 
 def encode_kernel(obj_ref, out_ref):
@@ -467,7 +468,8 @@
     return parts[0]
 
 
-def sums_kernel(rows, parts_ref, out_ref):
+def sums_kernel(rows, parts_ref, *refs):
+    out_ref = refs[-1]
     for col in range(0, out_ref.shape[1], LANES):
         cols = pl.ds(col, LANES)
         total = added([decode_sums(parts_ref.at[k], cols, rows) for k in range(parts_ref.shape[0])])
@@ -733,13 +735,20 @@
             ins[k] = kept[n]
         kernel(*ins, *given)
 
+    fixed_outs = [
+        pltpu.HBM(out.shape, out.dtype) if spec is HBM else out
+        for out, spec in zip(outs if several else (outs,), out_specs if several else (out_specs,))
+    ]
+    stay = [spec is LOAD or spec is HBM for spec in in_specs]
+
     def called(*args):
+        args = [pltpu.with_memory_space_constraint(arg, pltpu.HBM) if kept else arg for arg, kept in zip(args, stay)]
         own = [pltpu.VMEM(args[k].shape, args[k].dtype) for k in loaded]
         if loaded:
             own.append(pltpu.SemaphoreType.DMA((len(loaded),)))
         return pl.pallas_call(
             body,
-            out_shape=outs,
+            out_shape=tuple(fixed_outs) if several else fixed_outs[0],
             out_specs=out_specs,
             in_specs=[HBM if spec is LOAD else spec for spec in in_specs],
             scratch_shapes=list(scratch) + own,
@@ -770,17 +779,17 @@
     return lax.ppermute(value, axis, [(k, k ^ mask) for k in range(lax.axis_size(axis))])
 
 
-def probe_update(me, probe, numer, kind):
+def probe_update(me, probe, numer, kind, *after):
     cols, order = lax.axis_size("col"), probe.shape[1]
     rows = order // cols
     parts = lax.all_to_all(numer, "col", split_axis=0, concat_axis=0, tiled=True)
-    total = call(functools.partial(sums_kernel, rows), shape((sums_rows(rows), order), jnp.int32), VMEM, [VMEM], [], 1 << 26)(parts)
+    total = call(functools.partial(sums_kernel, rows), shape((sums_rows(rows), order), jnp.int32), VMEM, [VMEM] + [FREE] * len(after), [], 1 << 26)(parts, *after)
     totals = [total] + [swapped(total, "row", mask) for mask in range(1, lax.axis_size("row"))]
     fresh = call(
         functools.partial(update_kernel, rows), shape((cols, rows + SUBLANES, order), jnp.int32), VMEM,
         [SMEM, kind] + [VMEM] * len(totals), [], 1 << 26,
     )(me, probe, *totals)
-    return fresh, lax.all_to_all(fresh, "col", split_axis=0, concat_axis=0, tiled=True)
+    return total, lax.all_to_all(fresh, "col", split_axis=0, concat_axis=0, tiled=True)
 
 
 def local(obj, probe, amplitudes, positions):
@@ -808,14 +817,14 @@
     diag = passed_along(right, "row", -1)
 
     outgoing = call(
-        functools.partial(outgoing_kernel, dims), shape((col_count * SEND, order, order), bf16), HBM, [SMEM, SMEM, HBM, HBM],
+        functools.partial(outgoing_kernel, dims), shape((col_count * SEND, order, order), bf16), HBM, [SMEM, SMEM, HBM, FREE, FREE],
         [pltpu.SemaphoreType.DMA((pat_count,))], 1 << 20,
-    )(pos, me, amplitudes, right)
+    )(pos, me, amplitudes, right, below)
     incoming = lax.all_to_all(outgoing, "col", split_axis=0, concat_axis=0, tiled=True)
 
     def weights(probe_now, span, kind):
         return call(
-            functools.partial(weights_kernel, dims, span), shape((span * tile_rows, span * tile_cols)), VMEM, [SMEM, SMEM, kind],
+            functools.partial(weights_kernel, dims, span), shape((span * tile_rows, span * tile_cols)), HBM, [SMEM, SMEM, kind],
             [pltpu.VMEM(((span + 2) * tile_rows, (span + 2) * tile_cols), f32), pltpu.VMEM((order, order), f32)], 8 << 30,
         )(pos, me, probe_now)
 
@@ -842,10 +851,10 @@
 
     from_above = passed_along(bottom, "row", 1)
     from_below = passed_along(top, "row", -1)
-    fresh, chunks = probe_update(me, probe, numer, LOAD)
+    total, chunks = probe_update(me, probe, numer, LOAD)
     sums, to_left, to_right = call(
-        functools.partial(rows_sum_kernel, dims), (shape(wide), coded_col, coded_col), (VMEM,) * 3, [LOAD, VMEM, VMEM, HBM], [], 1 << 26,
-    )(share, from_above, from_below, fresh)
+        functools.partial(rows_sum_kernel, dims), (shape(wide), coded_col, coded_col), (VMEM,) * 3, [LOAD, VMEM, VMEM, FREE], [], 1 << 26,
+    )(share, from_above, from_below, total)
     from_left = passed_along(to_right, "col", 1)
     from_right = passed_along(to_left, "col", -1)
 
@@ -862,10 +871,10 @@
     from_above = passed_along(to_below, "row", 1)
     from_diag = passed_both(to_diag, 1, 1)
     weights_new = weights(probe_now, 1, VMEM)
-    new_object = call(functools.partial(object_kernel, dims), shape(tile), VMEM, [LOAD] + [VMEM] * 4 + [LOAD, VMEM], [], 1 << 26)(
+    new_object = call(functools.partial(object_kernel, dims), shape(tile), VMEM, [LOAD] + [VMEM] * 4 + [LOAD, LOAD], [], 1 << 26)(
         current, own, from_left, from_above, from_diag, weights_old, weights_new
     )
-    _, chunks = probe_update(me, probe_now, numer, VMEM)
+    _, chunks = probe_update(me, probe_now, numer, VMEM, weights_new)
     new_probe = call(probe_kernel, shape(window), VMEM, [VMEM], [], 1 << 26)(chunks)
     return new_object, new_probe
 

time: 173 us -> 187 us (1.081)
  waiting for transfers between devices: 14.9 us -> 37.5 us
  Pallas kernels: 59.8 us -> 81.8 us
  blocking collectives: 40.5 us -> 24.1 us
  local copies, waits for them, and re-layouts: 16.5 us -> 3.04 us
    pallas_call x14, Pallas kernels: 59.8 us -> 81.8 us  [called(): pl.pallas_call(body, out_shape=tuple(fixed_outs) if several else fixed_ou...]
    unnamed x44 -> x8, local copies, waits for them, and re-layouts: 16.5 us -> 3.04 us
    all_to_all x2 -> x1, blocking collectives: 23.2 us -> 12.9 us  [probe_update(): lax.all_to_all(numer, 'col', split_axis=0, concat_axis=0, tiled=True)]
    all_to_all x1, waiting for transfers between devices: 0.01 us -> 6.09 us  [local(): lax.all_to_all(outgoing, 'col', split_axis=0, concat_axis=0, tiled=True)]
    all_to_all x1, blocking collectives: 17.3 us -> 11.3 us  [probe_update(): lax.all_to_all(fresh, 'col', split_axis=0, concat_axis=0, tiled=True)]
    ppermute x1, waiting for transfers between devices: 0.01 us -> 5.79 us  [passed_both(): return lax.ppermute(value, ('row', 'col'), pairs)]
    all_to_all x1, starting transfers between devices: 8.91 us -> 3.89 us  [local(): lax.all_to_all(outgoing, 'col', split_axis=0, concat_axis=0, tiled=True)]
    ppermute x9, waiting for transfers between devices: 8.91 us -> 13.6 us  [passed_along(): lax.ppermute(value, axis, [(source, source + steps) for source in range(l...]
  transfers between devices with their start and end apart: 18 -> 19, of which waited for: 6 -> 10; matrix products, arithmetic and copies ran while one was open for 0% -> 0% of each run, Pallas kernels for 14% -> 14%
where the time goes in v5:
time: 187 us; the launch traced here: 186 us
  Pallas kernels  81.8 us (44%)
  starting transfers between devices  38.3 us (20%)
  waiting for transfers between devices  37.5 us (20%)
  blocking collectives  24.1 us (13%)
  local copies, waits for them, and re-layouts  3.04 us (2%)
    pallas_call x14, Pallas kernels, called(): pl.pallas_call(body, out_shape=tuple(fixed_outs) if several else fixed_ou...  81.8 us
    ppermute x9, starting transfers between devices, passed_along(): lax.ppermute(value, axis, [(source, source + steps) for source in range(l...  15.5 us
    ppermute x9, waiting for transfers between devices, passed_along(): lax.ppermute(value, axis, [(source, source + steps) for source in range(l...  13.6 us
    all_to_all x1, blocking collectives, probe_update(): lax.all_to_all(numer, 'col', split_axis=0, concat_axis=0, tiled=True)  12.9 us
    all_to_all x1, blocking collectives, probe_update(): lax.all_to_all(fresh, 'col', split_axis=0, concat_axis=0, tiled=True)  11.3 us
    ppermute x6, starting transfers between devices, swapped(): lax.ppermute(value, axis, [(k, k ^ mask) for k in range(lax.axis_size(axi...  8.9 us
    ppermute x6, waiting for transfers between devices, swapped(): lax.ppermute(value, axis, [(k, k ^ mask) for k in range(lax.axis_size(axi...  7.9 us
    all_to_all x1, waiting for transfers between devices, local(): lax.all_to_all(outgoing, 'col', split_axis=0, concat_axis=0, tiled=True)  6.09 us
  transfers between devices with their start and end apart: 19, of which 10 were waited for; matrix products, arithmetic and copies ran while one was open for 0% of the time, Pallas kernels for 14%

profile of v5, /device:TPU:0, one launch (start us, length us, event | category | flops | bytes accessed | tf_op | source)
XLA Modules:
  0.0 185.8 jit_solution(16070822254056417193)
XLA Ops:
  4.5 8.7 %collective-permute-done.1.refs_4_ = s32[264,256]{1,0:T(8,128)S(1)} collective-permute-done((s32[264,256]{1,0:T(8,128)S(1)}, s32[264,256]{1,0:T(8,128)S(1)}, u32[]{:S(2)}, u32[]{:S(2)}) %collective-permute-start.1) | collective-permute-done | bytes 270368 | tf_op jit(solution)/shard_map/ppermute | solution.py:765
  13.9 17.6 %shard_map.89 = bf16[16,256,256]{2,1,0:T(8,128)(2,1)} custom-call(s32[256]{0:T(256)S(1)} %bitcast.5, s32[2]{0:T(128)S(1)} %pad_add_fusion.refs_1_.refs_0_, bf16[4,256,256]{2,1,0:T(8,128)(2,1)} %refs_2_.5, s32[264,256]{1,0:T(8,128)S(1)} %collective-permute-done.refs_3_, s32[264,256]{1,0:T(8,128)S(1)} %collective-permute-done.1.refs_4_), custom_call_target="tpu_custom_call" | custom-call | flops 1048576 | bytes 8388608 | tf_op jit(solution)/shard_map/pallas_call | solution.py:749
  31.5 3.9 %all-to-all-start = ((bf16[16,256,256]{2,1,0:T(8,128)(2,1)}), bf16[16,256,256]{2,1,0:T(8,128)(2,1)S(1)}, u32[]{:S(2)}, u32[]{:S(2)}) async-start(bf16[16,256,256]{2,1,0:T(8,128)(2,1)} %shard_map.89), calls=%async_computation | async-start | bytes 4194304 | tf_op jit(solution)/shard_map/all_to_all | solution.py:823
  36.7 7.7 %shard_map.88.refs_5_.refs_6_ = f32[512,512]{1,0:T(8,128)} custom-call(s32[256]{0:T(256)S(1)} %bitcast.6, s32[2]{0:T(128)S(1)} %pad_add_fusion.refs_1_.refs_0_, f32[2,256,256]{2,1,0:T(8,128)} %refs_1_.1), custom_call_target="tpu_custom_call" | custom-call | flops 8589934592 | bytes 8388608 | tf_op jit(solution)/shard_map/pallas_call | solution.py:749
  44.4 1.8 collective-permute-done.2.refs_5_
  46.2 9.8 %shard_map.87 = (f32[8,2,256,256]{3,2,1,0:T(8,128)}, f32[256,256]{1,0:T(8,128)S(1)}, f32[2,512,512]{2,1,0:T(8,128)}) custom-call(s32[256]{0:T(256)S(1)} %bitcast.7, s32[2]{0:T(128)S(1)} %pad_add_fusion.refs_1_.refs_0_, f32[2,256,256]{2,1,0:T(8,128)} %refs_2_.3, s32[264,256]{1,0:T(8,128)S(1)} %collective-permute-done.refs_3_, ...), custom_call_target="tpu_custom_call" | custom-call | flops 3221225472 | bytes 8388608 | tf_op jit(solution)/shard_map/pallas_call | solution.py:749
  56.0 6.1 %all-to-all-done.refs_7_ = bf16[16,256,256]{2,1,0:T(8,128)(2,1)S(1)} async-done(((bf16[16,256,256]{2,1,0:T(8,128)(2,1)}), bf16[16,256,256]{2,1,0:T(8,128)(2,1)S(1)}, u32[]{:S(2)}, u32[]{:S(2)}) %all-to-all-start) | async-done | bytes 2097184 | tf_op jit(solution)/shard_map/all_to_all | solution.py:823
  62.1 1.4 copy-done.3
  63.5 13.9 %shard_map.90 = (f32[2,512,512]{2,1,0:T(8,128)}, s32[264,512]{1,0:T(8,128)S(1)}, s32[264,512]{1,0:T(8,128)S(1)}, s32[8,56,256]{2,1,0:T(8,128)S(1)}, bf16[8,256,256]{2,1,0:T(8,128)(2,1)}) custom-call(s32[256]{0:T(256)S(1)} %bitcast.8, s32[2]{0:T(128)S(1)} %pad_add_fusion.refs_1_.refs_0_, f32[2,512,512]{2,1,0:T(8,128)} %get-tuple-element.20.refs_2_, ...), custom_call_target="tpu_custom_call" | custom-call | flops 3221225472 | bytes 8388608 | tf_op jit(solution)/shard_map/pallas_call | solution.py:749
  80.0 12.9 %all_to_all.25.refs_0_ = s32[8,56,256]{2,1,0:T(8,128)S(1)} all-to-all(s32[8,56,256]{2,1,0:T(8,128)S(1)} %get-tuple-element.26), channel_id=1, replica_groups=mesh['row'=4,'col'=8] {'col'}, dimensions={0} | all-to-all | bytes 917504 | tf_op jit(solution)/shard_map/all_to_all | solution.py:785
  93.1 2.6 %shard_map.92 = (f32[2,512,512]{2,1,0:T(8,128)S(1)}, s32[528,256]{1,0:T(8,128)S(1)}, s32[528,256]{1,0:T(8,128)S(1)}) custom-call(f32[2,512,512]{2,1,0:T(8,128)} %get-tuple-element.23.refs_0_, s32[264,512]{1,0:T(8,128)S(1)} %collective-permute-done.3.refs_1_, s32[264,512]{1,0:T(8,128)S(1)} %collective-permute-done.4.refs_2_, ...), custom_call_target="tpu_custom_call" | custom-call | flops 67108864 | bytes 8388608 | tf_op jit(solution)/shard_map/pallas_call | solution.py:749
  95.6 1.5 collective-permute-start.5
  98.4 2.5 %collective-permute-start.9 = (s32[56,256]{1,0:T(8,128)S(1)}, s32[56,256]{1,0:T(8,128)S(1)}, u32[]{:S(2)}, u32[]{:S(2)}) collective-permute-start(s32[56,256]{1,0:T(8,128)S(1)} %shard_map.91.refs_3_.refs_2_), channel_id=1, source_target_pairs={{0,24},{8,16},{16,8},{24,0},{1,25},{9,17},{17,9},{25,1},{2,26},{10... | collective-permute-start | bytes 172040 | tf_op jit(solution)/shard_map/ppermute | solution.py:779
  100.9 1.7 collective-permute-start.8
  102.9 1.6 collective-permute-done.9.refs_5_
  104.5 4.1 %collective-permute-done.8.refs_4_ = s32[56,256]{1,0:T(8,128)S(1)} collective-permute-done((s32[56,256]{1,0:T(8,128)S(1)}, s32[56,256]{1,0:T(8,128)S(1)}, u32[]{:S(2)}, u32[]{:S(2)}) %collective-permute-start.8) | collective-permute-done | bytes 57376 | tf_op jit(solution)/shard_map/ppermute | solution.py:779
  108.6 1.7 shard_map.93
  110.3 11.3 %all_to_all.26.refs_7_ = s32[8,40,256]{2,1,0:T(8,128)S(1)} all-to-all(s32[8,40,256]{2,1,0:T(8,128)S(1)} %shard_map.93), channel_id=1, replica_groups=mesh['row'=4,'col'=8] {'col'}, dimensions={0} | all-to-all | bytes 655360 | tf_op jit(solution)/shard_map/all_to_all | solution.py:792
  121.6 17.4 %shard_map.94 = (f32[2,256,256]{2,1,0:T(8,128)}, f32[2,256,256]{2,1,0:T(8,128)S(1)}, s32[264,256]{1,0:T(8,128)S(1)}, s32[264,256]{1,0:T(8,128)S(1)}, s32[264,256...) custom-call(s32[256]{0:T(256)S(1)} %bitcast.9, s32[2]{0:T(128)S(1)} %pad_add_fusion.refs_1_.refs_0_, ...), custom_call_target="tpu_custom_call" | custom-call | flops 6442450944 | bytes 8388608 | tf_op jit(solution)/shard_map/pallas_call | solution.py:749
  138.9 3.5 %all-to-all-start.3 = ((s32[8,56,256]{2,1,0:T(8,128)}), s32[8,56,256]{2,1,0:T(8,128)S(1)}, u32[]{:S(2)}, u32[]{:S(2)}) async-start(s32[8,56,256]{2,1,0:T(8,128)} %get-tuple-element.37), calls=%async_computation.3 | async-start | bytes 917504 | tf_op jit(solution)/shard_map/all_to_all | solution.py:785
  142.4 4.8 %shard_map.95.refs_6_.refs_1_ = f32[256,256]{1,0:T(8,128)} custom-call(s32[256]{0:T(256)S(1)} %bitcast.10, s32[2]{0:T(128)S(1)} %pad_add_fusion.refs_1_.refs_0_, f32[2,256,256]{2,1,0:T(8,128)S(1)} %get-tuple-element.36.refs_2_.refs_1_), custom_call_target="tpu_custom_call" | custom-call | flops 8589934592 | bytes 8388608 | tf_op jit(solution)/shard_map/pallas_call | solution.py:749
  147.2 4.2 %all-to-all-done.3.refs_0_ = s32[8,56,256]{2,1,0:T(8,128)S(1)} async-done(((s32[8,56,256]{2,1,0:T(8,128)}), s32[8,56,256]{2,1,0:T(8,128)S(1)}, u32[]{:S(2)}, u32[]{:S(2)}) %all-to-all-start.3) | async-done | bytes 458784 | tf_op jit(solution)/shard_map/all_to_all | solution.py:785
  153.0 4.0 %collective-permute-start.13 = (s32[56,256]{1,0:T(8,128)S(1)}, s32[56,256]{1,0:T(8,128)S(1)}, u32[]{:S(2)}, u32[]{:S(2)}) collective-permute-start(s32[56,256]{1,0:T(8,128)S(1)} %shard_map.97.refs_2_), channel_id=1, source_target_pairs={{0,8},{8,0},{16,24},{24,16},{1,9},{9,1},{17,25},{25,17},{2,10},{10... | collective-permute-start | bytes 172040 | tf_op jit(solution)/shard_map/ppermute | solution.py:779
  157.0 1.6 collective-permute-done.15.refs_5_
  159.2 1.4 shard_map.98
  160.6 3.4 %all-to-all-start.4 = ((s32[8,40,256]{2,1,0:T(8,128)}), s32[8,40,256]{2,1,0:T(8,128)S(1)}, u32[]{:S(2)}, u32[]{:S(2)}) async-start(s32[8,40,256]{2,1,0:T(8,128)} %shard_map.98), calls=%async_computation.4 | async-start | bytes 655360 | tf_op jit(solution)/shard_map/all_to_all | solution.py:792
  164.0 2.3 %collective-permute-start.10 = (s32[264,256]{1,0:T(8,128)S(1)}, s32[264,256]{1,0:T(8,128)S(1)}, u32[]{:S(2)}, u32[]{:S(2)}) collective-permute-start(s32[264,256]{1,0:T(8,128)S(1)} %get-tuple-element.33), channel_id=1, source_target_pairs={{0,1},{1,2},{2,3},{3,4},{4,5},{5,6},{6,7},{8,9},{9,10},{10,11},{11... | collective-permute-start | bytes 811016 | tf_op jit(solution)/shard_map/ppermute | solution.py:765
  166.3 3.9 %collective-permute-start.11 = (s32[264,256]{1,0:T(8,128)S(1)}, s32[264,256]{1,0:T(8,128)S(1)}, u32[]{:S(2)}, u32[]{:S(2)}) collective-permute-start(s32[264,256]{1,0:T(8,128)S(1)} %get-tuple-element.34), channel_id=1, source_target_pairs={{0,8},{8,16},{16,24},{1,9},{9,17},{17,25},{2,10},{10,18},{18,26},{... | collective-permute-start | bytes 811016 | tf_op jit(solution)/shard_map/ppermute | solution.py:765
  170.2 3.2 %collective-permute-start.12 = (s32[264,256]{1,0:T(8,128)S(1)}, s32[264,256]{1,0:T(8,128)S(1)}, u32[]{:S(2)}, u32[]{:S(2)}) collective-permute-start(s32[264,256]{1,0:T(8,128)S(1)} %get-tuple-element.35), channel_id=1, source_target_pairs={{0,9},{1,10},{2,11},{3,12},{4,13},{5,14},{6,15},{8,17},{9,18},{10,... | collective-permute-start | bytes 811016 | tf_op jit(solution)/shard_map/ppermute | solution.py:775
  173.4 3.1 %collective-permute-done.11.refs_3_ = s32[264,256]{1,0:T(8,128)S(1)} collective-permute-done((s32[264,256]{1,0:T(8,128)S(1)}, s32[264,256]{1,0:T(8,128)S(1)}, u32[]{:S(2)}, u32[]{:S(2)}) %collective-permute-start.11) | collective-permute-done | bytes 270368 | tf_op jit(solution)/shard_map/ppermute | solution.py:765
  176.5 5.8 %collective-permute-done.12.refs_4_ = s32[264,256]{1,0:T(8,128)S(1)} collective-permute-done((s32[264,256]{1,0:T(8,128)S(1)}, s32[264,256]{1,0:T(8,128)S(1)}, u32[]{:S(2)}, u32[]{:S(2)}) %collective-permute-start.12) | collective-permute-done | bytes 270368 | tf_op jit(solution)/shard_map/ppermute | solution.py:775
  182.3 2.6 %shard_map.96 = f32[2,256,256]{2,1,0:T(8,128)} custom-call(f32[2,256,256]{2,1,0:T(8,128)} %get-tuple-element.31.refs_0_, f32[2,256,256]{2,1,0:T(8,128)S(1)} %get-tuple-element.32.refs_1_, s32[264,256]{1,0:T(8,128)S(1)} %collective-permute-done.10.refs_2_, s32[264,256]{1,0:T(8,128)S(1)} %collective-permute-done.11.refs_3_, ...), custom_call_target="tpu_custom_call" | custom-call | flops 67108864 | bytes 8388608 | tf_op jit(solution)/shard_map/pallas_call | solution.py:749
  (31 shorter events, 13.3 us)
Async XLA Ops:
  1.9 11.4 %collective-permute-start.1 = (s32[264,256]{1,0:T(8,128)S(1)}, s32[264,256]{1,0:T(8,128)S(1)}, u32[]{:S(2)}, u32[]{:S(2)}) collective-permute-start(s32[264,256]{1,0:T(8,128)S(1)} %shard_map.86), channel_id=1, source_target_pairs={{8,0},{16,8},{24,16},{9,1},{17,9},{25,17},{10,2},{18,10},{26,18},{... | collective-permute-start | bytes 811016 | tf_op jit(solution)/shard_map/ppermute | solution.py:765
  3.2 10.1 %collective-permute-start = (s32[264,256]{1,0:T(8,128)S(1)}, s32[264,256]{1,0:T(8,128)S(1)}, u32[]{:S(2)}, u32[]{:S(2)}) collective-permute-start(s32[264,256]{1,0:T(8,128)S(1)} %shard_map.86), channel_id=1, source_target_pairs={{1,0},{2,1},{3,2},{4,3},{5,4},{6,5},{7,6},{9,8},{10,9},{11,10},{12... | collective-permute-start | bytes 811016 | tf_op jit(solution)/shard_map/ppermute | solution.py:765
  13.3 0.7 copy-start.1
  31.5 30.5 %all-to-all-start = ((bf16[16,256,256]{2,1,0:T(8,128)(2,1)}), bf16[16,256,256]{2,1,0:T(8,128)(2,1)S(1)}, u32[]{:S(2)}, u32[]{:S(2)}) async-start(bf16[16,256,256]{2,1,0:T(8,128)(2,1)} %shard_map.89), calls=%async_computation | async-start | bytes 4194304 | tf_op jit(solution)/shard_map/all_to_all | solution.py:823
  35.4 10.8 %collective-permute-start.2 = (s32[264,256]{1,0:T(8,128)S(1)}, s32[264,256]{1,0:T(8,128)S(1)}, u32[]{:S(2)}, u32[]{:S(2)}) collective-permute-start(s32[264,256]{1,0:T(8,128)S(1)} %collective-permute-done.refs_3_), channel_id=1, source_target_pairs={{8,0},{16,8},{24,16},{9,1},{17,9},{25,17},{10,2},{18,10},{26,18},{... | collective-permute-start | bytes 811016 | tf_op jit(solution)/shard_map/ppermute | solution.py:765
  62.1 1.4 copy-start.3
  77.4 15.7 %collective-permute-start.3 = (s32[264,512]{1,0:T(8,128)S(1)}, s32[264,512]{1,0:T(8,128)S(1)}, u32[]{:S(2)}, u32[]{:S(2)}) collective-permute-start(s32[264,512]{1,0:T(8,128)S(1)} %get-tuple-element.24), channel_id=1, source_target_pairs={{0,8},{8,16},{16,24},{1,9},{9,17},{17,25},{2,10},{10,18},{18,26},{... | collective-permute-start | bytes 1622024 | tf_op jit(solution)/shard_map/ppermute | solution.py:765
  78.7 14.3 %collective-permute-start.4 = (s32[264,512]{1,0:T(8,128)S(1)}, s32[264,512]{1,0:T(8,128)S(1)}, u32[]{:S(2)}, u32[]{:S(2)}) collective-permute-start(s32[264,512]{1,0:T(8,128)S(1)} %get-tuple-element.25), channel_id=1, source_target_pairs={{8,0},{16,8},{24,16},{9,1},{17,9},{25,17},{10,2},{18,10},{26,18},{... | collective-permute-start | bytes 1622024 | tf_op jit(solution)/shard_map/ppermute | solution.py:765
  93.1 28.5 %copy-start.2 = (s32[128,2]{0,1:T(2,128)S(1)}, s32[128,2]{0,1:T(2,128)}, u32[]{:S(2)}) copy-start(s32[128,2]{0,1:T(2,128)} %param.10) | copy-start | bytes 3076
  95.6 25.9 %collective-permute-start.5 = (s32[528,256]{1,0:T(8,128)S(1)}, s32[528,256]{1,0:T(8,128)S(1)}, u32[]{:S(2)}, u32[]{:S(2)}) collective-permute-start(s32[528,256]{1,0:T(8,128)S(1)} %get-tuple-element.28), channel_id=1, source_target_pairs={{0,1},{1,2},{2,3},{3,4},{4,5},{5,6},{6,7},{8,9},{9,10},{10,11},{11... | collective-permute-start | bytes 1622024 | tf_op jit(solution)/shard_map/ppermute | solution.py:765
  97.1 24.5 %collective-permute-start.6 = (s32[528,256]{1,0:T(8,128)S(1)}, s32[528,256]{1,0:T(8,128)S(1)}, u32[]{:S(2)}, u32[]{:S(2)}) collective-permute-start(s32[528,256]{1,0:T(8,128)S(1)} %get-tuple-element.29), channel_id=1, source_target_pairs={{1,0},{2,1},{3,2},{4,3},{5,4},{6,5},{7,6},{9,8},{10,9},{11,10},{12... | collective-permute-start | bytes 1622024 | tf_op jit(solution)/shard_map/ppermute | solution.py:765
  98.4 6.1 %collective-permute-start.9 = (s32[56,256]{1,0:T(8,128)S(1)}, s32[56,256]{1,0:T(8,128)S(1)}, u32[]{:S(2)}, u32[]{:S(2)}) collective-permute-start(s32[56,256]{1,0:T(8,128)S(1)} %shard_map.91.refs_3_.refs_2_), channel_id=1, source_target_pairs={{0,24},{8,16},{16,8},{24,0},{1,25},{9,17},{17,9},{25,1},{2,26},{10... | collective-permute-start | bytes 172040 | tf_op jit(solution)/shard_map/ppermute | solution.py:779
  100.9 7.7 %collective-permute-start.8 = (s32[56,256]{1,0:T(8,128)S(1)}, s32[56,256]{1,0:T(8,128)S(1)}, u32[]{:S(2)}, u32[]{:S(2)}) collective-permute-start(s32[56,256]{1,0:T(8,128)S(1)} %shard_map.91.refs_3_.refs_2_), channel_id=1, source_target_pairs={{0,16},{8,24},{16,0},{24,8},{1,17},{9,25},{17,1},{25,9},{2,18},{10... | collective-permute-start | bytes 172040 | tf_op jit(solution)/shard_map/ppermute | solution.py:779
  102.6 6.0 %collective-permute-start.7 = (s32[56,256]{1,0:T(8,128)S(1)}, s32[56,256]{1,0:T(8,128)S(1)}, u32[]{:S(2)}, u32[]{:S(2)}) collective-permute-start(s32[56,256]{1,0:T(8,128)S(1)} %shard_map.91.refs_3_.refs_2_), channel_id=1, source_target_pairs={{0,8},{8,0},{16,24},{24,16},{1,9},{9,1},{17,25},{25,17},{2,10},{10... | collective-permute-start | bytes 172040 | tf_op jit(solution)/shard_map/ppermute | solution.py:779
  138.9 12.5 %all-to-all-start.3 = ((s32[8,56,256]{2,1,0:T(8,128)}), s32[8,56,256]{2,1,0:T(8,128)S(1)}, u32[]{:S(2)}, u32[]{:S(2)}) async-start(s32[8,56,256]{2,1,0:T(8,128)} %get-tuple-element.37), calls=%async_computation.3 | async-start | bytes 917504 | tf_op jit(solution)/shard_map/all_to_all | solution.py:785
  151.4 1.0 copy-start
  152.5 6.0 %collective-permute-start.15 = (s32[56,256]{1,0:T(8,128)S(1)}, s32[56,256]{1,0:T(8,128)S(1)}, u32[]{:S(2)}, u32[]{:S(2)}) collective-permute-start(s32[56,256]{1,0:T(8,128)S(1)} %shard_map.97.refs_2_), channel_id=1, source_target_pairs={{0,24},{8,16},{16,8},{24,0},{1,25},{9,17},{17,9},{25,1},{2,26},{10... | collective-permute-start | bytes 172040 | tf_op jit(solution)/shard_map/ppermute | solution.py:779
  152.6 6.0 %collective-permute-start.14 = (s32[56,256]{1,0:T(8,128)S(1)}, s32[56,256]{1,0:T(8,128)S(1)}, u32[]{:S(2)}, u32[]{:S(2)}) collective-permute-start(s32[56,256]{1,0:T(8,128)S(1)} %shard_map.97.refs_2_), channel_id=1, source_target_pairs={{0,16},{8,24},{16,0},{24,8},{1,17},{9,25},{17,1},{25,9},{2,18},{10... | collective-permute-start | bytes 172040 | tf_op jit(solution)/shard_map/ppermute | solution.py:779
  153.0 6.2 %collective-permute-start.13 = (s32[56,256]{1,0:T(8,128)S(1)}, s32[56,256]{1,0:T(8,128)S(1)}, u32[]{:S(2)}, u32[]{:S(2)}) collective-permute-start(s32[56,256]{1,0:T(8,128)S(1)} %shard_map.97.refs_2_), channel_id=1, source_target_pairs={{0,8},{8,0},{16,24},{24,16},{1,9},{9,1},{17,25},{25,17},{2,10},{10... | collective-permute-start | bytes 172040 | tf_op jit(solution)/shard_map/ppermute | solution.py:779
  160.6 24.3 %all-to-all-start.4 = ((s32[8,40,256]{2,1,0:T(8,128)}), s32[8,40,256]{2,1,0:T(8,128)S(1)}, u32[]{:S(2)}, u32[]{:S(2)}) async-start(s32[8,40,256]{2,1,0:T(8,128)} %shard_map.98), calls=%async_computation.4 | async-start | bytes 655360 | tf_op jit(solution)/shard_map/all_to_all | solution.py:792
  164.0 9.4 %collective-permute-start.10 = (s32[264,256]{1,0:T(8,128)S(1)}, s32[264,256]{1,0:T(8,128)S(1)}, u32[]{:S(2)}, u32[]{:S(2)}) collective-permute-start(s32[264,256]{1,0:T(8,128)S(1)} %get-tuple-element.33), channel_id=1, source_target_pairs={{0,1},{1,2},{2,3},{3,4},{4,5},{5,6},{6,7},{8,9},{9,10},{10,11},{11... | collective-permute-start | bytes 811016 | tf_op jit(solution)/shard_map/ppermute | solution.py:765
  166.3 10.1 %collective-permute-start.11 = (s32[264,256]{1,0:T(8,128)S(1)}, s32[264,256]{1,0:T(8,128)S(1)}, u32[]{:S(2)}, u32[]{:S(2)}) collective-permute-start(s32[264,256]{1,0:T(8,128)S(1)} %get-tuple-element.34), channel_id=1, source_target_pairs={{0,8},{8,16},{16,24},{1,9},{9,17},{17,25},{2,10},{10,18},{18,26},{... | collective-permute-start | bytes 811016 | tf_op jit(solution)/shard_map/ppermute | solution.py:765
  170.2 12.0 %collective-permute-start.12 = (s32[264,256]{1,0:T(8,128)S(1)}, s32[264,256]{1,0:T(8,128)S(1)}, u32[]{:S(2)}, u32[]{:S(2)}) collective-permute-start(s32[264,256]{1,0:T(8,128)S(1)} %get-tuple-element.35), channel_id=1, source_target_pairs={{0,9},{1,10},{2,11},{3,12},{4,13},{5,14},{6,15},{8,17},{9,18},{10,... | collective-permute-start | bytes 811016 | tf_op jit(solution)/shard_map/ppermute | solution.py:775

commit v6 on v5

--- a/solution.py
+++ b/solution.py
@@ -468,20 +468,21 @@
     return parts[0]
 
 
-def sums_kernel(rows, parts_ref, *refs):
-    out_ref = refs[-1]
-    for col in range(0, out_ref.shape[1], LANES):
+def sums_kernel(rows, parts_ref, out_ref):
+    for col in range(0, out_ref.shape[2], LANES):
         cols = pl.ds(col, LANES)
         total = added([decode_sums(parts_ref.at[k], cols, rows) for k in range(parts_ref.shape[0])])
-        encode_sums(out_ref, cols, *total)
-
-
-def update_kernel(rows, me_ref, probe_ref, *refs):
-    *parts, out_ref = refs
+        encode_sums(out_ref.at[0], cols, *total)
+        for k in range(1, out_ref.shape[0]):
+            out_ref[k, :, cols] = out_ref[0, :, cols]
+
+
+def update_kernel(rows, me_ref, probe_ref, parts_ref, *refs):
+    out_ref = refs[-1]
     first = pl.multiple_of(me_ref[1] * rows, SUBLANES)
     for col in range(0, out_ref.shape[2], LANES):
         cols = pl.ds(col, LANES)
-        u_re, u_im, v = added([decode_sums(ref, cols, rows) for ref in parts])
+        u_re, u_im, v = added([decode_sums(parts_ref.at[k], cols, rows) for k in range(parts_ref.shape[0])])
         scale = 1.0 / (v + probe_regular)
         re = (probe_ref[0, pl.ds(first, rows), cols] + u_re) * scale
         im = (probe_ref[1, pl.ds(first, rows), cols] + u_im) * scale
@@ -775,20 +776,18 @@
     return lax.ppermute(value, ("row", "col"), pairs)
 
 
-def swapped(value, axis, mask):
-    return lax.ppermute(value, axis, [(k, k ^ mask) for k in range(lax.axis_size(axis))])
-
-
 def probe_update(me, probe, numer, kind, *after):
     cols, order = lax.axis_size("col"), probe.shape[1]
     rows = order // cols
     parts = lax.all_to_all(numer, "col", split_axis=0, concat_axis=0, tiled=True)
-    total = call(functools.partial(sums_kernel, rows), shape((sums_rows(rows), order), jnp.int32), VMEM, [VMEM] + [FREE] * len(after), [], 1 << 26)(parts, *after)
-    totals = [total] + [swapped(total, "row", mask) for mask in range(1, lax.axis_size("row"))]
+    total = call(
+        functools.partial(sums_kernel, rows), shape((lax.axis_size("row"), sums_rows(rows), order), jnp.int32), VMEM, [VMEM], [], 1 << 26,
+    )(parts)
+    parts = lax.all_to_all(total, "row", split_axis=0, concat_axis=0, tiled=True)
     fresh = call(
         functools.partial(update_kernel, rows), shape((cols, rows + SUBLANES, order), jnp.int32), VMEM,
-        [SMEM, kind] + [VMEM] * len(totals), [], 1 << 26,
-    )(me, probe, *totals)
+        [SMEM, kind, VMEM] + [spec for spec, _ in after], [], 1 << 26,
+    )(me, probe, parts, *[value for _, value in after])
     return total, lax.all_to_all(fresh, "col", split_axis=0, concat_axis=0, tiled=True)
 
 
@@ -817,7 +816,7 @@
     diag = passed_along(right, "row", -1)
 
     outgoing = call(
-        functools.partial(outgoing_kernel, dims), shape((col_count * SEND, order, order), bf16), HBM, [SMEM, SMEM, HBM, FREE, FREE],
+        functools.partial(outgoing_kernel, dims), shape((col_count * SEND, order, order), bf16), HBM, [SMEM, SMEM, LOAD, FREE, FREE],
         [pltpu.SemaphoreType.DMA((pat_count,))], 1 << 20,
     )(pos, me, amplitudes, right, below)
     incoming = lax.all_to_all(outgoing, "col", split_axis=0, concat_axis=0, tiled=True)
@@ -874,7 +873,7 @@
     new_object = call(functools.partial(object_kernel, dims), shape(tile), VMEM, [LOAD] + [VMEM] * 4 + [LOAD, LOAD], [], 1 << 26)(
         current, own, from_left, from_above, from_diag, weights_old, weights_new
     )
-    _, chunks = probe_update(me, probe_now, numer, VMEM, weights_new)
+    _, chunks = probe_update(me, probe_now, numer, VMEM, (HBM, weights_new), (FREE, from_left), (FREE, from_above), (FREE, from_diag))
     new_probe = call(probe_kernel, shape(window), VMEM, [VMEM], [], 1 << 26)(chunks)
     return new_object, new_probe
 

time: 187 us -> 165 us (0.88)
  Pallas kernels: 81.8 us -> 53.7 us
  starting transfers between devices: 38.3 us -> 49.4 us
  waiting for transfers between devices: 37.5 us -> 30.9 us
    pallas_call x14, Pallas kernels: 81.8 us -> 53.7 us  [called(): pl.pallas_call(body, out_shape=tuple(fixed_outs) if several else fixed_ou...]
    ppermute x6 -> x0, starting transfers between devices: 8.9 us -> none  [swapped(): lax.ppermute(value, axis, [(k, k ^ mask) for k in range(lax.axis_size(axi...]
    ppermute x9, starting transfers between devices: 15.5 us -> 23.5 us  [passed_along(): lax.ppermute(value, axis, [(source, source + steps) for source in range(l...]
    ppermute x6 -> x0, waiting for transfers between devices: 7.9 us -> none  [swapped(): lax.ppermute(value, axis, [(k, k ^ mask) for k in range(lax.axis_size(axi...]
    all_to_all x0 -> x2, starting transfers between devices: none -> 7.72 us  [probe_update(): lax.all_to_all(total, 'row', split_axis=0, concat_axis=0, tiled=True)]
    all_to_all x0 -> x2, waiting for transfers between devices: none -> 5.41 us  [probe_update(): lax.all_to_all(total, 'row', split_axis=0, concat_axis=0, tiled=True)]
    ppermute x1, waiting for transfers between devices: 5.79 us -> 0.45 us  [passed_both(): return lax.ppermute(value, ('row', 'col'), pairs)]
    all_to_all x1, waiting for transfers between devices: 0.01 us -> 4.94 us  [probe_update(): lax.all_to_all(fresh, 'col', split_axis=0, concat_axis=0, tiled=True)]
  transfers between devices with their start and end apart: 19 -> 15, of which waited for: 10 -> 7; matrix products, arithmetic and copies ran while one was open for 0% -> 0% of each run, Pallas kernels for 14% -> 16%
where the time goes in v6:
time: 165 us; the launch traced here: 164 us
  Pallas kernels  53.7 us (33%)
  starting transfers between devices  49.4 us (30%)
  waiting for transfers between devices  30.9 us (19%)
  blocking collectives  25.6 us (16%)
  local copies, waits for them, and re-layouts  3.59 us (2%)
    pallas_call x14, Pallas kernels, called(): pl.pallas_call(body, out_shape=tuple(fixed_outs) if several else fixed_ou...  53.7 us
    ppermute x9, starting transfers between devices, passed_along(): lax.ppermute(value, axis, [(source, source + steps) for source in range(l...  23.5 us
    all_to_all x1, blocking collectives, probe_update(): lax.all_to_all(fresh, 'col', split_axis=0, concat_axis=0, tiled=True)  14.2 us
    all_to_all x1, blocking collectives, probe_update(): lax.all_to_all(numer, 'col', split_axis=0, concat_axis=0, tiled=True)  11.4 us
    ppermute x9, waiting for transfers between devices, passed_along(): lax.ppermute(value, axis, [(source, source + steps) for source in range(l...  10.6 us
    all_to_all x1, waiting for transfers between devices, local(): lax.all_to_all(outgoing, 'col', split_axis=0, concat_axis=0, tiled=True)  9.47 us
    all_to_all x2, starting transfers between devices, probe_update(): lax.all_to_all(total, 'row', split_axis=0, concat_axis=0, tiled=True)  7.72 us
    all_to_all x1, starting transfers between devices, probe_update(): lax.all_to_all(numer, 'col', split_axis=0, concat_axis=0, tiled=True)  7.28 us
  transfers between devices with their start and end apart: 15, of which 7 were waited for; matrix products, arithmetic and copies ran while one was open for 0% of the time, Pallas kernels for 16%

profile of v6, /device:TPU:0, one launch (start us, length us, event | category | flops | bytes accessed | tf_op | source)
XLA Modules:
  0.0 164.2 jit_solution(850357321203113402)
XLA Ops:
  1.9 1.3 collective-permute-start.1
  3.2 1.3 collective-permute-start
  4.5 8.7 %collective-permute-done.1.refs_4_ = s32[264,256]{1,0:T(8,128)S(1)} collective-permute-done((s32[264,256]{1,0:T(8,128)S(1)}, s32[264,256]{1,0:T(8,128)S(1)}, u32[]{:S(2)}, u32[]{:S(2)}) %collective-permute-start.1) | collective-permute-done | bytes 270368 | tf_op jit(solution)/shard_map/ppermute | solution.py:766
  13.9 2.5 %shard_map.89 = bf16[16,256,256]{2,1,0:T(8,128)(2,1)} custom-call(s32[256]{0:T(256)S(1)} %bitcast.5, s32[2]{0:T(128)S(1)} %pad_add_fusion.refs_1_.refs_0_, bf16[4,256,256]{2,1,0:T(8,128)(2,1)} %refs_2_.5, s32[264,256]{1,0:T(8,128)S(1)} %collective-permute-done.refs_3_, s32[264,256]{1,0:T(8,128)S(1)} %collective-permute-done.1.refs_4_), custom_call_target="tpu_custom_call" | custom-call | flops 1048576 | bytes 8388608 | tf_op jit(solution)/shard_map/pallas_call | solution.py:750
  16.4 4.4 %all-to-all-start = ((bf16[16,256,256]{2,1,0:T(8,128)(2,1)}), bf16[16,256,256]{2,1,0:T(8,128)(2,1)}, u32[]{:S(2)}, u32[]{:S(2)}) async-start(bf16[16,256,256]{2,1,0:T(8,128)(2,1)} %shard_map.89), calls=%async_computation | async-start | bytes 4194304 | tf_op jit(solution)/shard_map/all_to_all | solution.py:822
  22.1 7.4 %shard_map.88.refs_5_.refs_6_ = f32[512,512]{1,0:T(8,128)} custom-call(s32[256]{0:T(256)S(1)} %bitcast.6, s32[2]{0:T(128)S(1)} %pad_add_fusion.refs_1_.refs_0_, f32[2,256,256]{2,1,0:T(8,128)} %refs_1_.1), custom_call_target="tpu_custom_call" | custom-call | flops 8589934592 | bytes 8388608 | tf_op jit(solution)/shard_map/pallas_call | solution.py:750
  29.5 1.9 %collective-permute-done.2.refs_5_ = s32[264,256]{1,0:T(8,128)S(1)} collective-permute-done((s32[264,256]{1,0:T(8,128)S(1)}, s32[264,256]{1,0:T(8,128)S(1)}, u32[]{:S(2)}, u32[]{:S(2)}) %collective-permute-start.2) | collective-permute-done | bytes 270368 | tf_op jit(solution)/shard_map/ppermute | solution.py:766
  31.4 6.5 %shard_map.87 = (f32[8,2,256,256]{3,2,1,0:T(8,128)}, f32[256,256]{1,0:T(8,128)S(1)}, f32[2,512,512]{2,1,0:T(8,128)}) custom-call(s32[256]{0:T(256)S(1)} %bitcast.7, s32[2]{0:T(128)S(1)} %pad_add_fusion.refs_1_.refs_0_, f32[2,256,256]{2,1,0:T(8,128)} %refs_2_.3, s32[264,256]{1,0:T(8,128)S(1)} %collective-permute-done.refs_3_, ...), custom_call_target="tpu_custom_call" | custom-call | flops 3221225472 | bytes 8388608 | tf_op jit(solution)/shard_map/pallas_call | solution.py:750
  38.0 9.5 %all-to-all-done.refs_7_ = bf16[16,256,256]{2,1,0:T(8,128)(2,1)} async-done(((bf16[16,256,256]{2,1,0:T(8,128)(2,1)}), bf16[16,256,256]{2,1,0:T(8,128)(2,1)}, u32[]{:S(2)}, u32[]{:S(2)}) %all-to-all-start) | async-done | bytes 2097184 | tf_op jit(solution)/shard_map/all_to_all | solution.py:822
  47.4 9.8 %shard_map.90 = (f32[2,512,512]{2,1,0:T(8,128)}, s32[264,512]{1,0:T(8,128)S(1)}, s32[264,512]{1,0:T(8,128)S(1)}, s32[8,56,256]{2,1,0:T(8,128)S(1)}, bf16[8,256,256]{2,1,0:T(8,128)(2,1)}) custom-call(s32[256]{0:T(256)S(1)} %bitcast.8, s32[2]{0:T(128)S(1)} %pad_add_fusion.refs_1_.refs_0_, f32[2,512,512]{2,1,0:T(8,128)} %get-tuple-element.20.refs_2_, ...), custom_call_target="tpu_custom_call" | custom-call | flops 3221225472 | bytes 8388608 | tf_op jit(solution)/shard_map/pallas_call | solution.py:750
  57.2 7.2 %collective-permute-start.3 = (s32[264,512]{1,0:T(8,128)S(1)}, s32[264,512]{1,0:T(8,128)S(1)}, u32[]{:S(2)}, u32[]{:S(2)}) collective-permute-start(s32[264,512]{1,0:T(8,128)S(1)} %get-tuple-element.24), channel_id=1, source_target_pairs={{0,8},{8,16},{16,24},{1,9},{9,17},{17,25},{2,10},{10,18},{18,26},{... | collective-permute-start | bytes 1622024 | tf_op jit(solution)/shard_map/ppermute | solution.py:766
  65.7 11.4 %all_to_all.35.refs_0_ = s32[8,56,256]{2,1,0:T(8,128)S(1)} all-to-all(s32[8,56,256]{2,1,0:T(8,128)S(1)} %get-tuple-element.26), channel_id=1, replica_groups=mesh['row'=4,'col'=8] {'col'}, dimensions={0} | all-to-all | bytes 917504 | tf_op jit(solution)/shard_map/all_to_all | solution.py:782
  78.1 4.3 %all-to-all-start.2 = ((s32[4,56,256]{2,1,0:T(8,128)}), s32[4,56,256]{2,1,0:T(8,128)S(1)}, u32[]{:S(2)}, u32[]{:S(2)}) async-start(s32[4,56,256]{2,1,0:T(8,128)} %shard_map.91.refs_3_), calls=%async_computation.2 | async-start | bytes 458752 | tf_op jit(solution)/shard_map/all_to_all | solution.py:786
  82.4 2.5 %shard_map.92 = (f32[2,512,512]{2,1,0:T(8,128)S(1)}, s32[528,256]{1,0:T(8,128)S(1)}, s32[528,256]{1,0:T(8,128)S(1)}) custom-call(f32[2,512,512]{2,1,0:T(8,128)} %get-tuple-element.23.refs_0_, s32[264,512]{1,0:T(8,128)S(1)} %collective-permute-done.3.refs_1_, s32[264,512]{1,0:T(8,128)S(1)} %collective-permute-done.4.refs_2_, s32[4,56,256]{2,1,0:T(8,128)} %shard_map.91.refs_3_), custom_call_target="tpu_custom_call" | custom-call | flops 67108864 | bytes 8388608 | tf_op jit(solution)/shard_map/pallas_call | solution.py:750
  84.9 1.3 copy-done.2
  86.3 1.3 collective-permute-start.5
  88.9 1.4 all-to-all-done.2.refs_2_
  90.3 1.7 %shard_map.93 = s32[8,40,256]{2,1,0:T(8,128)S(1)} custom-call(s32[2]{0:T(128)S(1)} %pad_add_fusion.refs_1_.refs_0_, f32[2,256,256]{2,1,0:T(8,128)} %refs_1_.1, s32[4,56,256]{2,1,0:T(8,128)S(1)} %all-to-all-done.2.refs_2_), custom_call_target="tpu_custom_call" | custom-call | flops 67108864 | bytes 8388608 | tf_op jit(solution)/shard_map/pallas_call | solution.py:750
  92.0 14.2 %all_to_all.36.refs_7_ = s32[8,40,256]{2,1,0:T(8,128)S(1)} all-to-all(s32[8,40,256]{2,1,0:T(8,128)S(1)} %shard_map.93), channel_id=1, replica_groups=mesh['row'=4,'col'=8] {'col'}, dimensions={0} | all-to-all | bytes 655360 | tf_op jit(solution)/shard_map/all_to_all | solution.py:791
  106.2 1.6 copy-done.3
  107.7 11.4 %shard_map.94 = (f32[2,256,256]{2,1,0:T(8,128)}, f32[2,256,256]{2,1,0:T(8,128)S(1)}, s32[264,256]{1,0:T(8,128)}, s32[264,256]{1,0:T(8,128)S(1)}, s32[264,256]{1,...) custom-call(s32[256]{0:T(256)S(1)} %bitcast.9, s32[2]{0:T(128)S(1)} %pad_add_fusion.refs_1_.refs_0_, ...), custom_call_target="tpu_custom_call" | custom-call | flops 6442450944 | bytes 8388608 | tf_op jit(solution)/shard_map/pallas_call | solution.py:750
  119.2 7.3 %all-to-all-start.4 = ((s32[8,56,256]{2,1,0:T(8,128)}), s32[8,56,256]{2,1,0:T(8,128)S(1)}, u32[]{:S(2)}, u32[]{:S(2)}) async-start(s32[8,56,256]{2,1,0:T(8,128)} %get-tuple-element.37), calls=%async_computation.4 | async-start | bytes 917504 | tf_op jit(solution)/shard_map/all_to_all | solution.py:782
  126.4 2.4 %collective-permute-start.7 = (s32[264,256]{1,0:T(8,128)}, s32[264,256]{1,0:T(8,128)S(1)}, u32[]{:S(2)}, u32[]{:S(2)}) collective-permute-start(s32[264,256]{1,0:T(8,128)} %get-tuple-element.33), channel_id=1, source_target_pairs={{0,1},{1,2},{2,3},{3,4},{4,5},{5,6},{6,7},{8,9},{9,10},{10,11},{11... | collective-permute-start | bytes 811016 | tf_op jit(solution)/shard_map/ppermute | solution.py:766
  128.9 6.0 %collective-permute-start.8 = (s32[264,256]{1,0:T(8,128)S(1)}, s32[264,256]{1,0:T(8,128)S(1)}, u32[]{:S(2)}, u32[]{:S(2)}) collective-permute-start(s32[264,256]{1,0:T(8,128)S(1)} %get-tuple-element.34), channel_id=1, source_target_pairs={{0,8},{8,16},{16,24},{1,9},{9,17},{17,25},{2,10},{10,18},{18,26},{... | collective-permute-start | bytes 811016 | tf_op jit(solution)/shard_map/ppermute | solution.py:766
  134.9 3.2 %collective-permute-start.9 = (s32[264,256]{1,0:T(8,128)S(1)}, s32[264,256]{1,0:T(8,128)S(1)}, u32[]{:S(2)}, u32[]{:S(2)}) collective-permute-start(s32[264,256]{1,0:T(8,128)S(1)} %get-tuple-element.35), channel_id=1, source_target_pairs={{0,9},{1,10},{2,11},{3,12},{4,13},{5,14},{6,15},{8,17},{9,18},{10,... | collective-permute-start | bytes 811016 | tf_op jit(solution)/shard_map/ppermute | solution.py:776
  138.9 3.4 %all-to-all-start.5 = ((s32[4,56,256]{2,1,0:T(8,128)}), s32[4,56,256]{2,1,0:T(8,128)S(1)}, u32[]{:S(2)}, u32[]{:S(2)}) async-start(s32[4,56,256]{2,1,0:T(8,128)} %shard_map.97), calls=%async_computation.5 | async-start | bytes 458752 | tf_op jit(solution)/shard_map/all_to_all | solution.py:786
  142.3 4.1 %shard_map.95.refs_6_.refs_3_ = f32[256,256]{1,0:T(8,128)} custom-call(s32[256]{0:T(256)S(1)} %bitcast.10, s32[2]{0:T(128)S(1)} %pad_add_fusion.refs_1_.refs_0_, f32[2,256,256]{2,1,0:T(8,128)S(1)} %get-tuple-element.36.refs_2_.refs_1_), custom_call_target="tpu_custom_call" | custom-call | flops 8589934592 | bytes 8388608 | tf_op jit(solution)/shard_map/pallas_call | solution.py:750
  146.9 4.0 %all-to-all-done.5.refs_2_ = s32[4,56,256]{2,1,0:T(8,128)S(1)} async-done(((s32[4,56,256]{2,1,0:T(8,128)}), s32[4,56,256]{2,1,0:T(8,128)S(1)}, u32[]{:S(2)}, u32[]{:S(2)}) %all-to-all-start.5) | async-done | bytes 229408 | tf_op jit(solution)/shard_map/all_to_all | solution.py:786
  150.9 1.4 shard_map.98
  152.3 3.4 %all-to-all-start.6 = ((s32[8,40,256]{2,1,0:T(8,128)}), s32[8,40,256]{2,1,0:T(8,128)S(1)}, u32[]{:S(2)}, u32[]{:S(2)}) async-start(s32[8,40,256]{2,1,0:T(8,128)} %shard_map.98), calls=%async_computation.6 | async-start | bytes 655360 | tf_op jit(solution)/shard_map/all_to_all | solution.py:791
  155.8 2.6 %shard_map.96 = f32[2,256,256]{2,1,0:T(8,128)} custom-call(f32[2,256,256]{2,1,0:T(8,128)} %get-tuple-element.31.refs_0_, f32[2,256,256]{2,1,0:T(8,128)S(1)} %get-tuple-element.32.refs_1_, s32[264,256]{1,0:T(8,128)S(1)} %collective-permute-done.7.refs_2_.refs_4_, s32[264,256]{1,0:T(8,128)S(1)} %collective-permute-done.8.refs_3_.refs_5_, ...), custom_call_target="tpu_custom_call" | custom-call | flops 67108864 | bytes 8388608 | tf_op jit(solution)/shard_map/pallas_call | solution.py:750
  158.4 4.9 %all-to-all-done.6.refs_0_ = s32[8,40,256]{2,1,0:T(8,128)S(1)} async-done(((s32[8,40,256]{2,1,0:T(8,128)}), s32[8,40,256]{2,1,0:T(8,128)S(1)}, u32[]{:S(2)}, u32[]{:S(2)}) %all-to-all-start.6) | async-done | bytes 327712 | tf_op jit(solution)/shard_map/all_to_all | solution.py:791
  (23 shorter events, 8.9 us)
Async XLA Ops:
  1.9 11.4 %collective-permute-start.1 = (s32[264,256]{1,0:T(8,128)S(1)}, s32[264,256]{1,0:T(8,128)S(1)}, u32[]{:S(2)}, u32[]{:S(2)}) collective-permute-start(s32[264,256]{1,0:T(8,128)S(1)} %shard_map.86), channel_id=1, source_target_pairs={{8,0},{16,8},{24,16},{9,1},{17,9},{25,17},{10,2},{18,10},{26,18},{... | collective-permute-start | bytes 811016 | tf_op jit(solution)/shard_map/ppermute | solution.py:766
  3.2 10.1 %collective-permute-start = (s32[264,256]{1,0:T(8,128)S(1)}, s32[264,256]{1,0:T(8,128)S(1)}, u32[]{:S(2)}, u32[]{:S(2)}) collective-permute-start(s32[264,256]{1,0:T(8,128)S(1)} %shard_map.86), channel_id=1, source_target_pairs={{1,0},{2,1},{3,2},{4,3},{5,4},{6,5},{7,6},{9,8},{10,9},{11,10},{12... | collective-permute-start | bytes 811016 | tf_op jit(solution)/shard_map/ppermute | solution.py:766
  13.3 0.7 copy-start
  16.4 31.0 %all-to-all-start = ((bf16[16,256,256]{2,1,0:T(8,128)(2,1)}), bf16[16,256,256]{2,1,0:T(8,128)(2,1)}, u32[]{:S(2)}, u32[]{:S(2)}) async-start(bf16[16,256,256]{2,1,0:T(8,128)(2,1)} %shard_map.89), calls=%async_computation | async-start | bytes 4194304 | tf_op jit(solution)/shard_map/all_to_all | solution.py:822
  20.8 10.7 %collective-permute-start.2 = (s32[264,256]{1,0:T(8,128)S(1)}, s32[264,256]{1,0:T(8,128)S(1)}, u32[]{:S(2)}, u32[]{:S(2)}) collective-permute-start(s32[264,256]{1,0:T(8,128)S(1)} %collective-permute-done.refs_3_), channel_id=1, source_target_pairs={{8,0},{16,8},{24,16},{9,1},{17,9},{25,17},{10,2},{18,10},{26,18},{... | collective-permute-start | bytes 811016 | tf_op jit(solution)/shard_map/ppermute | solution.py:766
  57.2 25.2 %collective-permute-start.3 = (s32[264,512]{1,0:T(8,128)S(1)}, s32[264,512]{1,0:T(8,128)S(1)}, u32[]{:S(2)}, u32[]{:S(2)}) collective-permute-start(s32[264,512]{1,0:T(8,128)S(1)} %get-tuple-element.24), channel_id=1, source_target_pairs={{0,8},{8,16},{16,24},{1,9},{9,17},{17,25},{2,10},{10,18},{18,26},{... | collective-permute-start | bytes 1622024 | tf_op jit(solution)/shard_map/ppermute | solution.py:766
  64.4 18.0 %collective-permute-start.4 = (s32[264,512]{1,0:T(8,128)S(1)}, s32[264,512]{1,0:T(8,128)S(1)}, u32[]{:S(2)}, u32[]{:S(2)}) collective-permute-start(s32[264,512]{1,0:T(8,128)S(1)} %get-tuple-element.25), channel_id=1, source_target_pairs={{8,0},{16,8},{24,16},{9,1},{17,9},{25,17},{10,2},{18,10},{26,18},{... | collective-permute-start | bytes 1622024 | tf_op jit(solution)/shard_map/ppermute | solution.py:766
  78.1 12.2 %all-to-all-start.2 = ((s32[4,56,256]{2,1,0:T(8,128)}), s32[4,56,256]{2,1,0:T(8,128)S(1)}, u32[]{:S(2)}, u32[]{:S(2)}) async-start(s32[4,56,256]{2,1,0:T(8,128)} %shard_map.91.refs_3_), calls=%async_computation.2 | async-start | bytes 458752 | tf_op jit(solution)/shard_map/all_to_all | solution.py:786
  82.4 23.7 %copy-start.1 = (s32[128,2]{0,1:T(2,128)S(1)}, s32[128,2]{0,1:T(2,128)}, u32[]{:S(2)}) copy-start(s32[128,2]{0,1:T(2,128)} %param.10) | copy-start | bytes 3076
  84.9 1.3 copy-start.2
  86.3 19.9 %collective-permute-start.5 = (s32[528,256]{1,0:T(8,128)S(1)}, s32[528,256]{1,0:T(8,128)S(1)}, u32[]{:S(2)}, u32[]{:S(2)}) collective-permute-start(s32[528,256]{1,0:T(8,128)S(1)} %get-tuple-element.28), channel_id=1, source_target_pairs={{0,1},{1,2},{2,3},{3,4},{4,5},{5,6},{6,7},{8,9},{9,10},{10,11},{11... | collective-permute-start | bytes 1622024 | tf_op jit(solution)/shard_map/ppermute | solution.py:766
  87.6 18.6 %collective-permute-start.6 = (s32[528,256]{1,0:T(8,128)S(1)}, s32[528,256]{1,0:T(8,128)S(1)}, u32[]{:S(2)}, u32[]{:S(2)}) collective-permute-start(s32[528,256]{1,0:T(8,128)S(1)} %get-tuple-element.29), channel_id=1, source_target_pairs={{1,0},{2,1},{3,2},{4,3},{5,4},{6,5},{7,6},{9,8},{10,9},{11,10},{12... | collective-permute-start | bytes 1622024 | tf_op jit(solution)/shard_map/ppermute | solution.py:766
  106.2 1.6 copy-start.3
  119.2 18.9 %all-to-all-start.4 = ((s32[8,56,256]{2,1,0:T(8,128)}), s32[8,56,256]{2,1,0:T(8,128)S(1)}, u32[]{:S(2)}, u32[]{:S(2)}) async-start(s32[8,56,256]{2,1,0:T(8,128)} %get-tuple-element.37), calls=%async_computation.4 | async-start | bytes 917504 | tf_op jit(solution)/shard_map/all_to_all | solution.py:782
  126.4 20.0 %collective-permute-start.7 = (s32[264,256]{1,0:T(8,128)}, s32[264,256]{1,0:T(8,128)S(1)}, u32[]{:S(2)}, u32[]{:S(2)}) collective-permute-start(s32[264,256]{1,0:T(8,128)} %get-tuple-element.33), channel_id=1, source_target_pairs={{0,1},{1,2},{2,3},{3,4},{4,5},{5,6},{6,7},{8,9},{9,10},{10,11},{11... | collective-permute-start | bytes 811016 | tf_op jit(solution)/shard_map/ppermute | solution.py:766
  128.9 17.6 %collective-permute-start.8 = (s32[264,256]{1,0:T(8,128)S(1)}, s32[264,256]{1,0:T(8,128)S(1)}, u32[]{:S(2)}, u32[]{:S(2)}) collective-permute-start(s32[264,256]{1,0:T(8,128)S(1)} %get-tuple-element.34), channel_id=1, source_target_pairs={{0,8},{8,16},{16,24},{1,9},{9,17},{17,25},{2,10},{10,18},{18,26},{... | collective-permute-start | bytes 811016 | tf_op jit(solution)/shard_map/ppermute | solution.py:766
  134.9 12.0 %collective-permute-start.9 = (s32[264,256]{1,0:T(8,128)S(1)}, s32[264,256]{1,0:T(8,128)S(1)}, u32[]{:S(2)}, u32[]{:S(2)}) collective-permute-start(s32[264,256]{1,0:T(8,128)S(1)} %get-tuple-element.35), channel_id=1, source_target_pairs={{0,9},{1,10},{2,11},{3,12},{4,13},{5,14},{6,15},{8,17},{9,18},{10,... | collective-permute-start | bytes 811016 | tf_op jit(solution)/shard_map/ppermute | solution.py:776
  138.9 12.0 %all-to-all-start.5 = ((s32[4,56,256]{2,1,0:T(8,128)}), s32[4,56,256]{2,1,0:T(8,128)S(1)}, u32[]{:S(2)}, u32[]{:S(2)}) async-start(s32[4,56,256]{2,1,0:T(8,128)} %shard_map.97), calls=%async_computation.5 | async-start | bytes 458752 | tf_op jit(solution)/shard_map/all_to_all | solution.py:786
  152.3 11.0 %all-to-all-start.6 = ((s32[8,40,256]{2,1,0:T(8,128)}), s32[8,40,256]{2,1,0:T(8,128)S(1)}, u32[]{:S(2)}, u32[]{:S(2)}) async-start(s32[8,40,256]{2,1,0:T(8,128)} %shard_map.98), calls=%async_computation.6 | async-start | bytes 655360 | tf_op jit(solution)/shard_map/all_to_all | solution.py:791

commit v7 on v6

--- a/solution.py
+++ b/solution.py
@@ -24,6 +24,7 @@
 HBM = pl.BlockSpec(memory_space=pltpu.HBM)
 LOAD = object()
 FREE = pl.BlockSpec(memory_space=pl.ANY)
+PIN = pl.BlockSpec(memory_space=pltpu.VMEM)
 f32 = jnp.float32
 bf16 = jnp.bfloat16
 
@@ -468,7 +469,8 @@
     return parts[0]
 
 
-def sums_kernel(rows, parts_ref, out_ref):
+def sums_kernel(rows, parts_ref, *refs):
+    out_ref = refs[-1]
     for col in range(0, out_ref.shape[2], LANES):
         cols = pl.ds(col, LANES)
         total = added([decode_sums(parts_ref.at[k], cols, rows) for k in range(parts_ref.shape[0])])
@@ -534,7 +536,7 @@
 
 
 def second_half_kernel(dims, pos_ref, me_ref, ext_ref, probe_ref, power_ref, weights_ref, far_in, amp_in, turns, twiddles, sorting,
-                       share_out, top_out, bottom_out, numer_out, amp_out,
+                       share_out, numer_out, amp_out,
                        sum_ref, win_ref, xa_ref, xb_ref, ya_ref, yb_ref, numer_ref, far_ref, amp_ref, sorted_ref, ys_ref, xs_ref, slots_ref, far_sems, amp_sems, out_sems, sum_sem):
     tile_rows, tile_cols, pat_count, col_count, capacity = dims
     order = probe_ref.shape[1]
@@ -591,8 +593,6 @@
             sum_ref[comp, rows, :] = sum_ref[comp, rows, :] * scale
     keep = pltpu.make_async_copy(sum_ref, share_out, sum_sem)
     keep.start()
-    encode(lambda comp, at, cols: sum_ref[comp, at, cols], top_out, tile_rows, 0, tile_rows)
-    encode(lambda comp, at, cols: sum_ref[comp, pl.ds(tile_rows + at.start, at.size), cols], bottom_out, tile_rows, 0, tile_rows)
     spread_sums(numer_out, numer_ref, power_ref)
 
     def settle(listed, carry):
@@ -601,6 +601,12 @@
 
     lax.fori_loop(0, 2 * pairs, settle, 0)
     keep.wait()
+
+
+def rows_code_kernel(dims, share_ref, top_out, bottom_out):
+    tile_rows = dims[0]
+    encode(lambda comp, at, cols: share_ref[comp, at, cols], top_out, tile_rows, 0, tile_rows)
+    encode(lambda comp, at, cols: share_ref[comp, pl.ds(tile_rows + at.start, at.size), cols], bottom_out, tile_rows, 0, tile_rows)
 
 
 def rows_sum_kernel(dims, share_ref, above_ref, below_ref, after_ref, sum_out, left_out, right_out):
@@ -623,8 +629,8 @@
 
 def whole_kernel(dims, pos_ref, me_ref, old_ref, sum_ref, from_left_ref, from_right_ref, weights_ref,
                  chunks_ref, amp_in, turns, twiddles,
-                 current_out, own_out, right_out, below_out, diag_out, numer_out, probe_ref,
-                 ext_ref, grad_ref, win_ref, xa_ref, xb_ref, ya_ref, yb_ref, numer_ref, far_ref, amp_ref, ys_ref, xs_ref, slots_ref, amp_sems, own_sem):
+                 current_out, top_out, bottom_out, numer_out, probe_ref,
+                 ext_ref, grad_ref, win_ref, xa_ref, xb_ref, ya_ref, yb_ref, numer_ref, far_ref, amp_ref, ys_ref, xs_ref, slots_ref, amp_sems, own_sem, top_sem):
     tile_rows, tile_cols, pat_count, col_count, capacity = dims
     order = probe_ref.shape[1]
     count = list_patterns(dims, pos_ref, me_ref, ys_ref, xs_ref, slots_ref)
@@ -675,30 +681,52 @@
         return carry
 
     lax.fori_loop(0, pairs, pair, 0)
-    own_out[...] = grad_ref[:, 0:tile_rows, 0:tile_cols]
-    for (i, j), ref in zip(((0, 1), (1, 0), (1, 1)), (right_out, below_out, diag_out)):
-
-        def read(comp, at, cols, i=i, j=j):
-            rows, cols = pl.ds(i * tile_rows + at.start, at.size), pl.ds(j * tile_cols + cols.start, cols.size)
-            return grad_ref[comp, rows, cols] / (weights_ref[rows, cols] + object_regular)
-
-        encode(read, ref, tile_rows, 0, tile_rows)
+    for first in range(0, tile_rows, CHUNK):
+        rows = pl.ds(first, CHUNK)
+        scale = 1.0 / (weights_ref[rows, :] + object_regular)
+        for comp in range(2):
+            grad_ref[comp, rows, :] = grad_ref[comp, rows, :] * scale
+    give = pltpu.make_async_copy(grad_ref.at[:, pl.ds(0, tile_rows), :], top_out, top_sem)
+    give.start()
+
+    def read(comp, at, cols):
+        rows = pl.ds(tile_rows + at.start, at.size)
+        return grad_ref[comp, rows, cols] / (weights_ref[rows, cols] + object_regular)
+
+    encode(read, bottom_out, tile_rows, 0, tile_rows)
     spread_sums(numer_out, numer_ref, numer_ref.at[2])
     keep.wait()
-
-
-def object_kernel(dims, current_ref, own_ref, left_ref, above_ref, diag_ref, before_ref, weights_ref, out_ref):
+    give.wait()
+
+
+def fold_kernel(dims, top_ref, above_ref, own_out, right_out, own_ref, sem):
+    tile_rows, tile_cols = dims[:2]
+    for col in range(0, 2 * tile_cols, LANES):
+        for start in range(0, tile_rows, CHUNK):
+            rows, cols = pl.ds(start, CHUNK), pl.ds(col, LANES)
+            parts = decode(above_ref, start, tile_rows, col)
+            for comp in range(2):
+                if col < tile_cols:
+                    own_ref[comp, rows, cols] = top_ref[comp, rows, cols] + parts[comp]
+                else:
+                    top_ref[comp, rows, cols] += parts[comp]
+    keep = pltpu.make_async_copy(own_ref, own_out, sem)
+    keep.start()
+    encode(lambda comp, at, cols: top_ref[comp, at, pl.ds(tile_cols + cols.start, cols.size)], right_out, tile_rows, 0, tile_rows)
+    keep.wait()
+
+
+def object_kernel(dims, current_ref, own_ref, left_ref, before_ref, weights_ref, out_ref):
     tile_rows, tile_cols = dims[:2]
     for col in range(0, tile_cols, LANES):
         for start in range(0, tile_rows, CHUNK):
             rows, cols = pl.ds(start, CHUNK), pl.ds(col, LANES)
             scale = 1.0 / (weights_ref[rows, cols] + object_regular)
             back = (before_ref[rows, cols] + object_regular) * scale
-            parts = [decode(ref, start, tile_rows, col) for ref in (left_ref, above_ref, diag_ref)]
+            parts = decode(left_ref, start, tile_rows, col)
             for comp in range(2):
-                coded = parts[0][comp] + parts[1][comp] + parts[2][comp]
-                old = object_regular * current_ref[comp, rows, cols] + own_ref[comp, rows, cols]
-                out_ref[comp, rows, cols] = old * scale + coded * back
+                old = object_regular * scale * current_ref[comp, rows, cols]
+                out_ref[comp, rows, cols] = old + (own_ref[comp, rows, cols] + parts[comp]) * back
 
 
 def shape(dims, dtype=f32):
@@ -737,13 +765,13 @@
         kernel(*ins, *given)
 
     fixed_outs = [
-        pltpu.HBM(out.shape, out.dtype) if spec is HBM else out
+        pltpu.HBM(out.shape, out.dtype) if spec is HBM else pltpu.VMEM(out.shape, out.dtype) if spec is PIN else out
         for out, spec in zip(outs if several else (outs,), out_specs if several else (out_specs,))
     ]
-    stay = [spec is LOAD or spec is HBM for spec in in_specs]
+    places = [pltpu.HBM if spec is LOAD or spec is HBM else pltpu.VMEM if spec is PIN else None for spec in in_specs]
 
     def called(*args):
-        args = [pltpu.with_memory_space_constraint(arg, pltpu.HBM) if kept else arg for arg, kept in zip(args, stay)]
+        args = [arg if place is None else pltpu.with_memory_space_constraint(arg, place) for arg, place in zip(args, places)]
         own = [pltpu.VMEM(args[k].shape, args[k].dtype) for k in loaded]
         if loaded:
             own.append(pltpu.SemaphoreType.DMA((len(loaded),)))
@@ -766,28 +794,21 @@
     return lax.ppermute(value, axis, [(source, source + steps) for source in range(leading, last)])
 
 
-def passed_both(value, row_steps, col_steps):
-    rows, cols = lax.axis_size("row"), lax.axis_size("col")
-    pairs = []
-    for r in range(rows):
-        for c in range(cols):
-            if 0 <= r + row_steps < rows and 0 <= c + col_steps < cols:
-                pairs.append((r * cols + c, (r + row_steps) * cols + c + col_steps))
-    return lax.ppermute(value, ("row", "col"), pairs)
-
-
-def probe_update(me, probe, numer, kind, *after):
+def probe_update(me, probe, numer, kind, weights=None, fold=None):
     cols, order = lax.axis_size("col"), probe.shape[1]
     rows = order // cols
+    before_sum = [] if weights is None else [weights]
+    before_update = [] if fold is None else [fold]
     parts = lax.all_to_all(numer, "col", split_axis=0, concat_axis=0, tiled=True)
     total = call(
-        functools.partial(sums_kernel, rows), shape((lax.axis_size("row"), sums_rows(rows), order), jnp.int32), VMEM, [VMEM], [], 1 << 26,
-    )(parts)
+        functools.partial(sums_kernel, rows), shape((lax.axis_size("row"), sums_rows(rows), order), jnp.int32), VMEM,
+        [VMEM] + [HBM] * len(before_sum), [], 1 << 26,
+    )(parts, *before_sum)
     parts = lax.all_to_all(total, "row", split_axis=0, concat_axis=0, tiled=True)
     fresh = call(
         functools.partial(update_kernel, rows), shape((cols, rows + SUBLANES, order), jnp.int32), VMEM,
-        [SMEM, kind, VMEM] + [spec for spec, _ in after], [], 1 << 26,
-    )(me, probe, parts, *[value for _, value in after])
+        [SMEM, kind, VMEM] + [FREE] * len(before_update), [], 1 << 26,
+    )(me, probe, parts, *before_update)
     return total, lax.all_to_all(fresh, "col", split_axis=0, concat_axis=0, tiled=True)
 
 
@@ -837,10 +858,10 @@
         capacity * one_pattern // 2,
     )(pos, me, obj, right, below, diag, probe, turns, twiddles)
 
-    share, top, bottom, numer, sorted_amps = call(
+    share, numer, sorted_amps = call(
         functools.partial(second_half_kernel, dims),
-        (shape(wide), coded_row, coded_row, shares, shape((capacity, order, order), bf16)),
-        (HBM, VMEM, VMEM, VMEM, HBM),
+        (shape(wide), shares, shape((capacity, order, order), bf16)),
+        (HBM, VMEM, HBM),
         [SMEM, SMEM, LOAD, LOAD, VMEM, LOAD, HBM, HBM] + [LOAD] * 3,
         [pltpu.VMEM(wide, f32)] + work_scratch(order)
         + [pltpu.VMEM(window, f32), pltpu.VMEM((capacity,) + window, f32), pltpu.VMEM((capacity, order, order), bf16), pltpu.VMEM((capacity, order, order), bf16)]
@@ -848,32 +869,35 @@
         capacity * one_pattern // 2,
     )(pos, me, ext, probe, power, weights_old, far, incoming, turns, twiddles, sorting)
 
+    top, bottom = call(functools.partial(rows_code_kernel, dims), (coded_row, coded_row), (VMEM, VMEM), [LOAD], [], 1 << 26)(share)
     from_above = passed_along(bottom, "row", 1)
     from_below = passed_along(top, "row", -1)
     total, chunks = probe_update(me, probe, numer, LOAD)
     sums, to_left, to_right = call(
-        functools.partial(rows_sum_kernel, dims), (shape(wide), coded_col, coded_col), (VMEM,) * 3, [LOAD, VMEM, VMEM, FREE], [], 1 << 26,
+        functools.partial(rows_sum_kernel, dims), (shape(wide), coded_col, coded_col), (PIN, VMEM, VMEM), [LOAD, VMEM, VMEM, FREE], [], 1 << 26,
     )(share, from_above, from_below, total)
     from_left = passed_along(to_right, "col", 1)
     from_right = passed_along(to_left, "col", -1)
 
-    current, own, to_right, to_below, to_diag, numer, probe_now = call(
-        functools.partial(whole_kernel, dims), (shape(tile), shape(tile), coded_tile, coded_tile, coded_tile, shares, shape(window)), (HBM,) + (VMEM,) * 6,
-        [SMEM, SMEM, LOAD] + [VMEM] * 3 + [LOAD, VMEM, HBM, LOAD, LOAD],
+    current, top, bottom, numer, probe_now = call(
+        functools.partial(whole_kernel, dims), (shape(tile), shape((2, tile_rows, 2 * tile_cols)), coded_row, shares, shape(window)), (HBM, HBM) + (VMEM,) * 3,
+        [SMEM, SMEM, LOAD, PIN, VMEM, VMEM, LOAD, VMEM, HBM, LOAD, LOAD],
         [pltpu.VMEM(wide, f32), pltpu.VMEM(wide, f32)] + work_scratch(order)
         + [pltpu.VMEM((3, order, order), f32), pltpu.VMEM((2,) + window, f32), pltpu.VMEM((capacity, order, order), bf16)]
-        + list_scratch(capacity) + [pltpu.SemaphoreType.DMA((capacity,)), pltpu.SemaphoreType.DMA],
+        + list_scratch(capacity) + [pltpu.SemaphoreType.DMA((capacity,)), pltpu.SemaphoreType.DMA, pltpu.SemaphoreType.DMA],
         capacity * one_pattern,
     )(pos, me, ext, sums, from_left, from_right, weights_old, chunks, sorted_amps, turns, twiddles)
 
+    from_above = passed_along(bottom, "row", 1)
+    weights_new = weights(probe_now, 1, VMEM)
+    own, to_right = call(
+        functools.partial(fold_kernel, dims), (shape(tile), coded_tile), (HBM, VMEM), [LOAD, VMEM], [pltpu.VMEM(tile, f32), pltpu.SemaphoreType.DMA], 1 << 26,
+    )(top, from_above)
     from_left = passed_along(to_right, "col", 1)
-    from_above = passed_along(to_below, "row", 1)
-    from_diag = passed_both(to_diag, 1, 1)
-    weights_new = weights(probe_now, 1, VMEM)
-    new_object = call(functools.partial(object_kernel, dims), shape(tile), VMEM, [LOAD] + [VMEM] * 4 + [LOAD, LOAD], [], 1 << 26)(
-        current, own, from_left, from_above, from_diag, weights_old, weights_new
+    new_object = call(functools.partial(object_kernel, dims), shape(tile), VMEM, [LOAD, LOAD, VMEM, LOAD, LOAD], [], 1 << 26)(
+        current, own, from_left, weights_old, weights_new
     )
-    _, chunks = probe_update(me, probe_now, numer, VMEM, (HBM, weights_new), (FREE, from_left), (FREE, from_above), (FREE, from_diag))
+    _, chunks = probe_update(me, probe_now, numer, VMEM, weights_new, to_right)
     new_probe = call(probe_kernel, shape(window), VMEM, [VMEM], [], 1 << 26)(chunks)
     return new_object, new_probe
 

time: 165 us -> 172 us (1.042)
  the two profiles are of different devices: /device:TPU:0 before, /device:TPU:4 now
where the time goes in v7:
time: 172 us; the launch traced here: 168 us
  Pallas kernels  59.9 us (35%)
  starting transfers between devices  49.4 us (29%)
  waiting for transfers between devices  28.9 us (17%)
  blocking collectives  24.1 us (14%)
  local copies, waits for them, and re-layouts  5 us (3%)
    pallas_call x16, Pallas kernels, called(): pl.pallas_call(body, out_shape=tuple(fixed_outs) if several else fixed_ou...  59.9 us
    ppermute x9, starting transfers between devices, passed_along(): lax.ppermute(value, axis, [(source, source + steps) for source in range(l...  21.3 us
    ppermute x9, waiting for transfers between devices, passed_along(): lax.ppermute(value, axis, [(source, source + steps) for source in range(l...  14.4 us
    all_to_all x1, blocking collectives, probe_update(): lax.all_to_all(fresh, 'col', split_axis=0, concat_axis=0, tiled=True)  12.7 us
    all_to_all x1, blocking collectives, probe_update(): lax.all_to_all(numer, 'col', split_axis=0, concat_axis=0, tiled=True)  11.4 us
    all_to_all x2, starting transfers between devices, probe_update(): lax.all_to_all(total, 'row', split_axis=0, concat_axis=0, tiled=True)  10.6 us
    all_to_all x1, starting transfers between devices, probe_update(): lax.all_to_all(numer, 'col', split_axis=0, concat_axis=0, tiled=True)  8.75 us
    all_to_all x1, waiting for transfers between devices, local(): lax.all_to_all(outgoing, 'col', split_axis=0, concat_axis=0, tiled=True)  8.21 us
  transfers between devices with their start and end apart: 14, of which 7 were waited for; matrix products, arithmetic and copies ran while one was open for 0% of the time, Pallas kernels for 18%

profile of v7, /device:TPU:4, one launch (start us, length us, event | category | flops | bytes accessed | tf_op | source)
XLA Modules:
  0.0 168.2 jit_solution(1712307606489115572)
XLA Ops:
  3.2 2.8 %collective-permute-start = (s32[264,256]{1,0:T(8,128)S(1)}, s32[264,256]{1,0:T(8,128)S(1)}, u32[]{:S(2)}, u32[]{:S(2)}) collective-permute-start(s32[264,256]{1,0:T(8,128)S(1)} %shard_map.86), channel_id=1, source_target_pairs={{1,0},{2,1},{3,2},{4,3},{5,4},{6,5},{7,6},{9,8},{10,9},{11,10},{12... | collective-permute-start | bytes 811016 | tf_op jit(solution)/shard_map/ppermute | solution.py:794
  6.0 5.9 %collective-permute-done.1.refs_4_ = s32[264,256]{1,0:T(8,128)S(1)} collective-permute-done((s32[264,256]{1,0:T(8,128)S(1)}, s32[264,256]{1,0:T(8,128)S(1)}, u32[]{:S(2)}, u32[]{:S(2)}) %collective-permute-start.1) | collective-permute-done | bytes 270368 | tf_op jit(solution)/shard_map/ppermute | solution.py:794
  12.7 2.5 %shard_map.89 = bf16[16,256,256]{2,1,0:T(8,128)(2,1)} custom-call(s32[256]{0:T(256)S(1)} %bitcast.5, s32[2]{0:T(128)S(1)} %pad_add_fusion.refs_1_.refs_0_, bf16[4,256,256]{2,1,0:T(8,128)(2,1)} %refs_2_.5, s32[264,256]{1,0:T(8,128)S(1)} %collective-permute-done.refs_3_, s32[264,256]{1,0:T(8,128)S(1)} %collective-permute-done.1.refs_4_), custom_call_target="tpu_custom_call" | custom-call | flops 1048576 | bytes 8388608 | tf_op jit(solution)/shard_map/pallas_call | solution.py:778
  15.1 4.2 %all-to-all-start = ((bf16[16,256,256]{2,1,0:T(8,128)(2,1)}), bf16[16,256,256]{2,1,0:T(8,128)(2,1)S(1)}, u32[]{:S(2)}, u32[]{:S(2)}) async-start(bf16[16,256,256]{2,1,0:T(8,128)(2,1)} %shard_map.89), calls=%async_computation | async-start | bytes 4194304 | tf_op jit(solution)/shard_map/all_to_all | solution.py:843
  20.6 8.4 %shard_map.88.refs_5_.refs_6_.refs_3_ = f32[512,512]{1,0:T(8,128)} custom-call(s32[256]{0:T(256)S(1)} %bitcast.6, s32[2]{0:T(128)S(1)} %pad_add_fusion.refs_1_.refs_0_, f32[2,256,256]{2,1,0:T(8,128)} %refs_1_.1), custom_call_target="tpu_custom_call" | custom-call | flops 8589934592 | bytes 8388608 | tf_op jit(solution)/shard_map/pallas_call | solution.py:778
  29.8 6.5 %shard_map.87 = (f32[8,2,256,256]{3,2,1,0:T(8,128)}, f32[256,256]{1,0:T(8,128)S(1)}, f32[2,512,512]{2,1,0:T(8,128)}) custom-call(s32[256]{0:T(256)S(1)} %bitcast.7, s32[2]{0:T(128)S(1)} %pad_add_fusion.refs_1_.refs_0_, f32[2,256,256]{2,1,0:T(8,128)} %refs_2_.3, s32[264,256]{1,0:T(8,128)S(1)} %collective-permute-done.refs_3_, ...), custom_call_target="tpu_custom_call" | custom-call | flops 3221225472 | bytes 8388608 | tf_op jit(solution)/shard_map/pallas_call | solution.py:778
  36.3 8.2 %all-to-all-done.refs_7_ = bf16[16,256,256]{2,1,0:T(8,128)(2,1)S(1)} async-done(((bf16[16,256,256]{2,1,0:T(8,128)(2,1)}), bf16[16,256,256]{2,1,0:T(8,128)(2,1)S(1)}, u32[]{:S(2)}, u32[]{:S(2)}) %all-to-all-start) | async-done | bytes 2097184 | tf_op jit(solution)/shard_map/all_to_all | solution.py:843
  44.5 1.4 copy-done.4
  45.9 9.9 %shard_map.90 = (f32[2,512,512]{2,1,0:T(8,128)}, s32[8,56,256]{2,1,0:T(8,128)S(1)}, bf16[8,256,256]{2,1,0:T(8,128)(2,1)}) custom-call(s32[256]{0:T(256)S(1)} %bitcast.8, s32[2]{0:T(128)S(1)} %pad_add_fusion.refs_1_.refs_0_, f32[2,512,512]{2,1,0:T(8,128)} %get-tuple-element.20.refs_2_, f32[2,256,256]{2,1,0:T(8,128)} %refs_1_.1, ...), custom_call_target="tpu_custom_call" | custom-call | flops 3221225472 | bytes 8388608 | tf_op jit(solution)/shard_map/pallas_call | solution.py:778
  55.8 2.1 %shard_map.91 = (s32[264,512]{1,0:T(8,128)S(1)}, s32[264,512]{1,0:T(8,128)S(1)}) custom-call(f32[2,512,512]{2,1,0:T(8,128)} %get-tuple-element.23.refs_0_), custom_call_target="tpu_custom_call" | custom-call | flops 67108864 | bytes 8388608 | tf_op jit(solution)/shard_map/pallas_call | solution.py:778
  58.0 3.5 %collective-permute-start.3 = (s32[264,512]{1,0:T(8,128)S(1)}, s32[264,512]{1,0:T(8,128)S(1)}, u32[]{:S(2)}, u32[]{:S(2)}) collective-permute-start(s32[264,512]{1,0:T(8,128)S(1)} %get-tuple-element.24), channel_id=1, source_target_pairs={{0,8},{8,16},{16,24},{1,9},{9,17},{17,25},{2,10},{10,18},{18,26},{... | collective-permute-start | bytes 1622024 | tf_op jit(solution)/shard_map/ppermute | solution.py:794
  62.8 11.4 %all_to_all.35.refs_0_ = s32[8,56,256]{2,1,0:T(8,128)S(1)} all-to-all(s32[8,56,256]{2,1,0:T(8,128)S(1)} %get-tuple-element.26), channel_id=1, replica_groups=mesh['row'=4,'col'=8] {'col'}, dimensions={0} | all-to-all | bytes 917504 | tf_op jit(solution)/shard_map/all_to_all | solution.py:802
  75.1 5.3 %all-to-all-start.2 = ((s32[4,56,256]{2,1,0:T(8,128)}), s32[4,56,256]{2,1,0:T(8,128)S(1)}, u32[]{:S(2)}, u32[]{:S(2)}) async-start(s32[4,56,256]{2,1,0:T(8,128)} %shard_map.92.refs_3_), calls=%async_computation.2 | async-start | bytes 458752 | tf_op jit(solution)/shard_map/all_to_all | solution.py:807
  80.3 2.5 %shard_map.93 = (f32[2,512,512]{2,1,0:T(8,128)S(1)}, s32[528,256]{1,0:T(8,128)S(1)}, s32[528,256]{1,0:T(8,128)S(1)}) custom-call(f32[2,512,512]{2,1,0:T(8,128)} %get-tuple-element.23.refs_0_, s32[264,512]{1,0:T(8,128)S(1)} %collective-permute-done.3.refs_1_, s32[264,512]{1,0:T(8,128)S(1)} %collective-permute-done.4.refs_2_, s32[4,56,256]{2,1,0:T(8,128)} %shard_map.92.refs_3_), custom_call_target="tpu_custom_call" | custom-call | flops 67108864 | bytes 8388608 | tf_op jit(solution)/shard_map/pallas_call | solution.py:778
  82.9 1.3 copy-done.2
  84.2 1.9 %collective-permute-start.5 = (s32[528,256]{1,0:T(8,128)S(1)}, s32[528,256]{1,0:T(8,128)S(1)}, u32[]{:S(2)}, u32[]{:S(2)}) collective-permute-start(s32[528,256]{1,0:T(8,128)S(1)} %get-tuple-element.28), channel_id=1, source_target_pairs={{0,1},{1,2},{2,3},{3,4},{4,5},{5,6},{6,7},{8,9},{9,10},{10,11},{11... | collective-permute-start | bytes 1622024 | tf_op jit(solution)/shard_map/ppermute | solution.py:794
  86.1 4.5 %collective-permute-start.6 = (s32[528,256]{1,0:T(8,128)S(1)}, s32[528,256]{1,0:T(8,128)S(1)}, u32[]{:S(2)}, u32[]{:S(2)}) collective-permute-start(s32[528,256]{1,0:T(8,128)S(1)} %get-tuple-element.29), channel_id=1, source_target_pairs={{1,0},{2,1},{3,2},{4,3},{5,4},{6,5},{7,6},{9,8},{10,9},{11,10},{12... | collective-permute-start | bytes 1622024 | tf_op jit(solution)/shard_map/ppermute | solution.py:794
  90.7 1.7 %shard_map.94 = s32[8,40,256]{2,1,0:T(8,128)S(1)} custom-call(s32[2]{0:T(128)S(1)} %pad_add_fusion.refs_1_.refs_0_, f32[2,256,256]{2,1,0:T(8,128)} %refs_1_.1, s32[4,56,256]{2,1,0:T(8,128)S(1)} %all-to-all-done.2.refs_2_), custom_call_target="tpu_custom_call" | custom-call | flops 67108864 | bytes 8388608 | tf_op jit(solution)/shard_map/pallas_call | solution.py:778
  92.4 12.7 %all_to_all.36.refs_7_ = s32[8,40,256]{2,1,0:T(8,128)S(1)} all-to-all(s32[8,40,256]{2,1,0:T(8,128)S(1)} %shard_map.94), channel_id=1, replica_groups=mesh['row'=4,'col'=8] {'col'}, dimensions={0} | all-to-all | bytes 655360 | tf_op jit(solution)/shard_map/all_to_all | solution.py:812
  105.1 1.6 copy-done.3
  106.7 11.8 %shard_map.95 = (f32[2,256,256]{2,1,0:T(8,128)}, f32[2,256,512]{2,1,0:T(8,128)}, s32[264,512]{1,0:T(8,128)S(1)}, s32[8,56,256]{2,1,0:T(8,128)}, f32[2,256,256]{2,1,0:T(8,128)S(1)}) custom-call(s32[256]{0:T(256)S(1)} %bitcast.9, s32[2]{0:T(128)S(1)} %pad_add_fusion.refs_1_.refs_0_, f32[2,512,512]{2,1,0:T(8,128)} %get-tuple-element.20.refs_2_, ...), custom_call_target="tpu_custom_call" | custom-call | flops 6442450944 | bytes 8388608 | tf_op jit(solution)/shard_map/pallas_call | solution.py:778
  118.5 8.8 %all-to-all-start.4 = ((s32[8,56,256]{2,1,0:T(8,128)}), s32[8,56,256]{2,1,0:T(8,128)S(1)}, u32[]{:S(2)}, u32[]{:S(2)}) async-start(s32[8,56,256]{2,1,0:T(8,128)} %get-tuple-element.37), calls=%async_computation.4 | async-start | bytes 917504 | tf_op jit(solution)/shard_map/all_to_all | solution.py:802
  127.2 2.7 %collective-permute-start.7 = (s32[264,512]{1,0:T(8,128)S(1)}, s32[264,512]{1,0:T(8,128)S(1)}, u32[]{:S(2)}, u32[]{:S(2)}) collective-permute-start(s32[264,512]{1,0:T(8,128)S(1)} %get-tuple-element.33), channel_id=1, source_target_pairs={{0,8},{8,16},{16,24},{1,9},{9,17},{17,25},{2,10},{10,18},{18,26},{... | collective-permute-start | bytes 1622024 | tf_op jit(solution)/shard_map/ppermute | solution.py:794
  129.9 4.5 %shard_map.97.refs_4_.refs_1_ = f32[256,256]{1,0:T(8,128)} custom-call(s32[256]{0:T(256)S(1)} %bitcast.10, s32[2]{0:T(128)S(1)} %pad_add_fusion.refs_1_.refs_0_, f32[2,256,256]{2,1,0:T(8,128)S(1)} %get-tuple-element.36.refs_2_.refs_1_), custom_call_target="tpu_custom_call" | custom-call | flops 8589934592 | bytes 8388608 | tf_op jit(solution)/shard_map/pallas_call | solution.py:778
  135.7 5.3 %all-to-all-start.5 = ((s32[4,56,256]{2,1,0:T(8,128)}), s32[4,56,256]{2,1,0:T(8,128)S(1)}, u32[]{:S(2)}, u32[]{:S(2)}) async-start(s32[4,56,256]{2,1,0:T(8,128)} %shard_map.99), calls=%async_computation.5 | async-start | bytes 458752 | tf_op jit(solution)/shard_map/all_to_all | solution.py:807
  141.7 2.1 %shard_map.96 = (f32[2,256,256]{2,1,0:T(8,128)}, s32[264,256]{1,0:T(8,128)S(1)}) custom-call(f32[2,256,512]{2,1,0:T(8,128)} %get-tuple-element.32.refs_0_, s32[264,512]{1,0:T(8,128)S(1)} %collective-permute-done.7.refs_1_), custom_call_target="tpu_custom_call" | custom-call | flops 67108864 | bytes 8388608 | tf_op jit(solution)/shard_map/pallas_call | solution.py:778
  143.8 5.9 %all-to-all-done.5.refs_2_ = s32[4,56,256]{2,1,0:T(8,128)S(1)} async-done(((s32[4,56,256]{2,1,0:T(8,128)}), s32[4,56,256]{2,1,0:T(8,128)S(1)}, u32[]{:S(2)}, u32[]{:S(2)}) %all-to-all-start.5) | async-done | bytes 229408 | tf_op jit(solution)/shard_map/all_to_all | solution.py:807
  149.8 1.4 shard_map.100
  151.2 4.5 %all-to-all-start.6 = ((s32[8,40,256]{2,1,0:T(8,128)}), s32[8,40,256]{2,1,0:T(8,128)S(1)}, u32[]{:S(2)}, u32[]{:S(2)}) async-start(s32[8,40,256]{2,1,0:T(8,128)} %shard_map.100), calls=%async_computation.6 | async-start | bytes 655360 | tf_op jit(solution)/shard_map/all_to_all | solution.py:812
  155.7 2.0 %collective-permute-start.8 = (s32[264,256]{1,0:T(8,128)S(1)}, s32[264,256]{1,0:T(8,128)S(1)}, u32[]{:S(2)}, u32[]{:S(2)}) collective-permute-start(s32[264,256]{1,0:T(8,128)S(1)} %get-tuple-element.35.refs_3_), channel_id=1, source_target_pairs={{0,1},{1,2},{2,3},{3,4},{4,5},{5,6},{6,7},{8,9},{9,10},{10,11},{11... | collective-permute-start | bytes 811016 | tf_op jit(solution)/shard_map/ppermute | solution.py:794
  157.7 7.0 %collective-permute-done.8.refs_2_ = s32[264,256]{1,0:T(8,128)S(1)} collective-permute-done((s32[264,256]{1,0:T(8,128)S(1)}, s32[264,256]{1,0:T(8,128)S(1)}, u32[]{:S(2)}, u32[]{:S(2)}) %collective-permute-start.8) | collective-permute-done | bytes 270368 | tf_op jit(solution)/shard_map/ppermute | solution.py:794
  164.7 2.6 %shard_map.98 = f32[2,256,256]{2,1,0:T(8,128)} custom-call(f32[2,256,256]{2,1,0:T(8,128)} %get-tuple-element.31.refs_0_, f32[2,256,256]{2,1,0:T(8,128)} %get-tuple-element.34.refs_1_, s32[264,256]{1,0:T(8,128)S(1)} %collective-permute-done.8.refs_2_, f32[512,512]{1,0:T(8,128)} %shard_map.88.refs_5_.refs_6_.refs_3_, f32[256,256]{1,0:T(8,128)} %shard_map.97.refs_4_.refs_1_), custom_call_target="tpu_custom_call" | custom-call | flops 67108864 | bytes 8388608 | tf_op jit(solution)/shard_map/pallas_call | solution.py:778
  (25 shorter events, 10.3 us)
Async XLA Ops:
  1.9 10.1 %collective-permute-start.1 = (s32[264,256]{1,0:T(8,128)S(1)}, s32[264,256]{1,0:T(8,128)S(1)}, u32[]{:S(2)}, u32[]{:S(2)}) collective-permute-start(s32[264,256]{1,0:T(8,128)S(1)} %shard_map.86), channel_id=1, source_target_pairs={{8,0},{16,8},{24,16},{9,1},{17,9},{25,17},{10,2},{18,10},{26,18},{... | collective-permute-start | bytes 811016 | tf_op jit(solution)/shard_map/ppermute | solution.py:794
  3.2 8.8 %collective-permute-start = (s32[264,256]{1,0:T(8,128)S(1)}, s32[264,256]{1,0:T(8,128)S(1)}, u32[]{:S(2)}, u32[]{:S(2)}) collective-permute-start(s32[264,256]{1,0:T(8,128)S(1)} %shard_map.86), channel_id=1, source_target_pairs={{1,0},{2,1},{3,2},{4,3},{5,4},{6,5},{7,6},{9,8},{10,9},{11,10},{12... | collective-permute-start | bytes 811016 | tf_op jit(solution)/shard_map/ppermute | solution.py:794
  12.0 0.7 copy-start
  15.1 29.4 %all-to-all-start = ((bf16[16,256,256]{2,1,0:T(8,128)(2,1)}), bf16[16,256,256]{2,1,0:T(8,128)(2,1)S(1)}, u32[]{:S(2)}, u32[]{:S(2)}) async-start(bf16[16,256,256]{2,1,0:T(8,128)(2,1)} %shard_map.89), calls=%async_computation | async-start | bytes 4194304 | tf_op jit(solution)/shard_map/all_to_all | solution.py:843
  19.4 10.4 %collective-permute-start.2 = (s32[264,256]{1,0:T(8,128)S(1)}, s32[264,256]{1,0:T(8,128)S(1)}, u32[]{:S(2)}, u32[]{:S(2)}) collective-permute-start(s32[264,256]{1,0:T(8,128)S(1)} %collective-permute-done.refs_3_), channel_id=1, source_target_pairs={{8,0},{16,8},{24,16},{9,1},{17,9},{25,17},{10,2},{18,10},{26,18},{... | collective-permute-start | bytes 811016 | tf_op jit(solution)/shard_map/ppermute | solution.py:794
  44.5 1.4 copy-start.4
  58.0 22.4 %collective-permute-start.3 = (s32[264,512]{1,0:T(8,128)S(1)}, s32[264,512]{1,0:T(8,128)S(1)}, u32[]{:S(2)}, u32[]{:S(2)}) collective-permute-start(s32[264,512]{1,0:T(8,128)S(1)} %get-tuple-element.24), channel_id=1, source_target_pairs={{0,8},{8,16},{16,24},{1,9},{9,17},{17,25},{2,10},{10,18},{18,26},{... | collective-permute-start | bytes 1622024 | tf_op jit(solution)/shard_map/ppermute | solution.py:794
  61.5 18.9 %collective-permute-start.4 = (s32[264,512]{1,0:T(8,128)S(1)}, s32[264,512]{1,0:T(8,128)S(1)}, u32[]{:S(2)}, u32[]{:S(2)}) collective-permute-start(s32[264,512]{1,0:T(8,128)S(1)} %get-tuple-element.25), channel_id=1, source_target_pairs={{8,0},{16,8},{24,16},{9,1},{17,9},{25,17},{10,2},{18,10},{26,18},{... | collective-permute-start | bytes 1622024 | tf_op jit(solution)/shard_map/ppermute | solution.py:794
  75.1 15.6 %all-to-all-start.2 = ((s32[4,56,256]{2,1,0:T(8,128)}), s32[4,56,256]{2,1,0:T(8,128)S(1)}, u32[]{:S(2)}, u32[]{:S(2)}) async-start(s32[4,56,256]{2,1,0:T(8,128)} %shard_map.92.refs_3_), calls=%async_computation.2 | async-start | bytes 458752 | tf_op jit(solution)/shard_map/all_to_all | solution.py:807
  80.3 24.8 %copy-start.1 = (s32[128,2]{0,1:T(2,128)S(1)}, s32[128,2]{0,1:T(2,128)}, u32[]{:S(2)}) copy-start(s32[128,2]{0,1:T(2,128)} %param.10) | copy-start | bytes 3076
  82.9 1.3 copy-start.2
  84.2 20.9 %collective-permute-start.5 = (s32[528,256]{1,0:T(8,128)S(1)}, s32[528,256]{1,0:T(8,128)S(1)}, u32[]{:S(2)}, u32[]{:S(2)}) collective-permute-start(s32[528,256]{1,0:T(8,128)S(1)} %get-tuple-element.28), channel_id=1, source_target_pairs={{0,1},{1,2},{2,3},{3,4},{4,5},{5,6},{6,7},{8,9},{9,10},{10,11},{11... | collective-permute-start | bytes 1622024 | tf_op jit(solution)/shard_map/ppermute | solution.py:794
  86.1 19.0 %collective-permute-start.6 = (s32[528,256]{1,0:T(8,128)S(1)}, s32[528,256]{1,0:T(8,128)S(1)}, u32[]{:S(2)}, u32[]{:S(2)}) collective-permute-start(s32[528,256]{1,0:T(8,128)S(1)} %get-tuple-element.29), channel_id=1, source_target_pairs={{1,0},{2,1},{3,2},{4,3},{5,4},{6,5},{7,6},{9,8},{10,9},{11,10},{12... | collective-permute-start | bytes 1622024 | tf_op jit(solution)/shard_map/ppermute | solution.py:794
  105.1 1.6 copy-start.3
  118.5 16.3 %all-to-all-start.4 = ((s32[8,56,256]{2,1,0:T(8,128)}), s32[8,56,256]{2,1,0:T(8,128)S(1)}, u32[]{:S(2)}, u32[]{:S(2)}) async-start(s32[8,56,256]{2,1,0:T(8,128)} %get-tuple-element.37), calls=%async_computation.4 | async-start | bytes 917504 | tf_op jit(solution)/shard_map/all_to_all | solution.py:802
  127.2 14.5 %collective-permute-start.7 = (s32[264,512]{1,0:T(8,128)S(1)}, s32[264,512]{1,0:T(8,128)S(1)}, u32[]{:S(2)}, u32[]{:S(2)}) collective-permute-start(s32[264,512]{1,0:T(8,128)S(1)} %get-tuple-element.33), channel_id=1, source_target_pairs={{0,8},{8,16},{16,24},{1,9},{9,17},{17,25},{2,10},{10,18},{18,26},{... | collective-permute-start | bytes 1622024 | tf_op jit(solution)/shard_map/ppermute | solution.py:794
  135.7 14.1 %all-to-all-start.5 = ((s32[4,56,256]{2,1,0:T(8,128)}), s32[4,56,256]{2,1,0:T(8,128)S(1)}, u32[]{:S(2)}, u32[]{:S(2)}) async-start(s32[4,56,256]{2,1,0:T(8,128)} %shard_map.99), calls=%async_computation.5 | async-start | bytes 458752 | tf_op jit(solution)/shard_map/all_to_all | solution.py:807
  151.2 16.2 %all-to-all-start.6 = ((s32[8,40,256]{2,1,0:T(8,128)}), s32[8,40,256]{2,1,0:T(8,128)S(1)}, u32[]{:S(2)}, u32[]{:S(2)}) async-start(s32[8,40,256]{2,1,0:T(8,128)} %shard_map.100), calls=%async_computation.6 | async-start | bytes 655360 | tf_op jit(solution)/shard_map/all_to_all | solution.py:812
  155.7 9.1 %collective-permute-start.8 = (s32[264,256]{1,0:T(8,128)S(1)}, s32[264,256]{1,0:T(8,128)S(1)}, u32[]{:S(2)}, u32[]{:S(2)}) collective-permute-start(s32[264,256]{1,0:T(8,128)S(1)} %get-tuple-element.35.refs_3_), channel_id=1, source_target_pairs={{0,1},{1,2},{2,3},{3,4},{4,5},{5,6},{6,7},{8,9},{9,10},{10,11},{11... | collective-permute-start | bytes 811016 | tf_op jit(solution)/shard_map/ppermute | solution.py:794

commit v8 on v7

--- a/solution.py
+++ b/solution.py
@@ -479,12 +479,12 @@
             out_ref[k, :, cols] = out_ref[0, :, cols]
 
 
-def update_kernel(rows, me_ref, probe_ref, parts_ref, *refs):
+def update_kernel(rows, count, me_ref, probe_ref, *refs):
     out_ref = refs[-1]
     first = pl.multiple_of(me_ref[1] * rows, SUBLANES)
     for col in range(0, out_ref.shape[2], LANES):
         cols = pl.ds(col, LANES)
-        u_re, u_im, v = added([decode_sums(parts_ref.at[k], cols, rows) for k in range(parts_ref.shape[0])])
+        u_re, u_im, v = added([decode_sums(ref.at[k], cols, rows) for ref in refs[:count] for k in range(ref.shape[0])])
         scale = 1.0 / (v + probe_regular)
         re = (probe_ref[0, pl.ds(first, rows), cols] + u_re) * scale
         im = (probe_ref[1, pl.ds(first, rows), cols] + u_im) * scale
@@ -609,7 +609,7 @@
     encode(lambda comp, at, cols: share_ref[comp, pl.ds(tile_rows + at.start, at.size), cols], bottom_out, tile_rows, 0, tile_rows)
 
 
-def rows_sum_kernel(dims, share_ref, above_ref, below_ref, after_ref, sum_out, left_out, right_out):
+def rows_sum_kernel(dims, share_ref, above_ref, below_ref, after_ref, sum_out, left_out, right_out, sem):
     tile_rows, tile_cols = dims[:2]
     for i, ref in enumerate((above_ref, below_ref)):
         for col in range(0, 2 * tile_cols, LANES):
@@ -617,14 +617,17 @@
                 rows, cols = pl.ds(i * tile_rows + start, CHUNK), pl.ds(col, LANES)
                 parts = decode(ref, start, tile_rows, col)
                 for comp in range(2):
-                    sum_out[comp, rows, cols] = share_ref[comp, rows, cols] + parts[comp]
+                    share_ref[comp, rows, cols] += parts[comp]
+    keep = pltpu.make_async_copy(share_ref, sum_out, sem)
+    keep.start()
     for j, ref in enumerate((left_out, right_out)):
         for i in range(2):
 
             def read(comp, at, cols, i=i, j=j):
-                return sum_out[comp, pl.ds(i * tile_rows + at.start, at.size), pl.ds(j * tile_cols + cols.start, cols.size)]
+                return share_ref[comp, pl.ds(i * tile_rows + at.start, at.size), pl.ds(j * tile_cols + cols.start, cols.size)]
 
             encode(read, ref, tile_rows, i * tile_rows, 2 * tile_rows + i * SUBLANES)
+    keep.wait()
 
 
 def whole_kernel(dims, pos_ref, me_ref, old_ref, sum_ref, from_left_ref, from_right_ref, weights_ref,
@@ -794,21 +797,27 @@
     return lax.ppermute(value, axis, [(source, source + steps) for source in range(leading, last)])
 
 
-def probe_update(me, probe, numer, kind, weights=None, fold=None):
+def swapped(value, axis, mask):
+    return lax.ppermute(value, axis, [(k, k ^ mask) for k in range(lax.axis_size(axis))])
+
+
+def probe_update(me, probe, numer, kind, at_once, before_sum, before_update):
     cols, order = lax.axis_size("col"), probe.shape[1]
     rows = order // cols
-    before_sum = [] if weights is None else [weights]
-    before_update = [] if fold is None else [fold]
     parts = lax.all_to_all(numer, "col", split_axis=0, concat_axis=0, tiled=True)
+    blocks = lax.axis_size("row") if at_once else 1
     total = call(
-        functools.partial(sums_kernel, rows), shape((lax.axis_size("row"), sums_rows(rows), order), jnp.int32), VMEM,
-        [VMEM] + [HBM] * len(before_sum), [], 1 << 26,
-    )(parts, *before_sum)
-    parts = lax.all_to_all(total, "row", split_axis=0, concat_axis=0, tiled=True)
+        functools.partial(sums_kernel, rows), shape((blocks, sums_rows(rows), order), jnp.int32), VMEM,
+        [VMEM] + [spec for spec, _ in before_sum], [], 1 << 26,
+    )(parts, *[value for _, value in before_sum])
+    if at_once:
+        totals = [lax.all_to_all(total, "row", split_axis=0, concat_axis=0, tiled=True)]
+    else:
+        totals = [total] + [swapped(total, "row", mask) for mask in range(1, lax.axis_size("row"))]
     fresh = call(
-        functools.partial(update_kernel, rows), shape((cols, rows + SUBLANES, order), jnp.int32), VMEM,
-        [SMEM, kind, VMEM] + [FREE] * len(before_update), [], 1 << 26,
-    )(me, probe, parts, *before_update)
+        functools.partial(update_kernel, rows, len(totals)), shape((cols, rows + SUBLANES, order), jnp.int32), VMEM,
+        [SMEM, kind] + [VMEM] * len(totals) + [FREE] * len(before_update), [], 1 << 26,
+    )(me, probe, *totals, *before_update)
     return total, lax.all_to_all(fresh, "col", split_axis=0, concat_axis=0, tiled=True)
 
 
@@ -862,7 +871,7 @@
         functools.partial(second_half_kernel, dims),
         (shape(wide), shares, shape((capacity, order, order), bf16)),
         (HBM, VMEM, HBM),
-        [SMEM, SMEM, LOAD, LOAD, VMEM, LOAD, HBM, HBM] + [LOAD] * 3,
+        [SMEM, SMEM, LOAD, LOAD, VMEM, LOAD, HBM, FREE] + [LOAD] * 3,
         [pltpu.VMEM(wide, f32)] + work_scratch(order)
         + [pltpu.VMEM(window, f32), pltpu.VMEM((capacity,) + window, f32), pltpu.VMEM((capacity, order, order), bf16), pltpu.VMEM((capacity, order, order), bf16)]
         + list_scratch(capacity) + [pltpu.SemaphoreType.DMA((capacity,))] * 3 + [pltpu.SemaphoreType.DMA],
@@ -872,16 +881,16 @@
     top, bottom = call(functools.partial(rows_code_kernel, dims), (coded_row, coded_row), (VMEM, VMEM), [LOAD], [], 1 << 26)(share)
     from_above = passed_along(bottom, "row", 1)
     from_below = passed_along(top, "row", -1)
-    total, chunks = probe_update(me, probe, numer, LOAD)
+    total, chunks = probe_update(me, probe, numer, LOAD, True, [(FREE, top)], [])
     sums, to_left, to_right = call(
-        functools.partial(rows_sum_kernel, dims), (shape(wide), coded_col, coded_col), (PIN, VMEM, VMEM), [LOAD, VMEM, VMEM, FREE], [], 1 << 26,
+        functools.partial(rows_sum_kernel, dims), (shape(wide), coded_col, coded_col), (HBM, VMEM, VMEM), [LOAD, VMEM, VMEM, FREE], [pltpu.SemaphoreType.DMA], 1 << 26,
     )(share, from_above, from_below, total)
     from_left = passed_along(to_right, "col", 1)
     from_right = passed_along(to_left, "col", -1)
 
     current, top, bottom, numer, probe_now = call(
         functools.partial(whole_kernel, dims), (shape(tile), shape((2, tile_rows, 2 * tile_cols)), coded_row, shares, shape(window)), (HBM, HBM) + (VMEM,) * 3,
-        [SMEM, SMEM, LOAD, PIN, VMEM, VMEM, LOAD, VMEM, HBM, LOAD, LOAD],
+        [SMEM, SMEM, LOAD, LOAD, VMEM, VMEM, LOAD, VMEM, HBM, LOAD, LOAD],
         [pltpu.VMEM(wide, f32), pltpu.VMEM(wide, f32)] + work_scratch(order)
         + [pltpu.VMEM((3, order, order), f32), pltpu.VMEM((2,) + window, f32), pltpu.VMEM((capacity, order, order), bf16)]
         + list_scratch(capacity) + [pltpu.SemaphoreType.DMA((capacity,)), pltpu.SemaphoreType.DMA, pltpu.SemaphoreType.DMA],
@@ -897,7 +906,7 @@
     new_object = call(functools.partial(object_kernel, dims), shape(tile), VMEM, [LOAD, LOAD, VMEM, LOAD, LOAD], [], 1 << 26)(
         current, own, from_left, weights_old, weights_new
     )
-    _, chunks = probe_update(me, probe_now, numer, VMEM, weights_new, to_right)
+    _, chunks = probe_update(me, probe_now, numer, VMEM, False, [(HBM, weights_new)], [to_right])
     new_probe = call(probe_kernel, shape(window), VMEM, [VMEM], [], 1 << 26)(chunks)
     return new_object, new_probe
 

time: 172 us -> 169 us (0.983)
  the two profiles are of different devices: /device:TPU:4 before, /device:TPU:28 now
where the time goes in v8:
time: 169 us; the launch traced here: 167 us
  Pallas kernels  62.2 us (37%)
  starting transfers between devices  52.1 us (31%)
  waiting for transfers between devices  26.9 us (16%)
  blocking collectives  23.8 us (14%)
    pallas_call x16, Pallas kernels, called(): pl.pallas_call(body, out_shape=tuple(fixed_outs) if several else fixed_ou...  62.2 us
    ppermute x9, starting transfers between devices, passed_along(): lax.ppermute(value, axis, [(source, source + steps) for source in range(l...  23.8 us
    ppermute x9, waiting for transfers between devices, passed_along(): lax.ppermute(value, axis, [(source, source + steps) for source in range(l...  15.5 us
    all_to_all x1, blocking collectives, probe_update(): lax.all_to_all(fresh, 'col', split_axis=0, concat_axis=0, tiled=True)  12.9 us
    all_to_all x1, blocking collectives, probe_update(): lax.all_to_all(numer, 'col', split_axis=0, concat_axis=0, tiled=True)  10.9 us
    all_to_all x1, waiting for transfers between devices, local(): lax.all_to_all(outgoing, 'col', split_axis=0, concat_axis=0, tiled=True)  7.73 us
    all_to_all x1, starting transfers between devices, probe_update(): lax.all_to_all(total, 'row', split_axis=0, concat_axis=0, tiled=True)  7.52 us
    all_to_all x1, starting transfers between devices, probe_update(): lax.all_to_all(numer, 'col', split_axis=0, concat_axis=0, tiled=True)  7.43 us
  transfers between devices with their start and end apart: 16, of which 8 were waited for; matrix products, arithmetic and copies ran while one was open for 0% of the time, Pallas kernels for 19%

profile of v8, /device:TPU:28, one launch (start us, length us, event | category | flops | bytes accessed | tf_op | source)
XLA Modules:
  0.0 166.7 jit_solution(3750464909457870820)
XLA Ops:
  1.9 2.4 %collective-permute-start.1 = (s32[264,256]{1,0:T(8,128)S(1)}, s32[264,256]{1,0:T(8,128)S(1)}, u32[]{:S(2)}, u32[]{:S(2)}) collective-permute-start(s32[264,256]{1,0:T(8,128)S(1)} %shard_map.86), channel_id=1, source_target_pairs={{8,0},{16,8},{24,16},{9,1},{17,9},{25,17},{10,2},{18,10},{26,18},{... | collective-permute-start | bytes 811016 | tf_op jit(solution)/shard_map/ppermute | solution.py:797
  4.2 2.5 %collective-permute-start = (s32[264,256]{1,0:T(8,128)S(1)}, s32[264,256]{1,0:T(8,128)S(1)}, u32[]{:S(2)}, u32[]{:S(2)}) collective-permute-start(s32[264,256]{1,0:T(8,128)S(1)} %shard_map.86), channel_id=1, source_target_pairs={{1,0},{2,1},{3,2},{4,3},{5,4},{6,5},{7,6},{9,8},{10,9},{11,10},{12... | collective-permute-start | bytes 811016 | tf_op jit(solution)/shard_map/ppermute | solution.py:797
  6.8 3.1 %collective-permute-done.1.refs_4_ = s32[264,256]{1,0:T(8,128)S(1)} collective-permute-done((s32[264,256]{1,0:T(8,128)S(1)}, s32[264,256]{1,0:T(8,128)S(1)}, u32[]{:S(2)}, u32[]{:S(2)}) %collective-permute-start.1) | collective-permute-done | bytes 270368 | tf_op jit(solution)/shard_map/ppermute | solution.py:797
  11.4 2.4 %shard_map.89 = bf16[16,256,256]{2,1,0:T(8,128)(2,1)} custom-call(s32[256]{0:T(256)S(1)} %bitcast.5, s32[2]{0:T(128)S(1)} %pad_add_fusion.refs_1_.refs_0_, bf16[4,256,256]{2,1,0:T(8,128)(2,1)} %refs_2_.5, s32[264,256]{1,0:T(8,128)S(1)} %collective-permute-done.refs_3_, s32[264,256]{1,0:T(8,128)S(1)} %collective-permute-done.1.refs_4_), custom_call_target="tpu_custom_call" | custom-call | flops 1048576 | bytes 8388608 | tf_op jit(solution)/shard_map/pallas_call | solution.py:781
  13.8 4.7 %all-to-all-start = ((bf16[16,256,256]{2,1,0:T(8,128)(2,1)}), bf16[16,256,256]{2,1,0:T(8,128)(2,1)S(1)}, u32[]{:S(2)}, u32[]{:S(2)}) async-start(bf16[16,256,256]{2,1,0:T(8,128)(2,1)} %shard_map.89), calls=%async_computation | async-start | bytes 4194304 | tf_op jit(solution)/shard_map/all_to_all | solution.py:852
  18.5 3.3 %collective-permute-start.2 = (s32[264,256]{1,0:T(8,128)S(1)}, s32[264,256]{1,0:T(8,128)S(1)}, u32[]{:S(2)}, u32[]{:S(2)}) collective-permute-start(s32[264,256]{1,0:T(8,128)S(1)} %collective-permute-done.refs_3_), channel_id=1, source_target_pairs={{8,0},{16,8},{24,16},{9,1},{17,9},{25,17},{10,2},{18,10},{26,18},{... | collective-permute-start | bytes 811016 | tf_op jit(solution)/shard_map/ppermute | solution.py:797
  21.8 8.1 %shard_map.88.refs_5_.refs_6_.refs_3_ = f32[512,512]{1,0:T(8,128)} custom-call(s32[256]{0:T(256)S(1)} %bitcast.6, s32[2]{0:T(128)S(1)} %pad_add_fusion.refs_1_.refs_0_, f32[2,256,256]{2,1,0:T(8,128)} %refs_1_.1), custom_call_target="tpu_custom_call" | custom-call | flops 8589934592 | bytes 8388608 | tf_op jit(solution)/shard_map/pallas_call | solution.py:781
  29.9 6.5 %shard_map.87 = (f32[8,2,256,256]{3,2,1,0:T(8,128)}, f32[256,256]{1,0:T(8,128)S(1)}, f32[2,512,512]{2,1,0:T(8,128)}) custom-call(s32[256]{0:T(256)S(1)} %bitcast.7, s32[2]{0:T(128)S(1)} %pad_add_fusion.refs_1_.refs_0_, f32[2,256,256]{2,1,0:T(8,128)} %refs_2_.3, s32[264,256]{1,0:T(8,128)S(1)} %collective-permute-done.refs_3_, ...), custom_call_target="tpu_custom_call" | custom-call | flops 3221225472 | bytes 8388608 | tf_op jit(solution)/shard_map/pallas_call | solution.py:781
  36.4 7.7 %all-to-all-done.refs_7_ = bf16[16,256,256]{2,1,0:T(8,128)(2,1)S(1)} async-done(((bf16[16,256,256]{2,1,0:T(8,128)(2,1)}), bf16[16,256,256]{2,1,0:T(8,128)(2,1)S(1)}, u32[]{:S(2)}, u32[]{:S(2)}) %all-to-all-start) | async-done | bytes 2097184 | tf_op jit(solution)/shard_map/all_to_all | solution.py:852
  44.2 9.9 %shard_map.90 = (f32[2,512,512]{2,1,0:T(8,128)}, s32[8,56,256]{2,1,0:T(8,128)S(1)}, bf16[8,256,256]{2,1,0:T(8,128)(2,1)}) custom-call(s32[256]{0:T(256)S(1)} %bitcast.8, s32[2]{0:T(128)S(1)} %pad_add_fusion.refs_1_.refs_0_, f32[2,512,512]{2,1,0:T(8,128)} %get-tuple-element.20.refs_2_, f32[2,256,256]{2,1,0:T(8,128)} %refs_1_.1, ...), custom_call_target="tpu_custom_call" | custom-call | flops 3221225472 | bytes 8388608 | tf_op jit(solution)/shard_map/pallas_call | solution.py:781
  54.0 2.1 %shard_map.91 = (s32[264,512]{1,0:T(8,128)S(1)}, s32[264,512]{1,0:T(8,128)S(1)}) custom-call(f32[2,512,512]{2,1,0:T(8,128)} %get-tuple-element.23.refs_0_), custom_call_target="tpu_custom_call" | custom-call | flops 67108864 | bytes 8388608 | tf_op jit(solution)/shard_map/pallas_call | solution.py:781
  57.5 4.6 %collective-permute-start.4 = (s32[264,512]{1,0:T(8,128)S(1)}, s32[264,512]{1,0:T(8,128)S(1)}, u32[]{:S(2)}, u32[]{:S(2)}) collective-permute-start(s32[264,512]{1,0:T(8,128)S(1)} %get-tuple-element.25.refs_1_), channel_id=1, source_target_pairs={{8,0},{16,8},{24,16},{9,1},{17,9},{25,17},{10,2},{18,10},{26,18},{... | collective-permute-start | bytes 1622024 | tf_op jit(solution)/shard_map/ppermute | solution.py:797
  62.1 10.9 %all_to_all.30.refs_0_ = s32[8,56,256]{2,1,0:T(8,128)S(1)} all-to-all(s32[8,56,256]{2,1,0:T(8,128)S(1)} %get-tuple-element.26), channel_id=1, replica_groups=mesh['row'=4,'col'=8] {'col'}, dimensions={0} | all-to-all | bytes 917504 | tf_op jit(solution)/shard_map/all_to_all | solution.py:807
  73.9 7.5 %all-to-all-start.2 = ((s32[4,56,256]{2,1,0:T(8,128)}), s32[4,56,256]{2,1,0:T(8,128)S(1)}, u32[]{:S(2)}, u32[]{:S(2)}) async-start(s32[4,56,256]{2,1,0:T(8,128)} %shard_map.92.refs_3_), calls=%async_computation.2 | async-start | bytes 458752 | tf_op jit(solution)/shard_map/all_to_all | solution.py:814
  81.4 4.2 %shard_map.93 = (f32[2,512,512]{2,1,0:T(8,128)}, s32[528,256]{1,0:T(8,128)S(1)}, s32[528,256]{1,0:T(8,128)}) custom-call(f32[2,512,512]{2,1,0:T(8,128)} %get-tuple-element.23.refs_0_, s32[264,512]{1,0:T(8,128)S(1)} %collective-permute-done.3.refs_1_, s32[264,512]{1,0:T(8,128)S(1)} %collective-permute-done.4.refs_2_, s32[4,56,256]{2,1,0:T(8,128)} %shard_map.92.refs_3_), custom_call_target="tpu_custom_call" | custom-call | flops 67108864 | bytes 8388608 | tf_op jit(solution)/shard_map/pallas_call | solution.py:781
  85.6 1.9 %collective-permute-start.5 = (s32[528,256]{1,0:T(8,128)}, s32[528,256]{1,0:T(8,128)S(1)}, u32[]{:S(2)}, u32[]{:S(2)}) collective-permute-start(s32[528,256]{1,0:T(8,128)} %get-tuple-element.28), channel_id=1, source_target_pairs={{0,1},{1,2},{2,3},{3,4},{4,5},{5,6},{6,7},{8,9},{9,10},{10,11},{11... | collective-permute-start | bytes 1622024 | tf_op jit(solution)/shard_map/ppermute | solution.py:797
  87.5 4.5 %collective-permute-start.6 = (s32[528,256]{1,0:T(8,128)S(1)}, s32[528,256]{1,0:T(8,128)S(1)}, u32[]{:S(2)}, u32[]{:S(2)}) collective-permute-start(s32[528,256]{1,0:T(8,128)S(1)} %get-tuple-element.29), channel_id=1, source_target_pairs={{1,0},{2,1},{3,2},{4,3},{5,4},{6,5},{7,6},{9,8},{10,9},{11,10},{12... | collective-permute-start | bytes 1622024 | tf_op jit(solution)/shard_map/ppermute | solution.py:797
  92.1 1.7 %shard_map.94 = s32[8,40,256]{2,1,0:T(8,128)S(1)} custom-call(s32[2]{0:T(128)S(1)} %pad_add_fusion.refs_1_.refs_0_, f32[2,256,256]{2,1,0:T(8,128)} %refs_1_.1, s32[4,56,256]{2,1,0:T(8,128)S(1)} %all-to-all-done.2.refs_2_), custom_call_target="tpu_custom_call" | custom-call | flops 67108864 | bytes 8388608 | tf_op jit(solution)/shard_map/pallas_call | solution.py:781
  93.8 12.9 %all_to_all.31.refs_7_ = s32[8,40,256]{2,1,0:T(8,128)S(1)} all-to-all(s32[8,40,256]{2,1,0:T(8,128)S(1)} %shard_map.94), channel_id=1, replica_groups=mesh['row'=4,'col'=8] {'col'}, dimensions={0} | all-to-all | bytes 655360 | tf_op jit(solution)/shard_map/all_to_all | solution.py:821
  106.7 12.4 %shard_map.95 = (f32[2,256,256]{2,1,0:T(8,128)}, f32[2,256,512]{2,1,0:T(8,128)}, s32[264,512]{1,0:T(8,128)S(1)}, s32[8,56,256]{2,1,0:T(8,128)}, f32[2,256,256]{2,1,0:T(8,128)S(1)}) custom-call(s32[256]{0:T(256)S(1)} %bitcast.9, s32[2]{0:T(128)S(1)} %pad_add_fusion.refs_1_.refs_0_, f32[2,512,512]{2,1,0:T(8,128)} %get-tuple-element.20.refs_2_, ...), custom_call_target="tpu_custom_call" | custom-call | flops 6442450944 | bytes 8388608 | tf_op jit(solution)/shard_map/pallas_call | solution.py:781
  119.1 7.4 %all-to-all-start.4 = ((s32[8,56,256]{2,1,0:T(8,128)}), s32[8,56,256]{2,1,0:T(8,128)S(1)}, u32[]{:S(2)}, u32[]{:S(2)}) async-start(s32[8,56,256]{2,1,0:T(8,128)} %get-tuple-element.37), calls=%async_computation.4 | async-start | bytes 917504 | tf_op jit(solution)/shard_map/all_to_all | solution.py:807
  127.8 5.6 %shard_map.97.refs_4_.refs_1_ = f32[256,256]{1,0:T(8,128)} custom-call(s32[256]{0:T(256)S(1)} %bitcast.10, s32[2]{0:T(128)S(1)} %pad_add_fusion.refs_1_.refs_0_, f32[2,256,256]{2,1,0:T(8,128)S(1)} %get-tuple-element.36.refs_2_.refs_1_), custom_call_target="tpu_custom_call" | custom-call | flops 8589934592 | bytes 8388608 | tf_op jit(solution)/shard_map/pallas_call | solution.py:781
  134.3 3.4 %collective-permute-start.11 = (s32[1,56,256]{2,1,0:T(8,128)S(1)}, s32[1,56,256]{2,1,0:T(8,128)S(1)}, u32[]{:S(2)}, u32[]{:S(2)}) collective-permute-start(s32[1,56,256]{2,1,0:T(8,128)S(1)} %shard_map.99.refs_2_), channel_id=1, source_target_pairs={{0,24},{8,16},{16,8},{24,0},{1,25},{9,17},{17,9},{25,1},{2,26},{10... | collective-permute-start | bytes 172040 | tf_op jit(solution)/shard_map/ppermute | solution.py:801
  138.7 4.6 %collective-permute-done.7.refs_1_ = s32[264,512]{1,0:T(8,128)S(1)} collective-permute-done((s32[264,512]{1,0:T(8,128)S(1)}, s32[264,512]{1,0:T(8,128)S(1)}, u32[]{:S(2)}, u32[]{:S(2)}) %collective-permute-start.7) | collective-permute-done | bytes 540704 | tf_op jit(solution)/shard_map/ppermute | solution.py:797
  143.4 2.1 %shard_map.96 = (f32[2,256,256]{2,1,0:T(8,128)}, s32[264,256]{1,0:T(8,128)S(1)}) custom-call(f32[2,256,512]{2,1,0:T(8,128)} %get-tuple-element.32.refs_0_, s32[264,512]{1,0:T(8,128)S(1)} %collective-permute-done.7.refs_1_), custom_call_target="tpu_custom_call" | custom-call | flops 67108864 | bytes 8388608 | tf_op jit(solution)/shard_map/pallas_call | solution.py:781
  145.5 1.5 collective-permute-done.11.refs_5_
  147.0 1.6 collective-permute-done.10.refs_4_
  148.5 1.4 shard_map.100
  149.9 4.2 %all-to-all-start.5 = ((s32[8,40,256]{2,1,0:T(8,128)}), s32[8,40,256]{2,1,0:T(8,128)S(1)}, u32[]{:S(2)}, u32[]{:S(2)}) async-start(s32[8,40,256]{2,1,0:T(8,128)} %shard_map.100), calls=%async_computation.5 | async-start | bytes 655360 | tf_op jit(solution)/shard_map/all_to_all | solution.py:821
  154.1 2.0 %collective-permute-start.8 = (s32[264,256]{1,0:T(8,128)S(1)}, s32[264,256]{1,0:T(8,128)S(1)}, u32[]{:S(2)}, u32[]{:S(2)}) collective-permute-start(s32[264,256]{1,0:T(8,128)S(1)} %get-tuple-element.35.refs_6_), channel_id=1, source_target_pairs={{0,1},{1,2},{2,3},{3,4},{4,5},{5,6},{6,7},{8,9},{9,10},{10,11},{11... | collective-permute-start | bytes 811016 | tf_op jit(solution)/shard_map/ppermute | solution.py:797
  156.2 7.0 %collective-permute-done.8.refs_2_ = s32[264,256]{1,0:T(8,128)S(1)} collective-permute-done((s32[264,256]{1,0:T(8,128)S(1)}, s32[264,256]{1,0:T(8,128)S(1)}, u32[]{:S(2)}, u32[]{:S(2)}) %collective-permute-start.8) | collective-permute-done | bytes 270368 | tf_op jit(solution)/shard_map/ppermute | solution.py:797
  163.2 2.6 %shard_map.98 = f32[2,256,256]{2,1,0:T(8,128)} custom-call(f32[2,256,256]{2,1,0:T(8,128)} %get-tuple-element.31.refs_0_, f32[2,256,256]{2,1,0:T(8,128)} %get-tuple-element.34.refs_1_, s32[264,256]{1,0:T(8,128)S(1)} %collective-permute-done.8.refs_2_, f32[512,512]{1,0:T(8,128)} %shard_map.88.refs_5_.refs_6_.refs_3_, f32[256,256]{1,0:T(8,128)} %shard_map.97.refs_4_.refs_1_), custom_call_target="tpu_custom_call" | custom-call | flops 67108864 | bytes 8388608 | tf_op jit(solution)/shard_map/pallas_call | solution.py:781
  (23 shorter events, 8.9 us)
Async XLA Ops:
  1.9 8.1 %collective-permute-start.1 = (s32[264,256]{1,0:T(8,128)S(1)}, s32[264,256]{1,0:T(8,128)S(1)}, u32[]{:S(2)}, u32[]{:S(2)}) collective-permute-start(s32[264,256]{1,0:T(8,128)S(1)} %shard_map.86), channel_id=1, source_target_pairs={{8,0},{16,8},{24,16},{9,1},{17,9},{25,17},{10,2},{18,10},{26,18},{... | collective-permute-start | bytes 811016 | tf_op jit(solution)/shard_map/ppermute | solution.py:797
  4.2 6.5 %collective-permute-start = (s32[264,256]{1,0:T(8,128)S(1)}, s32[264,256]{1,0:T(8,128)S(1)}, u32[]{:S(2)}, u32[]{:S(2)}) collective-permute-start(s32[264,256]{1,0:T(8,128)S(1)} %shard_map.86), channel_id=1, source_target_pairs={{1,0},{2,1},{3,2},{4,3},{5,4},{6,5},{7,6},{9,8},{10,9},{11,10},{12... | collective-permute-start | bytes 811016 | tf_op jit(solution)/shard_map/ppermute | solution.py:797
  10.7 0.7 copy-start
  13.8 7.9 %copy-start.1 = (s32[128,2]{0,1:T(2,128)S(1)}, s32[128,2]{0,1:T(2,128)}, u32[]{:S(2)}) copy-start(s32[128,2]{0,1:T(2,128)} %param.10) | copy-start | bytes 3076
  13.8 30.3 %all-to-all-start = ((bf16[16,256,256]{2,1,0:T(8,128)(2,1)}), bf16[16,256,256]{2,1,0:T(8,128)(2,1)S(1)}, u32[]{:S(2)}, u32[]{:S(2)}) async-start(bf16[16,256,256]{2,1,0:T(8,128)(2,1)} %shard_map.89), calls=%async_computation | async-start | bytes 4194304 | tf_op jit(solution)/shard_map/all_to_all | solution.py:852
  18.5 11.4 %collective-permute-start.2 = (s32[264,256]{1,0:T(8,128)S(1)}, s32[264,256]{1,0:T(8,128)S(1)}, u32[]{:S(2)}, u32[]{:S(2)}) collective-permute-start(s32[264,256]{1,0:T(8,128)S(1)} %collective-permute-done.refs_3_), channel_id=1, source_target_pairs={{8,0},{16,8},{24,16},{9,1},{17,9},{25,17},{10,2},{18,10},{26,18},{... | collective-permute-start | bytes 811016 | tf_op jit(solution)/shard_map/ppermute | solution.py:797
  56.2 25.2 %collective-permute-start.3 = (s32[264,512]{1,0:T(8,128)S(1)}, s32[264,512]{1,0:T(8,128)S(1)}, u32[]{:S(2)}, u32[]{:S(2)}) collective-permute-start(s32[264,512]{1,0:T(8,128)S(1)} %get-tuple-element.24), channel_id=1, source_target_pairs={{0,8},{8,16},{16,24},{1,9},{9,17},{17,25},{2,10},{10,18},{18,26},{... | collective-permute-start | bytes 1622024 | tf_op jit(solution)/shard_map/ppermute | solution.py:797
  57.5 23.9 %collective-permute-start.4 = (s32[264,512]{1,0:T(8,128)S(1)}, s32[264,512]{1,0:T(8,128)S(1)}, u32[]{:S(2)}, u32[]{:S(2)}) collective-permute-start(s32[264,512]{1,0:T(8,128)S(1)} %get-tuple-element.25.refs_1_), channel_id=1, source_target_pairs={{8,0},{16,8},{24,16},{9,1},{17,9},{25,17},{10,2},{18,10},{26,18},{... | collective-permute-start | bytes 1622024 | tf_op jit(solution)/shard_map/ppermute | solution.py:797
  73.9 18.2 %all-to-all-start.2 = ((s32[4,56,256]{2,1,0:T(8,128)}), s32[4,56,256]{2,1,0:T(8,128)S(1)}, u32[]{:S(2)}, u32[]{:S(2)}) async-start(s32[4,56,256]{2,1,0:T(8,128)} %shard_map.92.refs_3_), calls=%async_computation.2 | async-start | bytes 458752 | tf_op jit(solution)/shard_map/all_to_all | solution.py:814
  85.6 21.1 %collective-permute-start.5 = (s32[528,256]{1,0:T(8,128)}, s32[528,256]{1,0:T(8,128)S(1)}, u32[]{:S(2)}, u32[]{:S(2)}) collective-permute-start(s32[528,256]{1,0:T(8,128)} %get-tuple-element.28), channel_id=1, source_target_pairs={{0,1},{1,2},{2,3},{3,4},{4,5},{5,6},{6,7},{8,9},{9,10},{10,11},{11... | collective-permute-start | bytes 1622024 | tf_op jit(solution)/shard_map/ppermute | solution.py:797
  87.5 19.2 %collective-permute-start.6 = (s32[528,256]{1,0:T(8,128)S(1)}, s32[528,256]{1,0:T(8,128)S(1)}, u32[]{:S(2)}, u32[]{:S(2)}) collective-permute-start(s32[528,256]{1,0:T(8,128)S(1)} %get-tuple-element.29), channel_id=1, source_target_pairs={{1,0},{2,1},{3,2},{4,3},{5,4},{6,5},{7,6},{9,8},{10,9},{11,10},{12... | collective-permute-start | bytes 1622024 | tf_op jit(solution)/shard_map/ppermute | solution.py:797
  119.1 15.0 %all-to-all-start.4 = ((s32[8,56,256]{2,1,0:T(8,128)}), s32[8,56,256]{2,1,0:T(8,128)S(1)}, u32[]{:S(2)}, u32[]{:S(2)}) async-start(s32[8,56,256]{2,1,0:T(8,128)} %get-tuple-element.37), calls=%async_computation.4 | async-start | bytes 917504 | tf_op jit(solution)/shard_map/all_to_all | solution.py:807
  126.5 16.8 %collective-permute-start.7 = (s32[264,512]{1,0:T(8,128)S(1)}, s32[264,512]{1,0:T(8,128)S(1)}, u32[]{:S(2)}, u32[]{:S(2)}) collective-permute-start(s32[264,512]{1,0:T(8,128)S(1)} %get-tuple-element.33), channel_id=1, source_target_pairs={{0,8},{8,16},{16,24},{1,9},{9,17},{17,25},{2,10},{10,18},{18,26},{... | collective-permute-start | bytes 1622024 | tf_op jit(solution)/shard_map/ppermute | solution.py:797
  134.3 12.7 %collective-permute-start.11 = (s32[1,56,256]{2,1,0:T(8,128)S(1)}, s32[1,56,256]{2,1,0:T(8,128)S(1)}, u32[]{:S(2)}, u32[]{:S(2)}) collective-permute-start(s32[1,56,256]{2,1,0:T(8,128)S(1)} %shard_map.99.refs_2_), channel_id=1, source_target_pairs={{0,24},{8,16},{16,8},{24,0},{1,25},{9,17},{17,9},{25,1},{2,26},{10... | collective-permute-start | bytes 172040 | tf_op jit(solution)/shard_map/ppermute | solution.py:801
  137.7 10.8 %collective-permute-start.10 = (s32[1,56,256]{2,1,0:T(8,128)S(1)}, s32[1,56,256]{2,1,0:T(8,128)S(1)}, u32[]{:S(2)}, u32[]{:S(2)}) collective-permute-start(s32[1,56,256]{2,1,0:T(8,128)S(1)} %shard_map.99.refs_2_), channel_id=1, source_target_pairs={{0,16},{8,24},{16,0},{24,8},{1,17},{9,25},{17,1},{25,9},{2,18},{10... | collective-permute-start | bytes 172040 | tf_op jit(solution)/shard_map/ppermute | solution.py:801
  138.3 10.2 %collective-permute-start.9 = (s32[1,56,256]{2,1,0:T(8,128)S(1)}, s32[1,56,256]{2,1,0:T(8,128)S(1)}, u32[]{:S(2)}, u32[]{:S(2)}) collective-permute-start(s32[1,56,256]{2,1,0:T(8,128)S(1)} %shard_map.99.refs_2_), channel_id=1, source_target_pairs={{0,8},{8,0},{16,24},{24,16},{1,9},{9,1},{17,25},{25,17},{2,10},{10... | collective-permute-start | bytes 172040 | tf_op jit(solution)/shard_map/ppermute | solution.py:801
  149.9 15.9 %all-to-all-start.5 = ((s32[8,40,256]{2,1,0:T(8,128)}), s32[8,40,256]{2,1,0:T(8,128)S(1)}, u32[]{:S(2)}, u32[]{:S(2)}) async-start(s32[8,40,256]{2,1,0:T(8,128)} %shard_map.100), calls=%async_computation.5 | async-start | bytes 655360 | tf_op jit(solution)/shard_map/all_to_all | solution.py:821
  154.1 9.1 %collective-permute-start.8 = (s32[264,256]{1,0:T(8,128)S(1)}, s32[264,256]{1,0:T(8,128)S(1)}, u32[]{:S(2)}, u32[]{:S(2)}) collective-permute-start(s32[264,256]{1,0:T(8,128)S(1)} %get-tuple-element.35.refs_6_), channel_id=1, source_target_pairs={{0,1},{1,2},{2,3},{3,4},{4,5},{5,6},{6,7},{8,9},{9,10},{10,11},{11... | collective-permute-start | bytes 811016 | tf_op jit(solution)/shard_map/ppermute | solution.py:797

commit v9 on v8

--- a/solution.py
+++ b/solution.py
@@ -23,6 +23,7 @@
 SMEM = pl.BlockSpec(memory_space=pltpu.SMEM)
 HBM = pl.BlockSpec(memory_space=pltpu.HBM)
 LOAD = object()
+LATE = object()
 FREE = pl.BlockSpec(memory_space=pl.ANY)
 PIN = pl.BlockSpec(memory_space=pltpu.VMEM)
 f32 = jnp.float32
@@ -323,7 +324,7 @@
             rows = pl.ds(first, CHUNK)
             below = pl.ds(half + first, CHUNK)
             far_re, far_im = far_ref[k, rows, :], far_ref[k, below, :]
-            amp = amp_ref[pl.ds(k * half + first, CHUNK), :].astype(f32)
+            amp = amp_ref[pl.ds(k * half + first, CHUNK), :].astype(f32) * weight
             factor = amp * lax.rsqrt(far_re * far_re + far_im * far_im + amplitude_floor)
             store_split(x_ref, rows, slice(None), far_re * factor)
             store_split(x_ref, below, slice(None), far_im * factor)
@@ -365,7 +366,6 @@
         terms = ([], [])
         for k, (wave_re, wave_im) in enumerate(waves):
             cols = pl.ds(k * half, half)
-            wave_re, wave_im = weight * wave_re, weight * wave_im
             p_re, p_im = probe_ref[0, rows, cols], probe_ref[1, rows, cols]
             w_re, w_im = win_ref[0, rows, cols], win_ref[1, rows, cols]
             terms[0].append(p_re * wave_re + p_im * wave_im)
@@ -500,7 +500,7 @@
 
 
 def first_half_kernel(dims, pos_ref, me_ref, own_ref, right_ref, below_ref, diag_ref, probe_ref, turns, twiddles,
-                      far_out, power_out, ext_out, ext_ref, win_ref, xa_ref, xb_ref, ya_ref, yb_ref, far_ref, ys_ref, xs_ref, slots_ref, sems, ext_sem):
+                      far_out, win_out, power_out, ext_out, ext_ref, xa_ref, xb_ref, ya_ref, yb_ref, far_ref, win_ref, ys_ref, xs_ref, slots_ref, sems, win_sems, ext_sem):
     tile_rows, tile_cols, pat_count, col_count, capacity = dims
     order = probe_ref.shape[1]
     count = list_patterns(dims, pos_ref, me_ref, ys_ref, xs_ref, slots_ref)
@@ -516,12 +516,13 @@
             listed = 2 * step + k
             weight = (listed < count).astype(f32)
             index = jnp.minimum(listed, count - 1)
-            stages.append(forward(order, ext_ref, probe_ref, consts, ys_ref[index], xs_ref[index], win_ref.at[k], power_out, weight,
+            stages.append(forward(order, ext_ref, probe_ref, consts, ys_ref[index], xs_ref[index], win_ref.at[listed], power_out, weight,
                                   xa_ref.at[k], xb_ref.at[k], ya_ref.at[k], yb_ref.at[k], far_ref.at[listed]))
         interleaved(*stages)
         for k in range(2):
             listed = 2 * step + k
             pltpu.make_async_copy(far_ref.at[listed], far_out.at[listed], sems.at[listed]).start()
+            pltpu.make_async_copy(win_ref.at[listed], win_out.at[listed], win_sems.at[listed]).start()
         return carry
 
     pairs = lax.div(count + 1, 2)
@@ -529,24 +530,25 @@
 
     def settle(listed, carry):
         pltpu.make_async_copy(far_ref.at[listed], far_out.at[listed], sems.at[listed]).wait()
+        pltpu.make_async_copy(win_ref.at[listed], win_out.at[listed], win_sems.at[listed]).wait()
         return carry
 
     lax.fori_loop(0, 2 * pairs, settle, 0)
     keep.wait()
 
 
-def second_half_kernel(dims, pos_ref, me_ref, ext_ref, probe_ref, power_ref, weights_ref, far_in, amp_in, turns, twiddles, sorting,
-                       share_out, numer_out, amp_out,
-                       sum_ref, win_ref, xa_ref, xb_ref, ya_ref, yb_ref, numer_ref, far_ref, amp_ref, sorted_ref, ys_ref, xs_ref, slots_ref, far_sems, amp_sems, out_sems, sum_sem):
+def second_half_kernel(dims, pos_ref, me_ref, probe_ref, power_ref, late_weights, far_in, win_in, amp_in, turns, twiddles, sorting,
+                       share_out, top_out, bottom_out, numer_out, amp_out,
+                       sum_ref, xa_ref, xb_ref, ya_ref, yb_ref, numer_ref, far_ref, win_ref, amp_ref, sorted_ref, ys_ref, xs_ref, slots_ref, far_sems, win_sems, amp_sems, out_sems, sum_sem):
     tile_rows, tile_cols, pat_count, col_count, capacity = dims
     order = probe_ref.shape[1]
-    half = order // 2
     count = list_patterns(dims, pos_ref, me_ref, ys_ref, xs_ref, slots_ref)
     pairs = lax.div(count + 1, 2)
 
     def copies(listed):
         return (
             pltpu.make_async_copy(far_in.at[listed], far_ref.at[listed], far_sems.at[listed]),
+            pltpu.make_async_copy(win_in.at[listed], win_ref.at[listed], win_sems.at[listed]),
             pltpu.make_async_copy(amp_in.at[slots_ref[jnp.minimum(listed, count - 1)]], amp_ref.at[listed], amp_sems.at[listed]),
         )
 
@@ -573,11 +575,7 @@
             y, x = ys_ref[index], xs_ref[index]
             rows_sorted = jnp.dot(sorting[0], amp_ref[listed], preferred_element_type=f32).astype(bf16)
             sorted_ref[listed] = jnp.dot(rows_sorted, sorting[1], preferred_element_type=f32).astype(bf16)
-            for first in range(0, order, CHUNK):
-                for comp in range(2):
-                    for c, tile in enumerate(cut_chunk(ext_ref, comp, first, y, x, CHUNK)):
-                        win_ref[k, comp, pl.ds(first, CHUNK), pl.ds(c * half, half)] = tile
-            stages.append(backward(order, far_ref.at[listed], sorted_ref.at[listed], consts, y, x, weight, probe_ref, win_ref.at[k],
+            stages.append(backward(order, far_ref.at[listed], sorted_ref.at[listed], consts, y, x, weight, probe_ref, win_ref.at[listed],
                                    xa_ref.at[k], xb_ref.at[k], ya_ref.at[k], yb_ref.at[k], sum_ref, numer_ref))
         interleaved(*stages)
         for k in range(2):
@@ -586,6 +584,8 @@
         return carry
 
     lax.fori_loop(0, pairs, pair, 0)
+    weights_ref, weights_come = late_weights
+    weights_come()
     for first in range(0, 2 * tile_rows, CHUNK):
         rows = pl.ds(first, CHUNK)
         scale = 1.0 / (weights_ref[rows, :] + object_regular)
@@ -593,6 +593,8 @@
             sum_ref[comp, rows, :] = sum_ref[comp, rows, :] * scale
     keep = pltpu.make_async_copy(sum_ref, share_out, sum_sem)
     keep.start()
+    encode(lambda comp, at, cols: sum_ref[comp, at, cols], top_out, tile_rows, 0, tile_rows)
+    encode(lambda comp, at, cols: sum_ref[comp, pl.ds(tile_rows + at.start, at.size), cols], bottom_out, tile_rows, 0, tile_rows)
     spread_sums(numer_out, numer_ref, power_ref)
 
     def settle(listed, carry):
@@ -601,12 +603,6 @@
 
     lax.fori_loop(0, 2 * pairs, settle, 0)
     keep.wait()
-
-
-def rows_code_kernel(dims, share_ref, top_out, bottom_out):
-    tile_rows = dims[0]
-    encode(lambda comp, at, cols: share_ref[comp, at, cols], top_out, tile_rows, 0, tile_rows)
-    encode(lambda comp, at, cols: share_ref[comp, pl.ds(tile_rows + at.start, at.size), cols], bottom_out, tile_rows, 0, tile_rows)
 
 
 def rows_sum_kernel(dims, share_ref, above_ref, below_ref, after_ref, sum_out, left_out, right_out, sem):
@@ -738,7 +734,6 @@
 
 def work_scratch(order):
     return [
-        pltpu.VMEM((2, 2, order, order), f32),
         pltpu.VMEM((2, 2, order, order), bf16),
         pltpu.VMEM((2, 2, order, order), bf16),
         pltpu.VMEM((2, order, order), f32),
@@ -754,7 +749,7 @@
     several = isinstance(outs, tuple)
     out_count = len(outs) if several else 1
     in_count = len(in_specs)
-    loaded = [k for k, spec in enumerate(in_specs) if spec is LOAD]
+    loaded = [k for k, spec in enumerate(in_specs) if spec is LOAD or spec is LATE]
 
     def body(*refs):
         ins, rest = list(refs[:in_count]), refs[in_count:]
@@ -763,15 +758,18 @@
         for copy in copies:
             copy.start()
         for n, k in enumerate(loaded):
-            copies[n].wait()
-            ins[k] = kept[n]
+            if in_specs[k] is LOAD:
+                copies[n].wait()
+                ins[k] = kept[n]
+            else:
+                ins[k] = (kept[n], copies[n].wait)
         kernel(*ins, *given)
 
     fixed_outs = [
         pltpu.HBM(out.shape, out.dtype) if spec is HBM else pltpu.VMEM(out.shape, out.dtype) if spec is PIN else out
         for out, spec in zip(outs if several else (outs,), out_specs if several else (out_specs,))
     ]
-    places = [pltpu.HBM if spec is LOAD or spec is HBM else pltpu.VMEM if spec is PIN else None for spec in in_specs]
+    places = [pltpu.HBM if spec in (LOAD, LATE, HBM) else pltpu.VMEM if spec is PIN else None for spec in in_specs]
 
     def called(*args):
         args = [arg if place is None else pltpu.with_memory_space_constraint(arg, place) for arg, place in zip(args, places)]
@@ -782,7 +780,7 @@
             body,
             out_shape=tuple(fixed_outs) if several else fixed_outs[0],
             out_specs=out_specs,
-            in_specs=[HBM if spec is LOAD else spec for spec in in_specs],
+            in_specs=[HBM if spec in (LOAD, LATE) else spec for spec in in_specs],
             scratch_shapes=list(scratch) + own,
             compiler_params=pltpu.CompilerParams(vmem_limit_bytes=limit),
             cost_estimate=pl.CostEstimate(flops=flops, bytes_accessed=8 << 20, transcendentals=0),
@@ -859,29 +857,28 @@
 
     weights_old = weights(probe, 2, LOAD)
 
-    far, power, ext = call(
-        functools.partial(first_half_kernel, dims), (shape((capacity,) + window), shape((order, order)), shape(wide)), (HBM, VMEM, HBM),
+    far, wins, power, ext = call(
+        functools.partial(first_half_kernel, dims), (shape((capacity,) + window), shape((capacity,) + window), shape((order, order)), shape(wide)), (HBM, HBM, VMEM, HBM),
         [SMEM, SMEM, LOAD] + [VMEM] * 3 + [LOAD] * 3,
-        [pltpu.VMEM(wide, f32)] + work_scratch(order) + [pltpu.VMEM((capacity,) + window, f32)] + list_scratch(capacity)
-        + [pltpu.SemaphoreType.DMA((capacity,)), pltpu.SemaphoreType.DMA],
+        [pltpu.VMEM(wide, f32)] + work_scratch(order) + [pltpu.VMEM((capacity,) + window, f32)] * 2 + list_scratch(capacity)
+        + [pltpu.SemaphoreType.DMA((capacity,))] * 2 + [pltpu.SemaphoreType.DMA],
         capacity * one_pattern // 2,
     )(pos, me, obj, right, below, diag, probe, turns, twiddles)
 
-    share, numer, sorted_amps = call(
+    share, top, bottom, numer, sorted_amps = call(
         functools.partial(second_half_kernel, dims),
-        (shape(wide), shares, shape((capacity, order, order), bf16)),
-        (HBM, VMEM, HBM),
-        [SMEM, SMEM, LOAD, LOAD, VMEM, LOAD, HBM, FREE] + [LOAD] * 3,
+        (shape(wide), coded_row, coded_row, shares, shape((capacity, order, order), bf16)),
+        (HBM, VMEM, VMEM, VMEM, HBM),
+        [SMEM, SMEM, LOAD, VMEM, LATE, HBM, HBM, FREE] + [LOAD] * 3,
         [pltpu.VMEM(wide, f32)] + work_scratch(order)
-        + [pltpu.VMEM(window, f32), pltpu.VMEM((capacity,) + window, f32), pltpu.VMEM((capacity, order, order), bf16), pltpu.VMEM((capacity, order, order), bf16)]
-        + list_scratch(capacity) + [pltpu.SemaphoreType.DMA((capacity,))] * 3 + [pltpu.SemaphoreType.DMA],
+        + [pltpu.VMEM(window, f32)] + [pltpu.VMEM((capacity,) + window, f32)] * 2 + [pltpu.VMEM((capacity, order, order), bf16)] * 2
+        + list_scratch(capacity) + [pltpu.SemaphoreType.DMA((capacity,))] * 4 + [pltpu.SemaphoreType.DMA],
         capacity * one_pattern // 2,
-    )(pos, me, ext, probe, power, weights_old, far, incoming, turns, twiddles, sorting)
-
-    top, bottom = call(functools.partial(rows_code_kernel, dims), (coded_row, coded_row), (VMEM, VMEM), [LOAD], [], 1 << 26)(share)
+    )(pos, me, probe, power, weights_old, far, wins, incoming, turns, twiddles, sorting)
+
     from_above = passed_along(bottom, "row", 1)
     from_below = passed_along(top, "row", -1)
-    total, chunks = probe_update(me, probe, numer, LOAD, True, [(FREE, top)], [])
+    total, chunks = probe_update(me, probe, numer, LOAD, True, [], [])
     sums, to_left, to_right = call(
         functools.partial(rows_sum_kernel, dims), (shape(wide), coded_col, coded_col), (HBM, VMEM, VMEM), [LOAD, VMEM, VMEM, FREE], [pltpu.SemaphoreType.DMA], 1 << 26,
     )(share, from_above, from_below, total)
@@ -891,7 +888,7 @@
     current, top, bottom, numer, probe_now = call(
         functools.partial(whole_kernel, dims), (shape(tile), shape((2, tile_rows, 2 * tile_cols)), coded_row, shares, shape(window)), (HBM, HBM) + (VMEM,) * 3,
         [SMEM, SMEM, LOAD, LOAD, VMEM, VMEM, LOAD, VMEM, HBM, LOAD, LOAD],
-        [pltpu.VMEM(wide, f32), pltpu.VMEM(wide, f32)] + work_scratch(order)
+        [pltpu.VMEM(wide, f32), pltpu.VMEM(wide, f32), pltpu.VMEM((2,) + window, f32)] + work_scratch(order)
         + [pltpu.VMEM((3, order, order), f32), pltpu.VMEM((2,) + window, f32), pltpu.VMEM((capacity, order, order), bf16)]
         + list_scratch(capacity) + [pltpu.SemaphoreType.DMA((capacity,)), pltpu.SemaphoreType.DMA, pltpu.SemaphoreType.DMA],
         capacity * one_pattern,
@@ -906,7 +903,7 @@
     new_object = call(functools.partial(object_kernel, dims), shape(tile), VMEM, [LOAD, LOAD, VMEM, LOAD, LOAD], [], 1 << 26)(
         current, own, from_left, weights_old, weights_new
     )
-    _, chunks = probe_update(me, probe_now, numer, VMEM, False, [(HBM, weights_new)], [to_right])
+    _, chunks = probe_update(me, probe_now, numer, VMEM, False, [(HBM, weights_new)], [from_left])
     new_probe = call(probe_kernel, shape(window), VMEM, [VMEM], [], 1 << 26)(chunks)
     return new_object, new_probe
 

time: 169 us -> 168 us (level)
  the two profiles are of different devices: /device:TPU:28 before, /device:TPU:0 now
where the time goes in v9:
time: 168 us; the launch traced here: 167 us
  Pallas kernels  55.7 us (33%)
  starting transfers between devices  48.1 us (29%)
  waiting for transfers between devices  36.2 us (22%)
  blocking collectives  25.7 us (15%)
    pallas_call x15, Pallas kernels, called(): pl.pallas_call(body, out_shape=tuple(fixed_outs) if several else fixed_ou...  55.7 us
    ppermute x9, starting transfers between devices, passed_along(): lax.ppermute(value, axis, [(source, source + steps) for source in range(l...  16.7 us
    ppermute x9, waiting for transfers between devices, passed_along(): lax.ppermute(value, axis, [(source, source + steps) for source in range(l...  14.8 us
    all_to_all x1, blocking collectives, probe_update(): lax.all_to_all(fresh, 'col', split_axis=0, concat_axis=0, tiled=True)  13.7 us
    all_to_all x1, blocking collectives, probe_update(): lax.all_to_all(numer, 'col', split_axis=0, concat_axis=0, tiled=True)  12 us
    all_to_all x1, waiting for transfers between devices, local(): lax.all_to_all(outgoing, 'col', split_axis=0, concat_axis=0, tiled=True)  9.13 us
    all_to_all x1, starting transfers between devices, probe_update(): lax.all_to_all(numer, 'col', split_axis=0, concat_axis=0, tiled=True)  7.76 us
    all_to_all x1, starting transfers between devices, probe_update(): lax.all_to_all(fresh, 'col', split_axis=0, concat_axis=0, tiled=True)  7.34 us
  transfers between devices with their start and end apart: 16, of which 8 were waited for; matrix products, arithmetic and copies ran while one was open for 0% of the time, Pallas kernels for 17%

profile of v9, /device:TPU:0, one launch (start us, length us, event | category | flops | bytes accessed | tf_op | source)
XLA Modules:
  0.0 167.3 jit_solution(15156276175741228647)
XLA Ops:
  1.9 1.3 collective-permute-start.1
  3.2 1.3 collective-permute-start
  4.5 8.7 %collective-permute-done.1.refs_4_ = s32[264,256]{1,0:T(8,128)S(1)} collective-permute-done((s32[264,256]{1,0:T(8,128)S(1)}, s32[264,256]{1,0:T(8,128)S(1)}, u32[]{:S(2)}, u32[]{:S(2)}) %collective-permute-start.1) | collective-permute-done | bytes 270368 | tf_op jit(solution)/shard_map/ppermute | solution.py:795
  13.9 2.5 %shard_map.89 = bf16[16,256,256]{2,1,0:T(8,128)(2,1)} custom-call(s32[256]{0:T(256)S(1)} %bitcast.5, s32[2]{0:T(128)S(1)} %pad_add_fusion.refs_1_.refs_0_, bf16[4,256,256]{2,1,0:T(8,128)(2,1)} %refs_2_.6, s32[264,256]{1,0:T(8,128)S(1)} %collective-permute-done.refs_3_, s32[264,256]{1,0:T(8,128)S(1)} %collective-permute-done.1.refs_4_), custom_call_target="tpu_custom_call" | custom-call | flops 1048576 | bytes 8388608 | tf_op jit(solution)/shard_map/pallas_call | solution.py:779
  16.4 3.8 %all-to-all-start = ((bf16[16,256,256]{2,1,0:T(8,128)(2,1)}), bf16[16,256,256]{2,1,0:T(8,128)(2,1)S(1)}, u32[]{:S(2)}, u32[]{:S(2)}) async-start(bf16[16,256,256]{2,1,0:T(8,128)(2,1)} %shard_map.89), calls=%async_computation | async-start | bytes 4194304 | tf_op jit(solution)/shard_map/all_to_all | solution.py:850
  21.6 7.0 %shard_map.88.refs_4_.refs_6_.refs_3_ = f32[512,512]{1,0:T(8,128)} custom-call(s32[256]{0:T(256)S(1)} %bitcast.6, s32[2]{0:T(128)S(1)} %pad_add_fusion.refs_1_.refs_0_, f32[2,256,256]{2,1,0:T(8,128)} %refs_1_.1), custom_call_target="tpu_custom_call" | custom-call | flops 8589934592 | bytes 8388608 | tf_op jit(solution)/shard_map/pallas_call | solution.py:779
  28.5 2.6 %collective-permute-done.2.refs_5_ = s32[264,256]{1,0:T(8,128)S(1)} collective-permute-done((s32[264,256]{1,0:T(8,128)S(1)}, s32[264,256]{1,0:T(8,128)S(1)}, u32[]{:S(2)}, u32[]{:S(2)}) %collective-permute-start.2) | collective-permute-done | bytes 270368 | tf_op jit(solution)/shard_map/ppermute | solution.py:795
  31.2 6.6 %shard_map.87 = (f32[8,2,256,256]{3,2,1,0:T(8,128)}, f32[8,2,256,256]{3,2,1,0:T(8,128)}, f32[256,256]{1,0:T(8,128)S(1)}, f32[2,512,512]{2,1,0:T(8,128)}) custom-call(s32[256]{0:T(256)S(1)} %bitcast.7, s32[2]{0:T(128)S(1)} %pad_add_fusion.refs_1_.refs_0_, f32[2,256,256]{2,1,0:T(8,128)} %refs_2_.4, s32[264,256]{1,0:T(8,128)S(1)} %collective-permute-done.refs_3_, ...), custom_call_target="tpu_custom_call" | custom-call | flops 3221225472 | bytes 8388608 | tf_op jit(solution)/shard_map/pallas_call | solution.py:779
  37.8 9.1 %all-to-all-done.refs_7_ = bf16[16,256,256]{2,1,0:T(8,128)(2,1)S(1)} async-done(((bf16[16,256,256]{2,1,0:T(8,128)(2,1)}), bf16[16,256,256]{2,1,0:T(8,128)(2,1)S(1)}, u32[]{:S(2)}, u32[]{:S(2)}) %all-to-all-start) | async-done | bytes 2097184 | tf_op jit(solution)/shard_map/all_to_all | solution.py:850
  46.9 9.1 %shard_map.90 = (f32[2,512,512]{2,1,0:T(8,128)}, s32[264,512]{1,0:T(8,128)S(1)}, s32[264,512]{1,0:T(8,128)S(1)}, s32[8,56,256]{2,1,0:T(8,128)S(1)}, bf16[8,256,256]{2,1,0:T(8,128)(2,1)}) custom-call(s32[256]{0:T(256)S(1)} %bitcast.8, s32[2]{0:T(128)S(1)} %pad_add_fusion.refs_1_.refs_0_, f32[2,256,256]{2,1,0:T(8,128)} %refs_1_.1, ...), custom_call_target="tpu_custom_call" | custom-call | flops 3221225472 | bytes 8388608 | tf_op jit(solution)/shard_map/pallas_call | solution.py:779
  56.0 3.6 %collective-permute-start.3 = (s32[264,512]{1,0:T(8,128)S(1)}, s32[264,512]{1,0:T(8,128)S(1)}, u32[]{:S(2)}, u32[]{:S(2)}) collective-permute-start(s32[264,512]{1,0:T(8,128)S(1)} %get-tuple-element.26), channel_id=1, source_target_pairs={{0,8},{8,16},{16,24},{1,9},{9,17},{17,25},{2,10},{10,18},{18,26},{... | collective-permute-start | bytes 1622024 | tf_op jit(solution)/shard_map/ppermute | solution.py:795
  60.9 12.0 %all_to_all.30.refs_0_ = s32[8,56,256]{2,1,0:T(8,128)S(1)} all-to-all(s32[8,56,256]{2,1,0:T(8,128)S(1)} %get-tuple-element.28), channel_id=1, replica_groups=mesh['row'=4,'col'=8] {'col'}, dimensions={0} | all-to-all | bytes 917504 | tf_op jit(solution)/shard_map/all_to_all | solution.py:805
  73.8 7.0 %all-to-all-start.2 = ((s32[4,56,256]{2,1,0:T(8,128)}), s32[4,56,256]{2,1,0:T(8,128)S(1)}, u32[]{:S(2)}, u32[]{:S(2)}) async-start(s32[4,56,256]{2,1,0:T(8,128)} %shard_map.91.refs_3_), calls=%async_computation.2 | async-start | bytes 458752 | tf_op jit(solution)/shard_map/all_to_all | solution.py:812
  80.8 3.3 %shard_map.92 = (f32[2,512,512]{2,1,0:T(8,128)}, s32[528,256]{1,0:T(8,128)S(1)}, s32[528,256]{1,0:T(8,128)S(1)}) custom-call(f32[2,512,512]{2,1,0:T(8,128)} %get-tuple-element.25.refs_0_, s32[264,512]{1,0:T(8,128)S(1)} %collective-permute-done.3.refs_1_, s32[264,512]{1,0:T(8,128)S(1)} %collective-permute-done.4.refs_2_, s32[4,56,256]{2,1,0:T(8,128)} %shard_map.91.refs_3_), custom_call_target="tpu_custom_call" | custom-call | flops 67108864 | bytes 8388608 | tf_op jit(solution)/shard_map/pallas_call | solution.py:779
  84.2 1.3 collective-permute-start.5
  86.8 1.9 %all-to-all-done.2.refs_2_ = s32[4,56,256]{2,1,0:T(8,128)S(1)} async-done(((s32[4,56,256]{2,1,0:T(8,128)}), s32[4,56,256]{2,1,0:T(8,128)S(1)}, u32[]{:S(2)}, u32[]{:S(2)}) %all-to-all-start.2) | async-done | bytes 229408 | tf_op jit(solution)/shard_map/all_to_all | solution.py:812
  88.7 1.7 %shard_map.93 = s32[8,40,256]{2,1,0:T(8,128)S(1)} custom-call(s32[2]{0:T(128)S(1)} %pad_add_fusion.refs_1_.refs_0_, f32[2,256,256]{2,1,0:T(8,128)} %refs_1_.1, s32[4,56,256]{2,1,0:T(8,128)S(1)} %all-to-all-done.2.refs_2_), custom_call_target="tpu_custom_call" | custom-call | flops 67108864 | bytes 8388608 | tf_op jit(solution)/shard_map/pallas_call | solution.py:779
  90.4 13.7 %all_to_all.31.refs_7_ = s32[8,40,256]{2,1,0:T(8,128)S(1)} all-to-all(s32[8,40,256]{2,1,0:T(8,128)S(1)} %shard_map.93), channel_id=1, replica_groups=mesh['row'=4,'col'=8] {'col'}, dimensions={0} | all-to-all | bytes 655360 | tf_op jit(solution)/shard_map/all_to_all | solution.py:819
  104.0 12.1 %shard_map.94 = (f32[2,256,256]{2,1,0:T(8,128)}, f32[2,256,512]{2,1,0:T(8,128)}, s32[264,512]{1,0:T(8,128)S(1)}, s32[8,56,256]{2,1,0:T(8,128)}, f32[2,256,256]{2,1,0:T(8,128)S(1)}) custom-call(s32[256]{0:T(256)S(1)} %bitcast.9, s32[2]{0:T(128)S(1)} %pad_add_fusion.refs_1_.refs_0_, f32[2,512,512]{2,1,0:T(8,128)} %get-tuple-element.21.refs_2_, ...), custom_call_target="tpu_custom_call" | custom-call | flops 6442450944 | bytes 8388608 | tf_op jit(solution)/shard_map/pallas_call | solution.py:779
  116.2 4.0 %collective-permute-start.7 = (s32[264,512]{1,0:T(8,128)S(1)}, s32[264,512]{1,0:T(8,128)S(1)}, u32[]{:S(2)}, u32[]{:S(2)}) collective-permute-start(s32[264,512]{1,0:T(8,128)S(1)} %get-tuple-element.35), channel_id=1, source_target_pairs={{0,8},{8,16},{16,24},{1,9},{9,17},{17,25},{2,10},{10,18},{18,26},{... | collective-permute-start | bytes 1622024 | tf_op jit(solution)/shard_map/ppermute | solution.py:795
  120.2 7.8 %all-to-all-start.4 = ((s32[8,56,256]{2,1,0:T(8,128)}), s32[8,56,256]{2,1,0:T(8,128)S(1)}, u32[]{:S(2)}, u32[]{:S(2)}) async-start(s32[8,56,256]{2,1,0:T(8,128)} %get-tuple-element.39), calls=%async_computation.4 | async-start | bytes 917504 | tf_op jit(solution)/shard_map/all_to_all | solution.py:805
  128.0 3.5 %collective-permute-done.7.refs_1_ = s32[264,512]{1,0:T(8,128)S(1)} collective-permute-done((s32[264,512]{1,0:T(8,128)S(1)}, s32[264,512]{1,0:T(8,128)S(1)}, u32[]{:S(2)}, u32[]{:S(2)}) %collective-permute-start.7) | collective-permute-done | bytes 540704 | tf_op jit(solution)/shard_map/ppermute | solution.py:795
  131.4 2.1 %shard_map.95 = (f32[2,256,256]{2,1,0:T(8,128)}, s32[264,256]{1,0:T(8,128)S(1)}) custom-call(f32[2,256,512]{2,1,0:T(8,128)} %get-tuple-element.34.refs_0_, s32[264,512]{1,0:T(8,128)S(1)} %collective-permute-done.7.refs_1_), custom_call_target="tpu_custom_call" | custom-call | flops 67108864 | bytes 8388608 | tf_op jit(solution)/shard_map/pallas_call | solution.py:779
  133.6 1.3 collective-permute-start.8
  134.9 4.3 %shard_map.96.refs_4_.refs_1_ = f32[256,256]{1,0:T(8,128)} custom-call(s32[256]{0:T(256)S(1)} %bitcast.10, s32[2]{0:T(128)S(1)} %pad_add_fusion.refs_1_.refs_0_, f32[2,256,256]{2,1,0:T(8,128)S(1)} %get-tuple-element.38.refs_2_.refs_1_), custom_call_target="tpu_custom_call" | custom-call | flops 8589934592 | bytes 8388608 | tf_op jit(solution)/shard_map/pallas_call | solution.py:779
  139.3 4.8 %collective-permute-start.11 = (s32[1,56,256]{2,1,0:T(8,128)S(1)}, s32[1,56,256]{2,1,0:T(8,128)S(1)}, u32[]{:S(2)}, u32[]{:S(2)}) collective-permute-start(s32[1,56,256]{2,1,0:T(8,128)S(1)} %shard_map.98.refs_2_), channel_id=1, source_target_pairs={{0,24},{8,16},{16,8},{24,0},{1,25},{9,17},{17,9},{25,1},{2,26},{10... | collective-permute-start | bytes 172040 | tf_op jit(solution)/shard_map/ppermute | solution.py:799
  144.8 1.6 collective-permute-done.11.refs_5_
  146.4 3.7 %collective-permute-done.10.refs_4_ = s32[1,56,256]{2,1,0:T(8,128)S(1)} collective-permute-done((s32[1,56,256]{2,1,0:T(8,128)S(1)}, s32[1,56,256]{2,1,0:T(8,128)S(1)}, u32[]{:S(2)}, u32[]{:S(2)}) %collective-permute-start.10) | collective-permute-done | bytes 57376 | tf_op jit(solution)/shard_map/ppermute | solution.py:799
  150.1 1.4 shard_map.99
  151.5 7.3 %all-to-all-start.5 = ((s32[8,40,256]{2,1,0:T(8,128)}), s32[8,40,256]{2,1,0:T(8,128)S(1)}, u32[]{:S(2)}, u32[]{:S(2)}) async-start(s32[8,40,256]{2,1,0:T(8,128)} %shard_map.99), calls=%async_computation.5 | async-start | bytes 655360 | tf_op jit(solution)/shard_map/all_to_all | solution.py:819
  158.8 2.6 %shard_map.97 = f32[2,256,256]{2,1,0:T(8,128)} custom-call(f32[2,256,256]{2,1,0:T(8,128)} %get-tuple-element.33.refs_0_, f32[2,256,256]{2,1,0:T(8,128)} %get-tuple-element.36.refs_1_, s32[264,256]{1,0:T(8,128)S(1)} %collective-permute-done.8.refs_2_.refs_6_, f32[512,512]{1,0:T(8,128)} %shard_map.88.refs_4_.refs_6_.refs_3_, f32[256,256]{1,0:T(8,128)} %shard_map.96.refs_4_.refs_1_), custom_call_target="tpu_custom_call" | custom-call | flops 67108864 | bytes 8388608 | tf_op jit(solution)/shard_map/pallas_call | solution.py:779
  161.4 5.0 %all-to-all-done.5.refs_0_ = s32[8,40,256]{2,1,0:T(8,128)S(1)} async-done(((s32[8,40,256]{2,1,0:T(8,128)}), s32[8,40,256]{2,1,0:T(8,128)S(1)}, u32[]{:S(2)}, u32[]{:S(2)}) %all-to-all-start.5) | async-done | bytes 327712 | tf_op jit(solution)/shard_map/all_to_all | solution.py:819
  (22 shorter events, 8.4 us)
Async XLA Ops:
  1.9 11.4 %collective-permute-start.1 = (s32[264,256]{1,0:T(8,128)S(1)}, s32[264,256]{1,0:T(8,128)S(1)}, u32[]{:S(2)}, u32[]{:S(2)}) collective-permute-start(s32[264,256]{1,0:T(8,128)S(1)} %shard_map.86), channel_id=1, source_target_pairs={{8,0},{16,8},{24,16},{9,1},{17,9},{25,17},{10,2},{18,10},{26,18},{... | collective-permute-start | bytes 811016 | tf_op jit(solution)/shard_map/ppermute | solution.py:795
  3.2 10.1 %collective-permute-start = (s32[264,256]{1,0:T(8,128)S(1)}, s32[264,256]{1,0:T(8,128)S(1)}, u32[]{:S(2)}, u32[]{:S(2)}) collective-permute-start(s32[264,256]{1,0:T(8,128)S(1)} %shard_map.86), channel_id=1, source_target_pairs={{1,0},{2,1},{3,2},{4,3},{5,4},{6,5},{7,6},{9,8},{10,9},{11,10},{12... | collective-permute-start | bytes 811016 | tf_op jit(solution)/shard_map/ppermute | solution.py:795
  13.3 0.7 copy-start
  16.4 30.5 %all-to-all-start = ((bf16[16,256,256]{2,1,0:T(8,128)(2,1)}), bf16[16,256,256]{2,1,0:T(8,128)(2,1)S(1)}, u32[]{:S(2)}, u32[]{:S(2)}) async-start(bf16[16,256,256]{2,1,0:T(8,128)(2,1)} %shard_map.89), calls=%async_computation | async-start | bytes 4194304 | tf_op jit(solution)/shard_map/all_to_all | solution.py:850
  20.3 10.9 %copy-start.1 = (s32[128,2]{0,1:T(2,128)S(1)}, s32[128,2]{0,1:T(2,128)}, u32[]{:S(2)}) copy-start(s32[128,2]{0,1:T(2,128)} %param.10) | copy-start | bytes 3076
  20.3 10.9 %collective-permute-start.2 = (s32[264,256]{1,0:T(8,128)S(1)}, s32[264,256]{1,0:T(8,128)S(1)}, u32[]{:S(2)}, u32[]{:S(2)}) collective-permute-start(s32[264,256]{1,0:T(8,128)S(1)} %collective-permute-done.refs_3_), channel_id=1, source_target_pairs={{8,0},{16,8},{24,16},{9,1},{17,9},{25,17},{10,2},{18,10},{26,18},{... | collective-permute-start | bytes 811016 | tf_op jit(solution)/shard_map/ppermute | solution.py:795
  56.0 24.8 %collective-permute-start.3 = (s32[264,512]{1,0:T(8,128)S(1)}, s32[264,512]{1,0:T(8,128)S(1)}, u32[]{:S(2)}, u32[]{:S(2)}) collective-permute-start(s32[264,512]{1,0:T(8,128)S(1)} %get-tuple-element.26), channel_id=1, source_target_pairs={{0,8},{8,16},{16,24},{1,9},{9,17},{17,25},{2,10},{10,18},{18,26},{... | collective-permute-start | bytes 1622024 | tf_op jit(solution)/shard_map/ppermute | solution.py:795
  59.6 21.2 %collective-permute-start.4 = (s32[264,512]{1,0:T(8,128)S(1)}, s32[264,512]{1,0:T(8,128)S(1)}, u32[]{:S(2)}, u32[]{:S(2)}) collective-permute-start(s32[264,512]{1,0:T(8,128)S(1)} %get-tuple-element.27), channel_id=1, source_target_pairs={{8,0},{16,8},{24,16},{9,1},{17,9},{25,17},{10,2},{18,10},{26,18},{... | collective-permute-start | bytes 1622024 | tf_op jit(solution)/shard_map/ppermute | solution.py:795
  73.8 14.9 %all-to-all-start.2 = ((s32[4,56,256]{2,1,0:T(8,128)}), s32[4,56,256]{2,1,0:T(8,128)S(1)}, u32[]{:S(2)}, u32[]{:S(2)}) async-start(s32[4,56,256]{2,1,0:T(8,128)} %shard_map.91.refs_3_), calls=%async_computation.2 | async-start | bytes 458752 | tf_op jit(solution)/shard_map/all_to_all | solution.py:812
  84.2 19.9 %collective-permute-start.5 = (s32[528,256]{1,0:T(8,128)S(1)}, s32[528,256]{1,0:T(8,128)S(1)}, u32[]{:S(2)}, u32[]{:S(2)}) collective-permute-start(s32[528,256]{1,0:T(8,128)S(1)} %get-tuple-element.30), channel_id=1, source_target_pairs={{0,1},{1,2},{2,3},{3,4},{4,5},{5,6},{6,7},{8,9},{9,10},{10,11},{11... | collective-permute-start | bytes 1622024 | tf_op jit(solution)/shard_map/ppermute | solution.py:795
  85.5 18.6 %collective-permute-start.6 = (s32[528,256]{1,0:T(8,128)S(1)}, s32[528,256]{1,0:T(8,128)S(1)}, u32[]{:S(2)}, u32[]{:S(2)}) collective-permute-start(s32[528,256]{1,0:T(8,128)S(1)} %get-tuple-element.31), channel_id=1, source_target_pairs={{1,0},{2,1},{3,2},{4,3},{5,4},{6,5},{7,6},{9,8},{10,9},{11,10},{12... | collective-permute-start | bytes 1622024 | tf_op jit(solution)/shard_map/ppermute | solution.py:795
  116.2 15.2 %collective-permute-start.7 = (s32[264,512]{1,0:T(8,128)S(1)}, s32[264,512]{1,0:T(8,128)S(1)}, u32[]{:S(2)}, u32[]{:S(2)}) collective-permute-start(s32[264,512]{1,0:T(8,128)S(1)} %get-tuple-element.35), channel_id=1, source_target_pairs={{0,8},{8,16},{16,24},{1,9},{9,17},{17,25},{2,10},{10,18},{18,26},{... | collective-permute-start | bytes 1622024 | tf_op jit(solution)/shard_map/ppermute | solution.py:795
  120.2 18.9 %all-to-all-start.4 = ((s32[8,56,256]{2,1,0:T(8,128)}), s32[8,56,256]{2,1,0:T(8,128)S(1)}, u32[]{:S(2)}, u32[]{:S(2)}) async-start(s32[8,56,256]{2,1,0:T(8,128)} %get-tuple-element.39), calls=%async_computation.4 | async-start | bytes 917504 | tf_op jit(solution)/shard_map/all_to_all | solution.py:805
  133.6 16.6 %collective-permute-start.8 = (s32[264,256]{1,0:T(8,128)S(1)}, s32[264,256]{1,0:T(8,128)S(1)}, u32[]{:S(2)}, u32[]{:S(2)}) collective-permute-start(s32[264,256]{1,0:T(8,128)S(1)} %get-tuple-element.37), channel_id=1, source_target_pairs={{0,1},{1,2},{2,3},{3,4},{4,5},{5,6},{6,7},{8,9},{9,10},{10,11},{11... | collective-permute-start | bytes 811016 | tf_op jit(solution)/shard_map/ppermute | solution.py:795
  139.3 7.1 %collective-permute-start.11 = (s32[1,56,256]{2,1,0:T(8,128)S(1)}, s32[1,56,256]{2,1,0:T(8,128)S(1)}, u32[]{:S(2)}, u32[]{:S(2)}) collective-permute-start(s32[1,56,256]{2,1,0:T(8,128)S(1)} %shard_map.98.refs_2_), channel_id=1, source_target_pairs={{0,24},{8,16},{16,8},{24,0},{1,25},{9,17},{17,9},{25,1},{2,26},{10... | collective-permute-start | bytes 172040 | tf_op jit(solution)/shard_map/ppermute | solution.py:799
  144.1 6.0 %collective-permute-start.10 = (s32[1,56,256]{2,1,0:T(8,128)S(1)}, s32[1,56,256]{2,1,0:T(8,128)S(1)}, u32[]{:S(2)}, u32[]{:S(2)}) collective-permute-start(s32[1,56,256]{2,1,0:T(8,128)S(1)} %shard_map.98.refs_2_), channel_id=1, source_target_pairs={{0,16},{8,24},{16,0},{24,8},{1,17},{9,25},{17,1},{25,9},{2,18},{10... | collective-permute-start | bytes 172040 | tf_op jit(solution)/shard_map/ppermute | solution.py:799
  144.1 6.0 %collective-permute-start.9 = (s32[1,56,256]{2,1,0:T(8,128)S(1)}, s32[1,56,256]{2,1,0:T(8,128)S(1)}, u32[]{:S(2)}, u32[]{:S(2)}) collective-permute-start(s32[1,56,256]{2,1,0:T(8,128)S(1)} %shard_map.98.refs_2_), channel_id=1, source_target_pairs={{0,8},{8,0},{16,24},{24,16},{1,9},{9,1},{17,25},{25,17},{2,10},{10... | collective-permute-start | bytes 172040 | tf_op jit(solution)/shard_map/ppermute | solution.py:799
  151.5 15.0 %all-to-all-start.5 = ((s32[8,40,256]{2,1,0:T(8,128)}), s32[8,40,256]{2,1,0:T(8,128)S(1)}, u32[]{:S(2)}, u32[]{:S(2)}) async-start(s32[8,40,256]{2,1,0:T(8,128)} %shard_map.99), calls=%async_computation.5 | async-start | bytes 655360 | tf_op jit(solution)/shard_map/all_to_all | solution.py:819

commit v10 on v9

--- a/solution.py
+++ b/solution.py
@@ -814,8 +814,8 @@
         totals = [total] + [swapped(total, "row", mask) for mask in range(1, lax.axis_size("row"))]
     fresh = call(
         functools.partial(update_kernel, rows, len(totals)), shape((cols, rows + SUBLANES, order), jnp.int32), VMEM,
-        [SMEM, kind] + [VMEM] * len(totals) + [FREE] * len(before_update), [], 1 << 26,
-    )(me, probe, *totals, *before_update)
+        [SMEM, kind] + [VMEM] * len(totals) + [spec for spec, _ in before_update], [], 1 << 26,
+    )(me, probe, *totals, *[value for _, value in before_update])
     return total, lax.all_to_all(fresh, "col", split_axis=0, concat_axis=0, tiled=True)
 
 
@@ -903,7 +903,7 @@
     new_object = call(functools.partial(object_kernel, dims), shape(tile), VMEM, [LOAD, LOAD, VMEM, LOAD, LOAD], [], 1 << 26)(
         current, own, from_left, weights_old, weights_new
     )
-    _, chunks = probe_update(me, probe_now, numer, VMEM, False, [(HBM, weights_new)], [from_left])
+    _, chunks = probe_update(me, probe_now, numer, VMEM, False, [(FREE, to_right)], [(FREE, from_left), (HBM, weights_new)])
     new_probe = call(probe_kernel, shape(window), VMEM, [VMEM], [], 1 << 26)(chunks)
     return new_object, new_probe
 

time: 168 us -> 165 us (0.982)
  Pallas kernels: 55.7 us -> 70.4 us
  starting transfers between devices: 48.1 us -> 35.3 us
  waiting for transfers between devices: 36.2 us -> 30.5 us
    pallas_call x15, Pallas kernels: 55.7 us -> 70.4 us  [called(): pl.pallas_call(body, out_shape=tuple(fixed_outs) if several else fixed_ou...]
    ppermute x3, waiting for transfers between devices: 5.32 us -> 0.01 us  [swapped(): lax.ppermute(value, axis, [(k, k ^ mask) for k in range(lax.axis_size(axi...]
    all_to_all x1, starting transfers between devices: 7.76 us -> 3.49 us  [probe_update(): lax.all_to_all(numer, 'col', split_axis=0, concat_axis=0, tiled=True)]
    ppermute x9, starting transfers between devices: 16.7 us -> 12.7 us  [passed_along(): lax.ppermute(value, axis, [(source, source + steps) for source in range(l...]
    all_to_all x1, starting transfers between devices: 7.34 us -> 3.43 us  [probe_update(): lax.all_to_all(fresh, 'col', split_axis=0, concat_axis=0, tiled=True)]
    all_to_all x1, waiting for transfers between devices: 9.13 us -> 5.91 us  [local(): lax.all_to_all(outgoing, 'col', split_axis=0, concat_axis=0, tiled=True)]
    ppermute x9, waiting for transfers between devices: 14.8 us -> 17.7 us  [passed_along(): lax.ppermute(value, axis, [(source, source + steps) for source in range(l...]
  transfers between devices with their start and end apart: 16 -> 16, of which waited for: 8 -> 6; matrix products, arithmetic and copies ran while one was open for 0% -> 0% of each run, Pallas kernels for 17% -> 21%
where the time goes in v10:
time: 165 us; the launch traced here: 163 us
  Pallas kernels  70.4 us (43%)
  starting transfers between devices  35.3 us (21%)
  waiting for transfers between devices  30.5 us (18%)
  blocking collectives  25.1 us (15%)
    pallas_call x15, Pallas kernels, called(): pl.pallas_call(body, out_shape=tuple(fixed_outs) if several else fixed_ou...  70.4 us
    ppermute x9, waiting for transfers between devices, passed_along(): lax.ppermute(value, axis, [(source, source + steps) for source in range(l...  17.7 us
    all_to_all x1, blocking collectives, probe_update(): lax.all_to_all(fresh, 'col', split_axis=0, concat_axis=0, tiled=True)  13.6 us
    ppermute x9, starting transfers between devices, passed_along(): lax.ppermute(value, axis, [(source, source + steps) for source in range(l...  12.7 us
    all_to_all x1, blocking collectives, probe_update(): lax.all_to_all(numer, 'col', split_axis=0, concat_axis=0, tiled=True)  11.4 us
    all_to_all x1, starting transfers between devices, probe_update(): lax.all_to_all(total, 'row', split_axis=0, concat_axis=0, tiled=True)  7.23 us
    all_to_all x1, waiting for transfers between devices, local(): lax.all_to_all(outgoing, 'col', split_axis=0, concat_axis=0, tiled=True)  5.91 us
    all_to_all x1, waiting for transfers between devices, probe_update(): lax.all_to_all(fresh, 'col', split_axis=0, concat_axis=0, tiled=True)  4.97 us
  transfers between devices with their start and end apart: 16, of which 6 were waited for; matrix products, arithmetic and copies ran while one was open for 0% of the time, Pallas kernels for 21%

profile of v10, /device:TPU:0, one launch (start us, length us, event | category | flops | bytes accessed | tf_op | source)
XLA Modules:
  0.0 163.0 jit_solution(3889732714242223918)
XLA Ops:
  1.9 1.3 collective-permute-start.1
  3.2 1.3 collective-permute-start
  4.5 8.7 %collective-permute-done.1.refs_4_ = s32[264,256]{1,0:T(8,128)S(1)} collective-permute-done((s32[264,256]{1,0:T(8,128)S(1)}, s32[264,256]{1,0:T(8,128)S(1)}, u32[]{:S(2)}, u32[]{:S(2)}) %collective-permute-start.1) | collective-permute-done | bytes 270368 | tf_op jit(solution)/shard_map/ppermute | solution.py:795
  13.9 2.5 %shard_map.89 = bf16[16,256,256]{2,1,0:T(8,128)(2,1)} custom-call(s32[256]{0:T(256)S(1)} %bitcast.5, s32[2]{0:T(128)S(1)} %pad_add_fusion.refs_1_.refs_0_, bf16[4,256,256]{2,1,0:T(8,128)(2,1)} %refs_2_.6, s32[264,256]{1,0:T(8,128)S(1)} %collective-permute-done.refs_3_, s32[264,256]{1,0:T(8,128)S(1)} %collective-permute-done.1.refs_4_), custom_call_target="tpu_custom_call" | custom-call | flops 1048576 | bytes 8388608 | tf_op jit(solution)/shard_map/pallas_call | solution.py:779
  16.4 3.9 %all-to-all-start = ((bf16[16,256,256]{2,1,0:T(8,128)(2,1)}), bf16[16,256,256]{2,1,0:T(8,128)(2,1)S(1)}, u32[]{:S(2)}, u32[]{:S(2)}) async-start(bf16[16,256,256]{2,1,0:T(8,128)(2,1)} %shard_map.89), calls=%async_computation | async-start | bytes 4194304 | tf_op jit(solution)/shard_map/all_to_all | solution.py:850
  20.3 1.3 collective-permute-start.2
  21.6 8.5 %shard_map.88.refs_4_.refs_6_.refs_3_ = f32[512,512]{1,0:T(8,128)} custom-call(s32[256]{0:T(256)S(1)} %bitcast.6, s32[2]{0:T(128)S(1)} %pad_add_fusion.refs_1_.refs_0_, f32[2,256,256]{2,1,0:T(8,128)} %refs_1_.1), custom_call_target="tpu_custom_call" | custom-call | flops 8589934592 | bytes 8388608 | tf_op jit(solution)/shard_map/pallas_call | solution.py:779
  31.2 9.8 %shard_map.87 = (f32[8,2,256,256]{3,2,1,0:T(8,128)}, f32[8,2,256,256]{3,2,1,0:T(8,128)}, f32[256,256]{1,0:T(8,128)S(1)}, f32[2,512,512]{2,1,0:T(8,128)}) custom-call(s32[256]{0:T(256)S(1)} %bitcast.7, s32[2]{0:T(128)S(1)} %pad_add_fusion.refs_1_.refs_0_, f32[2,256,256]{2,1,0:T(8,128)} %refs_2_.4, s32[264,256]{1,0:T(8,128)S(1)} %collective-permute-done.refs_3_, ...), custom_call_target="tpu_custom_call" | custom-call | flops 3221225472 | bytes 8388608 | tf_op jit(solution)/shard_map/pallas_call | solution.py:779
  41.0 5.9 %all-to-all-done.refs_7_ = bf16[16,256,256]{2,1,0:T(8,128)(2,1)S(1)} async-done(((bf16[16,256,256]{2,1,0:T(8,128)(2,1)}), bf16[16,256,256]{2,1,0:T(8,128)(2,1)S(1)}, u32[]{:S(2)}, u32[]{:S(2)}) %all-to-all-start) | async-done | bytes 2097184 | tf_op jit(solution)/shard_map/all_to_all | solution.py:850
  46.9 12.6 %shard_map.90 = (f32[2,512,512]{2,1,0:T(8,128)}, s32[264,512]{1,0:T(8,128)S(1)}, s32[264,512]{1,0:T(8,128)S(1)}, s32[8,56,256]{2,1,0:T(8,128)S(1)}, bf16[8,256,256]{2,1,0:T(8,128)(2,1)}) custom-call(s32[256]{0:T(256)S(1)} %bitcast.8, s32[2]{0:T(128)S(1)} %pad_add_fusion.refs_1_.refs_0_, f32[2,256,256]{2,1,0:T(8,128)} %refs_1_.1, ...), custom_call_target="tpu_custom_call" | custom-call | flops 3221225472 | bytes 8388608 | tf_op jit(solution)/shard_map/pallas_call | solution.py:779
  59.6 1.3 collective-permute-start.3
  60.9 1.3 collective-permute-start.4
  62.2 11.4 %all_to_all.30.refs_0_ = s32[8,56,256]{2,1,0:T(8,128)S(1)} all-to-all(s32[8,56,256]{2,1,0:T(8,128)S(1)} %get-tuple-element.28), channel_id=1, replica_groups=mesh['row'=4,'col'=8] {'col'}, dimensions={0} | all-to-all | bytes 917504 | tf_op jit(solution)/shard_map/all_to_all | solution.py:805
  74.5 7.2 %all-to-all-start.2 = ((s32[4,56,256]{2,1,0:T(8,128)}), s32[4,56,256]{2,1,0:T(8,128)S(1)}, u32[]{:S(2)}, u32[]{:S(2)}) async-start(s32[4,56,256]{2,1,0:T(8,128)} %shard_map.91.refs_3_), calls=%async_computation.2 | async-start | bytes 458752 | tf_op jit(solution)/shard_map/all_to_all | solution.py:812
  81.8 3.3 %shard_map.92 = (f32[2,512,512]{2,1,0:T(8,128)}, s32[528,256]{1,0:T(8,128)S(1)}, s32[528,256]{1,0:T(8,128)S(1)}) custom-call(f32[2,512,512]{2,1,0:T(8,128)} %get-tuple-element.25.refs_0_, s32[264,512]{1,0:T(8,128)S(1)} %collective-permute-done.3.refs_1_, s32[264,512]{1,0:T(8,128)S(1)} %collective-permute-done.4.refs_2_, s32[4,56,256]{2,1,0:T(8,128)} %shard_map.91.refs_3_), custom_call_target="tpu_custom_call" | custom-call | flops 67108864 | bytes 8388608 | tf_op jit(solution)/shard_map/pallas_call | solution.py:779
  85.1 1.3 collective-permute-start.5
  86.4 1.3 collective-permute-start.6
  87.7 1.9 %all-to-all-done.2.refs_2_ = s32[4,56,256]{2,1,0:T(8,128)S(1)} async-done(((s32[4,56,256]{2,1,0:T(8,128)}), s32[4,56,256]{2,1,0:T(8,128)S(1)}, u32[]{:S(2)}, u32[]{:S(2)}) %all-to-all-start.2) | async-done | bytes 229408 | tf_op jit(solution)/shard_map/all_to_all | solution.py:812
  89.6 1.7 %shard_map.93 = s32[8,40,256]{2,1,0:T(8,128)S(1)} custom-call(s32[2]{0:T(128)S(1)} %pad_add_fusion.refs_1_.refs_0_, f32[2,256,256]{2,1,0:T(8,128)} %refs_1_.1, s32[4,56,256]{2,1,0:T(8,128)S(1)} %all-to-all-done.2.refs_2_), custom_call_target="tpu_custom_call" | custom-call | flops 67108864 | bytes 8388608 | tf_op jit(solution)/shard_map/pallas_call | solution.py:779
  91.3 13.6 %all_to_all.31.refs_7_ = s32[8,40,256]{2,1,0:T(8,128)S(1)} all-to-all(s32[8,40,256]{2,1,0:T(8,128)S(1)} %shard_map.93), channel_id=1, replica_groups=mesh['row'=4,'col'=8] {'col'}, dimensions={0} | all-to-all | bytes 655360 | tf_op jit(solution)/shard_map/all_to_all | solution.py:819
  105.0 18.0 %shard_map.94 = (f32[2,256,256]{2,1,0:T(8,128)}, f32[2,256,512]{2,1,0:T(8,128)}, s32[264,512]{1,0:T(8,128)S(1)}, s32[8,56,256]{2,1,0:T(8,128)}, f32[2,256,256]{2,1,0:T(8,128)S(1)}) custom-call(s32[256]{0:T(256)S(1)} %bitcast.9, s32[2]{0:T(128)S(1)} %pad_add_fusion.refs_1_.refs_0_, f32[2,512,512]{2,1,0:T(8,128)} %get-tuple-element.21.refs_2_, ...), custom_call_target="tpu_custom_call" | custom-call | flops 6442450944 | bytes 8388608 | tf_op jit(solution)/shard_map/pallas_call | solution.py:779
  123.0 1.3 collective-permute-start.7
  124.3 3.5 %all-to-all-start.4 = ((s32[8,56,256]{2,1,0:T(8,128)}), s32[8,56,256]{2,1,0:T(8,128)S(1)}, u32[]{:S(2)}, u32[]{:S(2)}) async-start(s32[8,56,256]{2,1,0:T(8,128)} %get-tuple-element.39), calls=%async_computation.4 | async-start | bytes 917504 | tf_op jit(solution)/shard_map/all_to_all | solution.py:805
  127.8 7.9 %collective-permute-done.7.refs_1_ = s32[264,512]{1,0:T(8,128)S(1)} collective-permute-done((s32[264,512]{1,0:T(8,128)S(1)}, s32[264,512]{1,0:T(8,128)S(1)}, u32[]{:S(2)}, u32[]{:S(2)}) %collective-permute-start.7) | collective-permute-done | bytes 540704 | tf_op jit(solution)/shard_map/ppermute | solution.py:795
  135.7 2.1 %shard_map.95 = (f32[2,256,256]{2,1,0:T(8,128)}, s32[264,256]{1,0:T(8,128)S(1)}) custom-call(f32[2,256,512]{2,1,0:T(8,128)} %get-tuple-element.34.refs_0_, s32[264,512]{1,0:T(8,128)S(1)} %collective-permute-done.7.refs_1_), custom_call_target="tpu_custom_call" | custom-call | flops 67108864 | bytes 8388608 | tf_op jit(solution)/shard_map/pallas_call | solution.py:779
  138.0 2.9 %collective-permute-start.11 = (s32[1,56,256]{2,1,0:T(8,128)S(1)}, s32[1,56,256]{2,1,0:T(8,128)S(1)}, u32[]{:S(2)}, u32[]{:S(2)}) collective-permute-start(s32[1,56,256]{2,1,0:T(8,128)S(1)} %shard_map.98.refs_2_), channel_id=1, source_target_pairs={{0,24},{8,16},{16,8},{24,0},{1,25},{9,17},{17,9},{25,1},{2,26},{10... | collective-permute-start | bytes 172040 | tf_op jit(solution)/shard_map/ppermute | solution.py:799
  142.6 2.3 %collective-permute-start.8 = (s32[264,256]{1,0:T(8,128)S(1)}, s32[264,256]{1,0:T(8,128)S(1)}, u32[]{:S(2)}, u32[]{:S(2)}) collective-permute-start(s32[264,256]{1,0:T(8,128)S(1)} %get-tuple-element.37.refs_1_), channel_id=1, source_target_pairs={{0,1},{1,2},{2,3},{3,4},{4,5},{5,6},{6,7},{8,9},{9,10},{10,11},{11... | collective-permute-start | bytes 811016 | tf_op jit(solution)/shard_map/ppermute | solution.py:795
  144.9 4.8 %shard_map.96.refs_4_.refs_7_ = f32[256,256]{1,0:T(8,128)} custom-call(s32[256]{0:T(256)S(1)} %bitcast.10, s32[2]{0:T(128)S(1)} %pad_add_fusion.refs_1_.refs_0_, f32[2,256,256]{2,1,0:T(8,128)S(1)} %get-tuple-element.38.refs_2_.refs_1_), custom_call_target="tpu_custom_call" | custom-call | flops 8589934592 | bytes 8388608 | tf_op jit(solution)/shard_map/pallas_call | solution.py:779
  149.7 1.4 shard_map.99
  151.1 3.4 %all-to-all-start.5 = ((s32[8,40,256]{2,1,0:T(8,128)}), s32[8,40,256]{2,1,0:T(8,128)S(1)}, u32[]{:S(2)}, u32[]{:S(2)}) async-start(s32[8,40,256]{2,1,0:T(8,128)} %shard_map.99), calls=%async_computation.5 | async-start | bytes 655360 | tf_op jit(solution)/shard_map/all_to_all | solution.py:819
  154.5 2.6 %shard_map.97 = f32[2,256,256]{2,1,0:T(8,128)} custom-call(f32[2,256,256]{2,1,0:T(8,128)} %get-tuple-element.33.refs_0_, f32[2,256,256]{2,1,0:T(8,128)} %get-tuple-element.36.refs_1_, s32[264,256]{1,0:T(8,128)S(1)} %collective-permute-done.8.refs_2_.refs_6_, f32[512,512]{1,0:T(8,128)} %shard_map.88.refs_4_.refs_6_.refs_3_, f32[256,256]{1,0:T(8,128)} %shard_map.96.refs_4_.refs_7_), custom_call_target="tpu_custom_call" | custom-call | flops 67108864 | bytes 8388608 | tf_op jit(solution)/shard_map/pallas_call | solution.py:779
  157.1 5.0 %all-to-all-done.5.refs_0_ = s32[8,40,256]{2,1,0:T(8,128)S(1)} async-done(((s32[8,40,256]{2,1,0:T(8,128)}), s32[8,40,256]{2,1,0:T(8,128)S(1)}, u32[]{:S(2)}, u32[]{:S(2)}) %all-to-all-start.5) | async-done | bytes 327712 | tf_op jit(solution)/shard_map/all_to_all | solution.py:819
  (22 shorter events, 6.8 us)
Async XLA Ops:
  1.9 11.4 %collective-permute-start.1 = (s32[264,256]{1,0:T(8,128)S(1)}, s32[264,256]{1,0:T(8,128)S(1)}, u32[]{:S(2)}, u32[]{:S(2)}) collective-permute-start(s32[264,256]{1,0:T(8,128)S(1)} %shard_map.86), channel_id=1, source_target_pairs={{8,0},{16,8},{24,16},{9,1},{17,9},{25,17},{10,2},{18,10},{26,18},{... | collective-permute-start | bytes 811016 | tf_op jit(solution)/shard_map/ppermute | solution.py:795
  3.2 10.1 %collective-permute-start = (s32[264,256]{1,0:T(8,128)S(1)}, s32[264,256]{1,0:T(8,128)S(1)}, u32[]{:S(2)}, u32[]{:S(2)}) collective-permute-start(s32[264,256]{1,0:T(8,128)S(1)} %shard_map.86), channel_id=1, source_target_pairs={{1,0},{2,1},{3,2},{4,3},{5,4},{6,5},{7,6},{9,8},{10,9},{11,10},{12... | collective-permute-start | bytes 811016 | tf_op jit(solution)/shard_map/ppermute | solution.py:795
  13.3 0.7 copy-start
  16.4 30.5 %all-to-all-start = ((bf16[16,256,256]{2,1,0:T(8,128)(2,1)}), bf16[16,256,256]{2,1,0:T(8,128)(2,1)S(1)}, u32[]{:S(2)}, u32[]{:S(2)}) async-start(bf16[16,256,256]{2,1,0:T(8,128)(2,1)} %shard_map.89), calls=%async_computation | async-start | bytes 4194304 | tf_op jit(solution)/shard_map/all_to_all | solution.py:850
  20.3 10.9 %copy-start.1 = (s32[128,2]{0,1:T(2,128)S(1)}, s32[128,2]{0,1:T(2,128)}, u32[]{:S(2)}) copy-start(s32[128,2]{0,1:T(2,128)} %param.10) | copy-start | bytes 3076
  20.3 10.9 %collective-permute-start.2 = (s32[264,256]{1,0:T(8,128)S(1)}, s32[264,256]{1,0:T(8,128)S(1)}, u32[]{:S(2)}, u32[]{:S(2)}) collective-permute-start(s32[264,256]{1,0:T(8,128)S(1)} %collective-permute-done.refs_3_), channel_id=1, source_target_pairs={{8,0},{16,8},{24,16},{9,1},{17,9},{25,17},{10,2},{18,10},{26,18},{... | collective-permute-start | bytes 811016 | tf_op jit(solution)/shard_map/ppermute | solution.py:795
  59.6 22.2 %collective-permute-start.3 = (s32[264,512]{1,0:T(8,128)S(1)}, s32[264,512]{1,0:T(8,128)S(1)}, u32[]{:S(2)}, u32[]{:S(2)}) collective-permute-start(s32[264,512]{1,0:T(8,128)S(1)} %get-tuple-element.26), channel_id=1, source_target_pairs={{0,8},{8,16},{16,24},{1,9},{9,17},{17,25},{2,10},{10,18},{18,26},{... | collective-permute-start | bytes 1622024 | tf_op jit(solution)/shard_map/ppermute | solution.py:795
  60.9 20.9 %collective-permute-start.4 = (s32[264,512]{1,0:T(8,128)S(1)}, s32[264,512]{1,0:T(8,128)S(1)}, u32[]{:S(2)}, u32[]{:S(2)}) collective-permute-start(s32[264,512]{1,0:T(8,128)S(1)} %get-tuple-element.27), channel_id=1, source_target_pairs={{8,0},{16,8},{24,16},{9,1},{17,9},{25,17},{10,2},{18,10},{26,18},{... | collective-permute-start | bytes 1622024 | tf_op jit(solution)/shard_map/ppermute | solution.py:795
  74.5 15.1 %all-to-all-start.2 = ((s32[4,56,256]{2,1,0:T(8,128)}), s32[4,56,256]{2,1,0:T(8,128)S(1)}, u32[]{:S(2)}, u32[]{:S(2)}) async-start(s32[4,56,256]{2,1,0:T(8,128)} %shard_map.91.refs_3_), calls=%async_computation.2 | async-start | bytes 458752 | tf_op jit(solution)/shard_map/all_to_all | solution.py:812
  85.1 19.9 %collective-permute-start.5 = (s32[528,256]{1,0:T(8,128)S(1)}, s32[528,256]{1,0:T(8,128)S(1)}, u32[]{:S(2)}, u32[]{:S(2)}) collective-permute-start(s32[528,256]{1,0:T(8,128)S(1)} %get-tuple-element.30), channel_id=1, source_target_pairs={{0,1},{1,2},{2,3},{3,4},{4,5},{5,6},{6,7},{8,9},{9,10},{10,11},{11... | collective-permute-start | bytes 1622024 | tf_op jit(solution)/shard_map/ppermute | solution.py:795
  86.4 18.6 %collective-permute-start.6 = (s32[528,256]{1,0:T(8,128)S(1)}, s32[528,256]{1,0:T(8,128)S(1)}, u32[]{:S(2)}, u32[]{:S(2)}) collective-permute-start(s32[528,256]{1,0:T(8,128)S(1)} %get-tuple-element.31), channel_id=1, source_target_pairs={{1,0},{2,1},{3,2},{4,3},{5,4},{6,5},{7,6},{9,8},{10,9},{11,10},{12... | collective-permute-start | bytes 1622024 | tf_op jit(solution)/shard_map/ppermute | solution.py:795
  123.0 12.7 %collective-permute-start.7 = (s32[264,512]{1,0:T(8,128)S(1)}, s32[264,512]{1,0:T(8,128)S(1)}, u32[]{:S(2)}, u32[]{:S(2)}) collective-permute-start(s32[264,512]{1,0:T(8,128)S(1)} %get-tuple-element.35), channel_id=1, source_target_pairs={{0,8},{8,16},{16,24},{1,9},{9,17},{17,25},{2,10},{10,18},{18,26},{... | collective-permute-start | bytes 1622024 | tf_op jit(solution)/shard_map/ppermute | solution.py:795
  124.3 13.5 %all-to-all-start.4 = ((s32[8,56,256]{2,1,0:T(8,128)}), s32[8,56,256]{2,1,0:T(8,128)S(1)}, u32[]{:S(2)}, u32[]{:S(2)}) async-start(s32[8,56,256]{2,1,0:T(8,128)} %get-tuple-element.39), calls=%async_computation.4 | async-start | bytes 917504 | tf_op jit(solution)/shard_map/all_to_all | solution.py:805
  138.0 11.7 %collective-permute-start.11 = (s32[1,56,256]{2,1,0:T(8,128)S(1)}, s32[1,56,256]{2,1,0:T(8,128)S(1)}, u32[]{:S(2)}, u32[]{:S(2)}) collective-permute-start(s32[1,56,256]{2,1,0:T(8,128)S(1)} %shard_map.98.refs_2_), channel_id=1, source_target_pairs={{0,24},{8,16},{16,8},{24,0},{1,25},{9,17},{17,9},{25,1},{2,26},{10... | collective-permute-start | bytes 172040 | tf_op jit(solution)/shard_map/ppermute | solution.py:799
  140.9 8.8 %collective-permute-start.10 = (s32[1,56,256]{2,1,0:T(8,128)S(1)}, s32[1,56,256]{2,1,0:T(8,128)S(1)}, u32[]{:S(2)}, u32[]{:S(2)}) collective-permute-start(s32[1,56,256]{2,1,0:T(8,128)S(1)} %shard_map.98.refs_2_), channel_id=1, source_target_pairs={{0,16},{8,24},{16,0},{24,8},{1,17},{9,25},{17,1},{25,9},{2,18},{10... | collective-permute-start | bytes 172040 | tf_op jit(solution)/shard_map/ppermute | solution.py:799
  142.1 7.6 %collective-permute-start.9 = (s32[1,56,256]{2,1,0:T(8,128)S(1)}, s32[1,56,256]{2,1,0:T(8,128)S(1)}, u32[]{:S(2)}, u32[]{:S(2)}) collective-permute-start(s32[1,56,256]{2,1,0:T(8,128)S(1)} %shard_map.98.refs_2_), channel_id=1, source_target_pairs={{0,8},{8,0},{16,24},{24,16},{1,9},{9,1},{17,25},{25,17},{2,10},{10... | collective-permute-start | bytes 172040 | tf_op jit(solution)/shard_map/ppermute | solution.py:799
  142.6 7.1 %collective-permute-start.8 = (s32[264,256]{1,0:T(8,128)S(1)}, s32[264,256]{1,0:T(8,128)S(1)}, u32[]{:S(2)}, u32[]{:S(2)}) collective-permute-start(s32[264,256]{1,0:T(8,128)S(1)} %get-tuple-element.37.refs_1_), channel_id=1, source_target_pairs={{0,1},{1,2},{2,3},{3,4},{4,5},{5,6},{6,7},{8,9},{9,10},{10,11},{11... | collective-permute-start | bytes 811016 | tf_op jit(solution)/shard_map/ppermute | solution.py:795
  151.1 11.0 %all-to-all-start.5 = ((s32[8,40,256]{2,1,0:T(8,128)}), s32[8,40,256]{2,1,0:T(8,128)S(1)}, u32[]{:S(2)}, u32[]{:S(2)}) async-start(s32[8,40,256]{2,1,0:T(8,128)} %shard_map.99), calls=%async_computation.5 | async-start | bytes 655360 | tf_op jit(solution)/shard_map/all_to_all | solution.py:819

commit v11 on v10

--- a/solution.py
+++ b/solution.py
@@ -605,7 +605,7 @@
     keep.wait()
 
 
-def rows_sum_kernel(dims, share_ref, above_ref, below_ref, after_ref, sum_out, left_out, right_out, sem):
+def rows_sum_kernel(dims, share_ref, above_ref, below_ref, sum_out, left_out, right_out, sem):
     tile_rows, tile_cols = dims[:2]
     for i, ref in enumerate((above_ref, below_ref)):
         for col in range(0, 2 * tile_cols, LANES):
@@ -698,7 +698,7 @@
     give.wait()
 
 
-def fold_kernel(dims, top_ref, above_ref, own_out, right_out, own_ref, sem):
+def fold_kernel(dims, top_ref, above_ref, after_ref, own_out, right_out, own_ref, sem):
     tile_rows, tile_cols = dims[:2]
     for col in range(0, 2 * tile_cols, LANES):
         for start in range(0, tile_rows, CHUNK):
@@ -799,24 +799,20 @@
     return lax.ppermute(value, axis, [(k, k ^ mask) for k in range(lax.axis_size(axis))])
 
 
-def probe_update(me, probe, numer, kind, at_once, before_sum, before_update):
+def probe_update(me, probe, numer, kind, before_sum, before_update):
     cols, order = lax.axis_size("col"), probe.shape[1]
     rows = order // cols
     parts = lax.all_to_all(numer, "col", split_axis=0, concat_axis=0, tiled=True)
-    blocks = lax.axis_size("row") if at_once else 1
     total = call(
-        functools.partial(sums_kernel, rows), shape((blocks, sums_rows(rows), order), jnp.int32), VMEM,
+        functools.partial(sums_kernel, rows), shape((1, sums_rows(rows), order), jnp.int32), VMEM,
         [VMEM] + [spec for spec, _ in before_sum], [], 1 << 26,
     )(parts, *[value for _, value in before_sum])
-    if at_once:
-        totals = [lax.all_to_all(total, "row", split_axis=0, concat_axis=0, tiled=True)]
-    else:
-        totals = [total] + [swapped(total, "row", mask) for mask in range(1, lax.axis_size("row"))]
+    totals = [total] + [swapped(total, "row", mask) for mask in range(1, lax.axis_size("row"))]
     fresh = call(
         functools.partial(update_kernel, rows, len(totals)), shape((cols, rows + SUBLANES, order), jnp.int32), VMEM,
         [SMEM, kind] + [VMEM] * len(totals) + [spec for spec, _ in before_update], [], 1 << 26,
     )(me, probe, *totals, *[value for _, value in before_update])
-    return total, lax.all_to_all(fresh, "col", split_axis=0, concat_axis=0, tiled=True)
+    return lax.all_to_all(fresh, "col", split_axis=0, concat_axis=0, tiled=True)
 
 
 def local(obj, probe, amplitudes, positions):
@@ -878,12 +874,12 @@
 
     from_above = passed_along(bottom, "row", 1)
     from_below = passed_along(top, "row", -1)
-    total, chunks = probe_update(me, probe, numer, LOAD, True, [], [])
     sums, to_left, to_right = call(
-        functools.partial(rows_sum_kernel, dims), (shape(wide), coded_col, coded_col), (HBM, VMEM, VMEM), [LOAD, VMEM, VMEM, FREE], [pltpu.SemaphoreType.DMA], 1 << 26,
-    )(share, from_above, from_below, total)
+        functools.partial(rows_sum_kernel, dims), (shape(wide), coded_col, coded_col), (HBM, VMEM, VMEM), [LOAD, VMEM, VMEM], [pltpu.SemaphoreType.DMA], 1 << 26,
+    )(share, from_above, from_below)
     from_left = passed_along(to_right, "col", 1)
     from_right = passed_along(to_left, "col", -1)
+    chunks = probe_update(me, probe, numer, LOAD, [(FREE, to_left)], [])
 
     current, top, bottom, numer, probe_now = call(
         functools.partial(whole_kernel, dims), (shape(tile), shape((2, tile_rows, 2 * tile_cols)), coded_row, shares, shape(window)), (HBM, HBM) + (VMEM,) * 3,
@@ -897,13 +893,13 @@
     from_above = passed_along(bottom, "row", 1)
     weights_new = weights(probe_now, 1, VMEM)
     own, to_right = call(
-        functools.partial(fold_kernel, dims), (shape(tile), coded_tile), (HBM, VMEM), [LOAD, VMEM], [pltpu.VMEM(tile, f32), pltpu.SemaphoreType.DMA], 1 << 26,
-    )(top, from_above)
+        functools.partial(fold_kernel, dims), (shape(tile), coded_tile), (HBM, VMEM), [LOAD, VMEM, HBM], [pltpu.VMEM(tile, f32), pltpu.SemaphoreType.DMA], 1 << 26,
+    )(top, from_above, weights_new)
     from_left = passed_along(to_right, "col", 1)
     new_object = call(functools.partial(object_kernel, dims), shape(tile), VMEM, [LOAD, LOAD, VMEM, LOAD, LOAD], [], 1 << 26)(
         current, own, from_left, weights_old, weights_new
     )
-    _, chunks = probe_update(me, probe_now, numer, VMEM, False, [(FREE, to_right)], [(FREE, from_left), (HBM, weights_new)])
+    chunks = probe_update(me, probe_now, numer, VMEM, [(FREE, to_right)], [(FREE, from_left)])
     new_probe = call(probe_kernel, shape(window), VMEM, [VMEM], [], 1 << 26)(chunks)
     return new_object, new_probe
 

time: 165 us -> 169 us (1.024); the launches traced: 163 us -> 169 us
  waiting for transfers between devices: 30.5 us -> 42.3 us
  blocking collectives: 25.1 us -> 15.2 us
  starting transfers between devices: 35.3 us -> 39.6 us
    all_to_all x2 -> x1, blocking collectives: 25.1 us -> 15.2 us  [probe_update(): return lax.all_to_all(fresh, 'col', split_axis=0, concat_axis=0, tiled=True)]
    ppermute x3 -> x6, waiting for transfers between devices: 0.01 us -> 7.48 us  [swapped(): lax.ppermute(value, axis, [(k, k ^ mask) for k in range(lax.axis_size(axi...]
    all_to_all x2 -> x1, starting transfers between devices: 10.7 us -> 3.95 us  [probe_update(): return lax.all_to_all(fresh, 'col', split_axis=0, concat_axis=0, tiled=True)]
    ppermute x9, waiting for transfers between devices: 17.7 us -> 23.8 us  [passed_along(): lax.ppermute(value, axis, [(source, source + steps) for source in range(l...]
    ppermute x3 -> x6, starting transfers between devices: 4.6 us -> 8.9 us  [swapped(): lax.ppermute(value, axis, [(k, k ^ mask) for k in range(lax.axis_size(axi...]
    all_to_all x1 -> x2, starting transfers between devices: 3.49 us -> 6.97 us  [probe_update(): lax.all_to_all(numer, 'col', split_axis=0, concat_axis=0, tiled=True)]
    ppermute x9, starting transfers between devices: 12.7 us -> 15.9 us  [passed_along(): lax.ppermute(value, axis, [(source, source + steps) for source in range(l...]
    all_to_all x2 -> x1, waiting for transfers between devices: 6.87 us -> 5.05 us  [probe_update(): return lax.all_to_all(fresh, 'col', split_axis=0, concat_axis=0, tiled=True)]
  transfers between devices with their start and end apart: 16 -> 19, of which waited for: 6 -> 11; matrix products, arithmetic and copies ran while one was open for 0% -> 0% of each run, Pallas kernels for 21% -> 19%
where the time goes in v11:
time: 169 us
  Pallas kernels  70.3 us (42%)
  waiting for transfers between devices  42.3 us (25%)
  starting transfers between devices  39.6 us (23%)
  blocking collectives  15.2 us (9%)
    pallas_call x15, Pallas kernels, called(): pl.pallas_call(body, out_shape=tuple(fixed_outs) if several else fixed_ou...  70.3 us
    ppermute x9, waiting for transfers between devices, passed_along(): lax.ppermute(value, axis, [(source, source + steps) for source in range(l...  23.8 us
    ppermute x9, starting transfers between devices, passed_along(): lax.ppermute(value, axis, [(source, source + steps) for source in range(l...  15.9 us
    all_to_all x1, blocking collectives, probe_update(): return lax.all_to_all(fresh, 'col', split_axis=0, concat_axis=0, tiled=True)  15.2 us
    ppermute x6, starting transfers between devices, swapped(): lax.ppermute(value, axis, [(k, k ^ mask) for k in range(lax.axis_size(axi...  8.9 us
    ppermute x6, waiting for transfers between devices, swapped(): lax.ppermute(value, axis, [(k, k ^ mask) for k in range(lax.axis_size(axi...  7.48 us
    all_to_all x2, starting transfers between devices, probe_update(): lax.all_to_all(numer, 'col', split_axis=0, concat_axis=0, tiled=True)  6.97 us
    all_to_all x1, waiting for transfers between devices, local(): lax.all_to_all(outgoing, 'col', split_axis=0, concat_axis=0, tiled=True)  5.95 us
  transfers between devices with their start and end apart: 19, of which 11 were waited for; matrix products, arithmetic and copies ran while one was open for 0% of the time, Pallas kernels for 19%

profile of v11, /device:TPU:0, one launch (start us, length us, event | category | flops | bytes accessed | tf_op | source)
XLA Modules:
  0.0 169.1 jit_solution(11160068760724208562)
XLA Ops:
  4.5 8.7 %collective-permute-done.1.refs_4_ = s32[264,256]{1,0:T(8,128)S(1)} collective-permute-done((s32[264,256]{1,0:T(8,128)S(1)}, s32[264,256]{1,0:T(8,128)S(1)}, u32[]{:S(2)}, u32[]{:S(2)}) %collective-permute-start.1) | collective-permute-done | bytes 270368 | tf_op jit(solution)/shard_map/ppermute | solution.py:795
  13.9 2.4 %shard_map.89 = bf16[16,256,256]{2,1,0:T(8,128)(2,1)} custom-call(s32[256]{0:T(256)S(1)} %bitcast.5, s32[2]{0:T(128)S(1)} %pad_add_fusion.refs_1_.refs_0_, bf16[4,256,256]{2,1,0:T(8,128)(2,1)} %refs_2_.6, s32[264,256]{1,0:T(8,128)S(1)} %collective-permute-done.refs_3_, s32[264,256]{1,0:T(8,128)S(1)} %collective-permute-done.1.refs_4_), custom_call_target="tpu_custom_call" | custom-call | flops 1048576 | bytes 8388608 | tf_op jit(solution)/shard_map/pallas_call | solution.py:779
  16.4 3.9 %all-to-all-start = ((bf16[16,256,256]{2,1,0:T(8,128)(2,1)}), bf16[16,256,256]{2,1,0:T(8,128)(2,1)S(1)}, u32[]{:S(2)}, u32[]{:S(2)}) async-start(bf16[16,256,256]{2,1,0:T(8,128)(2,1)} %shard_map.89), calls=%async_computation | async-start | bytes 4194304 | tf_op jit(solution)/shard_map/all_to_all | solution.py:846
  21.6 8.2 %shard_map.88.refs_4_.refs_6_.refs_3_ = f32[512,512]{1,0:T(8,128)} custom-call(s32[256]{0:T(256)S(1)} %bitcast.6, s32[2]{0:T(128)S(1)} %pad_add_fusion.refs_1_.refs_0_, f32[2,256,256]{2,1,0:T(8,128)} %refs_1_.1), custom_call_target="tpu_custom_call" | custom-call | flops 8589934592 | bytes 8388608 | tf_op jit(solution)/shard_map/pallas_call | solution.py:779
  29.8 1.4 collective-permute-done.2.refs_5_
  31.2 9.8 %shard_map.87 = (f32[8,2,256,256]{3,2,1,0:T(8,128)}, f32[8,2,256,256]{3,2,1,0:T(8,128)}, f32[256,256]{1,0:T(8,128)S(1)}, f32[2,512,512]{2,1,0:T(8,128)}) custom-call(s32[256]{0:T(256)S(1)} %bitcast.7, s32[2]{0:T(128)S(1)} %pad_add_fusion.refs_1_.refs_0_, f32[2,256,256]{2,1,0:T(8,128)} %refs_2_.4, s32[264,256]{1,0:T(8,128)S(1)} %collective-permute-done.refs_3_, ...), custom_call_target="tpu_custom_call" | custom-call | flops 3221225472 | bytes 8388608 | tf_op jit(solution)/shard_map/pallas_call | solution.py:779
  41.0 5.9 %all-to-all-done.refs_7_ = bf16[16,256,256]{2,1,0:T(8,128)(2,1)S(1)} async-done(((bf16[16,256,256]{2,1,0:T(8,128)(2,1)}), bf16[16,256,256]{2,1,0:T(8,128)(2,1)S(1)}, u32[]{:S(2)}, u32[]{:S(2)}) %all-to-all-start) | async-done | bytes 2097184 | tf_op jit(solution)/shard_map/all_to_all | solution.py:846
  46.9 13.3 %shard_map.90 = (f32[2,512,512]{2,1,0:T(8,128)}, s32[264,512]{1,0:T(8,128)S(1)}, s32[264,512]{1,0:T(8,128)S(1)}, s32[8,56,256]{2,1,0:T(8,128)}, bf16[8,256,256]{2,1,0:T(8,128)(2,1)}) custom-call(s32[256]{0:T(256)S(1)} %bitcast.8, s32[2]{0:T(128)S(1)} %pad_add_fusion.refs_1_.refs_0_, f32[2,256,256]{2,1,0:T(8,128)} %refs_1_.1, ...), custom_call_target="tpu_custom_call" | custom-call | flops 3221225472 | bytes 8388608 | tf_op jit(solution)/shard_map/pallas_call | solution.py:779
  60.3 3.6 %collective-permute-start.3 = (s32[264,512]{1,0:T(8,128)S(1)}, s32[264,512]{1,0:T(8,128)S(1)}, u32[]{:S(2)}, u32[]{:S(2)}) collective-permute-start(s32[264,512]{1,0:T(8,128)S(1)} %get-tuple-element.26), channel_id=1, source_target_pairs={{0,8},{8,16},{16,24},{1,9},{9,17},{17,25},{2,10},{10,18},{18,26},{... | collective-permute-start | bytes 1622024 | tf_op jit(solution)/shard_map/ppermute | solution.py:795
  65.2 3.5 %all-to-all-start.1 = ((s32[8,56,256]{2,1,0:T(8,128)}), s32[8,56,256]{2,1,0:T(8,128)S(1)}, u32[]{:S(2)}, u32[]{:S(2)}) async-start(s32[8,56,256]{2,1,0:T(8,128)} %get-tuple-element.31), calls=%async_computation.1 | async-start | bytes 917504 | tf_op jit(solution)/shard_map/all_to_all | solution.py:805
  68.7 2.0 %collective-permute-done.3.refs_1_ = s32[264,512]{1,0:T(8,128)S(1)} collective-permute-done((s32[264,512]{1,0:T(8,128)S(1)}, s32[264,512]{1,0:T(8,128)S(1)}, u32[]{:S(2)}, u32[]{:S(2)}) %collective-permute-start.3) | collective-permute-done | bytes 540704 | tf_op jit(solution)/shard_map/ppermute | solution.py:795
  70.7 4.4 %collective-permute-done.4.refs_2_ = s32[264,512]{1,0:T(8,128)S(1)} collective-permute-done((s32[264,512]{1,0:T(8,128)S(1)}, s32[264,512]{1,0:T(8,128)S(1)}, u32[]{:S(2)}, u32[]{:S(2)}) %collective-permute-start.4) | collective-permute-done | bytes 540704 | tf_op jit(solution)/shard_map/ppermute | solution.py:795
  75.1 3.3 %shard_map.91 = (f32[2,512,512]{2,1,0:T(8,128)}, s32[528,256]{1,0:T(8,128)S(1)}, s32[528,256]{1,0:T(8,128)S(1)}) custom-call(f32[2,512,512]{2,1,0:T(8,128)} %get-tuple-element.25.refs_0_, s32[264,512]{1,0:T(8,128)S(1)} %collective-permute-done.3.refs_1_, s32[264,512]{1,0:T(8,128)S(1)} %collective-permute-done.4.refs_2_), custom_call_target="tpu_custom_call" | custom-call | flops 67108864 | bytes 8388608 | tf_op jit(solution)/shard_map/pallas_call | solution.py:779
  81.4 1.4 collective-permute-start.8
  82.8 2.9 %collective-permute-start.7 = (s32[1,56,256]{2,1,0:T(8,128)S(1)}, s32[1,56,256]{2,1,0:T(8,128)S(1)}, u32[]{:S(2)}, u32[]{:S(2)}) collective-permute-start(s32[1,56,256]{2,1,0:T(8,128)S(1)} %shard_map.92.refs_2_), channel_id=1, source_target_pairs={{0,8},{8,0},{16,24},{24,16},{1,9},{9,1},{17,25},{25,17},{2,10},{10... | collective-permute-start | bytes 172040 | tf_op jit(solution)/shard_map/ppermute | solution.py:799
  85.7 1.6 collective-permute-done.9.refs_5_
  88.0 1.7 %shard_map.93 = s32[8,40,256]{2,1,0:T(8,128)S(1)} custom-call(s32[2]{0:T(128)S(1)} %pad_add_fusion.refs_1_.refs_0_, f32[2,256,256]{2,1,0:T(8,128)} %refs_1_.1, s32[1,56,256]{2,1,0:T(8,128)S(1)} %shard_map.92.refs_2_, s32[1,56,256]{2,1,0:T(8,128)S(1)} %collective-permute-done.7.refs_3_, s32[1,56,256]{2,1,0:T(8,128)S(1)} %collective-permute-done.8.refs_4_, ...), custom_call_target="tpu_custom_call" | custom-call | flops 67108864 | bytes 8388608 | tf_op jit(solution)/shard_map/pallas_call | solution.py:779
  89.7 15.2 %all_to_all.25.refs_7_ = s32[8,40,256]{2,1,0:T(8,128)S(1)} all-to-all(s32[8,40,256]{2,1,0:T(8,128)S(1)} %shard_map.93), channel_id=1, replica_groups=mesh['row'=4,'col'=8] {'col'}, dimensions={0} | all-to-all | bytes 655360 | tf_op jit(solution)/shard_map/all_to_all | solution.py:815
  104.9 18.2 %shard_map.94 = (f32[2,256,256]{2,1,0:T(8,128)}, f32[2,256,512]{2,1,0:T(8,128)}, s32[264,512]{1,0:T(8,128)S(1)}, s32[8,56,256]{2,1,0:T(8,128)}, f32[2,256,256]{2,1,0:T(8,128)S(1)}) custom-call(s32[256]{0:T(256)S(1)} %bitcast.9, s32[2]{0:T(128)S(1)} %pad_add_fusion.refs_1_.refs_0_, f32[2,512,512]{2,1,0:T(8,128)} %get-tuple-element.21.refs_2_, ...), custom_call_target="tpu_custom_call" | custom-call | flops 6442450944 | bytes 8388608 | tf_op jit(solution)/shard_map/pallas_call | solution.py:779
  123.1 3.5 %all-to-all-start.3 = ((s32[8,56,256]{2,1,0:T(8,128)}), s32[8,56,256]{2,1,0:T(8,128)S(1)}, u32[]{:S(2)}, u32[]{:S(2)}) async-start(s32[8,56,256]{2,1,0:T(8,128)} %get-tuple-element.39), calls=%async_computation.3 | async-start | bytes 917504 | tf_op jit(solution)/shard_map/all_to_all | solution.py:805
  126.6 3.0 %collective-permute-start.10 = (s32[264,512]{1,0:T(8,128)S(1)}, s32[264,512]{1,0:T(8,128)S(1)}, u32[]{:S(2)}, u32[]{:S(2)}) collective-permute-start(s32[264,512]{1,0:T(8,128)S(1)} %get-tuple-element.35), channel_id=1, source_target_pairs={{0,8},{8,16},{16,24},{1,9},{9,17},{17,25},{2,10},{10,18},{18,26},{... | collective-permute-start | bytes 1622024 | tf_op jit(solution)/shard_map/ppermute | solution.py:795
  129.6 4.8 %shard_map.95.refs_2_.refs_4_ = f32[256,256]{1,0:T(8,128)} custom-call(s32[256]{0:T(256)S(1)} %bitcast.10, s32[2]{0:T(128)S(1)} %pad_add_fusion.refs_1_.refs_0_, f32[2,256,256]{2,1,0:T(8,128)S(1)} %get-tuple-element.36.refs_2_.refs_1_), custom_call_target="tpu_custom_call" | custom-call | flops 8589934592 | bytes 8388608 | tf_op jit(solution)/shard_map/pallas_call | solution.py:779
  134.4 7.2 %collective-permute-done.10.refs_1_ = s32[264,512]{1,0:T(8,128)S(1)} collective-permute-done((s32[264,512]{1,0:T(8,128)S(1)}, s32[264,512]{1,0:T(8,128)S(1)}, u32[]{:S(2)}, u32[]{:S(2)}) %collective-permute-start.10) | collective-permute-done | bytes 540704 | tf_op jit(solution)/shard_map/ppermute | solution.py:795
  141.6 2.1 %shard_map.96 = (f32[2,256,256]{2,1,0:T(8,128)}, s32[264,256]{1,0:T(8,128)S(1)}) custom-call(f32[2,256,512]{2,1,0:T(8,128)} %get-tuple-element.34.refs_0_, s32[264,512]{1,0:T(8,128)S(1)} %collective-permute-done.10.refs_1_, f32[256,256]{1,0:T(8,128)} %shard_map.95.refs_2_.refs_4_), custom_call_target="tpu_custom_call" | custom-call | flops 67108864 | bytes 8388608 | tf_op jit(solution)/shard_map/pallas_call | solution.py:779
  143.8 1.5 collective-permute-start.11
  145.5 2.4 %collective-permute-start.14 = (s32[1,56,256]{2,1,0:T(8,128)S(1)}, s32[1,56,256]{2,1,0:T(8,128)S(1)}, u32[]{:S(2)}, u32[]{:S(2)}) collective-permute-start(s32[1,56,256]{2,1,0:T(8,128)S(1)} %shard_map.98.refs_2_), channel_id=1, source_target_pairs={{0,24},{8,16},{16,8},{24,0},{1,25},{9,17},{17,9},{25,1},{2,26},{10... | collective-permute-start | bytes 172040 | tf_op jit(solution)/shard_map/ppermute | solution.py:799
  147.8 1.6 collective-permute-start.13
  149.9 1.6 collective-permute-done.14.refs_5_
  151.6 3.6 %collective-permute-done.13.refs_4_ = s32[1,56,256]{2,1,0:T(8,128)S(1)} collective-permute-done((s32[1,56,256]{2,1,0:T(8,128)S(1)}, s32[1,56,256]{2,1,0:T(8,128)S(1)}, u32[]{:S(2)}, u32[]{:S(2)}) %collective-permute-start.13) | collective-permute-done | bytes 57376 | tf_op jit(solution)/shard_map/ppermute | solution.py:799
  156.6 3.9 %all-to-all-start.4 = ((s32[8,40,256]{2,1,0:T(8,128)}), s32[8,40,256]{2,1,0:T(8,128)S(1)}, u32[]{:S(2)}, u32[]{:S(2)}) async-start(s32[8,40,256]{2,1,0:T(8,128)} %shard_map.99), calls=%async_computation.4 | async-start | bytes 655360 | tf_op jit(solution)/shard_map/all_to_all | solution.py:815
  160.6 2.6 %shard_map.97 = f32[2,256,256]{2,1,0:T(8,128)} custom-call(f32[2,256,256]{2,1,0:T(8,128)} %get-tuple-element.33.refs_0_, f32[2,256,256]{2,1,0:T(8,128)} %get-tuple-element.37.refs_1_, s32[264,256]{1,0:T(8,128)S(1)} %collective-permute-done.11.refs_2_.refs_6_, f32[512,512]{1,0:T(8,128)} %shard_map.88.refs_4_.refs_6_.refs_3_, f32[256,256]{1,0:T(8,128)} %shard_map.95.refs_2_.refs_4_), custom_call_target="tpu_custom_call" | custom-call | flops 67108864 | bytes 8388608 | tf_op jit(solution)/shard_map/pallas_call | solution.py:779
  163.1 5.0 %all-to-all-done.4.refs_0_ = s32[8,40,256]{2,1,0:T(8,128)S(1)} async-done(((s32[8,40,256]{2,1,0:T(8,128)}), s32[8,40,256]{2,1,0:T(8,128)S(1)}, u32[]{:S(2)}, u32[]{:S(2)}) %all-to-all-start.4) | async-done | bytes 327712 | tf_op jit(solution)/shard_map/all_to_all | solution.py:815
  (27 shorter events, 13.5 us)
Async XLA Ops:
  1.9 11.4 %collective-permute-start.1 = (s32[264,256]{1,0:T(8,128)S(1)}, s32[264,256]{1,0:T(8,128)S(1)}, u32[]{:S(2)}, u32[]{:S(2)}) collective-permute-start(s32[264,256]{1,0:T(8,128)S(1)} %shard_map.86), channel_id=1, source_target_pairs={{8,0},{16,8},{24,16},{9,1},{17,9},{25,17},{10,2},{18,10},{26,18},{... | collective-permute-start | bytes 811016 | tf_op jit(solution)/shard_map/ppermute | solution.py:795
  3.2 10.1 %collective-permute-start = (s32[264,256]{1,0:T(8,128)S(1)}, s32[264,256]{1,0:T(8,128)S(1)}, u32[]{:S(2)}, u32[]{:S(2)}) collective-permute-start(s32[264,256]{1,0:T(8,128)S(1)} %shard_map.86), channel_id=1, source_target_pairs={{1,0},{2,1},{3,2},{4,3},{5,4},{6,5},{7,6},{9,8},{10,9},{11,10},{12... | collective-permute-start | bytes 811016 | tf_op jit(solution)/shard_map/ppermute | solution.py:795
  13.3 0.7 copy-start
  16.4 30.5 %all-to-all-start = ((bf16[16,256,256]{2,1,0:T(8,128)(2,1)}), bf16[16,256,256]{2,1,0:T(8,128)(2,1)S(1)}, u32[]{:S(2)}, u32[]{:S(2)}) async-start(bf16[16,256,256]{2,1,0:T(8,128)(2,1)} %shard_map.89), calls=%async_computation | async-start | bytes 4194304 | tf_op jit(solution)/shard_map/all_to_all | solution.py:846
  20.3 10.9 %copy-start.1 = (s32[128,2]{0,1:T(2,128)S(1)}, s32[128,2]{0,1:T(2,128)}, u32[]{:S(2)}) copy-start(s32[128,2]{0,1:T(2,128)} %param.10) | copy-start | bytes 3076
  20.3 10.9 %collective-permute-start.2 = (s32[264,256]{1,0:T(8,128)S(1)}, s32[264,256]{1,0:T(8,128)S(1)}, u32[]{:S(2)}, u32[]{:S(2)}) collective-permute-start(s32[264,256]{1,0:T(8,128)S(1)} %collective-permute-done.refs_3_), channel_id=1, source_target_pairs={{8,0},{16,8},{24,16},{9,1},{17,9},{25,17},{10,2},{18,10},{26,18},{... | collective-permute-start | bytes 811016 | tf_op jit(solution)/shard_map/ppermute | solution.py:795
  60.3 10.4 %collective-permute-start.3 = (s32[264,512]{1,0:T(8,128)S(1)}, s32[264,512]{1,0:T(8,128)S(1)}, u32[]{:S(2)}, u32[]{:S(2)}) collective-permute-start(s32[264,512]{1,0:T(8,128)S(1)} %get-tuple-element.26), channel_id=1, source_target_pairs={{0,8},{8,16},{16,24},{1,9},{9,17},{17,25},{2,10},{10,18},{18,26},{... | collective-permute-start | bytes 1622024 | tf_op jit(solution)/shard_map/ppermute | solution.py:795
  63.9 11.3 %collective-permute-start.4 = (s32[264,512]{1,0:T(8,128)S(1)}, s32[264,512]{1,0:T(8,128)S(1)}, u32[]{:S(2)}, u32[]{:S(2)}) collective-permute-start(s32[264,512]{1,0:T(8,128)S(1)} %get-tuple-element.27), channel_id=1, source_target_pairs={{8,0},{16,8},{24,16},{9,1},{17,9},{25,17},{10,2},{18,10},{26,18},{... | collective-permute-start | bytes 1622024 | tf_op jit(solution)/shard_map/ppermute | solution.py:795
  65.2 15.9 %all-to-all-start.1 = ((s32[8,56,256]{2,1,0:T(8,128)}), s32[8,56,256]{2,1,0:T(8,128)S(1)}, u32[]{:S(2)}, u32[]{:S(2)}) async-start(s32[8,56,256]{2,1,0:T(8,128)} %get-tuple-element.31), calls=%async_computation.1 | async-start | bytes 917504 | tf_op jit(solution)/shard_map/all_to_all | solution.py:805
  78.5 26.4 %collective-permute-start.5 = (s32[528,256]{1,0:T(8,128)S(1)}, s32[528,256]{1,0:T(8,128)S(1)}, u32[]{:S(2)}, u32[]{:S(2)}) collective-permute-start(s32[528,256]{1,0:T(8,128)S(1)} %get-tuple-element.29), channel_id=1, source_target_pairs={{0,1},{1,2},{2,3},{3,4},{4,5},{5,6},{6,7},{8,9},{9,10},{10,11},{11... | collective-permute-start | bytes 1622024 | tf_op jit(solution)/shard_map/ppermute | solution.py:795
  79.8 25.1 %collective-permute-start.6 = (s32[528,256]{1,0:T(8,128)S(1)}, s32[528,256]{1,0:T(8,128)S(1)}, u32[]{:S(2)}, u32[]{:S(2)}) collective-permute-start(s32[528,256]{1,0:T(8,128)S(1)} %get-tuple-element.30.refs_1_), channel_id=1, source_target_pairs={{1,0},{2,1},{3,2},{4,3},{5,4},{6,5},{7,6},{9,8},{10,9},{11,10},{12... | collective-permute-start | bytes 1622024 | tf_op jit(solution)/shard_map/ppermute | solution.py:795
  81.3 6.0 %collective-permute-start.9 = (s32[1,56,256]{2,1,0:T(8,128)S(1)}, s32[1,56,256]{2,1,0:T(8,128)S(1)}, u32[]{:S(2)}, u32[]{:S(2)}) collective-permute-start(s32[1,56,256]{2,1,0:T(8,128)S(1)} %shard_map.92.refs_2_), channel_id=1, source_target_pairs={{0,24},{8,16},{16,8},{24,0},{1,25},{9,17},{17,9},{25,1},{2,26},{10... | collective-permute-start | bytes 172040 | tf_op jit(solution)/shard_map/ppermute | solution.py:799
  81.4 6.0 %collective-permute-start.8 = (s32[1,56,256]{2,1,0:T(8,128)S(1)}, s32[1,56,256]{2,1,0:T(8,128)S(1)}, u32[]{:S(2)}, u32[]{:S(2)}) collective-permute-start(s32[1,56,256]{2,1,0:T(8,128)S(1)} %shard_map.92.refs_2_), channel_id=1, source_target_pairs={{0,16},{8,24},{16,0},{24,8},{1,17},{9,25},{17,1},{25,9},{2,18},{10... | collective-permute-start | bytes 172040 | tf_op jit(solution)/shard_map/ppermute | solution.py:799
  82.8 5.1 %collective-permute-start.7 = (s32[1,56,256]{2,1,0:T(8,128)S(1)}, s32[1,56,256]{2,1,0:T(8,128)S(1)}, u32[]{:S(2)}, u32[]{:S(2)}) collective-permute-start(s32[1,56,256]{2,1,0:T(8,128)S(1)} %shard_map.92.refs_2_), channel_id=1, source_target_pairs={{0,8},{8,0},{16,24},{24,16},{1,9},{9,1},{17,25},{25,17},{2,10},{10... | collective-permute-start | bytes 172040 | tf_op jit(solution)/shard_map/ppermute | solution.py:799
  123.1 22.2 %all-to-all-start.3 = ((s32[8,56,256]{2,1,0:T(8,128)}), s32[8,56,256]{2,1,0:T(8,128)S(1)}, u32[]{:S(2)}, u32[]{:S(2)}) async-start(s32[8,56,256]{2,1,0:T(8,128)} %get-tuple-element.39), calls=%async_computation.3 | async-start | bytes 917504 | tf_op jit(solution)/shard_map/all_to_all | solution.py:805
  126.6 15.0 %collective-permute-start.10 = (s32[264,512]{1,0:T(8,128)S(1)}, s32[264,512]{1,0:T(8,128)S(1)}, u32[]{:S(2)}, u32[]{:S(2)}) collective-permute-start(s32[264,512]{1,0:T(8,128)S(1)} %get-tuple-element.35), channel_id=1, source_target_pairs={{0,8},{8,16},{16,24},{1,9},{9,17},{17,25},{2,10},{10,18},{18,26},{... | collective-permute-start | bytes 1622024 | tf_op jit(solution)/shard_map/ppermute | solution.py:795
  143.8 11.4 %collective-permute-start.11 = (s32[264,256]{1,0:T(8,128)S(1)}, s32[264,256]{1,0:T(8,128)S(1)}, u32[]{:S(2)}, u32[]{:S(2)}) collective-permute-start(s32[264,256]{1,0:T(8,128)S(1)} %get-tuple-element.38.refs_1_), channel_id=1, source_target_pairs={{0,1},{1,2},{2,3},{3,4},{4,5},{5,6},{6,7},{8,9},{9,10},{10,11},{11... | collective-permute-start | bytes 811016 | tf_op jit(solution)/shard_map/ppermute | solution.py:795
  145.5 6.1 %collective-permute-start.14 = (s32[1,56,256]{2,1,0:T(8,128)S(1)}, s32[1,56,256]{2,1,0:T(8,128)S(1)}, u32[]{:S(2)}, u32[]{:S(2)}) collective-permute-start(s32[1,56,256]{2,1,0:T(8,128)S(1)} %shard_map.98.refs_2_), channel_id=1, source_target_pairs={{0,24},{8,16},{16,8},{24,0},{1,25},{9,17},{17,9},{25,1},{2,26},{10... | collective-permute-start | bytes 172040 | tf_op jit(solution)/shard_map/ppermute | solution.py:799
  147.8 7.4 %collective-permute-start.13 = (s32[1,56,256]{2,1,0:T(8,128)S(1)}, s32[1,56,256]{2,1,0:T(8,128)S(1)}, u32[]{:S(2)}, u32[]{:S(2)}) collective-permute-start(s32[1,56,256]{2,1,0:T(8,128)S(1)} %shard_map.98.refs_2_), channel_id=1, source_target_pairs={{0,16},{8,24},{16,0},{24,8},{1,17},{9,25},{17,1},{25,9},{2,18},{10... | collective-permute-start | bytes 172040 | tf_op jit(solution)/shard_map/ppermute | solution.py:799
  149.5 5.7 %collective-permute-start.12 = (s32[1,56,256]{2,1,0:T(8,128)S(1)}, s32[1,56,256]{2,1,0:T(8,128)S(1)}, u32[]{:S(2)}, u32[]{:S(2)}) collective-permute-start(s32[1,56,256]{2,1,0:T(8,128)S(1)} %shard_map.98.refs_2_), channel_id=1, source_target_pairs={{0,8},{8,0},{16,24},{24,16},{1,9},{9,1},{17,25},{25,17},{2,10},{10... | collective-permute-start | bytes 172040 | tf_op jit(solution)/shard_map/ppermute | solution.py:799
  156.6 11.6 %all-to-all-start.4 = ((s32[8,40,256]{2,1,0:T(8,128)}), s32[8,40,256]{2,1,0:T(8,128)S(1)}, u32[]{:S(2)}, u32[]{:S(2)}) async-start(s32[8,40,256]{2,1,0:T(8,128)} %shard_map.99), calls=%async_computation.4 | async-start | bytes 655360 | tf_op jit(solution)/shard_map/all_to_all | solution.py:815

commit v12 on v10

--- a/solution.py
+++ b/solution.py
@@ -903,7 +903,7 @@
     new_object = call(functools.partial(object_kernel, dims), shape(tile), VMEM, [LOAD, LOAD, VMEM, LOAD, LOAD], [], 1 << 26)(
         current, own, from_left, weights_old, weights_new
     )
-    _, chunks = probe_update(me, probe_now, numer, VMEM, False, [(FREE, to_right)], [(FREE, from_left), (HBM, weights_new)])
+    _, chunks = probe_update(me, probe_now, numer, VMEM, False, [(FREE, to_right)], [(FREE, from_left)])
     new_probe = call(probe_kernel, shape(window), VMEM, [VMEM], [], 1 << 26)(chunks)
     return new_object, new_probe
 

time: 165 us -> 162 us (0.982)
  Pallas kernels: 70.4 us -> 56.2 us
  starting transfers between devices: 35.3 us -> 45.3 us
    pallas_call x15, Pallas kernels: 70.4 us -> 56.2 us  [called(): pl.pallas_call(body, out_shape=tuple(fixed_outs) if several else fixed_ou...]
    ppermute x9, starting transfers between devices: 12.7 us -> 26.1 us  [passed_along(): lax.ppermute(value, axis, [(source, source + steps) for source in range(l...]
    all_to_all x1, waiting for transfers between devices: 4.97 us -> 0.86 us  [probe_update(): lax.all_to_all(fresh, 'col', split_axis=0, concat_axis=0, tiled=True)]
    ppermute x9, waiting for transfers between devices: 17.7 us -> 14 us  [passed_along(): lax.ppermute(value, axis, [(source, source + steps) for source in range(l...]
    all_to_all x1, starting transfers between devices: 7.23 us -> 3.91 us  [probe_update(): lax.all_to_all(total, 'row', split_axis=0, concat_axis=0, tiled=True)]
    all_to_all x1, waiting for transfers between devices: 5.91 us -> 9.13 us  [local(): lax.all_to_all(outgoing, 'col', split_axis=0, concat_axis=0, tiled=True)]
    ppermute x3, waiting for transfers between devices: 0.01 us -> 3.17 us  [swapped(): lax.ppermute(value, axis, [(k, k ^ mask) for k in range(lax.axis_size(axi...]
    all_to_all x1, waiting for transfers between devices: 0.01 us -> 2.2 us  [probe_update(): lax.all_to_all(numer, 'col', split_axis=0, concat_axis=0, tiled=True)]
  transfers between devices with their start and end apart: 16 -> 16, of which waited for: 6 -> 9; matrix products, arithmetic and copies ran while one was open for 0% -> 0% of each run, Pallas kernels for 21% -> 18%
where the time goes in v12:
time: 162 us; the launch traced here: 159 us
  Pallas kernels  56.2 us (35%)
  starting transfers between devices  45.3 us (28%)
  waiting for transfers between devices  31.3 us (19%)
  blocking collectives  25.1 us (15%)
    pallas_call x15, Pallas kernels, called(): pl.pallas_call(body, out_shape=tuple(fixed_outs) if several else fixed_ou...  56.2 us
    ppermute x9, starting transfers between devices, passed_along(): lax.ppermute(value, axis, [(source, source + steps) for source in range(l...  26.1 us
    ppermute x9, waiting for transfers between devices, passed_along(): lax.ppermute(value, axis, [(source, source + steps) for source in range(l...  14 us
    all_to_all x1, blocking collectives, probe_update(): lax.all_to_all(fresh, 'col', split_axis=0, concat_axis=0, tiled=True)  13.6 us
    all_to_all x1, blocking collectives, probe_update(): lax.all_to_all(numer, 'col', split_axis=0, concat_axis=0, tiled=True)  11.4 us
    all_to_all x1, waiting for transfers between devices, local(): lax.all_to_all(outgoing, 'col', split_axis=0, concat_axis=0, tiled=True)  9.13 us
    ppermute x3, starting transfers between devices, swapped(): lax.ppermute(value, axis, [(k, k ^ mask) for k in range(lax.axis_size(axi...  4.45 us
    all_to_all x1, starting transfers between devices, local(): lax.all_to_all(outgoing, 'col', split_axis=0, concat_axis=0, tiled=True)  3.93 us
  transfers between devices with their start and end apart: 16, of which 9 were waited for; matrix products, arithmetic and copies ran while one was open for 0% of the time, Pallas kernels for 18%

profile of v12, /device:TPU:0, one launch (start us, length us, event | category | flops | bytes accessed | tf_op | source)
XLA Modules:
  0.0 159.5 jit_solution(17631580816566605681)
XLA Ops:
  1.9 1.3 collective-permute-start.1
  3.2 1.3 collective-permute-start
  4.5 8.7 %collective-permute-done.1.refs_4_ = s32[264,256]{1,0:T(8,128)S(1)} collective-permute-done((s32[264,256]{1,0:T(8,128)S(1)}, s32[264,256]{1,0:T(8,128)S(1)}, u32[]{:S(2)}, u32[]{:S(2)}) %collective-permute-start.1) | collective-permute-done | bytes 270368 | tf_op jit(solution)/shard_map/ppermute | solution.py:795
  13.9 2.4 %shard_map.89 = bf16[16,256,256]{2,1,0:T(8,128)(2,1)} custom-call(s32[256]{0:T(256)S(1)} %bitcast.5, s32[2]{0:T(128)S(1)} %pad_add_fusion.refs_1_.refs_0_, bf16[4,256,256]{2,1,0:T(8,128)(2,1)} %refs_2_.6, s32[264,256]{1,0:T(8,128)S(1)} %collective-permute-done.refs_3_, s32[264,256]{1,0:T(8,128)S(1)} %collective-permute-done.1.refs_4_), custom_call_target="tpu_custom_call" | custom-call | flops 1048576 | bytes 8388608 | tf_op jit(solution)/shard_map/pallas_call | solution.py:779
  16.4 3.9 %all-to-all-start = ((bf16[16,256,256]{2,1,0:T(8,128)(2,1)}), bf16[16,256,256]{2,1,0:T(8,128)(2,1)S(1)}, u32[]{:S(2)}, u32[]{:S(2)}) async-start(bf16[16,256,256]{2,1,0:T(8,128)(2,1)} %shard_map.89), calls=%async_computation | async-start | bytes 4194304 | tf_op jit(solution)/shard_map/all_to_all | solution.py:850
  20.3 1.3 collective-permute-start.2
  21.6 7.6 %shard_map.88.refs_4_.refs_6_.refs_3_ = f32[512,512]{1,0:T(8,128)} custom-call(s32[256]{0:T(256)S(1)} %bitcast.6, s32[2]{0:T(128)S(1)} %pad_add_fusion.refs_1_.refs_0_, f32[2,256,256]{2,1,0:T(8,128)} %refs_1_.1), custom_call_target="tpu_custom_call" | custom-call | flops 8589934592 | bytes 8388608 | tf_op jit(solution)/shard_map/pallas_call | solution.py:779
  29.3 2.0 %collective-permute-done.2.refs_5_ = s32[264,256]{1,0:T(8,128)S(1)} collective-permute-done((s32[264,256]{1,0:T(8,128)S(1)}, s32[264,256]{1,0:T(8,128)S(1)}, u32[]{:S(2)}, u32[]{:S(2)}) %collective-permute-start.2) | collective-permute-done | bytes 270368 | tf_op jit(solution)/shard_map/ppermute | solution.py:795
  31.2 6.6 %shard_map.87 = (f32[8,2,256,256]{3,2,1,0:T(8,128)}, f32[8,2,256,256]{3,2,1,0:T(8,128)}, f32[256,256]{1,0:T(8,128)S(1)}, f32[2,512,512]{2,1,0:T(8,128)}) custom-call(s32[256]{0:T(256)S(1)} %bitcast.7, s32[2]{0:T(128)S(1)} %pad_add_fusion.refs_1_.refs_0_, f32[2,256,256]{2,1,0:T(8,128)} %refs_2_.4, s32[264,256]{1,0:T(8,128)S(1)} %collective-permute-done.refs_3_, ...), custom_call_target="tpu_custom_call" | custom-call | flops 3221225472 | bytes 8388608 | tf_op jit(solution)/shard_map/pallas_call | solution.py:779
  37.8 9.1 %all-to-all-done.refs_7_ = bf16[16,256,256]{2,1,0:T(8,128)(2,1)S(1)} async-done(((bf16[16,256,256]{2,1,0:T(8,128)(2,1)}), bf16[16,256,256]{2,1,0:T(8,128)(2,1)S(1)}, u32[]{:S(2)}, u32[]{:S(2)}) %all-to-all-start) | async-done | bytes 2097184 | tf_op jit(solution)/shard_map/all_to_all | solution.py:850
  47.0 9.1 %shard_map.90 = (f32[2,512,512]{2,1,0:T(8,128)}, s32[264,512]{1,0:T(8,128)S(1)}, s32[264,512]{1,0:T(8,128)S(1)}, s32[8,56,256]{2,1,0:T(8,128)S(1)}, bf16[8,256,256]{2,1,0:T(8,128)(2,1)}) custom-call(s32[256]{0:T(256)S(1)} %bitcast.8, s32[2]{0:T(128)S(1)} %pad_add_fusion.refs_1_.refs_0_, f32[2,256,256]{2,1,0:T(8,128)} %refs_1_.1, ...), custom_call_target="tpu_custom_call" | custom-call | flops 3221225472 | bytes 8388608 | tf_op jit(solution)/shard_map/pallas_call | solution.py:779
  56.0 7.1 %collective-permute-start.3 = (s32[264,512]{1,0:T(8,128)S(1)}, s32[264,512]{1,0:T(8,128)S(1)}, u32[]{:S(2)}, u32[]{:S(2)}) collective-permute-start(s32[264,512]{1,0:T(8,128)S(1)} %get-tuple-element.26), channel_id=1, source_target_pairs={{0,8},{8,16},{16,24},{1,9},{9,17},{17,25},{2,10},{10,18},{18,26},{... | collective-permute-start | bytes 1622024 | tf_op jit(solution)/shard_map/ppermute | solution.py:795
  64.4 11.4 %all_to_all.30.refs_0_ = s32[8,56,256]{2,1,0:T(8,128)S(1)} all-to-all(s32[8,56,256]{2,1,0:T(8,128)S(1)} %get-tuple-element.28), channel_id=1, replica_groups=mesh['row'=4,'col'=8] {'col'}, dimensions={0} | all-to-all | bytes 917504 | tf_op jit(solution)/shard_map/all_to_all | solution.py:805
  76.7 3.9 %all-to-all-start.2 = ((s32[4,56,256]{2,1,0:T(8,128)}), s32[4,56,256]{2,1,0:T(8,128)S(1)}, u32[]{:S(2)}, u32[]{:S(2)}) async-start(s32[4,56,256]{2,1,0:T(8,128)} %shard_map.91.refs_3_), calls=%async_computation.2 | async-start | bytes 458752 | tf_op jit(solution)/shard_map/all_to_all | solution.py:812
  80.7 3.3 %shard_map.92 = (f32[2,512,512]{2,1,0:T(8,128)}, s32[528,256]{1,0:T(8,128)S(1)}, s32[528,256]{1,0:T(8,128)S(1)}) custom-call(f32[2,512,512]{2,1,0:T(8,128)} %get-tuple-element.25.refs_0_, s32[264,512]{1,0:T(8,128)S(1)} %collective-permute-done.3.refs_1_, s32[264,512]{1,0:T(8,128)S(1)} %collective-permute-done.4.refs_2_, s32[4,56,256]{2,1,0:T(8,128)} %shard_map.91.refs_3_), custom_call_target="tpu_custom_call" | custom-call | flops 67108864 | bytes 8388608 | tf_op jit(solution)/shard_map/pallas_call | solution.py:779
  84.0 1.3 collective-permute-start.5
  86.6 1.9 %all-to-all-done.2.refs_2_ = s32[4,56,256]{2,1,0:T(8,128)S(1)} async-done(((s32[4,56,256]{2,1,0:T(8,128)}), s32[4,56,256]{2,1,0:T(8,128)S(1)}, u32[]{:S(2)}, u32[]{:S(2)}) %all-to-all-start.2) | async-done | bytes 229408 | tf_op jit(solution)/shard_map/all_to_all | solution.py:812
  88.5 1.7 %shard_map.93 = s32[8,40,256]{2,1,0:T(8,128)S(1)} custom-call(s32[2]{0:T(128)S(1)} %pad_add_fusion.refs_1_.refs_0_, f32[2,256,256]{2,1,0:T(8,128)} %refs_1_.1, s32[4,56,256]{2,1,0:T(8,128)S(1)} %all-to-all-done.2.refs_2_), custom_call_target="tpu_custom_call" | custom-call | flops 67108864 | bytes 8388608 | tf_op jit(solution)/shard_map/pallas_call | solution.py:779
  90.2 13.6 %all_to_all.31.refs_7_ = s32[8,40,256]{2,1,0:T(8,128)S(1)} all-to-all(s32[8,40,256]{2,1,0:T(8,128)S(1)} %shard_map.93), channel_id=1, replica_groups=mesh['row'=4,'col'=8] {'col'}, dimensions={0} | all-to-all | bytes 655360 | tf_op jit(solution)/shard_map/all_to_all | solution.py:819
  103.9 12.1 %shard_map.94 = (f32[2,256,256]{2,1,0:T(8,128)}, f32[2,256,512]{2,1,0:T(8,128)}, s32[264,512]{1,0:T(8,128)S(1)}, s32[8,56,256]{2,1,0:T(8,128)}, f32[2,256,256]{2,1,0:T(8,128)S(1)}) custom-call(s32[256]{0:T(256)S(1)} %bitcast.9, s32[2]{0:T(128)S(1)} %pad_add_fusion.refs_1_.refs_0_, f32[2,512,512]{2,1,0:T(8,128)} %get-tuple-element.21.refs_2_, ...), custom_call_target="tpu_custom_call" | custom-call | flops 6442450944 | bytes 8388608 | tf_op jit(solution)/shard_map/pallas_call | solution.py:779
  116.0 9.9 %collective-permute-start.7 = (s32[264,512]{1,0:T(8,128)S(1)}, s32[264,512]{1,0:T(8,128)S(1)}, u32[]{:S(2)}, u32[]{:S(2)}) collective-permute-start(s32[264,512]{1,0:T(8,128)S(1)} %get-tuple-element.35), channel_id=1, source_target_pairs={{0,8},{8,16},{16,24},{1,9},{9,17},{17,25},{2,10},{10,18},{18,26},{... | collective-permute-start | bytes 1622024 | tf_op jit(solution)/shard_map/ppermute | solution.py:795
  126.0 3.5 %all-to-all-start.4 = ((s32[8,56,256]{2,1,0:T(8,128)}), s32[8,56,256]{2,1,0:T(8,128)S(1)}, u32[]{:S(2)}, u32[]{:S(2)}) async-start(s32[8,56,256]{2,1,0:T(8,128)} %get-tuple-element.39), calls=%async_computation.4 | async-start | bytes 917504 | tf_op jit(solution)/shard_map/all_to_all | solution.py:805
  129.5 3.3 %collective-permute-done.7.refs_1_ = s32[264,512]{1,0:T(8,128)S(1)} collective-permute-done((s32[264,512]{1,0:T(8,128)S(1)}, s32[264,512]{1,0:T(8,128)S(1)}, u32[]{:S(2)}, u32[]{:S(2)}) %collective-permute-start.7) | collective-permute-done | bytes 540704 | tf_op jit(solution)/shard_map/ppermute | solution.py:795
  132.8 2.1 %shard_map.95 = (f32[2,256,256]{2,1,0:T(8,128)}, s32[264,256]{1,0:T(8,128)S(1)}) custom-call(f32[2,256,512]{2,1,0:T(8,128)} %get-tuple-element.34.refs_0_, s32[264,512]{1,0:T(8,128)S(1)} %collective-permute-done.7.refs_1_), custom_call_target="tpu_custom_call" | custom-call | flops 67108864 | bytes 8388608 | tf_op jit(solution)/shard_map/pallas_call | solution.py:779
  134.9 1.3 collective-permute-start.8
  136.2 2.2 %all-to-all-done.4.refs_0_ = s32[8,56,256]{2,1,0:T(8,128)S(1)} async-done(((s32[8,56,256]{2,1,0:T(8,128)}), s32[8,56,256]{2,1,0:T(8,128)S(1)}, u32[]{:S(2)}, u32[]{:S(2)}) %all-to-all-start.4) | async-done | bytes 458784 | tf_op jit(solution)/shard_map/all_to_all | solution.py:805
  140.4 2.6 %collective-permute-start.9 = (s32[1,56,256]{2,1,0:T(8,128)S(1)}, s32[1,56,256]{2,1,0:T(8,128)S(1)}, u32[]{:S(2)}, u32[]{:S(2)}) collective-permute-start(s32[1,56,256]{2,1,0:T(8,128)S(1)} %shard_map.98.refs_2_), channel_id=1, source_target_pairs={{0,8},{8,0},{16,24},{24,16},{1,9},{9,1},{17,25},{25,17},{2,10},{10... | collective-permute-start | bytes 172040 | tf_op jit(solution)/shard_map/ppermute | solution.py:799
  143.1 2.2 %collective-permute-done.11.refs_5_ = s32[1,56,256]{2,1,0:T(8,128)S(1)} collective-permute-done((s32[1,56,256]{2,1,0:T(8,128)S(1)}, s32[1,56,256]{2,1,0:T(8,128)S(1)}, u32[]{:S(2)}, u32[]{:S(2)}) %collective-permute-start.11) | collective-permute-done | bytes 57376 | tf_op jit(solution)/shard_map/ppermute | solution.py:799
  146.2 1.4 shard_map.99
  147.6 3.4 %all-to-all-start.5 = ((s32[8,40,256]{2,1,0:T(8,128)}), s32[8,40,256]{2,1,0:T(8,128)S(1)}, u32[]{:S(2)}, u32[]{:S(2)}) async-start(s32[8,40,256]{2,1,0:T(8,128)} %shard_map.99), calls=%async_computation.5 | async-start | bytes 655360 | tf_op jit(solution)/shard_map/all_to_all | solution.py:819
  151.1 4.1 %shard_map.96.refs_4_ = f32[256,256]{1,0:T(8,128)} custom-call(s32[256]{0:T(256)S(1)} %bitcast.10, s32[2]{0:T(128)S(1)} %pad_add_fusion.refs_1_.refs_0_, f32[2,256,256]{2,1,0:T(8,128)S(1)} %get-tuple-element.38.refs_2_.refs_1_), custom_call_target="tpu_custom_call" | custom-call | flops 8589934592 | bytes 8388608 | tf_op jit(solution)/shard_map/pallas_call | solution.py:779
  155.2 2.6 %shard_map.97 = f32[2,256,256]{2,1,0:T(8,128)} custom-call(f32[2,256,256]{2,1,0:T(8,128)} %get-tuple-element.33.refs_0_, f32[2,256,256]{2,1,0:T(8,128)} %get-tuple-element.36.refs_1_, s32[264,256]{1,0:T(8,128)S(1)} %collective-permute-done.8.refs_2_.refs_6_, f32[512,512]{1,0:T(8,128)} %shard_map.88.refs_4_.refs_6_.refs_3_, f32[256,256]{1,0:T(8,128)} %shard_map.96.refs_4_), custom_call_target="tpu_custom_call" | custom-call | flops 67108864 | bytes 8388608 | tf_op jit(solution)/shard_map/pallas_call | solution.py:779
  (22 shorter events, 10.1 us)
Async XLA Ops:
  1.9 11.4 %collective-permute-start.1 = (s32[264,256]{1,0:T(8,128)S(1)}, s32[264,256]{1,0:T(8,128)S(1)}, u32[]{:S(2)}, u32[]{:S(2)}) collective-permute-start(s32[264,256]{1,0:T(8,128)S(1)} %shard_map.86), channel_id=1, source_target_pairs={{8,0},{16,8},{24,16},{9,1},{17,9},{25,17},{10,2},{18,10},{26,18},{... | collective-permute-start | bytes 811016 | tf_op jit(solution)/shard_map/ppermute | solution.py:795
  3.2 10.1 %collective-permute-start = (s32[264,256]{1,0:T(8,128)S(1)}, s32[264,256]{1,0:T(8,128)S(1)}, u32[]{:S(2)}, u32[]{:S(2)}) collective-permute-start(s32[264,256]{1,0:T(8,128)S(1)} %shard_map.86), channel_id=1, source_target_pairs={{1,0},{2,1},{3,2},{4,3},{5,4},{6,5},{7,6},{9,8},{10,9},{11,10},{12... | collective-permute-start | bytes 811016 | tf_op jit(solution)/shard_map/ppermute | solution.py:795
  13.3 0.7 copy-start
  16.4 30.6 %all-to-all-start = ((bf16[16,256,256]{2,1,0:T(8,128)(2,1)}), bf16[16,256,256]{2,1,0:T(8,128)(2,1)S(1)}, u32[]{:S(2)}, u32[]{:S(2)}) async-start(bf16[16,256,256]{2,1,0:T(8,128)(2,1)} %shard_map.89), calls=%async_computation | async-start | bytes 4194304 | tf_op jit(solution)/shard_map/all_to_all | solution.py:850
  20.3 10.9 %copy-start.1 = (s32[128,2]{0,1:T(2,128)S(1)}, s32[128,2]{0,1:T(2,128)}, u32[]{:S(2)}) copy-start(s32[128,2]{0,1:T(2,128)} %param.10) | copy-start | bytes 3076
  20.3 10.9 %collective-permute-start.2 = (s32[264,256]{1,0:T(8,128)S(1)}, s32[264,256]{1,0:T(8,128)S(1)}, u32[]{:S(2)}, u32[]{:S(2)}) collective-permute-start(s32[264,256]{1,0:T(8,128)S(1)} %collective-permute-done.refs_3_), channel_id=1, source_target_pairs={{8,0},{16,8},{24,16},{9,1},{17,9},{25,17},{10,2},{18,10},{26,18},{... | collective-permute-start | bytes 811016 | tf_op jit(solution)/shard_map/ppermute | solution.py:795
  56.0 24.6 %collective-permute-start.3 = (s32[264,512]{1,0:T(8,128)S(1)}, s32[264,512]{1,0:T(8,128)S(1)}, u32[]{:S(2)}, u32[]{:S(2)}) collective-permute-start(s32[264,512]{1,0:T(8,128)S(1)} %get-tuple-element.26), channel_id=1, source_target_pairs={{0,8},{8,16},{16,24},{1,9},{9,17},{17,25},{2,10},{10,18},{18,26},{... | collective-permute-start | bytes 1622024 | tf_op jit(solution)/shard_map/ppermute | solution.py:795
  63.1 17.5 %collective-permute-start.4 = (s32[264,512]{1,0:T(8,128)S(1)}, s32[264,512]{1,0:T(8,128)S(1)}, u32[]{:S(2)}, u32[]{:S(2)}) collective-permute-start(s32[264,512]{1,0:T(8,128)S(1)} %get-tuple-element.27), channel_id=1, source_target_pairs={{8,0},{16,8},{24,16},{9,1},{17,9},{25,17},{10,2},{18,10},{26,18},{... | collective-permute-start | bytes 1622024 | tf_op jit(solution)/shard_map/ppermute | solution.py:795
  76.7 11.8 %all-to-all-start.2 = ((s32[4,56,256]{2,1,0:T(8,128)}), s32[4,56,256]{2,1,0:T(8,128)S(1)}, u32[]{:S(2)}, u32[]{:S(2)}) async-start(s32[4,56,256]{2,1,0:T(8,128)} %shard_map.91.refs_3_), calls=%async_computation.2 | async-start | bytes 458752 | tf_op jit(solution)/shard_map/all_to_all | solution.py:812
  84.0 19.9 %collective-permute-start.5 = (s32[528,256]{1,0:T(8,128)S(1)}, s32[528,256]{1,0:T(8,128)S(1)}, u32[]{:S(2)}, u32[]{:S(2)}) collective-permute-start(s32[528,256]{1,0:T(8,128)S(1)} %get-tuple-element.30), channel_id=1, source_target_pairs={{0,1},{1,2},{2,3},{3,4},{4,5},{5,6},{6,7},{8,9},{9,10},{10,11},{11... | collective-permute-start | bytes 1622024 | tf_op jit(solution)/shard_map/ppermute | solution.py:795
  85.3 18.6 %collective-permute-start.6 = (s32[528,256]{1,0:T(8,128)S(1)}, s32[528,256]{1,0:T(8,128)S(1)}, u32[]{:S(2)}, u32[]{:S(2)}) collective-permute-start(s32[528,256]{1,0:T(8,128)S(1)} %get-tuple-element.31), channel_id=1, source_target_pairs={{1,0},{2,1},{3,2},{4,3},{5,4},{6,5},{7,6},{9,8},{10,9},{11,10},{12... | collective-permute-start | bytes 1622024 | tf_op jit(solution)/shard_map/ppermute | solution.py:795
  116.0 16.7 %collective-permute-start.7 = (s32[264,512]{1,0:T(8,128)S(1)}, s32[264,512]{1,0:T(8,128)S(1)}, u32[]{:S(2)}, u32[]{:S(2)}) collective-permute-start(s32[264,512]{1,0:T(8,128)S(1)} %get-tuple-element.35), channel_id=1, source_target_pairs={{0,8},{8,16},{16,24},{1,9},{9,17},{17,25},{2,10},{10,18},{18,26},{... | collective-permute-start | bytes 1622024 | tf_op jit(solution)/shard_map/ppermute | solution.py:795
  126.0 12.5 %all-to-all-start.4 = ((s32[8,56,256]{2,1,0:T(8,128)}), s32[8,56,256]{2,1,0:T(8,128)S(1)}, u32[]{:S(2)}, u32[]{:S(2)}) async-start(s32[8,56,256]{2,1,0:T(8,128)} %get-tuple-element.39), calls=%async_computation.4 | async-start | bytes 917504 | tf_op jit(solution)/shard_map/all_to_all | solution.py:805
  134.9 11.3 %collective-permute-start.8 = (s32[264,256]{1,0:T(8,128)S(1)}, s32[264,256]{1,0:T(8,128)S(1)}, u32[]{:S(2)}, u32[]{:S(2)}) collective-permute-start(s32[264,256]{1,0:T(8,128)S(1)} %get-tuple-element.37.refs_1_), channel_id=1, source_target_pairs={{0,1},{1,2},{2,3},{3,4},{4,5},{5,6},{6,7},{8,9},{9,10},{10,11},{11... | collective-permute-start | bytes 811016 | tf_op jit(solution)/shard_map/ppermute | solution.py:795
  138.6 6.6 %collective-permute-start.11 = (s32[1,56,256]{2,1,0:T(8,128)S(1)}, s32[1,56,256]{2,1,0:T(8,128)S(1)}, u32[]{:S(2)}, u32[]{:S(2)}) collective-permute-start(s32[1,56,256]{2,1,0:T(8,128)S(1)} %shard_map.98.refs_2_), channel_id=1, source_target_pairs={{0,24},{8,16},{16,8},{24,0},{1,25},{9,17},{17,9},{25,1},{2,26},{10... | collective-permute-start | bytes 172040 | tf_op jit(solution)/shard_map/ppermute | solution.py:799
  139.3 6.9 %collective-permute-start.10 = (s32[1,56,256]{2,1,0:T(8,128)S(1)}, s32[1,56,256]{2,1,0:T(8,128)S(1)}, u32[]{:S(2)}, u32[]{:S(2)}) collective-permute-start(s32[1,56,256]{2,1,0:T(8,128)S(1)} %shard_map.98.refs_2_), channel_id=1, source_target_pairs={{0,16},{8,24},{16,0},{24,8},{1,17},{9,25},{17,1},{25,9},{2,18},{10... | collective-permute-start | bytes 172040 | tf_op jit(solution)/shard_map/ppermute | solution.py:799
  140.4 5.8 %collective-permute-start.9 = (s32[1,56,256]{2,1,0:T(8,128)S(1)}, s32[1,56,256]{2,1,0:T(8,128)S(1)}, u32[]{:S(2)}, u32[]{:S(2)}) collective-permute-start(s32[1,56,256]{2,1,0:T(8,128)S(1)} %shard_map.98.refs_2_), channel_id=1, source_target_pairs={{0,8},{8,0},{16,24},{24,16},{1,9},{9,1},{17,25},{25,17},{2,10},{10... | collective-permute-start | bytes 172040 | tf_op jit(solution)/shard_map/ppermute | solution.py:799
  147.6 11.0 %all-to-all-start.5 = ((s32[8,40,256]{2,1,0:T(8,128)}), s32[8,40,256]{2,1,0:T(8,128)S(1)}, u32[]{:S(2)}, u32[]{:S(2)}) async-start(s32[8,40,256]{2,1,0:T(8,128)} %shard_map.99), calls=%async_computation.5 | async-start | bytes 655360 | tf_op jit(solution)/shard_map/all_to_all | solution.py:819
